TPU v7x, 32 devices: a whole 2x2x4 slice. The times are simulated.
32 devices in a mesh: img: 16 (over z, x, core), seq: 2 (over y).
Axes of the slice: x: 2, y: 2, z: 4, core: 2. Of those that a mesh axis runs over, the one named last changes fastest.
Arguments:
- tokens: bfloat16 [16, 640, 768], P('img', 'seq'), may hold values from -6 to 6
- masked: int32 [16, 640], P('img', 'seq'), may hold values from 0 to 1, as said below
- out_grad: bfloat16 [16, 640, 768], P('img', 'seq'), may hold values from -6 to 6
- norm1_gain: float32 [768], replicated, may hold values from 0.5 to 1.5
- norm1_bias: float32 [768], replicated, may hold values from -3 to 3
- qkv_weight: bfloat16 [768, 2304], replicated, may hold values from -0.21875 to 0.21875
- query_bias: float32 [768], replicated, may hold values from -3 to 3
- value_bias: float32 [768], replicated, may hold values from -3 to 3
- rel_table: float32 [2212, 12], replicated, may hold values from -4 to 4
- proj_weight: bfloat16 [768, 768], replicated, may hold values from -1 to 1
- proj_bias: float32 [768], replicated, may hold values from -3 to 3
- scale1: float32 [768], replicated, may hold values from 0.1 to 1.9
- norm2_gain: float32 [768], replicated, may hold values from 0.5 to 1.5
- norm2_bias: float32 [768], replicated, may hold values from -3 to 3
- fc1_weight: bfloat16 [768, 3072], replicated, may hold values from -0.21875 to 0.21875
- fc1_bias: float32 [3072], replicated, may hold values from -3 to 3
- fc2_weight: bfloat16 [3072, 768], replicated, may hold values from -0.109375 to 0.109375
- fc2_bias: float32 [768], replicated, may hold values from -3 to 3
- scale2: float32 [768], replicated, may hold values from 0.1 to 1.9
Outputs:
- result: bfloat16 [16, 640, 768], P('img', 'seq')
- tokens_grad: bfloat16 [16, 640, 768], P('img', 'seq')
- norm1_gain_grad: float32 [768], replicated
- norm1_bias_grad: float32 [768], replicated
- qkv_weight_grad: float32 [768, 2304], P('img', 'seq')
- query_bias_grad: float32 [768], replicated
- value_bias_grad: float32 [768], replicated
- rel_table_grad: float32 [2212, 12], replicated
- proj_weight_grad: float32 [768, 768], P('img', 'seq')
- proj_bias_grad: float32 [768], replicated
- scale1_grad: float32 [768], replicated
- norm2_gain_grad: float32 [768], replicated
- norm2_bias_grad: float32 [768], replicated
- fc1_weight_grad: float32 [768, 3072], P('img', 'seq')
- fc1_bias_grad: float32 [3072], replicated
- fc2_weight_grad: float32 [3072, 768], P('img', 'seq')
- fc2_bias_grad: float32 [768], replicated
- scale2_grad: float32 [768], replicated
Inputs may be any that keep to these rules, and one draw needn't show every extreme that they name: masked is 0 at slot 0 and at slots past 24 * 24; each image has between 120 and 320 ones among its patches, and some image has exactly 320.
All inputs are finite; a program needn't handle non-finite values.
Results may differ from a plain program's by a relative error of at most 0.02.
Values may be sent and summed in bfloat16 or wider, within the bound.
No kernel may reach another device: no remote copies, remote signals or barrier semaphores. Data moves between devices by JAX's collectives and lax.ppermute only.
A program may use at most 320 MiB of HBM per device.

v0:
```python
import jax
import jax.numpy as jnp
from jax import lax
from jax.sharding import PartitionSpec as P

GRID = 24


EPSILON = 1e-06
NEGATIVE = -1e30
ROOT_HALF = 0.7071067811865476
GAUSS_NORM = 0.3989422804014327


def passed_along(value, axis, steps):
    count = lax.axis_size(axis)
    pairs = [(source, (source + steps) % count) for source in range(count)]
    return lax.ppermute(value, axis, pairs)


def gap_onehot():
    span_width = 2 * GRID - 1
    grid_ids = jnp.arange(GRID, dtype=jnp.int32)
    gaps = grid_ids[:, None, None] - grid_ids[None, :, None] + GRID - 1
    return (gaps == jnp.arange(span_width, dtype=jnp.int32)[None, None, :]).astype(jnp.float32)


def bias_full(rel_table, all_slots):
    highest = lax.Precision.HIGHEST
    span_width = 2 * GRID - 1
    far_index = span_width * span_width
    cells = GRID * GRID
    head_count = rel_table.shape[1]
    spare = all_slots - 1 - cells
    selector = gap_onehot()
    patch_table = rel_table[0:far_index].reshape(span_width, span_width, head_count)
    row_pick = jnp.einsum("pqa,abh->pqbh", selector, patch_table, precision=highest)
    spread = jnp.einsum("pqbh,rsb->hprqs", row_pick, selector, precision=highest)
    patch_bias = spread.reshape(head_count, cells, cells)
    patch_bias = jnp.concatenate(
        [
            patch_bias,
            jnp.broadcast_to(patch_bias[:, cells - 1 : cells, :], (head_count, spare, cells)),
        ],
        axis=1,
    )
    patch_bias = jnp.concatenate(
        [
            patch_bias,
            jnp.broadcast_to(
                patch_bias[:, :, cells - 1 : cells], (head_count, cells + spare, spare)
            ),
        ],
        axis=2,
    )
    top_row = jnp.broadcast_to(rel_table[far_index][:, None, None], (head_count, 1, all_slots - 1))
    left_col = jnp.broadcast_to(
        rel_table[far_index + 1][:, None, None], (head_count, all_slots - 1, 1)
    )
    corner = rel_table[far_index + 2][:, None, None]
    upper = jnp.concatenate([corner, top_row], axis=2)
    lower = jnp.concatenate([left_col, patch_bias], axis=2)
    return jnp.concatenate([upper, lower], axis=1)


def table_back(grad_full):
    highest = lax.Precision.HIGHEST
    span_width = 2 * GRID - 1
    cells = GRID * GRID
    head_count = grad_full.shape[0]
    corner = grad_full[:, 0, 0]
    far_grad = jnp.sum(grad_full[:, 0, 1:], axis=1)
    near_grad = jnp.sum(grad_full[:, 1:, 0], axis=1)
    patch_grad = grad_full[:, 1:, 1:]
    patch_grad = jnp.concatenate(
        [
            patch_grad[:, 0 : cells - 1, :],
            jnp.sum(patch_grad[:, cells - 1 :, :], axis=1, keepdims=True),
        ],
        axis=1,
    )
    patch_grad = jnp.concatenate(
        [
            patch_grad[:, :, 0 : cells - 1],
            jnp.sum(patch_grad[:, :, cells - 1 :], axis=2, keepdims=True),
        ],
        axis=2,
    )
    selector = gap_onehot()
    spread = patch_grad.reshape(head_count, GRID, GRID, GRID, GRID)
    row_sums = jnp.einsum("hprqs,rsb->pqbh", spread, selector, precision=highest)
    patch_table = jnp.einsum("pqa,pqbh->abh", selector, row_sums, precision=highest)
    tail = jnp.stack([far_grad, near_grad, corner], axis=0)
    return jnp.concatenate([patch_table.reshape(span_width * span_width, head_count), tail], axis=0)


def gelu_value(argument):
    return 0.5 * argument * (1.0 + lax.erf(argument * ROOT_HALF))


def gelu_slope(argument):
    return (
        0.5 * (1.0 + lax.erf(argument * ROOT_HALF))
        + argument * jnp.exp(-0.5 * argument * argument) * GAUSS_NORM
    )


def normalize(values, gain, shift):
    center = values - jnp.mean(values, axis=-1, keepdims=True)
    inverse = lax.rsqrt(jnp.mean(center * center, axis=-1, keepdims=True) + EPSILON)
    normed = center * inverse
    return (normed * gain + shift, normed, inverse)


def normalize_back(grad_out, normed, inverse, gain):
    signal = grad_out * gain
    inner = (
        signal
        - jnp.mean(signal, axis=-1, keepdims=True)
        - normed * jnp.mean(signal * normed, axis=-1, keepdims=True)
    )
    return (inverse * inner, jnp.sum(grad_out * normed, axis=0), jnp.sum(grad_out, axis=0))


def body(
    tokens,
    masked,
    out_grad,
    norm1_gain,
    norm1_bias,
    qkv_weight,
    query_bias,
    value_bias,
    rel_table,
    proj_weight,
    proj_bias,
    scale1,
    norm2_gain,
    norm2_bias,
    fc1_weight,
    fc1_bias,
    fc2_weight,
    fc2_bias,
    scale2,
):
    images, local_rows, model_width = tokens.shape
    head_count = rel_table.shape[1]
    head_size = model_width // head_count
    head_scale = head_size ** (-0.5)
    cycle_size = lax.axis_size("seq")
    position = lax.axis_index("seq")
    all_slots = local_rows * cycle_size
    key_pos = jnp.arange(all_slots, dtype=jnp.int32)
    position_bias = lax.dynamic_slice_in_dim(
        bias_full(rel_table, all_slots), position * local_rows, local_rows, 1
    )
    key_valid = key_pos <= GRID * GRID
    flat_rows = images * local_rows
    head_shape = (images, local_rows, head_count, head_size)
    inputs = tokens.astype(jnp.float32).reshape(flat_rows, model_width)
    normed1, centred1, inverse1 = normalize(inputs, norm1_gain, norm1_bias)
    hidden1 = normed1.astype(jnp.bfloat16)
    projected = jnp.dot(hidden1, qkv_weight, preferred_element_type=jnp.float32)
    queries = ((projected[:, 0:model_width] + query_bias) * head_scale).astype(jnp.bfloat16)
    keys_local = (
        projected[:, model_width : 2 * model_width]
        .astype(jnp.bfloat16)
        .reshape(images, local_rows, model_width)
    )
    values_local = (
        (projected[:, 2 * model_width :] + value_bias)
        .astype(jnp.bfloat16)
        .reshape(images, local_rows, model_width)
    )
    query_heads = queries.reshape(head_shape)

    def block_scores(key_block, offset):
        key_count = key_block.shape[1]
        key_heads = key_block.reshape(images, key_count, head_count, head_size)
        logits = jnp.einsum(
            "gqhd,gkhd->ghqk", query_heads, key_heads, preferred_element_type=jnp.float32
        )
        logits = logits + lax.dynamic_slice_in_dim(position_bias, offset, key_count, 2)[None]
        usable = lax.dynamic_slice_in_dim(key_valid, offset, key_count, 0)
        return (jnp.where(usable, logits, NEGATIVE), usable)

    row_max = jnp.full((images, head_count, local_rows), NEGATIVE, jnp.float32)
    key_block = lax.all_gather(keys_local, "seq", axis=1, tiled=True)
    value_block = lax.all_gather(values_local, "seq", axis=1, tiled=True)
    key_count = key_block.shape[1]
    scores, usable = block_scores(key_block, jnp.int32(0))
    new_max = jnp.maximum(row_max, jnp.max(scores, axis=-1))
    weights = jnp.where(usable, jnp.exp(scores - new_max[..., None]), 0.0)
    totals = jnp.sum(weights, axis=-1)
    value_heads = value_block.reshape(images, key_count, head_count, head_size)
    update = jnp.einsum(
        "ghqk,gkhd->gqhd",
        weights.astype(jnp.bfloat16),
        value_heads,
        preferred_element_type=jnp.float32,
    )
    weighted = update
    row_max, totals, weighted = (new_max, totals, weighted)
    log_total = row_max + jnp.log(totals)
    attended = weighted / jnp.transpose(totals, (0, 2, 1))[..., None]
    attn_low = attended.reshape(flat_rows, model_width).astype(jnp.bfloat16)
    mixed_out = jnp.dot(attn_low, proj_weight, preferred_element_type=jnp.float32) + proj_bias
    residual1 = inputs + scale1 * mixed_out
    normed2, centred2, inverse2 = normalize(residual1, norm2_gain, norm2_bias)
    hidden2 = normed2.astype(jnp.bfloat16)
    pre_act = jnp.dot(hidden2, fc1_weight, preferred_element_type=jnp.float32) + fc1_bias
    activated = gelu_value(pre_act).astype(jnp.bfloat16)
    ffn_out = jnp.dot(activated, fc2_weight, preferred_element_type=jnp.float32) + fc2_bias
    result = (residual1 + scale2 * ffn_out).astype(jnp.bfloat16).reshape(tokens.shape)
    cotangent = (out_grad.astype(jnp.float32) * masked.astype(jnp.float32)[..., None]).reshape(
        flat_rows, model_width
    )
    d_ffn = (scale2 * cotangent).astype(jnp.bfloat16)
    scale2_grad = jnp.sum(cotangent * ffn_out, axis=0)
    fc2_bias_grad = jnp.sum(d_ffn.astype(jnp.float32), axis=0)
    fc2_weight_grad = jnp.einsum("nf,nd->fd", activated, d_ffn, preferred_element_type=jnp.float32)
    d_act = jnp.einsum("nd,fd->nf", d_ffn, fc2_weight, preferred_element_type=jnp.float32)
    d_pre = (d_act * gelu_slope(pre_act)).astype(jnp.bfloat16)
    fc1_bias_grad = jnp.sum(d_pre.astype(jnp.float32), axis=0)
    fc1_weight_grad = jnp.einsum("nd,nf->df", hidden2, d_pre, preferred_element_type=jnp.float32)
    d_hidden2 = jnp.einsum("nf,df->nd", d_pre, fc1_weight, preferred_element_type=jnp.float32)
    back_two, norm2_gain_grad, norm2_bias_grad = normalize_back(
        d_hidden2, centred2, inverse2, norm2_gain
    )
    d_resid1 = cotangent + back_two
    d_mixed = (scale1 * d_resid1).astype(jnp.bfloat16)
    scale1_grad = jnp.sum(d_resid1 * mixed_out, axis=0)
    proj_bias_grad = jnp.sum(d_mixed.astype(jnp.float32), axis=0)
    proj_weight_grad = jnp.einsum(
        "nc,nd->cd", attn_low, d_mixed, preferred_element_type=jnp.float32
    )
    d_attn = jnp.einsum(
        "nd,cd->nc", d_mixed, proj_weight, preferred_element_type=jnp.float32
    ).astype(jnp.bfloat16)
    d_attn_heads = d_attn.reshape(head_shape)
    row_delta = jnp.transpose(
        jnp.sum(d_attn_heads.astype(jnp.float32) * attended, axis=-1), (0, 2, 1)
    )

    def back_block(key_block, value_block, offset):
        key_count = key_block.shape[1]
        scores, usable = block_scores(key_block, offset)
        prob_full = jnp.where(usable, jnp.exp(scores - log_total[..., None]), 0.0)
        prob_low = prob_full.astype(jnp.bfloat16)
        key_heads = key_block.reshape(images, key_count, head_count, head_size)
        value_heads = value_block.reshape(images, key_count, head_count, head_size)
        d_value = jnp.einsum(
            "ghqk,gqhd->gkhd", prob_low, d_attn_heads, preferred_element_type=jnp.float32
        )
        d_probs = jnp.einsum(
            "gqhd,gkhd->ghqk", d_attn_heads, value_heads, preferred_element_type=jnp.float32
        )
        d_scores = (prob_full * (d_probs - row_delta[..., None])).astype(jnp.bfloat16)
        d_query = jnp.einsum(
            "ghqk,gkhd->gqhd", d_scores, key_heads, preferred_element_type=jnp.float32
        )
        d_key = jnp.einsum(
            "ghqk,gqhd->gkhd", d_scores, query_heads, preferred_element_type=jnp.float32
        )
        table_part = jnp.sum(d_scores.astype(jnp.float32), axis=0)
        return (
            d_query,
            d_key.reshape(images, key_count, model_width),
            d_value.reshape(images, key_count, model_width),
            table_part,
        )

    def turn_grads(grad_pair):
        return (
            passed_along(grad_pair[0].astype(jnp.bfloat16), "seq", 1).astype(jnp.float32),
            passed_along(grad_pair[1].astype(jnp.bfloat16), "seq", 1).astype(jnp.float32),
        )

    def cycle_step(turn_index, cycle_state):
        key_block, value_block, d_key_acc, d_value_acc, d_query_acc, table_acc = cycle_state
        owner_rank = (position - turn_index) % cycle_size
        offset = owner_rank * local_rows
        d_query, d_key, d_value, table_part = back_block(key_block, value_block, offset)
        table_acc = lax.dynamic_update_slice_in_dim(table_acc, table_part, offset, 2)
        d_key_acc, d_value_acc = turn_grads((d_key_acc + d_key, d_value_acc + d_value))
        key_block, value_block = passed_along((key_block, value_block), "seq", 1)
        return (key_block, value_block, d_key_acc, d_value_acc, d_query_acc + d_query, table_acc)

    kv_zeros = jnp.zeros((images, local_rows, model_width), jnp.float32)
    initial = (
        keys_local,
        values_local,
        kv_zeros,
        kv_zeros,
        jnp.zeros(head_shape, jnp.float32),
        jnp.zeros((head_count, local_rows, all_slots), jnp.float32),
    )
    cycle_state = lax.fori_loop(0, cycle_size - 1, cycle_step, initial)
    key_block, value_block, d_key_acc, d_value_acc, d_query_acc, table_acc = cycle_state
    offset = (position + 1) % cycle_size * local_rows
    d_query, d_key, d_value, table_part = back_block(key_block, value_block, offset)
    table_acc = lax.dynamic_update_slice_in_dim(table_acc, table_part, offset, 2)
    d_key_all, d_value_all = turn_grads((d_key_acc + d_key, d_value_acc + d_value))
    d_query_all = d_query_acc + d_query
    d_query_low = d_query_all.reshape(flat_rows, model_width).astype(jnp.bfloat16) * head_scale
    d_key_low = d_key_all.reshape(flat_rows, model_width).astype(jnp.bfloat16)
    d_value_low = d_value_all.reshape(flat_rows, model_width).astype(jnp.bfloat16)
    d_qkv = jnp.concatenate([d_query_low, d_key_low, d_value_low], axis=1)
    qkv_weight_grad = jnp.einsum("nd,ne->de", hidden1, d_qkv, preferred_element_type=jnp.float32)
    query_bias_grad = jnp.sum(d_query_low.astype(jnp.float32), axis=0)
    value_bias_grad = jnp.sum(d_value_low.astype(jnp.float32), axis=0)
    d_hidden1 = jnp.einsum("ne,de->nd", d_qkv, qkv_weight, preferred_element_type=jnp.float32)
    back_one, norm1_gain_grad, norm1_bias_grad = normalize_back(
        d_hidden1, centred1, inverse1, norm1_gain
    )
    tokens_grad = (d_resid1 + back_one).astype(jnp.bfloat16).reshape(tokens.shape)
    grad_square = lax.dynamic_update_slice_in_dim(
        jnp.zeros((head_count, all_slots, all_slots), jnp.float32),
        table_acc,
        position * local_rows,
        1,
    )
    table_grad = table_back(grad_square)
    half_summed = (
        lax.psum_scatter(
            qkv_weight_grad.astype(jnp.bfloat16), "img", scatter_dimension=0, tiled=True
        ).astype(jnp.float32),
        lax.psum_scatter(
            proj_weight_grad.astype(jnp.bfloat16), "img", scatter_dimension=0, tiled=True
        ).astype(jnp.float32),
        lax.psum_scatter(
            fc1_weight_grad.astype(jnp.bfloat16), "img", scatter_dimension=0, tiled=True
        ).astype(jnp.float32),
        lax.psum_scatter(
            fc2_weight_grad.astype(jnp.bfloat16), "img", scatter_dimension=0, tiled=True
        ).astype(jnp.float32),
    )
    summed = (
        lax.psum_scatter(
            half_summed[0].astype(jnp.bfloat16), "seq", scatter_dimension=1, tiled=True
        ).astype(jnp.float32),
        lax.psum_scatter(
            half_summed[1].astype(jnp.bfloat16), "seq", scatter_dimension=1, tiled=True
        ).astype(jnp.float32),
        lax.psum_scatter(
            half_summed[2].astype(jnp.bfloat16), "seq", scatter_dimension=1, tiled=True
        ).astype(jnp.float32),
        lax.psum_scatter(
            half_summed[3].astype(jnp.bfloat16), "seq", scatter_dimension=1, tiled=True
        ).astype(jnp.float32),
    )
    smalls = lax.psum(
        (
            table_grad,
            norm1_gain_grad,
            norm1_bias_grad,
            query_bias_grad,
            value_bias_grad,
            proj_bias_grad,
            scale1_grad,
            norm2_gain_grad,
            norm2_bias_grad,
            fc1_bias_grad,
            fc2_bias_grad,
            scale2_grad,
        ),
        ("img", "seq"),
    )
    return (
        result,
        tokens_grad,
        smalls[1],
        smalls[2],
        summed[0],
        smalls[3],
        smalls[4],
        smalls[0],
        summed[1],
        smalls[5],
        smalls[6],
        smalls[7],
        smalls[8],
        summed[2],
        smalls[9],
        summed[3],
        smalls[10],
        smalls[11],
    )


def solution(mesh):
    in_specs = (
        P("img", "seq", None),
        P("img", "seq"),
        P("img", "seq", None),
        P(),
        P(),
        P(),
        P(),
        P(),
        P(),
        P(),
        P(),
        P(),
        P(),
        P(),
        P(),
        P(),
        P(),
        P(),
        P(),
    )
    out_specs = (
        P("img", "seq", None),
        P("img", "seq", None),
        P(),
        P(),
        P("img", "seq"),
        P(),
        P(),
        P(),
        P("img", "seq"),
        P(),
        P(),
        P(),
        P(),
        P("img", "seq"),
        P(),
        P("img", "seq"),
        P(),
        P(),
    )
    return jax.shard_map(body, mesh=mesh, in_specs=in_specs, out_specs=out_specs, check_vma=False)
```

profile of v0, /device:TPU:0, one launch (start us, length us, event | category | flops | bytes accessed | tf_op | source)
XLA Modules:
  0.0 837.6 jit_solution(17125029480029487338)
XLA Ops:
  14.1 3.0 collective-permute-start
  19.1 30.6 %all-gather = bf16[640,768]{1,0:T(8,128)(2,1)} all-gather(bf16[320,768]{1,0:T(8,128)(2,1)} %get-tuple-element.94), channel_id=2, replica_groups=mesh['img'=16,'seq'=2] {'seq'}, dimensions={0}, use_global_device_ids=true | all-gather | bytes 1474560 | tf_op jit(solution)/shard_map/all_gather | solution.py:189
  53.1 2.6 fusion.68
  55.6 39.4 %convolution_bitcast_fusion = f32[12,24,24,24,24]{3,4,0,1,2:T(8,128)} fusion(f32[24,24,47,12]{2,1,3,0:T(8,128)S(1)} %fusion.68, s32[24,24]{1,0:T(8,128)S(1)} %subtract_add_fusion), kind=kOutput, calls=%fused_computation | convolution fusion | flops 2245487104 | bytes 17227008 | tf_op jit(solution)/shard_map/pqbh,rsb->hprqs/dot_general | solution.py:38
  95.0 82.5 %copy.99 = f32[12,24,24,24,24]{4,3,2,1,0:T(8,128)} copy(f32[12,24,24,24,24]{3,4,0,1,2:T(8,128)} %convolution_bitcast_fusion) | data formatting | bytes 31850496 | tf_op jit(solution)/shard_map/pqbh,rsb->hprqs/transpose | solution.py:38
  177.5 55.6 %reshape.371 = f32[12,576,576]{2,1,0:T(8,128)} reshape(f32[12,24,24,24,24]{4,3,2,1,0:T(8,128)} %copy.99) | data formatting | bytes 31850496 | tf_op jit(solution)/shard_map/reshape | solution.py:39
  234.3 5.5 fusion.12
  241.9 15.0 %all-gather.1 = bf16[640,768]{1,0:T(8,128)(2,1)} all-gather(bf16[320,768]{1,0:T(8,128)(2,1)} %slice.96), channel_id=3, replica_groups=mesh['img'=16,'seq'=2] {'seq'}, dimensions={0}, use_global_device_ids=true | all-gather | bytes 1474560 | tf_op jit(solution)/shard_map/all_gather | solution.py:188
  261.2 2.9 broadcast_in_dim.124
  264.2 13.5 %maximum_maximum_fusion = f32[12,640,640]{2,1,0:T(8,128)S(1)} fusion(f32[12,639,63]{2,1,0:T(8,128)S(1)} %broadcast_in_dim.128, f32[12,63,576]{2,1,0:T(8,128)S(1)} %copy-done.12, f32[12,576,576]{2,1,0:T(8,128)} %reshape.371, f32[12,639,1]{2,1,0:T(8,128)} %broadcast_in_dim.124, f32[12,1,639]{2,1,0:T(1,128)S(1)} %broadcast_in_dim.67, ...), kind=kLoop, calls=%fused_computation.1 | loop fusion | flops 24576000 | bytes 39321600 | tf_op jit(solution)/shard_map/concatenate | solution.py:63
  277.7 6.1 fusion.85
  283.8 3.5 copy-done.1
  290.8 7.0 fusion
  297.9 4.2 fusion.86
  305.7 4.2 convert_reduce_fusion
  309.9 2.6 multiply_reduce_fusion.1
  312.5 3.4 fusion.53
  320.3 2.8 convolution_convert_fusion.5
  335.0 6.5 exponential_select_fusion.2
  341.6 3.8 fusion.87
  351.0 4.3 fusion.25
  361.5 8.3 exponential_select_fusion.1
  371.9 6.9 fusion.88
  382.1 2.6 copy.107
  387.4 4.5 fusion.17
  392.0 2.6 copy.109
  398.4 3.0 fusion.89
  406.0 2.6 collective-permute-done.5
  408.6 5.8 convolution_convert_fusion
  414.6 6.6 convolution_convert_fusion.1
  421.9 7.0 convolution_convert_fusion.2
  428.9 4.7 broadcast_in_dim.131
  433.7 30.8 %dynamic_update_slice.10 = f32[12,320,640]{2,1,0:T(8,128)} dynamic-update-slice(f32[12,320,640]{2,1,0:T(8,128)} %broadcast_in_dim.131, f32[12,320,320]{2,1,0:T(8,128)} %get-tuple-element.113, s32[]{:T(128)} %constant.102.clone.1, s32[]{:T(128)} %constant.102.clone.1, s32[]{:T(128)S(6)} %select_n.66) | dynamic-update-slice | bytes 9830404 | tf_op jit(solution)/shard_map/while/body/eval_jaxpr/dynamic_update_slice | solution.py:284
  464.5 34.0 %dynamic_update_slice.11 = f32[12,320,640]{2,1,0:T(8,128)} dynamic-update-slice(f32[12,320,640]{2,1,0:T(8,128)} %dynamic_update_slice.10, f32[12,320,320]{2,1,0:T(8,128)} %get-tuple-element.115, s32[]{:T(128)} %constant.102.clone.1, s32[]{:T(128)} %constant.102.clone.1, s32[]{:T(128)S(6)} %select_n.72) | dynamic-update-slice | bytes 9830404 | tf_op jit(solution)/shard_map/dynamic_update_slice | solution.py:302
  498.5 10.3 %broadcast_in_dim.136 = f32[12,640,640]{2,1,0:T(8,128)} broadcast(f32[]{:T(128)} %constant.96.clone.1), dimensions={} | broadcast | bytes 19660804 | tf_op jit(solution)/shard_map/broadcast_in_dim | solution.py:318
  508.7 4.3 constant_dynamic-update-slice_fusion
  513.1 14.6 %slice.72 = f32[12,575,639]{2,1,0:T(8,128)} slice(f32[12,640,640]{2,1,0:T(8,128)} %constant_dynamic-update-slice_fusion), slice={[0:12], [1:576], [1:640]} | slice | bytes 35272800 | tf_op jit(solution)/shard_map/slice | solution.py:77
  532.2 12.2 %slice_maximum_fusion = f32[12,576,575]{2,1,0:T(8,128)} fusion(f32[12,1,639]{2,1,0:T(1,128)} %broadcast_in_dim.137, f32[12,575,639]{2,1,0:T(8,128)} %slice.72), kind=kLoop, calls=%fused_computation.2 | loop fusion | flops 3974400 | bytes 33564672 | tf_op jit(solution)/shard_map/concatenate | solution.py:75
  544.5 4.7 fusion.13
  549.2 3.2 copy.111
  554.5 13.2 %pad_maximum_fusion = f32[12,576,576]{2,1,0:T(8,128)} fusion(f32[12,576,1]{2,1,0:T(8,128)} %copy.111, f32[12,576,575]{2,1,0:T(8,128)} %slice_maximum_fusion), kind=kLoop, calls=%fused_computation.3 | loop fusion | flops 3981312 | bytes 31850496 | tf_op jit(solution)/shard_map/concatenate | solution.py:82
  567.7 52.3 %reshape.382 = f32[12,24,24,24,24]{4,3,2,1,0:T(8,128)} reshape(f32[12,576,576]{2,1,0:T(8,128)} %pad_maximum_fusion) | data formatting | bytes 31850496 | tf_op jit(solution)/shard_map/reshape | solution.py:90
  622.0 67.0 %fusion.65 = f32[47,12,24,24,1]{0,3,4,2,1:T(8,128)} fusion(f32[12,24,24,24,24]{4,3,2,1,0:T(8,128)} %reshape.382, s32[24,24]{1,0:T(8,128)S(1)} %copy-done.25), kind=kOutput, calls=%fused_computation.112 | convolution fusion | flops 2245487104 | bytes 17227008 | tf_op jit(solution)/shard_map/hprqs,rsb->pqbh/dot_general | solution.py:91
  690.6 4.2 fusion.31
  700.5 3.3 slice_reduce_fusion
  707.6 3.7 fusion.47
  713.6 41.7 %all-reduce = (f32[768]{0:T(1024)}, f32[768]{0:T(1024)}, f32[768]{0:T(1024)}, f32[768]{0:T(1024)}, f32[768]{0:T(1024)}, /*index=5*/f32[768]{0:T(1024)}, f32[768]...) all-reduce(f32[768]{0:T(1024)} %get-tuple-element.65, ...), channel_id=1, replica_groups=mesh['img'=16,'seq'=2] {'img','seq'}, use_global_device_ids=true, to_apply=%region_12.13 | all-reduce | flops 10752 | bytes 86016 | tf_op jit(solution)/shard_map/psum | solution.py:352
  766.7 61.6 %all-reduce.3.cloned.1.call-done = f32[2212,12]{0,1:T(8,128)} async-done(((f32[2212,12]{0,1:T(8,128)}), f32[2212,12]{0,1:T(8,128)}) %all-reduce.3.cloned.1.call-update) | async-done | bytes 106192 | tf_op jit(solution)/shard_map/psum | solution.py:352
  (244 shorter events, 105.9 us)
Async XLA Ops:
  8.0 522.4 %reduce-scatter.17.cloned.1.call-start = ((), (), s32[]{:S(2)}) async-start(), calls=%async_computation.10 | async-start | bytes 1253376 | tf_op jit(solution)/shard_map/reduce_scatter | solution.py:328
  10.8 6.3 copy-start.41
  10.8 6.3 copy-start.42
  14.1 345.3 %collective-permute-start = (bf16[1,320,768]{2,1,0:T(8,128)(2,1)}, bf16[1,320,768]{2,1,0:T(8,128)(2,1)}, u32[]{:S(2)}, u32[]{:S(2)}) collective-permute-start(bf16[1,320,768]{2,1,0:T(8,128)(2,1)} %slice_bitcast_fusion), channel_id=1, source_target_pairs={{0,1},{1,0},{2,3},{3,2},{4,5},{5,4},{6,7},{7,6},{8,9},{9,8},{10,11... | collective-permute-start | bytes 1474568 | tf_op jit(solution)/shard_map/while/body/eval_jaxpr/ppermute | solution.py:18
  18.2 351.6 %collective-permute-start.1 = (bf16[1,320,768]{2,1,0:T(8,128)(2,1)}, bf16[1,320,768]{2,1,0:T(8,128)(2,1)}, u32[]{:S(2)}, u32[]{:S(2)}) collective-permute-start(bf16[1,320,768]{2,1,0:T(8,128)(2,1)} %bitcast.27), channel_id=1, source_target_pairs={{0,1},{1,0},{2,3},{3,2},{4,5},{5,4},{6,7},{7,6},{8,9},{9,8},{10,11... | collective-permute-start | bytes 1474568 | tf_op jit(solution)/shard_map/while/body/eval_jaxpr/ppermute | solution.py:18
  18.2 76.8 %copy-start.24 = (s32[24,24]{1,0:T(8,128)}, s32[24,24]{1,0:T(8,128)S(1)}, u32[]{:S(2)}) copy-start(s32[24,24]{1,0:T(8,128)S(1)} %subtract_add_fusion) | copy-start | bytes 6916
  234.2 5.5 copy-start.11
  234.2 5.5 copy-start.51
  264.2 13.5 %copy-start.8 = (bf16[320,768]{0,1:T(8,128)(2,1)S(1)}, bf16[320,768]{0,1:T(8,128)(2,1)}, u32[]{:S(2)}) copy-start(bf16[320,768]{0,1:T(8,128)(2,1)} %copy.96) | copy-start | bytes 1474564
  264.2 13.5 %copy-start.20 = (bf16[640,768]{0,1:T(8,128)(2,1)S(1)}, bf16[640,768]{0,1:T(8,128)(2,1)}, u32[]{:S(2)}) copy-start(bf16[640,768]{0,1:T(8,128)(2,1)} %copy.97) | copy-start | bytes 2949124
  277.7 9.6 %copy-start.1 = (f32[12,640,640]{2,1,0:T(8,128)}, f32[12,640,640]{2,1,0:T(8,128)S(1)}, u32[]{:S(2)}) copy-start(f32[12,640,640]{2,1,0:T(8,128)S(1)} %maximum_maximum_fusion) | copy-start | bytes 58982404
  290.8 7.0 copy-start.3
  290.8 7.0 copy-start.29
  297.8 5.5 slice-start
  297.9 7.7 slice-start.2
  303.0 9.5 %copy-start.19 = (f32[320,768]{1,0:T(8,128)}, f32[320,768]{1,0:T(8,128)S(1)}, u32[]{:S(2)}) copy-start(f32[320,768]{1,0:T(8,128)S(1)} %get-tuple-element.92) | copy-start | bytes 2949124
  303.3 9.2 %copy-start.49 = (f32[320]{0:T(512)}, f32[320]{0:T(512)S(1)}, u32[]{:S(2)}) copy-start(f32[320]{0:T(512)S(1)} %add_rsqrt_fusion) | copy-start | bytes 3844
  303.4 9.1 %copy-start.48 = (f32[320]{0:T(512)}, f32[320]{0:T(512)S(1)}, u32[]{:S(2)}) copy-start(f32[320]{0:T(512)S(1)} %convert_reduce_fusion.6) | copy-start | bytes 3844
  305.6 6.9 copy-start.61
  320.2 232.1 %reduce-scatter.15.cloned.1.call-start = ((), (), s32[]{:S(2)}) async-start(), calls=%async_computation.8 | async-start | bytes 3760128 | tf_op jit(solution)/shard_map/reduce_scatter | solution.py:325
  335.0 6.6 copy-start.27
  335.0 6.6 copy-start.13
  335.0 6.6 copy-start.21
  341.6 5.8 copy-start.9
  351.0 33.7 %collective-permute-start.2 = (bf16[1,320,768]{2,1,0:T(8,128)(2,1)}, bf16[1,320,768]{2,1,0:T(8,128)(2,1)}, u32[]{:S(2)}, u32[]{:S(2)}) collective-permute-start(bf16[1,320,768]{2,1,0:T(8,128)(2,1)} %copy.106), channel_id=1, source_target_pairs={{0,1},{1,0},{2,3},{3,2},{4,5},{5,4},{6,7},{7,6},{8,9},{9,8},{10,11... | collective-permute-start | bytes 1474568 | tf_op jit(solution)/shard_map/while/body/eval_jaxpr/ppermute | solution.py:18
  357.4 37.2 %collective-permute-start.4 = (bf16[1,320,768]{2,1,0:T(8,128)(2,1)}, bf16[1,320,768]{2,1,0:T(8,128)(2,1)}, u32[]{:S(2)}, u32[]{:S(2)}) collective-permute-start(bf16[1,320,768]{2,1,0:T(8,128)(2,1)} %copy.108), channel_id=1, source_target_pairs={{0,1},{1,0},{2,3},{3,2},{4,5},{5,4},{6,7},{7,6},{8,9},{9,8},{10,11... | collective-permute-start | bytes 1474568 | tf_op jit(solution)/shard_map/while/body/eval_jaxpr/ppermute | solution.py:18
  371.9 8.5 %copy-start.10 = (bf16[320,768]{0,1:T(8,128)(2,1)S(1)}, bf16[320,768]{0,1:T(8,128)(2,1)}, u32[]{:S(2)}) copy-start(bf16[320,768]{0,1:T(8,128)(2,1)} %copy.96) | copy-start | bytes 1474564
  386.9 19.1 %collective-permute-start.3 = (bf16[1,320,768]{2,1,0:T(8,128)(2,1)}, bf16[1,320,768]{2,1,0:T(8,128)(2,1)}, u32[]{:S(2)}, u32[]{:S(2)}) collective-permute-start(bf16[1,320,768]{2,1,0:T(8,128)(2,1)} %add_convert_fusion.1), channel_id=1, source_target_pairs={{0,1},{1,0},{2,3},{3,2},{4,5},{5,4},{6,7},{7,6},{8,9},{9,8},{10,11... | collective-permute-start | bytes 1474568 | tf_op jit(solution)/shard_map/ppermute | solution.py:18
  394.6 6.9 copy-start.7
  394.6 6.9 copy-start.16
  396.9 11.7 %collective-permute-start.5 = (bf16[1,320,768]{2,1,0:T(8,128)(2,1)}, bf16[1,320,768]{2,1,0:T(8,128)(2,1)}, u32[]{:S(2)}, u32[]{:S(2)}) collective-permute-start(bf16[1,320,768]{2,1,0:T(8,128)(2,1)} %add_convert_fusion), channel_id=1, source_target_pairs={{0,1},{1,0},{2,3},{3,2},{4,5},{5,4},{6,7},{7,6},{8,9},{9,8},{10,11... | collective-permute-start | bytes 1474568 | tf_op jit(solution)/shard_map/ppermute | solution.py:18
  401.5 7.2 copy-start.33
  401.5 7.1 copy-start.39
  401.5 7.1 copy-start.43
  414.5 205.5 %reduce-scatter.23.cloned.1.call-start = ((), (), s32[]{:S(2)}) async-start(), calls=%async_computation.13 | async-start | bytes 5013504 | tf_op jit(solution)/shard_map/reduce_scatter | solution.py:334
  421.2 269.1 %reduce-scatter.19.cloned.1.call-start = ((), (), s32[]{:S(2)}) async-start(), calls=%async_computation.11 | async-start | bytes 5013504 | tf_op jit(solution)/shard_map/reduce_scatter | solution.py:331
  428.9 326.5 %reduce-scatter.27.cloned.1.call-start = ((), (), s32[]{:S(2)}) async-start(), calls=%async_computation.15 | async-start | bytes 294912
  498.4 10.3 %copy-start.4 = (f32[12,320,640]{2,1,0:T(8,128)S(1)}, f32[12,320,640]{2,1,0:T(8,128)}, u32[]{:S(2)}) copy-start(f32[12,320,640]{2,1,0:T(8,128)} %dynamic_update_slice.11) | copy-start | bytes 29491204
  532.2 226.2 %reduce-scatter.25.cloned.1.call-start = ((), (), s32[]{:S(2)}) async-start(), calls=%async_computation.14 | async-start | bytes 884736
  532.2 12.3 %copy-start.26 = (f32[12,1,639]{2,1,0:T(1,128)S(1)}, f32[12,1,639]{2,1,0:T(1,128)}, u32[]{:S(2)}) copy-start(f32[12,1,639]{2,1,0:T(1,128)} %broadcast_in_dim.137) | copy-start | bytes 92020
  554.4 207.3 %reduce-scatter.29.cloned.1.call-start = ((), (), s32[]{:S(2)}) async-start(), calls=%async_computation.16 | async-start | bytes 589824
  567.7 54.2 %copy-start.25 = (s32[24,24]{1,0:T(8,128)S(1)}, s32[24,24]{1,0:T(8,128)}, u32[]{:S(2)}) copy-start(s32[24,24]{1,0:T(8,128)} %copy-done.24) | copy-start | bytes 6916
  621.9 143.2 %reduce-scatter.21.cloned.1.call-start = ((), (), s32[]{:S(2)}) async-start(), calls=%async_computation.12 | async-start | bytes 442368 | tf_op jit(solution)/shard_map/reduce_scatter | solution.py:345
  690.4 138.0 %all-reduce.3.cloned.1.call-start = ((), (), s32[]{:S(2)}) async-start(), calls=%async_computation.9 | async-start | bytes 294912 | tf_op jit(solution)/shard_map/psum | solution.py:352
  694.9 10.2 %copy-start.31 = (f32[12,64]{1,0:T(8,128)S(1)}, f32[12,64]{1,0:T(8,128)}, u32[]{:S(2)}) copy-start(f32[12,64]{1,0:T(8,128)} %get-tuple-element.109) | copy-start | bytes 9220
  707.5 6.1 copy-start.35
  707.5 6.1 copy-start.36
  707.5 6.1 copy-start.45
  (34 other events, 94.0 us)
Sparse Core Ops, SparseCore 0:
  320.4 58.4 reduce-scatter.16
  414.6 68.5 reduce-scatter.14
  487.1 74.4 reduce-scatter.22
  565.8 74.5 reduce-scatter.18
  643.1 9.9 reduce-scatter.26
  655.2 15.2 reduce-scatter.24
  672.8 13.1 reduce-scatter.28
  690.5 12.3 reduce-scatter.20
Sparse Core Ops, SparseCore 1:
  707.6 120.7 all-reduce.2
where the time goes:
time: 848 us; the launch traced here: 838 us
  local copies, waits for them, and re-layouts  366 us (43%)
  matrix products  210 us (25%)
  blocking collectives  87.4 us (10%)
  other arithmetic  85.1 us (10%)
  waiting for transfers between devices  64.4 us (8%)
  between operations  16.7 us (2%)
    transpose x1, local copies, waits for them, and re-layouts, bias_full(): jnp.einsum('pqbh,rsb->hprqs', row_pick, selector, precision=highest)  82.5 us
    dot_general x1, matrix products, table_back(): jnp.einsum('hprqs,rsb->pqbh', spread, selector, precision=highest)  67 us
    psum x1, waiting for transfers between devices, body(): lax.psum((table_grad, norm1_gain_grad, norm1_bias_grad, query_bias_grad,...  61.6 us
    reshape x1, local copies, waits for them, and re-layouts, bias_full(): patch_bias = spread.reshape(head_count, cells, cells)  55.6 us
    reshape x1, local copies, waits for them, and re-layouts, table_back(): spread = patch_grad.reshape(head_count, GRID, GRID, GRID, GRID)  52.3 us
    psum x1, blocking collectives, body(): lax.psum((table_grad, norm1_gain_grad, norm1_bias_grad, query_bias_grad,...  41.7 us
    dot_general x1, matrix products, bias_full(): jnp.einsum('pqbh,rsb->hprqs', row_pick, selector, precision=highest)  39.4 us
    dynamic_update_slice x1, local copies, waits for them, and re-layouts, body(): lax.dynamic_update_slice_in_dim(table_acc, table_part, offset, 2)  34 us
  transfers between devices with their start and end apart: 15, of which 2 were waited for; matrix products, arithmetic and copies ran while one was open for 77% of the time, Pallas kernels for 0%

commit v1 on v0

--- a/solution.py
+++ b/solution.py
@@ -1,6 +1,11 @@
+import functools
+
 import jax
 import jax.numpy as jnp
+import numpy as np
 from jax import lax
+from jax.experimental import pallas as pl
+from jax.experimental.pallas import tpu as pltpu
 from jax.sharding import PartitionSpec as P
 
 GRID = 24
@@ -122,7 +127,7 @@
     return (inverse * inner, jnp.sum(grad_out * normed, axis=0), jnp.sum(grad_out, axis=0))
 
 
-def body(
+def general_body(
     tokens,
     masked,
     out_grad,
@@ -388,6 +393,766 @@
     )
 
 
+LANES = 128
+STRIP = 24
+STRIP_WIDTH = 1280
+MEGA = 1 << 20
+NT = (((1,), (1,)), ((), ()))
+TN = (((0,), (0,)), ((), ()))
+NN = (((1,), (0,)), ((), ()))
+BF = jnp.bfloat16
+F32 = jnp.float32
+
+
+def mul(left, right, dims=NN):
+    return lax.dot_general(left, right, dims, preferred_element_type=F32)
+
+
+def bits_of(img, seq):
+    ring = img >> 2
+    gray = ring ^ (ring >> 1)
+    return {"core": img & 1, "x": (img >> 1) & 1, "za": gray & 1, "zb": gray >> 1, "y": seq}
+
+
+def label_of(img, seq, order):
+    bits = bits_of(img, seq)
+    total = 0
+    for name in order:
+        total = total * 2 + bits[name]
+    return total
+
+
+def swap_pairs(name):
+    order = ("core", "x", "za", "zb", "y")
+    where = {label_of(img, seq, order): img * 2 + seq for img in range(16) for seq in range(2)}
+    flip = 1 << (len(order) - 1 - order.index(name))
+    return [(device, where[label ^ flip]) for label, device in where.items()]
+
+
+def swapped(value, name):
+    return lax.ppermute(value, ("img", "seq"), swap_pairs(name))
+
+
+def reduce_scatter(keep, send, order):
+    terms = [keep, swapped(send, order[0])]
+    half = keep.shape[0]
+    for name in order[1:]:
+        half //= 2
+        out = sum(term[half : 2 * half].astype(F32) for term in terms).astype(BF)
+        terms = [term[:half] for term in terms] + [swapped(out, name)]
+    return sum(term[0].astype(F32) for term in terms)
+
+
+def layer_norm(values):
+    center = values - jnp.mean(values, axis=-1, keepdims=True)
+    inverse = lax.rsqrt(jnp.mean(center * center, axis=-1, keepdims=True) + EPSILON)
+    return center * inverse, inverse
+
+
+def layer_norm_back(grad_out, normed, inverse, gain):
+    signal = grad_out * gain
+    return inverse * (
+        signal
+        - jnp.mean(signal, axis=-1, keepdims=True)
+        - normed * jnp.mean(signal * normed, axis=-1, keepdims=True)
+    )
+
+
+def spec(block, index):
+    return pl.BlockSpec(block, index)
+
+
+def full(shape):
+    zeros = (0,) * len(shape)
+    return pl.BlockSpec(shape, lambda *_: zeros)
+
+
+def run(kernel, place, grid, in_specs, out_specs, out_shapes, scratch, operands, flops, vmem=48):
+    moved = sum(int(np.prod(o.shape)) * o.dtype.itemsize for o in (*operands, *out_shapes))
+    return pl.pallas_call(
+        kernel,
+        grid_spec=pltpu.PrefetchScalarGridSpec(
+            num_scalar_prefetch=1,
+            grid=grid,
+            in_specs=in_specs,
+            out_specs=out_specs,
+            scratch_shapes=scratch,
+        ),
+        out_shape=out_shapes,
+        compiler_params=pltpu.CompilerParams(vmem_limit_bytes=vmem * MEGA),
+        cost_estimate=pl.CostEstimate(flops=flops, bytes_accessed=moved, transcendentals=0),
+    )(place, *operands)
+
+
+def shape(dims, dtype):
+    return jax.ShapeDtypeStruct(dims, dtype)
+
+
+def qkv_kernel(place, own, other, vecs, weight, qb, vb, qkv_out, hidden_out):
+    step = pl.program_id(0)
+    rows = own.shape[0]
+
+    @pl.when(step == 0)
+    def _():
+        for source, side in ((own, place[0]), (other, 1 - place[0])):
+            normed, _ = layer_norm(source[...].astype(F32))
+            low = (normed * vecs[0:1, :] + vecs[1:2, :]).astype(BF)
+            hidden_out[pl.ds(pl.multiple_of(side * rows, 64), rows), :] = low
+
+    wide = mul(hidden_out[...], weight[...])
+    shift = jnp.where(step == 0, qb[...], jnp.where(step == 2, vb[...], 0.0))
+    factor = jnp.where(step == 0, 0.125, 1.0)
+    qkv_out[0] = ((wide + shift) * factor).astype(BF)
+
+
+def window(strip, block):
+    off = (STRIP - block) * STRIP
+    base = off // LANES * LANES
+    held = strip[:, base : base + 6 * LANES]
+    if off - base:
+        held = pltpu.roll(held, 6 * LANES - (off - base), axis=1)
+    return held[:, : 5 * LANES]
+
+
+CHUNKS = tuple((start * 144, 144) for start in range(4)) + ((576, 64),)
+
+
+def attend_kernel(place, qkv, strips, even_mask, own_out, send_out, expo_out, inv_out, strip, attended):
+    slots = qkv.shape[1]
+    half = slots // 2
+    side = place[0]
+    lane = lax.broadcasted_iota(jnp.int32, (1, LANES), 1)
+    first = lane < LANES // 2
+    masks = (jnp.where(first, 1.0, 0.0).astype(BF), jnp.where(first, 0.0, 1.0).astype(BF))
+    keys = [qkv[1] * m for m in masks]
+    values = [qkv[2] * m for m in masks]
+    picks = even_mask[...] > 0.5
+    for head in range(2):
+        rolled = [
+            pltpu.roll(
+                jnp.broadcast_to(strips[0, head, par : par + 1, :], (STRIP, STRIP_WIDTH)),
+                1,
+                axis=1,
+                stride=1,
+                stride_axis=0,
+            )
+            for par in range(2)
+        ]
+        strip[head] = jnp.where(picks, rolled[0], rolled[1])
+    block_lane = lax.broadcasted_iota(jnp.int32, (STRIP, LANES), 1)
+    block_row = lax.broadcasted_iota(jnp.int32, (STRIP, LANES), 0)
+    for start, count in CHUNKS:
+        query = qkv[0, start : start + count, :]
+        total = None
+        scale = None
+        for head in range(2):
+            far = strips[0, head, 0:1, 1152:1153]
+            near = strips[0, head, 0:1, 1153:1154]
+            corner = strips[0, head, 0:1, 1154:1155]
+            biases = []
+            for block in range(start // STRIP, -(-(start + count) // STRIP)):
+                if start == 576:
+                    row = window(strip.at[head, 0:8, :], STRIP)[0:1, :]
+                    piece = jnp.broadcast_to(row, (count, 5 * LANES))
+                    ids = lax.broadcasted_iota(jnp.int32, (count, LANES), 1)
+                else:
+                    piece = window(strip.at[head], block)
+                    ids = block_lane
+                left = jnp.where(ids == 0, near, piece[:, :LANES])
+                if block == 0:
+                    piece = jnp.concatenate(
+                        [
+                            jnp.where(
+                                block_row == 0, jnp.where(ids == 0, corner, far), left
+                            )
+                        ]
+                        + [
+                            jnp.where(block_row == 0, far, piece[:, n * LANES : (n + 1) * LANES])
+                            for n in range(1, 4)
+                        ]
+                        + [
+                            jnp.where(
+                                ids > 64, NEGATIVE, jnp.where(block_row == 0, far, piece[:, 4 * LANES :])
+                            )
+                        ],
+                        axis=1,
+                    )
+                else:
+                    piece = jnp.concatenate(
+                        [
+                            left,
+                            piece[:, LANES : 4 * LANES],
+                            jnp.where(ids > 64, NEGATIVE, piece[:, 4 * LANES :]),
+                        ],
+                        axis=1,
+                    )
+                biases.append(piece)
+                if start == 576:
+                    break
+            scores = mul(query, keys[head], NT) + jnp.concatenate(biases, axis=0)
+            top = jnp.max(scores, axis=1, keepdims=True)
+            expo = jnp.exp(scores - top)
+            inverse = 1.0 / jnp.sum(expo, axis=1, keepdims=True)
+            low = expo.astype(BF)
+            expo_out[head, start : start + count, :] = low
+            part = mul(low, values[head]) * inverse
+            total = part if head == 0 else total + part
+            spread = jnp.broadcast_to(inverse, (count, LANES))
+            scale = spread if head == 0 else jnp.where(first, scale, spread)
+        attended[start : start + count, :] = total
+        inv_out[start : start + count, :] = scale
+    own_out[...] = attended[pl.ds(pl.multiple_of(side * half, 64), half), :].astype(BF)
+    send_out[...] = attended[pl.ds(pl.multiple_of((1 - side) * half, 64), half), :].astype(BF)
+
+
+def attend_back_kernel(
+    place, qkv, expo, attn_own, attn_send, grad_own, grad_other, inv, even_mask,
+    dqkv_out, strip_out, grad_all, attn_all, d_scores, strip, dq_all,
+):
+    slots = qkv.shape[1]
+    half = slots // 2
+    here = pl.ds(pl.multiple_of(place[0] * half, 64), half)
+    there = pl.ds(pl.multiple_of((1 - place[0]) * half, 64), half)
+    lane = lax.broadcasted_iota(jnp.int32, (1, LANES), 1)
+    first = lane < LANES // 2
+    masks = (jnp.where(first, 1.0, 0.0).astype(BF), jnp.where(first, 0.0, 1.0).astype(BF))
+    scaled = grad_own[...].astype(F32) * inv[here, :]
+    grad_all[here, :] = scaled
+    attn_all[here, :] = scaled * attn_own[...].astype(F32)
+    scaled = grad_other[...].astype(F32) * inv[there, :]
+    grad_all[there, :] = scaled
+    attn_all[there, :] = scaled * attn_send[...].astype(F32)
+    keys = [qkv[1] * m for m in masks]
+    values = [qkv[2] * m for m in masks]
+    block_lane = lax.broadcasted_iota(jnp.int32, (STRIP, LANES), 1)
+    block_row = lax.broadcasted_iota(jnp.int32, (STRIP, LANES), 0)
+    strip[...] = jnp.zeros_like(strip)
+    columns = [jnp.zeros((8, LANES), F32) for _ in range(2)]
+    tops = [None, None]
+    zeros = jnp.zeros((STRIP, LANES), F32)
+    for start, count in CHUNKS:
+        grads = grad_all[start : start + count, :].astype(BF)
+        products = attn_all[start : start + count, :]
+        total = None
+        for head in range(2):
+            chosen = first if head == 0 else jnp.logical_not(first)
+            delta = jnp.sum(jnp.where(chosen, products, 0.0), axis=1, keepdims=True)
+            d_probs = mul(grads, values[head], NT)
+            d_score = expo[head, start : start + count, :].astype(F32) * (d_probs - delta)
+            low = d_score.astype(BF)
+            d_scores[head, start : start + count, :] = low
+            part = mul(low, keys[head])
+            total = part if head == 0 else total + part
+            if start == 576:
+                for tile in range(count // 8):
+                    columns[head] = columns[head] + d_score[8 * tile : 8 * tile + 8, :LANES]
+                line = jnp.sum(d_score, axis=0, keepdims=True)
+                line = jnp.concatenate([jnp.where(lane == 0, 0.0, line[:, :LANES]), line[:, LANES:]], axis=1)
+                strip[head, 0:1, : 5 * LANES] = strip[head, 0:1, : 5 * LANES] + line
+            else:
+                for block in range(start // STRIP, (start + count) // STRIP):
+                    at = block * STRIP - start
+                    piece = d_score[at : at + STRIP, :]
+                    left = piece[:, :LANES]
+                    rest = piece[:, LANES:]
+                    if block == 0:
+                        tops[head] = piece[0:1, :]
+                        left = jnp.where(block_row == 0, 0.0, left)
+                        rest = jnp.concatenate(
+                            [
+                                jnp.where(block_row == 0, 0.0, rest[:, n * LANES : (n + 1) * LANES])
+                                for n in range(4)
+                            ],
+                            axis=1,
+                        )
+                    columns[head] = columns[head] + left[0:8] + left[8:16] + left[16:24]
+                    piece = jnp.concatenate(
+                        [jnp.where(block_lane == 0, 0.0, left), rest, zeros], axis=1
+                    )
+                    off = (STRIP - block) * STRIP
+                    base = off // LANES * LANES
+                    if off - base:
+                        piece = pltpu.roll(piece, off - base, axis=1)
+                    strip[head, :, base : base + 6 * LANES] = (
+                        strip[head, :, base : base + 6 * LANES] + piece
+                    )
+        dq_all[start : start + count, :] = total
+    dqkv_out[0] = dq_all[...].astype(BF) * BF(0.125)
+    d_key = None
+    d_value = None
+    low_grads = grad_all[...].astype(BF)
+    for head in range(2):
+        part = mul(d_scores[head], qkv[0] * masks[head], TN)
+        d_key = part if head == 0 else d_key + part
+        part = mul(expo[head], low_grads * masks[head], TN)
+        d_value = part if head == 0 else d_value + part
+    dqkv_out[1] = d_key.astype(BF)
+    dqkv_out[2] = d_value.astype(BF)
+    picks = even_mask[...] > 0.5
+    row_id = lax.broadcasted_iota(jnp.int32, (STRIP, STRIP_WIDTH), 0)
+    wide_lane = lax.broadcasted_iota(jnp.int32, (1, STRIP_WIDTH), 1)
+    for head in range(2):
+        held = strip[head]
+        lines = []
+        for par in range(2):
+            part = jnp.where(picks, held, 0.0) if par == 0 else jnp.where(picks, 0.0, held)
+            part = pltpu.roll(part, STRIP_WIDTH - 1, axis=1)
+            for bit in (1, 2, 4, 8, 16):
+                part = jnp.where(
+                    (row_id & bit) > 0, pltpu.roll(part, STRIP_WIDTH - bit, axis=1), part
+                )
+            lines.append(jnp.sum(part, axis=0, keepdims=True))
+        near = jnp.sum(jnp.where(lane == 0, columns[head], 0.0)).reshape(1, 1)
+        corner = tops[head][:, 0:1]
+        far = jnp.sum(tops[head], axis=1, keepdims=True) - corner
+        line = lines[0]
+        line = jnp.where(wide_lane >= 1152, 0.0, line)
+        line = jnp.where(wide_lane == 1152, far, line)
+        line = jnp.where(wide_lane == 1153, near, line)
+        line = jnp.where(wide_lane == 1154, corner, line)
+        strip_out[0, head, 0:1, :] = line
+        strip_out[0, head, 1:2, :] = lines[1]
+
+
+def ffn_kernel(
+    place, tokens, cot, attn_own, attn_other, vecs, proj, fc1, fc1_bias, fc2, proj_own, proj_other,
+    act_out, d_pre_out, fc1_bias_out, hidden_out, resid_out, d_ffn_out, attn_out, d_mixed_out, d_resid_out,
+    grad_own_out, grad_send_out, small_out, mixed_held, d_hidden,
+):
+    step = pl.program_id(0)
+    width = attn_own.shape[1]
+
+    @pl.when(step == 0)
+    def _():
+        attn_out[:, pl.ds(pl.multiple_of(place[0] * width, LANES), width)] = attn_own[...]
+        attn_out[:, pl.ds(pl.multiple_of((1 - place[0]) * width, LANES), width)] = attn_other[...]
+        mixed = mul(attn_out[...], proj[...]) + vecs[2:3, :]
+        mixed_held[...] = mixed
+        resid = tokens[...].astype(F32) + vecs[3:4, :] * mixed
+        resid_out[...] = resid
+        normed, _ = layer_norm(resid)
+        hidden_out[...] = (normed * vecs[4:5, :] + vecs[5:6, :]).astype(BF)
+        d_ffn = (vecs[7:8, :] * cot[...].astype(F32)).astype(BF)
+        d_ffn_out[...] = d_ffn
+        d_hidden[...] = jnp.zeros_like(d_hidden)
+
+    pre = mul(hidden_out[...], fc1[...]) + fc1_bias[...]
+    gate = 0.5 * (1.0 + lax.erf(pre * ROOT_HALF))
+    act_out[...] = (pre * gate).astype(BF)
+    slope = gate + pre * jnp.exp(-0.5 * pre * pre) * GAUSS_NORM
+    d_pre = (mul(d_ffn_out[...], fc2[...], NT) * slope).astype(BF)
+    d_pre_out[...] = d_pre
+    fc1_bias_out[...] = jnp.sum(d_pre.astype(F32), axis=0, keepdims=True)
+    d_hidden[...] += mul(d_pre, fc1[...], NT)
+
+    @pl.when(step == pl.num_programs(0) - 1)
+    def _():
+        grad = d_hidden[...]
+        mixed = mixed_held[...]
+        normed, inverse = layer_norm(resid_out[...])
+        d_resid = cot[...].astype(F32) + layer_norm_back(grad, normed, inverse, vecs[4:5, :])
+        d_resid_out[...] = d_resid
+        d_mixed = (vecs[3:4, :] * d_resid).astype(BF)
+        d_mixed_out[...] = d_mixed
+        small_out[0:1, :] = jnp.sum(grad * normed, axis=0, keepdims=True)
+        small_out[1:2, :] = jnp.sum(grad, axis=0, keepdims=True)
+        small_out[2:3, :] = jnp.sum(d_resid * mixed, axis=0, keepdims=True)
+        small_out[3:4, :] = jnp.sum(d_mixed.astype(F32), axis=0, keepdims=True)
+        small_out[4:5, :] = jnp.sum(d_ffn_out[...].astype(F32), axis=0, keepdims=True)
+        small_out[5:8, :] = jnp.zeros((3, small_out.shape[1]), F32)
+        grad_own_out[...] = mul(d_mixed, proj_own[...], NT).astype(BF)
+        grad_send_out[...] = mul(d_mixed, proj_other[...], NT).astype(BF)
+
+
+def fc2_grad_kernel(place, act, d_ffn, keep_out, send_out, held, *, y_shift, rest):
+    step = pl.program_id(0)
+    held[...] = mul(act[...], d_ffn[...], TN)
+    core = place[1]
+    for pair in range(2):
+        for seq in range(2):
+            at = rest(pair, step, seq) ^ place[2]
+            columns = slice(384 * seq, 384 * seq + 384)
+            low = pl.multiple_of(384 * pair + 192 * core, 64)
+            high = pl.multiple_of(384 * pair + 192 * (1 - core), 64)
+            keep_out[at] = held[pl.ds(low, 192), columns].astype(BF)
+            send_out[at] = held[pl.ds(high, 192), columns].astype(BF)
+
+
+def fc1_grad_kernel(place, hidden, d_pre, attn, d_mixed, keep_out, send_out, held, *, rest):
+    step = pl.program_id(0)
+    core = place[1]
+    held[...] = mul(hidden[...], d_pre[...], TN)
+    seq = step // 2
+    lanes = pl.ds(pl.multiple_of((step % 2) * 768, LANES), 768)
+    for pair in range(8):
+        at = rest(pair % 2, pair // 2, seq) ^ place[3]
+        low = pl.multiple_of(96 * pair + 48 * core, 16)
+        high = pl.multiple_of(96 * pair + 48 * (1 - core), 16)
+        keep_out[at, :, lanes] = held[pl.ds(low, 48), :].astype(BF)
+        send_out[at, :, lanes] = held[pl.ds(high, 48), :].astype(BF)
+
+    @pl.when(step == pl.num_programs(0) - 1)
+    def _():
+        held[...] = mul(attn[...], d_mixed[...], TN)
+        for pair in range(8):
+            low = pl.multiple_of(96 * pair + 48 * core, 16)
+            high = pl.multiple_of(96 * pair + 48 * (1 - core), 16)
+            for side in range(2):
+                at = rest(pair % 2, pair // 2, side) ^ place[3]
+                columns = slice(384 * side, 384 * side + 384)
+                keep_out[at, :, 1536:1920] = held[pl.ds(low, 48), columns].astype(BF)
+                send_out[at, :, 1536:1920] = held[pl.ds(high, 48), columns].astype(BF)
+
+
+def result_kernel(place, act, fc2, resid, cot, vecs, result_out, small_out, total):
+    step = pl.program_id(0)
+
+    @pl.when(step == 0)
+    def _():
+        total[...] = jnp.zeros_like(total)
+
+    total[...] += mul(act[...], fc2[...])
+
+    @pl.when(step == pl.num_programs(0) - 1)
+    def _():
+        ffn = total[...] + vecs[6:7, :]
+        result_out[...] = (resid[...] + vecs[7:8, :] * ffn).astype(BF)
+        small_out[0:1, :] = jnp.sum(cot[...].astype(F32) * ffn, axis=0, keepdims=True)
+        small_out[1:8, :] = jnp.zeros((7, small_out.shape[1]), F32)
+
+
+def hidden1_grad_kernel(place, dqkv, weight, own, other, keep_out, send_out, small_out, total):
+    step = pl.program_id(0)
+    rows = own.shape[0]
+    here = pl.ds(pl.multiple_of(place[0] * rows, 64), rows)
+    there = pl.ds(pl.multiple_of((1 - place[0]) * rows, 64), rows)
+
+    @pl.when(step == 0)
+    def _():
+        total[...] = jnp.zeros_like(total)
+        small_out[...] = jnp.zeros_like(small_out)
+
+    grads = dqkv[0]
+    total[...] += mul(grads, weight[...], NT)
+    line = jnp.sum(grads.astype(F32), axis=0, keepdims=True)
+
+    @pl.when(step == 0)
+    def _():
+        small_out[2:3, :384] = line
+
+    @pl.when(step == 2)
+    def _():
+        small_out[2:3, 384:] = line
+        mine = total[here, :]
+        theirs = total[there, :]
+        keep_out[...] = mine
+        send_out[...] = theirs.astype(BF)
+        normed_mine, _ = layer_norm(own[...].astype(F32))
+        normed_theirs, _ = layer_norm(other[...].astype(F32))
+        small_out[0:1, :] = jnp.sum(mine * normed_mine, axis=0, keepdims=True) + jnp.sum(
+            theirs * normed_theirs, axis=0, keepdims=True
+        )
+        small_out[1:2, :] = jnp.sum(mine, axis=0, keepdims=True) + jnp.sum(
+            theirs, axis=0, keepdims=True
+        )
+
+
+def qkv_grad_kernel(place, hidden, dqkv, keep_out, send_out, held, *, rest):
+    step = pl.program_id(0)
+    core = place[1]
+    held[...] = mul(hidden[...], dqkv[0], TN)
+    lanes = pl.ds(pl.multiple_of(step * 384, LANES), 384)
+    for pair in range(8):
+        at = rest(pair % 2, pair // 2, 0) ^ place[4]
+        low = pl.multiple_of(96 * pair + 48 * core, 16)
+        high = pl.multiple_of(96 * pair + 48 * (1 - core), 16)
+        keep_out[at, :, lanes] = held[pl.ds(low, 48), :].astype(BF)
+        send_out[at, :, lanes] = held[pl.ds(high, 48), :].astype(BF)
+
+
+def tokens_grad_kernel(place, keep, recv, own, d_resid, vecs, grad_out):
+    grad = keep[...] + recv[...].astype(F32)
+    normed, inverse = layer_norm(own[...].astype(F32))
+    back = layer_norm_back(grad, normed, inverse, vecs[0:1, :])
+    grad_out[...] = (d_resid[...] + back).astype(BF)
+
+
+def rest_label(order):
+    def rest(x_bit, ring, seq):
+        gray = ring ^ (ring >> 1)
+        bits = {"x": x_bit, "za": gray & 1, "zb": gray >> 1, "y": seq}
+        total = 0
+        for name in order[1:]:
+            total = total * 2 + bits[name]
+        return total
+
+    return rest
+
+
+ORDER_A = ("core", "x", "y", "za", "zb")
+ORDER_B = ("core", "za", "zb", "x", "y")
+ORDER_Q = ("core", "x", "za", "zb")
+
+
+def strips_of(table, seq, heads):
+    own = lax.dynamic_slice_in_dim(table, seq * heads, heads, 1).T
+    span = 2 * GRID - 1
+    cells = span * span
+    patch = own[:, :cells][:, ::-1].reshape(heads, span, span)
+    patch = jnp.pad(patch, ((0, 0), (0, 1), (0, 1))).reshape(heads, 24, 2, 48)
+    even = jnp.concatenate(
+        [patch[:, :, 0].reshape(heads, 1152), own[:, cells:], jnp.zeros((heads, 125), F32)], axis=1
+    )
+    odd = jnp.pad(patch[:, :, 1].reshape(heads, 1152), ((0, 0), (24, 104)))
+    return jnp.stack([even, odd], axis=1).reshape(heads // 2, 2, 2, STRIP_WIDTH)
+
+
+def table_of(strips):
+    heads = strips.shape[0]
+    span = 2 * GRID - 1
+    even = strips[:, 0, :1152].reshape(heads, 24, 1, 48)
+    odd = strips[:, 1, 24:1176].reshape(heads, 24, 1, 48)
+    patch = jnp.concatenate([even, odd], axis=2).reshape(heads, 48, 48)[:, :span, :span]
+    flat = patch.reshape(heads, span * span)[:, ::-1]
+    return jnp.concatenate([flat, strips[:, 0, 1152:1155]], axis=1)
+
+
+def even_places():
+    lane = np.arange(STRIP_WIDTH)[None, :]
+    row = np.arange(STRIP)[:, None]
+    turn = (lane - 1) // STRIP
+    return np.where(row == 0, turn % 2 == 0, turn % 2 == 1).astype(np.float32)
+
+
+def split_body(
+    tokens,
+    masked,
+    out_grad,
+    norm1_gain,
+    norm1_bias,
+    qkv_weight,
+    query_bias,
+    value_bias,
+    rel_table,
+    proj_weight,
+    proj_bias,
+    scale1,
+    norm2_gain,
+    norm2_bias,
+    fc1_weight,
+    fc1_bias,
+    fc2_weight,
+    fc2_bias,
+    scale2,
+):
+    _, rows, width = tokens.shape
+    slots = 2 * rows
+    heads = rel_table.shape[1] // 2
+    pairs = heads // 2
+    share = width // 2
+    hidden = fc1_weight.shape[1]
+    seq = lax.axis_index("seq")
+    img = lax.axis_index("img")
+    core = img & 1
+    ring = img >> 2
+    x_bit = (img >> 1) & 1
+    place = jnp.stack(
+        [
+            seq,
+            core,
+            rest_label(ORDER_A)(x_bit, ring, seq),
+            rest_label(ORDER_B)(x_bit, ring, seq),
+            rest_label(ORDER_Q)(x_bit, ring, seq),
+        ]
+    ).astype(jnp.int32)
+    own = tokens.reshape(rows, width)
+    other = swapped(own, "y")
+    cot = (out_grad.astype(F32) * masked.astype(F32)[..., None]).astype(BF).reshape(rows, width)
+    vecs = jnp.stack(
+        [norm1_gain, norm1_bias, proj_bias, scale1, norm2_gain, norm2_bias, fc2_bias, scale2]
+    )
+    strips = strips_of(rel_table, seq, heads)
+    even_mask = jnp.asarray(even_places())
+
+    qkv, hidden1 = run(
+        qkv_kernel, place, (3,),
+        [
+            full((rows, width)), full((rows, width)), full((8, width)),
+            spec((width, share), lambda t, p: (0, 2 * t + p[0])),
+            spec((1, share), lambda t, p: (0, p[0])), spec((1, share), lambda t, p: (0, p[0])),
+        ],
+        [spec((1, slots, share), lambda t, p: (t, 0, 0)), full((slots, width))],
+        [shape((3, slots, share), BF), shape((slots, width), BF)],
+        [],
+        (own, other, vecs, qkv_weight, query_bias.reshape(1, width), value_bias.reshape(1, width)),
+        2 * slots * width * 3 * share,
+    )
+    pair_rows = spec((slots, LANES), lambda n, p: (0, n))
+    pair_half = spec((rows, LANES), lambda n, p: (0, n))
+    pair_qkv = spec((3, slots, LANES), lambda n, p: (0, 0, n))
+    pair_expo = spec((2, slots, slots), lambda n, p: (n, 0, 0))
+    pair_strip = spec((1, 2, 2, STRIP_WIDTH), lambda n, p: (n, 0, 0, 0))
+    attn_own, attn_send, expo, inv = run(
+        attend_kernel, place, (pairs,),
+        [pair_qkv, pair_strip, full((STRIP, STRIP_WIDTH))],
+        [pair_half, pair_half, pair_expo, pair_rows],
+        [
+            shape((rows, share), BF), shape((rows, share), BF),
+            shape((heads, slots, slots), BF), shape((slots, share), F32),
+        ],
+        [pltpu.VMEM((2, STRIP, STRIP_WIDTH), F32), pltpu.VMEM((slots, LANES), F32)],
+        (qkv, strips, even_mask),
+        16 * slots * slots * 64 * heads,
+    )
+    attn_other = swapped(attn_send, "y")
+    parts = 4
+    part = hidden // parts
+    whole = full((rows, width))
+    sliced = spec((rows, part), lambda c, p: (0, c))
+    (
+        act, d_pre, fc1_bias_part, hidden2, resid, d_ffn, attn_low, d_mixed, d_resid,
+        grad_own, grad_send, small_ffn,
+    ) = run(
+        ffn_kernel, place, (parts,),
+        [
+            whole, whole, full((rows, share)), full((rows, share)), full((8, width)),
+            full((width, width)), spec((width, part), lambda c, p: (0, c)),
+            spec((1, part), lambda c, p: (0, c)), spec((part, width), lambda c, p: (c, 0)),
+            spec((share, width), lambda c, p: (p[0], 0)), spec((share, width), lambda c, p: (1 - p[0], 0)),
+        ],
+        [
+            sliced, sliced, spec((1, part), lambda c, p: (0, c)), whole, whole, whole, whole, whole, whole,
+            full((rows, share)), full((rows, share)), full((8, width)),
+        ],
+        [
+            shape((rows, hidden), BF), shape((rows, hidden), BF), shape((1, hidden), F32),
+            shape((rows, width), BF), shape((rows, width), F32), shape((rows, width), BF),
+            shape((rows, width), BF), shape((rows, width), BF), shape((rows, width), F32),
+            shape((rows, share), BF), shape((rows, share), BF), shape((8, width), F32),
+        ],
+        [pltpu.VMEM((rows, width), F32), pltpu.VMEM((rows, width), F32)],
+        (
+            own, cot, attn_own, attn_other, vecs, proj_weight, fc1_weight, fc1_bias.reshape(1, hidden),
+            fc2_weight, proj_weight, proj_weight,
+        ),
+        2 * rows * width * (3 * hidden + 2 * width),
+    )
+    grad_other = swapped(grad_send, "y")
+    block = (16, 192, share)
+    keep_a, send_a = run(
+        functools.partial(fc2_grad_kernel, y_shift=0, rest=rest_label(ORDER_A)), place, (parts,),
+        [sliced, whole], [full(block), full(block)], [shape(block, BF), shape(block, BF)],
+        [pltpu.VMEM((part, width), F32)], (act, d_ffn), 2 * rows * width * hidden,
+    )
+    block = (16, 48, 5 * share)
+    keep_b, send_b = run(
+        functools.partial(fc1_grad_kernel, rest=rest_label(ORDER_B)), place, (parts,),
+        [whole, sliced, whole, whole], [full(block), full(block)],
+        [shape(block, BF), shape(block, BF)],
+        [pltpu.VMEM((width, part), F32)], (hidden2, d_pre, attn_low, d_mixed),
+        2 * rows * width * (hidden + width),
+    )
+    result, small_result = run(
+        result_kernel, place, (parts,),
+        [sliced, spec((part, width), lambda c, p: (c, 0)), whole, whole, full((8, width))],
+        [whole, full((8, width))],
+        [shape((rows, width), BF), shape((8, width), F32)],
+        [pltpu.VMEM((rows, width), F32)], (act, fc2_weight, resid, cot, vecs),
+        2 * rows * width * hidden,
+    )
+    dqkv, strip_grad = run(
+        attend_back_kernel, place, (pairs,),
+        [
+            pair_qkv, pair_expo, pair_half, pair_half, pair_half, pair_half, pair_rows,
+            full((STRIP, STRIP_WIDTH)),
+        ],
+        [pair_qkv, pair_strip],
+        [shape((3, slots, share), BF), shape((pairs, 2, 2, STRIP_WIDTH), F32)],
+        [
+            pltpu.VMEM((slots, LANES), F32), pltpu.VMEM((slots, LANES), F32),
+            pltpu.VMEM((2, slots, slots), BF), pltpu.VMEM((2, STRIP, STRIP_WIDTH), F32),
+            pltpu.VMEM((slots, LANES), F32),
+        ],
+        (qkv, expo, attn_own, attn_send, grad_own, grad_other, inv, even_mask),
+        32 * slots * slots * 64 * heads,
+    )
+    third = spec((1, slots, share), lambda t, p: (t, 0, 0))
+    dh_keep, dh_send, small_last = run(
+        hidden1_grad_kernel, place, (3,),
+        [third, spec((width, share), lambda t, p: (0, 2 * t + p[0])), whole, whole],
+        [whole, whole, full((8, width))],
+        [shape((rows, width), F32), shape((rows, width), BF), shape((8, width), F32)],
+        [pltpu.VMEM((slots, width), F32)], (dqkv, qkv_weight, own, other),
+        2 * slots * width * 3 * share,
+    )
+    dh_recv = swapped(dh_send, "y")
+    block = (8, 48, 3 * share)
+    keep_q, send_q = run(
+        functools.partial(qkv_grad_kernel, rest=rest_label(ORDER_Q)), place, (3,),
+        [full((slots, width)), third], [full(block), full(block)],
+        [shape(block, BF), shape(block, BF)],
+        [pltpu.VMEM((width, share), F32)], (hidden1, dqkv), 2 * slots * width * 3 * share,
+    )
+    tokens_grad = run(
+        tokens_grad_kernel, place, (1,),
+        [whole, whole, whole, whole, full((8, width))], [whole],
+        [shape((rows, width), BF)], [], (dh_keep, dh_recv, own, d_resid, vecs), 0,
+    )[0]
+
+    fc2_grad = reduce_scatter(keep_a, send_a, ORDER_A)
+    fc1_proj = reduce_scatter(keep_b, send_b, ORDER_B)
+    qkv_part = reduce_scatter(keep_q, send_q, ORDER_Q)
+    fc1_grad = fc1_proj[:, : 4 * share]
+    proj_grad = fc1_proj[:, 4 * share :]
+    on_left = seq == 0
+    given = jnp.where(on_left, qkv_part[:, 2 * share :], qkv_part[:, :share]).astype(BF)
+    taken = swapped(given, "y").astype(F32)
+    qkv_grad = jnp.where(
+        on_left,
+        jnp.concatenate([qkv_part[:, :share], taken, qkv_part[:, share : 2 * share]], axis=1),
+        jnp.concatenate([qkv_part[:, share : 2 * share], taken, qkv_part[:, 2 * share :]], axis=1),
+    )
+
+    both = jnp.concatenate(
+        [small_ffn[:5], small_result[:1], fc1_bias_part.reshape(4, width), small_last[:2]], axis=0
+    )
+    single = jnp.concatenate([strip_grad.reshape(-1, LANES), small_last[2].reshape(-1, LANES)], axis=0)
+    cut = both.size // LANES
+    packed = jnp.concatenate([both.reshape(-1, LANES), single], axis=0)
+    for name in ("core", "x", "za", "zb"):
+        packed = packed + swapped(packed, name)
+    mate = swapped(packed, "y")
+    both = (packed[:cut] + mate[:cut]).reshape(-1, width)
+    ends = [jnp.where(on_left, packed[cut:], mate[cut:]), jnp.where(on_left, mate[cut:], packed[cut:])]
+    count = strip_grad.size // LANES
+    table_grad = jnp.concatenate(
+        [table_of(end[:count].reshape(heads, 2, STRIP_WIDTH)) for end in ends], axis=0
+    ).T
+    tail = [end[count:].reshape(2, share) for end in ends]
+    query_bias_grad = jnp.concatenate([tail[0][0], tail[1][0]])
+    value_bias_grad = jnp.concatenate([tail[0][1], tail[1][1]])
+    return (
+        result.reshape(tokens.shape),
+        tokens_grad.reshape(tokens.shape),
+        both[10],
+        both[11],
+        qkv_grad,
+        query_bias_grad,
+        value_bias_grad,
+        table_grad,
+        proj_grad,
+        both[3],
+        both[2],
+        both[0],
+        both[1],
+        fc1_grad,
+        both[6:10].reshape(hidden),
+        fc2_grad,
+        both[4],
+        both[5],
+    )
+
+
 def solution(mesh):
     in_specs = (
         P("img", "seq", None),
@@ -430,4 +1195,6 @@
         P(),
         P(),
     )
+    sizes = dict(mesh.shape)
+    body = split_body if (sizes["img"], sizes["seq"]) == (16, 2) else general_body
     return jax.shard_map(body, mesh=mesh, in_specs=in_specs, out_specs=out_specs, check_vma=False)

time: 848 us -> 246 us (0.29)
  the two profiles are of different devices: /device:TPU:0 before, /device:TPU:8 now
where the time goes in v1:
time: 246 us; the launch traced here: 245 us
  waiting for transfers between devices  88.3 us (36%)
  Pallas kernels  77.2 us (31%)
  local copies, waits for them, and re-layouts  32 us (13%)
  other arithmetic  23.4 us (10%)
  starting transfers between devices  22.4 us (9%)
    ppermute x24, waiting for transfers between devices, swapped(): return lax.ppermute(value, ('img', 'seq'), swap_pairs(name))  88.3 us
    pallas_call x10, Pallas kernels, run(): pl.pallas_call(kernel, grid_spec=pltpu.PrefetchScalarGridSpec(num_scalar_...  77.2 us
    ppermute x24, starting transfers between devices, swapped(): return lax.ppermute(value, ('img', 'seq'), swap_pairs(name))  22.4 us
    unnamed x78, local copies, waits for them, and re-layouts  19.2 us
    convert_element_type x11, other arithmetic, reduce_scatter(): out = sum((term[half:2 * half].astype(F32) for term in terms)).astype(BF)  14.1 us
    another operation x9, local copies, waits for them, and re-layouts, split_body(): jnp.stack([norm1_gain, norm1_bias, proj_bias, scale1, norm2_gain, norm2_b...  5.56 us
  transfers between devices with their start and end apart: 24, of which 11 were waited for; matrix products, arithmetic and copies ran while one was open for 15% of the time, Pallas kernels for 11%

profile of v1, /device:TPU:8, one launch (start us, length us, event | category | flops | bytes accessed | tf_op | source)
XLA Modules:
  0.0 244.6 jit_solution(5310364906016982986)
XLA Ops:
  0.7 1.6 collective-permute-start
  9.3 1.3 reverse
  12.6 1.3 collective-permute-done.other
  13.9 4.8 %shard_map.331 = (bf16[3,640,384]{2,1,0:T(8,128)(2,1)S(1)}, bf16[640,768]{1,0:T(8,128)(2,1)S(1)}) custom-call(s32[5]{0:T(128)S(1)} %stack.57.place, bf16[320,768]{1,0:T(8,128)(2,1)S(1)} %bitcast.66, bf16[320,768]{1,0:T(8,128)(2,1)S(1)} %collective-permute-done.other, f32[8,768]{1,0:T(8,128)S(1)} %stack.66.vecs, bf16[768,2304]{1,0:T(8,128)(2,1)} %weight.3, ...), custom_call_target="tpu_custom_call" | custom-call | flops 1132462080 | bytes 7010304 | tf_op jit(solution)/shard_map/pallas_call | solution.py:472
  18.7 12.4 %shard_map.332 = (bf16[320,384]{1,0:T(8,128)(2,1)S(1)}, bf16[320,384]{1,0:T(8,128)(2,1)S(1)}, bf16[6,640,640]{2,1,0:T(8,128)(2,1)}, f32[640,384]{1,0:T(8,128)S(1)}) custom-call(s32[5]{0:T(128)S(1)} %stack.57.place, bf16[3,640,384]{2,1,0:T(8,128)(2,1)S(1)} %get-tuple-element.49.qkv, f32[3,2,2,1280]{3,2,1,0:T(2,128)S(1)} %pad_maximum_fusion.7.strips, ...), custom_call_target="tpu_custom_call" | custom-call | flops 2516582400 | bytes 8048640 | tf_op jit(solution)/shard_map/pallas_call | solution.py:472
  31.2 1.5 collective-permute-start.1
  32.9 5.1 %collective-permute-done.1.attn_other = bf16[320,384]{1,0:T(8,128)(2,1)S(1)} collective-permute-done((bf16[320,384]{1,0:T(8,128)(2,1)S(1)}, bf16[320,384]{1,0:T(8,128)(2,1)S(1)}, u32[]{:S(2)}, u32[]{:S(2)}) %collective-permute-start.1) | collective-permute-done | bytes 245792 | tf_op jit(solution)/shard_map/ppermute | solution.py:433
  38.0 13.7 %shard_map.333 = (bf16[320,3072]{1,0:T(8,128)(2,1)}, bf16[320,3072]{1,0:T(8,128)(2,1)}, f32[1,3072]{1,0:T(1,128)S(1)}, bf16[320,768]{1,0:T(8,128)(2,1)S(1)}, f32...) custom-call(s32[5]{0:T(128)S(1)} %stack.57.place, ...), custom_call_target="tpu_custom_call" | custom-call | flops 5284823040 | bytes 22880256 | tf_op jit(solution)/shard_map/pallas_call | solution.py:472
  54.9 1.6 collective-permute-start.2
  56.5 1.5 copy-done.3
  58.0 6.0 %shard_map.334 = (bf16[320,768]{1,0:T(8,128)(2,1)}, f32[8,768]{1,0:T(8,128)S(1)}) custom-call(s32[5]{0:T(128)S(1)} %stack.57.place, bf16[320,3072]{1,0:T(8,128)(2,1)S(1)} %copy-done.3, bf16[3072,768]{1,0:T(8,128)(2,1)} %fc2.3, f32[320,768]{1,0:T(8,128)S(1)} %get-tuple-element.53.resid, bf16[320,768]{1,0:T(8,128)(2,1)S(1)} %fusion.cot, f32[8,768]{1,0:T(8,128)S(1)} %stack.66.vecs), custom_call_target="tpu_custom_call" | custom-call | flops 1509949440 | bytes 8699904 | tf_op jit(solution)/shard_map/pallas_call | solution.py:472
  65.3 1.2 copy-done.27
  68.4 14.0 %shard_map.335 = (bf16[3,640,384]{2,1,0:T(8,128)(2,1)S(1)}, f32[3,2,2,1280]{3,2,1,0:T(2,128)S(1)}) custom-call(s32[5]{0:T(128)S(1)} %stack.57.place, bf16[3,640,384]{2,1,0:T(8,128)(2,1)S(1)} %get-tuple-element.49.qkv, bf16[6,640,640]{2,1,0:T(8,128)(2,1)} %get-tuple-element.55.expo, bf16[320,384]{1,0:T(8,128)(2,1)S(1)} %copy-done.29, ...), custom_call_target="tpu_custom_call" | custom-call | flops 5033164800 | bytes 10014720 | tf_op jit(solution)/shard_map/pallas_call | solution.py:472
  82.4 6.4 %shard_map.336 = (f32[320,768]{1,0:T(8,128)S(1)}, bf16[320,768]{1,0:T(8,128)(2,1)}, f32[8,768]{1,0:T(8,128)S(1)}) custom-call(s32[5]{0:T(128)S(1)} %stack.57.place, bf16[3,640,384]{2,1,0:T(8,128)(2,1)S(1)} %get-tuple-element.59.dqkv, bf16[768,2304]{1,0:T(8,128)(2,1)} %weight.3, bf16[320,768]{1,0:T(8,128)(2,1)S(1)} %bitcast.68, ...), custom_call_target="tpu_custom_call" | custom-call | flops 1132462080 | bytes 7495680 | tf_op jit(solution)/shard_map/pallas_call | solution.py:472
  93.1 8.0 %shard_map.339 = (bf16[16,48,1920]{2,1,0:T(8,128)(2,1)}, bf16[16,48,1920]{2,1,0:T(8,128)(2,1)}) custom-call(s32[5]{0:T(128)S(1)} %stack.57.place, bf16[320,768]{1,0:T(8,128)(2,1)S(1)} %copy-done.21, bf16[320,3072]{1,0:T(8,128)(2,1)S(1)} %copy-done.17, bf16[320,768]{1,0:T(8,128)(2,1)S(1)} %copy-done.23, bf16[320,768]{1,0:T(8,128)(2,1)S(1)} %copy-done.25), custom_call_target="tpu_custom_call" | custom-call | flops 1887436800 | bytes 9338880 | tf_op jit(solution)/shard_map/pallas_call | solution.py:472
  102.0 1.6 collective-permute-start.5
  103.6 3.2 %collective-permute-done.5 = f32[198,128]{1,0:T(8,128)S(1)} collective-permute-done((f32[198,128]{1,0:T(8,128)S(1)}, f32[198,128]{1,0:T(8,128)S(1)}, u32[]{:S(2)}, u32[]{:S(2)}) %collective-permute-start.5) | collective-permute-done | bytes 101408 | tf_op jit(solution)/shard_map/ppermute | solution.py:433
  107.4 4.1 %collective-permute-done.6 = f32[198,128]{1,0:T(8,128)S(1)} collective-permute-done((f32[198,128]{1,0:T(8,128)S(1)}, f32[198,128]{1,0:T(8,128)S(1)}, u32[]{:S(2)}, u32[]{:S(2)}) %collective-permute-start.6) | collective-permute-done | bytes 101408 | tf_op jit(solution)/shard_map/ppermute | solution.py:433
  111.5 1.6 collective-permute-start.7
  113.2 1.5 copy-done.4
  115.7 6.0 %shard_map.340 = (bf16[16,192,384]{2,1,0:T(8,128)(2,1)S(1)}, bf16[16,192,384]{2,1,0:T(8,128)(2,1)}) custom-call(s32[5]{0:T(128)S(1)} %stack.57.place, bf16[320,3072]{1,0:T(8,128)(2,1)S(1)} %copy-done.4, bf16[320,768]{1,0:T(8,128)(2,1)S(1)} %copy-done.19), custom_call_target="tpu_custom_call" | custom-call | flops 1509949440 | bytes 7176192 | tf_op jit(solution)/shard_map/pallas_call | solution.py:472
  121.8 1.6 collective-permute-start.8
  123.4 4.0 %shard_map.338 = (bf16[8,48,1152]{2,1,0:T(8,128)(2,1)S(1)}, bf16[8,48,1152]{2,1,0:T(8,128)(2,1)}) custom-call(s32[5]{0:T(128)S(1)} %stack.57.place, bf16[640,768]{1,0:T(8,128)(2,1)S(1)} %copy-done.14, bf16[3,640,384]{2,1,0:T(8,128)(2,1)S(1)} %copy-done.6), custom_call_target="tpu_custom_call" | custom-call | flops 1132462080 | bytes 4227072 | tf_op jit(solution)/shard_map/pallas_call | solution.py:472
  127.7 2.0 shard_map.337
  132.0 1.3 reverse.2
  133.5 1.3 reverse.1
  138.3 1.3 add_convert_fusion.4
  139.6 1.6 collective-permute-start.10
  141.1 2.2 add_convert_fusion
  143.3 2.5 %collective-permute-start.15 = (bf16[8,48,1920]{2,1,0:T(8,128)(2,1)S(1)}, bf16[8,48,1920]{2,1,0:T(8,128)(2,1)S(1)}, u32[]{:S(2)}, u32[]{:S(2)}) collective-permute-start(bf16[8,48,1920]{2,1,0:T(8,128)(2,1)S(1)} %add_convert_fusion), channel_id=1, source_target_pairs={{0,8},{1,9},{2,10},{3,11},{4,12},{5,13},{6,14},{7,15},{8,0},{9,1},... | collective-permute-start | bytes 4423688 | tf_op jit(solution)/shard_map/ppermute | solution.py:433
  145.8 1.6 add_convert_fusion.1
  148.0 4.6 %collective-permute-done.10 = bf16[4,48,1152]{2,1,0:T(8,128)(2,1)S(1)} collective-permute-done((bf16[4,48,1152]{2,1,0:T(8,128)(2,1)S(1)}, bf16[4,48,1152]{2,1,0:T(8,128)(2,1)S(1)}, u32[]{:S(2)}, u32[]{:S(2)}) %collective-permute-start.10) | collective-permute-done | bytes 442400 | tf_op jit(solution)/shard_map/ppermute | solution.py:433
  153.6 2.5 %collective-permute-start.11 = (bf16[2,48,1152]{2,1,0:T(8,128)(2,1)S(1)}, bf16[2,48,1152]{2,1,0:T(8,128)(2,1)S(1)}, u32[]{:S(2)}, u32[]{:S(2)}) collective-permute-start(bf16[2,48,1152]{2,1,0:T(8,128)(2,1)S(1)} %add_convert_fusion.7), channel_id=1, source_target_pairs={{0,8},{1,9},{2,10},{3,11},{4,12},{5,13},{6,14},{7,15},{8,0},{9,1},... | collective-permute-start | bytes 663560 | tf_op jit(solution)/shard_map/ppermute | solution.py:433
  156.8 26.2 %collective-permute-done.11 = bf16[2,48,1152]{2,1,0:T(8,128)(2,1)S(1)} collective-permute-done((bf16[2,48,1152]{2,1,0:T(8,128)(2,1)S(1)}, bf16[2,48,1152]{2,1,0:T(8,128)(2,1)S(1)}, u32[]{:S(2)}, u32[]{:S(2)}) %collective-permute-start.11) | collective-permute-done | bytes 221216 | tf_op jit(solution)/shard_map/ppermute | solution.py:433
  184.1 1.3 add_convert_fusion.3
  185.9 1.4 add_convert_fusion.2
  187.3 2.1 collective-permute-start.16
  189.4 17.0 %collective-permute-done.12 = bf16[1,48,1152]{2,1,0:T(8,128)(2,1)S(1)} collective-permute-done((bf16[1,48,1152]{2,1,0:T(8,128)(2,1)S(1)}, bf16[1,48,1152]{2,1,0:T(8,128)(2,1)S(1)}, u32[]{:S(2)}, u32[]{:S(2)}) %collective-permute-start.12) | collective-permute-done | bytes 110624 | tf_op jit(solution)/shard_map/ppermute | solution.py:433
  207.5 3.9 %collective-permute-done.13 = bf16[48,384]{1,0:T(8,128)(2,1)S(1)} collective-permute-done((bf16[48,384]{1,0:T(8,128)(2,1)S(1)}, bf16[48,384]{1,0:T(8,128)(2,1)S(1)}, u32[]{:S(2)}, u32[]{:S(2)}) %collective-permute-start.13) | collective-permute-done | bytes 36896 | tf_op jit(solution)/shard_map/ppermute | solution.py:433
  211.4 1.1 add_convert_fusion.6
  212.6 11.7 %collective-permute-done.16 = bf16[4,48,1920]{2,1,0:T(8,128)(2,1)S(1)} collective-permute-done((bf16[4,48,1920]{2,1,0:T(8,128)(2,1)S(1)}, bf16[4,48,1920]{2,1,0:T(8,128)(2,1)S(1)}, u32[]{:S(2)}, u32[]{:S(2)}) %collective-permute-start.16) | collective-permute-done | bytes 737312 | tf_op jit(solution)/shard_map/ppermute | solution.py:433
  224.3 1.2 add_convert_fusion.5
  226.9 1.1 add_convert_fusion.9
  228.0 7.5 %collective-permute-done.17 = bf16[2,48,1920]{2,1,0:T(8,128)(2,1)S(1)} collective-permute-done((bf16[2,48,1920]{2,1,0:T(8,128)(2,1)S(1)}, bf16[2,48,1920]{2,1,0:T(8,128)(2,1)S(1)}, u32[]{:S(2)}, u32[]{:S(2)}) %collective-permute-start.17) | collective-permute-done | bytes 368672 | tf_op jit(solution)/shard_map/ppermute | solution.py:433
  235.5 1.1 add_convert_fusion.8
  236.9 1.7 add_bitcast_fusion.1
  238.6 3.5 %collective-permute-done.18 = bf16[1,48,1920]{2,1,0:T(8,128)(2,1)S(1)} collective-permute-done((bf16[1,48,1920]{2,1,0:T(8,128)(2,1)S(1)}, bf16[1,48,1920]{2,1,0:T(8,128)(2,1)S(1)}, u32[]{:S(2)}, u32[]{:S(2)}) %collective-permute-start.18) | collective-permute-done | bytes 184352 | tf_op jit(solution)/shard_map/ppermute | solution.py:433
  242.1 1.1 add_bitcast_fusion
  (177 shorter events, 36.6 us)
Async XLA Ops:
  0.7 1.6 copy-start
  0.7 13.2 %copy-start.2 = (bf16[1,320,768]{2,1,0:T(8,128)(2,1)S(1)}, bf16[1,320,768]{2,1,0:T(8,128)(2,1)}, u32[]{:S(2)}) copy-start(bf16[1,320,768]{2,1,0:T(8,128)(2,1)} %param.20) | copy-start | bytes 1474564
  0.7 13.2 %collective-permute-start = (bf16[320,768]{1,0:T(8,128)(2,1)}, bf16[320,768]{1,0:T(8,128)(2,1)S(1)}, u32[]{:S(2)}, u32[]{:S(2)}) collective-permute-start(bf16[320,768]{1,0:T(8,128)(2,1)} %bitcast.65), channel_id=1, source_target_pairs={{0,1},{1,0},{2,3},{3,2},{4,5},{5,4},{6,7},{7,6},{8,9},{9,8},{10,11... | collective-permute-start | bytes 1474568 | tf_op jit(solution)/shard_map/ppermute | solution.py:433
  11.8 7.0 %copy-start.16 = (f32[24,1280]{1,0:T(8,128)S(1)}, f32[24,1280]{1,0:T(8,128)}, u32[]{:S(2)}) copy-start(f32[24,1280]{1,0:T(8,128)} %constant.23.clone.even_mask) | copy-start | bytes 368644
  18.7 12.5 %copy-start.13 = (bf16[640,768]{1,0:T(8,128)(2,1)}, bf16[640,768]{1,0:T(8,128)(2,1)S(1)}, u32[]{:S(2)}) copy-start(bf16[640,768]{1,0:T(8,128)(2,1)S(1)} %get-tuple-element.68.hidden) | copy-start | bytes 2949124
  18.7 14.0 %copy-start.33 = (bf16[1,320,768]{2,1,0:T(8,128)(2,1)S(1)}, bf16[1,320,768]{2,1,0:T(8,128)(2,1)}, u32[]{:S(2)}) copy-start(bf16[1,320,768]{2,1,0:T(8,128)(2,1)} %param.22) | copy-start | bytes 1474564
  18.7 19.3 %copy-start.15 = (f32[3072]{0:T(1024)S(1)}, f32[3072]{0:T(1024)}, u32[]{:S(2)}) copy-start(f32[3072]{0:T(1024)} %param.35) | copy-start | bytes 36868
  31.2 6.8 %copy-start.26 = (f32[640,384]{1,0:T(8,128)}, f32[640,384]{1,0:T(8,128)S(1)}, u32[]{:S(2)}) copy-start(f32[640,384]{1,0:T(8,128)S(1)} %get-tuple-element.58.inv) | copy-start | bytes 2949124
  31.2 20.5 %copy-start.28 = (bf16[320,384]{1,0:T(8,128)(2,1)}, bf16[320,384]{1,0:T(8,128)(2,1)S(1)}, u32[]{:S(2)}) copy-start(bf16[320,384]{1,0:T(8,128)(2,1)S(1)} %get-tuple-element.50.attn_own) | copy-start | bytes 737284
  31.2 6.8 %collective-permute-start.1 = (bf16[320,384]{1,0:T(8,128)(2,1)S(1)}, bf16[320,384]{1,0:T(8,128)(2,1)S(1)}, u32[]{:S(2)}, u32[]{:S(2)}) collective-permute-start(bf16[320,384]{1,0:T(8,128)(2,1)S(1)} %get-tuple-element.51.attn_send), channel_id=1, source_target_pairs={{0,1},{1,0},{2,3},{3,2},{4,5},{5,4},{6,7},{7,6},{8,9},{9,8},{10,11... | collective-permute-start | bytes 737288 | tf_op jit(solution)/shard_map/ppermute | solution.py:433
  54.9 9.1 %copy-start.7 = (f32[320,768]{1,0:T(8,128)}, f32[320,768]{1,0:T(8,128)S(1)}, u32[]{:S(2)}) copy-start(f32[320,768]{1,0:T(8,128)S(1)} %get-tuple-element.62.d_resid) | copy-start | bytes 2949124
  54.9 9.1 %copy-start.30 = (bf16[320,384]{1,0:T(8,128)(2,1)}, bf16[320,384]{1,0:T(8,128)(2,1)S(1)}, u32[]{:S(2)}) copy-start(bf16[320,384]{1,0:T(8,128)(2,1)S(1)} %get-tuple-element.56.grad_own) | copy-start | bytes 737284
  54.9 10.4 %collective-permute-start.2 = (bf16[320,384]{1,0:T(8,128)(2,1)S(1)}, bf16[320,384]{1,0:T(8,128)(2,1)S(1)}, u32[]{:S(2)}, u32[]{:S(2)}) collective-permute-start(bf16[320,384]{1,0:T(8,128)(2,1)S(1)} %get-tuple-element.57), channel_id=1, source_target_pairs={{0,1},{1,0},{2,3},{3,2},{4,5},{5,4},{6,7},{7,6},{8,9},{9,8},{10,11... | collective-permute-start | bytes 737288 | tf_op jit(solution)/shard_map/ppermute | solution.py:433
  56.5 1.5 copy-start.3
  65.3 1.2 copy-start.27
  82.3 6.4 %copy-start.5 = (bf16[3,640,384]{2,1,0:T(8,128)(2,1)}, bf16[3,640,384]{2,1,0:T(8,128)(2,1)S(1)}, u32[]{:S(2)}) copy-start(bf16[3,640,384]{2,1,0:T(8,128)(2,1)S(1)} %get-tuple-element.59.dqkv) | copy-start | bytes 4423684
  82.4 7.6 %copy-start.17 = (bf16[320,3072]{1,0:T(8,128)(2,1)S(1)}, bf16[320,3072]{1,0:T(8,128)(2,1)}, u32[]{:S(2)}) copy-start(bf16[320,3072]{1,0:T(8,128)(2,1)} %get-tuple-element.72.d_pre) | copy-start | bytes 5898244
  89.9 12.1 %collective-permute-start.4 = (f32[198,128]{1,0:T(8,128)S(1)}, f32[198,128]{1,0:T(8,128)S(1)}, u32[]{:S(2)}, u32[]{:S(2)}) collective-permute-start(f32[198,128]{1,0:T(8,128)S(1)} %pad_maximum_fusion.6), channel_id=1, source_target_pairs={{0,2},{1,3},{2,0},{3,1},{4,6},{5,7},{6,4},{7,5},{8,10},{9,11},{10,... | collective-permute-start | bytes 304136 | tf_op jit(solution)/shard_map/ppermute | solution.py:433
  101.1 40.1 %collective-permute-start.14 = (bf16[16,48,1920]{2,1,0:T(8,128)(2,1)}, bf16[16,48,1920]{2,1,0:T(8,128)(2,1)}, u32[]{:S(2)}, u32[]{:S(2)}) collective-permute-start(bf16[16,48,1920]{2,1,0:T(8,128)(2,1)} %get-tuple-element.76), channel_id=1, source_target_pairs={{0,2},{1,3},{2,0},{3,1},{4,6},{5,7},{6,4},{7,5},{8,10},{9,11},{10,... | collective-permute-start | bytes 8847368 | tf_op jit(solution)/shard_map/ppermute | solution.py:433
  101.6 26.1 %collective-permute-start.3 = (bf16[320,768]{1,0:T(8,128)(2,1)}, bf16[320,768]{1,0:T(8,128)(2,1)S(1)}, u32[]{:S(2)}, u32[]{:S(2)}) collective-permute-start(bf16[320,768]{1,0:T(8,128)(2,1)} %get-tuple-element.61), channel_id=1, source_target_pairs={{0,1},{1,0},{2,3},{3,2},{4,5},{5,4},{6,7},{7,6},{8,9},{9,8},{10,11... | collective-permute-start | bytes 1474568 | tf_op jit(solution)/shard_map/ppermute | solution.py:433
  102.0 4.7 %collective-permute-start.5 = (f32[198,128]{1,0:T(8,128)S(1)}, f32[198,128]{1,0:T(8,128)S(1)}, u32[]{:S(2)}, u32[]{:S(2)}) collective-permute-start(f32[198,128]{1,0:T(8,128)S(1)} %fusion.6), channel_id=1, source_target_pairs={{0,4},{1,5},{2,6},{3,7},{4,0},{5,1},{6,2},{7,3},{8,12},{9,13},{10,... | collective-permute-start | bytes 304136 | tf_op jit(solution)/shard_map/ppermute | solution.py:433
  106.8 4.7 %collective-permute-start.6 = (f32[198,128]{1,0:T(8,128)S(1)}, f32[198,128]{1,0:T(8,128)S(1)}, u32[]{:S(2)}, u32[]{:S(2)}) collective-permute-start(f32[198,128]{1,0:T(8,128)S(1)} %add.191), channel_id=1, source_target_pairs={{0,8},{1,9},{2,10},{3,11},{4,12},{5,13},{6,14},{7,15},{8,0},{9,1},... | collective-permute-start | bytes 304136 | tf_op jit(solution)/shard_map/ppermute | solution.py:433
  111.5 10.2 %collective-permute-start.7 = (f32[198,128]{1,0:T(8,128)S(1)}, f32[198,128]{1,0:T(8,128)S(1)}, u32[]{:S(2)}, u32[]{:S(2)}) collective-permute-start(f32[198,128]{1,0:T(8,128)S(1)} %add.192), channel_id=1, source_target_pairs={{0,24},{1,25},{2,26},{3,27},{4,28},{5,29},{6,30},{7,31},{8,16},{9,... | collective-permute-start | bytes 304136 | tf_op jit(solution)/shard_map/ppermute | solution.py:433
  113.2 1.5 copy-start.4
  115.7 7.7 %copy-start.6 = (bf16[3,640,384]{2,1,0:T(8,128)(2,1)S(1)}, bf16[3,640,384]{2,1,0:T(8,128)(2,1)}, u32[]{:S(2)}) copy-start(bf16[3,640,384]{2,1,0:T(8,128)(2,1)} %copy-done.5) | copy-start | bytes 4423684
  115.7 7.7 %copy-start.14 = (bf16[640,768]{1,0:T(8,128)(2,1)S(1)}, bf16[640,768]{1,0:T(8,128)(2,1)}, u32[]{:S(2)}) copy-start(bf16[640,768]{1,0:T(8,128)(2,1)} %copy-done.13) | copy-start | bytes 2949124
  121.7 5.9 %copy-start.8 = (f32[320,768]{1,0:T(8,128)S(1)}, f32[320,768]{1,0:T(8,128)}, u32[]{:S(2)}) copy-start(f32[320,768]{1,0:T(8,128)} %copy-done.7) | copy-start | bytes 2949124
  121.7 5.9 %copy-start.10 = (f32[320,768]{1,0:T(8,128)S(1)}, f32[320,768]{1,0:T(8,128)}, u32[]{:S(2)}) copy-start(f32[320,768]{1,0:T(8,128)} %copy-done.9) | copy-start | bytes 2949124
  121.7 24.1 %collective-permute-start.19 = (bf16[16,192,384]{2,1,0:T(8,128)(2,1)}, bf16[16,192,384]{2,1,0:T(8,128)(2,1)}, u32[]{:S(2)}, u32[]{:S(2)}) collective-permute-start(bf16[16,192,384]{2,1,0:T(8,128)(2,1)} %get-tuple-element.79), channel_id=1, source_target_pairs={{0,2},{1,3},{2,0},{3,1},{4,6},{5,7},{6,4},{7,5},{8,10},{9,11},{10,... | collective-permute-start | bytes 7077896 | tf_op jit(solution)/shard_map/ppermute | solution.py:433
  121.8 7.9 %copy-start.34 = (f32[198,128]{1,0:T(8,128)}, f32[198,128]{1,0:T(8,128)S(1)}, u32[]{:S(2)}) copy-start(f32[198,128]{1,0:T(8,128)S(1)} %add.193) | copy-start | bytes 304132
  121.8 7.9 %collective-permute-start.8 = (f32[198,128]{1,0:T(8,128)S(1)}, f32[198,128]{1,0:T(8,128)S(1)}, u32[]{:S(2)}, u32[]{:S(2)}) collective-permute-start(f32[198,128]{1,0:T(8,128)S(1)} %add.193), channel_id=1, source_target_pairs={{0,1},{1,0},{2,3},{3,2},{4,5},{5,4},{6,7},{7,6},{8,9},{9,8},{10,11... | collective-permute-start | bytes 304136 | tf_op jit(solution)/shard_map/ppermute | solution.py:433
  127.4 2.2 copy-start.11
  127.4 10.9 %collective-permute-start.9 = (bf16[8,48,1152]{2,1,0:T(8,128)(2,1)}, bf16[8,48,1152]{2,1,0:T(8,128)(2,1)}, u32[]{:S(2)}, u32[]{:S(2)}) collective-permute-start(bf16[8,48,1152]{2,1,0:T(8,128)(2,1)} %get-tuple-element.70), channel_id=1, source_target_pairs={{0,2},{1,3},{2,0},{3,1},{4,6},{5,7},{6,4},{7,5},{8,10},{9,11},{10,... | collective-permute-start | bytes 2654216 | tf_op jit(solution)/shard_map/ppermute | solution.py:433
  139.6 13.1 %collective-permute-start.10 = (bf16[4,48,1152]{2,1,0:T(8,128)(2,1)S(1)}, bf16[4,48,1152]{2,1,0:T(8,128)(2,1)S(1)}, u32[]{:S(2)}, u32[]{:S(2)}) collective-permute-start(bf16[4,48,1152]{2,1,0:T(8,128)(2,1)S(1)} %add_convert_fusion.4), channel_id=1, source_target_pairs={{0,4},{1,5},{2,6},{3,7},{4,0},{5,1},{6,2},{7,3},{8,12},{9,13},{10,... | collective-permute-start | bytes 1327112 | tf_op jit(solution)/shard_map/ppermute | solution.py:433
  143.3 9.3 %copy-start.12 = (bf16[8,48,1152]{2,1,0:T(8,128)(2,1)S(1)}, bf16[8,48,1152]{2,1,0:T(8,128)(2,1)}, u32[]{:S(2)}) copy-start(bf16[8,48,1152]{2,1,0:T(8,128)(2,1)} %copy-done.11) | copy-start | bytes 2654212
  143.3 42.6 %collective-permute-start.15 = (bf16[8,48,1920]{2,1,0:T(8,128)(2,1)S(1)}, bf16[8,48,1920]{2,1,0:T(8,128)(2,1)S(1)}, u32[]{:S(2)}, u32[]{:S(2)}) collective-permute-start(bf16[8,48,1920]{2,1,0:T(8,128)(2,1)S(1)} %add_convert_fusion), channel_id=1, source_target_pairs={{0,8},{1,9},{2,10},{3,11},{4,12},{5,13},{6,14},{7,15},{8,0},{9,1},... | collective-permute-start | bytes 4423688 | tf_op jit(solution)/shard_map/ppermute | solution.py:433
  147.4 38.5 %copy-start.32 = (bf16[16,48,1920]{2,1,0:T(8,128)(2,1)S(1)}, bf16[16,48,1920]{2,1,0:T(8,128)(2,1)}, u32[]{:S(2)}) copy-start(bf16[16,48,1920]{2,1,0:T(8,128)(2,1)} %get-tuple-element.75) | copy-start | bytes 8847364
  147.4 36.7 %collective-permute-start.20 = (bf16[8,192,384]{2,1,0:T(8,128)(2,1)S(1)}, bf16[8,192,384]{2,1,0:T(8,128)(2,1)S(1)}, u32[]{:S(2)}, u32[]{:S(2)}) collective-permute-start(bf16[8,192,384]{2,1,0:T(8,128)(2,1)S(1)} %add_convert_fusion.1), channel_id=1, source_target_pairs={{0,4},{1,5},{2,6},{3,7},{4,0},{5,1},{6,2},{7,3},{8,12},{9,13},{10,... | collective-permute-start | bytes 3538952 | tf_op jit(solution)/shard_map/ppermute | solution.py:433
  153.6 29.4 %collective-permute-start.11 = (bf16[2,48,1152]{2,1,0:T(8,128)(2,1)S(1)}, bf16[2,48,1152]{2,1,0:T(8,128)(2,1)S(1)}, u32[]{:S(2)}, u32[]{:S(2)}) collective-permute-start(bf16[2,48,1152]{2,1,0:T(8,128)(2,1)S(1)} %add_convert_fusion.7), channel_id=1, source_target_pairs={{0,8},{1,9},{2,10},{3,11},{4,12},{5,13},{6,14},{7,15},{8,0},{9,1},... | collective-permute-start | bytes 663560 | tf_op jit(solution)/shard_map/ppermute | solution.py:433
  184.0 22.4 %collective-permute-start.12 = (bf16[1,48,1152]{2,1,0:T(8,128)(2,1)S(1)}, bf16[1,48,1152]{2,1,0:T(8,128)(2,1)S(1)}, u32[]{:S(2)}, u32[]{:S(2)}) collective-permute-start(bf16[1,48,1152]{2,1,0:T(8,128)(2,1)S(1)} %add_convert_fusion.10), channel_id=1, source_target_pairs={{0,24},{1,25},{2,26},{3,27},{4,28},{5,29},{6,30},{7,31},{8,16},{9,... | collective-permute-start | bytes 331784 | tf_op jit(solution)/shard_map/ppermute | solution.py:433
  185.4 26.0 %collective-permute-start.21 = (bf16[4,192,384]{2,1,0:T(8,128)(2,1)S(1)}, bf16[4,192,384]{2,1,0:T(8,128)(2,1)S(1)}, u32[]{:S(2)}, u32[]{:S(2)}) collective-permute-start(bf16[4,192,384]{2,1,0:T(8,128)(2,1)S(1)} %add_convert_fusion.3), channel_id=1, source_target_pairs={{0,1},{1,0},{2,3},{3,2},{4,5},{5,4},{6,7},{7,6},{8,9},{9,8},{10,11... | collective-permute-start | bytes 1769480 | tf_op jit(solution)/shard_map/ppermute | solution.py:433
  187.3 37.0 %collective-permute-start.16 = (bf16[4,48,1920]{2,1,0:T(8,128)(2,1)S(1)}, bf16[4,48,1920]{2,1,0:T(8,128)(2,1)S(1)}, u32[]{:S(2)}, u32[]{:S(2)}) collective-permute-start(bf16[4,48,1920]{2,1,0:T(8,128)(2,1)S(1)} %add_convert_fusion.2), channel_id=1, source_target_pairs={{0,24},{1,25},{2,26},{3,27},{4,28},{5,29},{6,30},{7,31},{8,16},{9,... | collective-permute-start | bytes 2211848 | tf_op jit(solution)/shard_map/ppermute | solution.py:433
  207.4 4.0 %collective-permute-start.13 = (bf16[48,384]{1,0:T(8,128)(2,1)S(1)}, bf16[48,384]{1,0:T(8,128)(2,1)S(1)}, u32[]{:S(2)}, u32[]{:S(2)}) collective-permute-start(bf16[48,384]{1,0:T(8,128)(2,1)S(1)} %select_convert_fusion), channel_id=1, source_target_pairs={{0,1},{1,0},{2,3},{3,2},{4,5},{5,4},{6,7},{7,6},{8,9},{9,8},{10,11... | collective-permute-start | bytes 110600 | tf_op jit(solution)/shard_map/ppermute | solution.py:433
  212.5 14.3 %collective-permute-start.22 = (bf16[2,192,384]{2,1,0:T(8,128)(2,1)S(1)}, bf16[2,192,384]{2,1,0:T(8,128)(2,1)S(1)}, u32[]{:S(2)}, u32[]{:S(2)}) collective-permute-start(bf16[2,192,384]{2,1,0:T(8,128)(2,1)S(1)} %add_convert_fusion.6), channel_id=1, source_target_pairs={{0,8},{1,9},{2,10},{3,11},{4,12},{5,13},{6,14},{7,15},{8,0},{9,1},... | collective-permute-start | bytes 884744 | tf_op jit(solution)/shard_map/ppermute | solution.py:433
  225.5 9.9 %collective-permute-start.17 = (bf16[2,48,1920]{2,1,0:T(8,128)(2,1)S(1)}, bf16[2,48,1920]{2,1,0:T(8,128)(2,1)S(1)}, u32[]{:S(2)}, u32[]{:S(2)}) collective-permute-start(bf16[2,48,1920]{2,1,0:T(8,128)(2,1)S(1)} %add_convert_fusion.5), channel_id=1, source_target_pairs={{0,4},{1,5},{2,6},{3,7},{4,0},{5,1},{6,2},{7,3},{8,12},{9,13},{10,... | collective-permute-start | bytes 1105928 | tf_op jit(solution)/shard_map/ppermute | solution.py:433
  226.9 17.7 %copy-start.1 = (f32[2212,12]{0,1:T(8,128)S(1)}, f32[2212,12]{0,1:T(8,128)}, u32[]{:S(2)}) copy-start(f32[2212,12]{0,1:T(8,128)} %param.28) | copy-start | bytes 318532
  227.9 8.9 %collective-permute-start.23 = (bf16[1,192,384]{2,1,0:T(8,128)(2,1)S(1)}, bf16[1,192,384]{2,1,0:T(8,128)(2,1)S(1)}, u32[]{:S(2)}, u32[]{:S(2)}) collective-permute-start(bf16[1,192,384]{2,1,0:T(8,128)(2,1)S(1)} %add_convert_fusion.9), channel_id=1, source_target_pairs={{0,24},{1,25},{2,26},{3,27},{4,28},{5,29},{6,30},{7,31},{8,16},{9,... | collective-permute-start | bytes 442376 | tf_op jit(solution)/shard_map/ppermute | solution.py:433
  236.5 5.6 %collective-permute-start.18 = (bf16[1,48,1920]{2,1,0:T(8,128)(2,1)S(1)}, bf16[1,48,1920]{2,1,0:T(8,128)(2,1)S(1)}, u32[]{:S(2)}, u32[]{:S(2)}) collective-permute-start(bf16[1,48,1920]{2,1,0:T(8,128)(2,1)S(1)} %add_convert_fusion.8), channel_id=1, source_target_pairs={{0,1},{1,0},{2,3},{3,2},{4,5},{5,4},{6,7},{7,6},{8,9},{9,8},{10,11... | collective-permute-start | bytes 552968 | tf_op jit(solution)/shard_map/ppermute | solution.py:433
  (12 other events, 10.9 us)

commit v2 on v1

--- a/solution.py
+++ b/solution.py
@@ -409,9 +409,8 @@
 
 
 def bits_of(img, seq):
-    ring = img >> 2
-    gray = ring ^ (ring >> 1)
-    return {"core": img & 1, "x": (img >> 1) & 1, "za": gray & 1, "zb": gray >> 1, "y": seq}
+    line = img >> 2
+    return {"core": img & 1, "x": (img >> 1) & 1, "z1": line & 1, "z2": line >> 1, "y": seq}
 
 
 def label_of(img, seq, order):
@@ -422,24 +421,23 @@
     return total
 
 
-def swap_pairs(name):
-    order = ("core", "x", "za", "zb", "y")
+def swap_pairs(*names):
+    order = ("core", "x", "z1", "z2", "y")
     where = {label_of(img, seq, order): img * 2 + seq for img in range(16) for seq in range(2)}
-    flip = 1 << (len(order) - 1 - order.index(name))
+    flip = sum(1 << (len(order) - 1 - order.index(name)) for name in names)
     return [(device, where[label ^ flip]) for label, device in where.items()]
 
 
-def swapped(value, name):
-    return lax.ppermute(value, ("img", "seq"), swap_pairs(name))
-
-
-def reduce_scatter(keep, send, order):
-    terms = [keep, swapped(send, order[0])]
-    half = keep.shape[0]
-    for name in order[1:]:
-        half //= 2
-        out = sum(term[half : 2 * half].astype(F32) for term in terms).astype(BF)
-        terms = [term[:half] for term in terms] + [swapped(out, name)]
+def swapped(value, *names):
+    return lax.ppermute(value, ("img", "seq"), swap_pairs(*names))
+
+
+def half_in(terms, out, name):
+    size = terms[0].shape[0] // 2
+    return [term[:size] for term in terms] + [swapped(out, name)]
+
+
+def added(terms):
     return sum(term[0].astype(F32) for term in terms)
 
 
@@ -467,8 +465,14 @@
     return pl.BlockSpec(shape, lambda *_: zeros)
 
 
-def run(kernel, place, grid, in_specs, out_specs, out_shapes, scratch, operands, flops, vmem=48):
-    moved = sum(int(np.prod(o.shape)) * o.dtype.itemsize for o in (*operands, *out_shapes))
+def run(kernel, place, grid, in_specs, out_specs, out_shapes, scratch, operands, flops, vmem=32, after=()):
+    held = len(operands)
+    inner = kernel
+
+    def kernel(place_ref, *refs):
+        inner(place_ref, *refs[:held], *refs[held + len(after) :])
+
+    in_specs = [*in_specs, *[pl.BlockSpec(memory_space=pl.ANY)] * len(after)]
     return pl.pallas_call(
         kernel,
         grid_spec=pltpu.PrefetchScalarGridSpec(
@@ -480,8 +484,34 @@
         ),
         out_shape=out_shapes,
         compiler_params=pltpu.CompilerParams(vmem_limit_bytes=vmem * MEGA),
-        cost_estimate=pl.CostEstimate(flops=flops, bytes_accessed=moved, transcendentals=0),
-    )(place, *operands)
+        cost_estimate=pl.CostEstimate(flops=1, bytes_accessed=1, transcendentals=0),
+    )(place, *operands, *after)
+
+
+def add_kernel(place, *refs):
+    refs[-1][...] = sum(ref[...].astype(F32) for ref in refs[:-1]).astype(BF)
+
+
+def half_out(place, terms, after=()):
+    size = terms[0].shape[0] // 2
+    block = (min(size, 4), *terms[0].shape[1:])
+    count = size // block[0]
+    return run(
+        add_kernel, place, (count,), [spec(block, lambda n, p: (n + count, 0, 0))] * len(terms),
+        [spec(block, lambda n, p: (n, 0, 0))], [shape((size, *block[1:]), BF)], [], tuple(terms), 0,
+        after=after,
+    )[0]
+
+
+def sum_kernel(place, left, right, out):
+    out[...] = left[...] + right[...]
+
+
+def summed(place, left, right, after=()):
+    return run(
+        sum_kernel, place, (1,), [full(left.shape)] * 2, [full(left.shape)],
+        [shape(left.shape, F32)], [], (left, right), 0, after=after,
+    )[0]
 
 
 def shape(dims, dtype):
@@ -527,10 +557,11 @@
     keys = [qkv[1] * m for m in masks]
     values = [qkv[2] * m for m in masks]
     picks = even_mask[...] > 0.5
+    at = side * 6 + 2 * pl.program_id(0)
     for head in range(2):
         rolled = [
             pltpu.roll(
-                jnp.broadcast_to(strips[0, head, par : par + 1, :], (STRIP, STRIP_WIDTH)),
+                jnp.broadcast_to(strips[at + head, par : par + 1, :], (STRIP, STRIP_WIDTH)),
                 1,
                 axis=1,
                 stride=1,
@@ -546,9 +577,10 @@
         total = None
         scale = None
         for head in range(2):
-            far = strips[0, head, 0:1, 1152:1153]
-            near = strips[0, head, 0:1, 1153:1154]
-            corner = strips[0, head, 0:1, 1154:1155]
+            lone = strips[at + head, 0:1, 1152:1280]
+            far = lone[:, 0:1]
+            near = lone[:, 1:2]
+            corner = lone[:, 2:3]
             biases = []
             for block in range(start // STRIP, -(-(start + count) // STRIP)):
                 if start == 576:
@@ -764,7 +796,7 @@
         grad_send_out[...] = mul(d_mixed, proj_other[...], NT).astype(BF)
 
 
-def fc2_grad_kernel(place, act, d_ffn, keep_out, send_out, held, *, y_shift, rest):
+def fc2_grad_kernel(place, act, d_ffn, attn, d_mixed, keep_out, send_out, held, *, rest):
     step = pl.program_id(0)
     held[...] = mul(act[...], d_ffn[...], TN)
     core = place[1]
@@ -774,11 +806,23 @@
             columns = slice(384 * seq, 384 * seq + 384)
             low = pl.multiple_of(384 * pair + 192 * core, 64)
             high = pl.multiple_of(384 * pair + 192 * (1 - core), 64)
-            keep_out[at] = held[pl.ds(low, 192), columns].astype(BF)
-            send_out[at] = held[pl.ds(high, 192), columns].astype(BF)
-
-
-def fc1_grad_kernel(place, hidden, d_pre, attn, d_mixed, keep_out, send_out, held, *, rest):
+            keep_out[at, :192] = held[pl.ds(low, 192), columns].astype(BF)
+            send_out[at, :192] = held[pl.ds(high, 192), columns].astype(BF)
+
+    @pl.when(step == pl.num_programs(0) - 1)
+    def _():
+        held[...] = mul(attn[...], d_mixed[...], TN)
+        for pair in range(8):
+            low = pl.multiple_of(96 * pair + 48 * core, 16)
+            high = pl.multiple_of(96 * pair + 48 * (1 - core), 16)
+            for side in range(2):
+                at = rest(pair % 2, pair // 2, side) ^ place[2]
+                columns = slice(384 * side, 384 * side + 384)
+                keep_out[at, 192:] = held[pl.ds(low, 48), columns].astype(BF)
+                send_out[at, 192:] = held[pl.ds(high, 48), columns].astype(BF)
+
+
+def fc1_grad_kernel(place, hidden, d_pre, keep_out, send_out, held, *, rest):
     step = pl.program_id(0)
     core = place[1]
     held[...] = mul(hidden[...], d_pre[...], TN)
@@ -791,18 +835,6 @@
         keep_out[at, :, lanes] = held[pl.ds(low, 48), :].astype(BF)
         send_out[at, :, lanes] = held[pl.ds(high, 48), :].astype(BF)
 
-    @pl.when(step == pl.num_programs(0) - 1)
-    def _():
-        held[...] = mul(attn[...], d_mixed[...], TN)
-        for pair in range(8):
-            low = pl.multiple_of(96 * pair + 48 * core, 16)
-            high = pl.multiple_of(96 * pair + 48 * (1 - core), 16)
-            for side in range(2):
-                at = rest(pair % 2, pair // 2, side) ^ place[3]
-                columns = slice(384 * side, 384 * side + 384)
-                keep_out[at, :, 1536:1920] = held[pl.ds(low, 48), columns].astype(BF)
-                send_out[at, :, 1536:1920] = held[pl.ds(high, 48), columns].astype(BF)
-
 
 def result_kernel(place, act, fc2, resid, cot, vecs, result_out, small_out, total):
     step = pl.program_id(0)
@@ -821,7 +853,9 @@
         small_out[1:8, :] = jnp.zeros((7, small_out.shape[1]), F32)
 
 
-def hidden1_grad_kernel(place, dqkv, weight, own, other, keep_out, send_out, small_out, total):
+def hidden1_grad_kernel(
+    place, dqkv0, dqkv1, dqkv2, weight, own, other, keep_out, send_out, small_out, total, joined
+):
     step = pl.program_id(0)
     rows = own.shape[0]
     here = pl.ds(pl.multiple_of(place[0] * rows, 64), rows)
@@ -832,7 +866,9 @@
         total[...] = jnp.zeros_like(total)
         small_out[...] = jnp.zeros_like(small_out)
 
-    grads = dqkv[0]
+    for n, part in enumerate((dqkv0, dqkv1, dqkv2)):
+        joined[:, LANES * n : LANES * (n + 1)] = part[0]
+    grads = joined[...]
     total[...] += mul(grads, weight[...], NT)
     line = jnp.sum(grads.astype(F32), axis=0, keepdims=True)
 
@@ -857,10 +893,14 @@
         )
 
 
-def qkv_grad_kernel(place, hidden, dqkv, keep_out, send_out, held, *, rest):
+def qkv_grad_kernel(
+    place, hidden, dqkv0, dqkv1, dqkv2, keep_out, send_out, held, joined, *, rest
+):
     step = pl.program_id(0)
     core = place[1]
-    held[...] = mul(hidden[...], dqkv[0], TN)
+    for n, part in enumerate((dqkv0, dqkv1, dqkv2)):
+        joined[:, LANES * n : LANES * (n + 1)] = part[0]
+    held[...] = mul(hidden[...], joined[...], TN)
     lanes = pl.ds(pl.multiple_of(step * 384, LANES), 384)
     for pair in range(8):
         at = rest(pair % 2, pair // 2, 0) ^ place[4]
@@ -878,9 +918,8 @@
 
 
 def rest_label(order):
-    def rest(x_bit, ring, seq):
-        gray = ring ^ (ring >> 1)
-        bits = {"x": x_bit, "za": gray & 1, "zb": gray >> 1, "y": seq}
+    def rest(x_bit, line, seq):
+        bits = {"x": x_bit, "z1": line & 1, "z2": line >> 1, "y": seq}
         total = 0
         for name in order[1:]:
             total = total * 2 + bits[name]
@@ -889,32 +928,126 @@
     return rest
 
 
-ORDER_A = ("core", "x", "y", "za", "zb")
-ORDER_B = ("core", "za", "zb", "x", "y")
-ORDER_Q = ("core", "x", "za", "zb")
-
-
-def strips_of(table, seq, heads):
-    own = lax.dynamic_slice_in_dim(table, seq * heads, heads, 1).T
-    span = 2 * GRID - 1
-    cells = span * span
-    patch = own[:, :cells][:, ::-1].reshape(heads, span, span)
-    patch = jnp.pad(patch, ((0, 0), (0, 1), (0, 1))).reshape(heads, 24, 2, 48)
-    even = jnp.concatenate(
-        [patch[:, :, 0].reshape(heads, 1152), own[:, cells:], jnp.zeros((heads, 125), F32)], axis=1
-    )
-    odd = jnp.pad(patch[:, :, 1].reshape(heads, 1152), ((0, 0), (24, 104)))
-    return jnp.stack([even, odd], axis=1).reshape(heads // 2, 2, 2, STRIP_WIDTH)
-
-
-def table_of(strips):
-    heads = strips.shape[0]
-    span = 2 * GRID - 1
-    even = strips[:, 0, :1152].reshape(heads, 24, 1, 48)
-    odd = strips[:, 1, 24:1176].reshape(heads, 24, 1, 48)
-    patch = jnp.concatenate([even, odd], axis=2).reshape(heads, 48, 48)[:, :span, :span]
-    flat = patch.reshape(heads, span * span)[:, ::-1]
-    return jnp.concatenate([flat, strips[:, 0, 1152:1155]], axis=1)
+ORDER_A = ("core", "x", "z1", "z2", "y")
+ORDER_B = ("core", "y", "x", "z1", "z2")
+ORDER_Q = ("core", "x", "z1", "z2")
+
+
+SPAN = 2 * GRID - 1
+CELLS = SPAN * SPAN
+
+
+def flips():
+    row = lax.broadcasted_iota(jnp.int32, (LANES, LANES), 0)
+    lane = lax.broadcasted_iota(jnp.int32, (LANES, LANES), 1)
+    return jnp.where(row + lane == LANES - 1, 1.0, 0.0)
+
+
+def exact(left, right, dims):
+    return lax.dot_general(
+        left, right, dims, precision=lax.Precision.HIGHEST, preferred_element_type=F32
+    )
+
+
+def moved_window(source, start, target):
+    base = start // LANES * LANES
+    place = target % LANES
+    held = source[:, base : base + 2 * LANES]
+    turn = (place - (start - base)) % (2 * LANES)
+    if turn:
+        held = pltpu.roll(held, turn, axis=1)
+    lane = lax.broadcasted_iota(jnp.int32, (1, 2 * LANES), 1)
+    return jnp.where((lane >= place) & (lane < place + SPAN), held, 0.0)
+
+
+def strips_kernel(place, table, strips_out, flat, sides):
+    heads = table.shape[0]
+    flat[...] = jnp.zeros_like(flat)
+    flat[:heads, : CELLS + 3] = table[...]
+    turned = pltpu.roll(flat[:, : 18 * LANES], 18 * LANES - CELLS, axis=1)
+    tail = turned[:, :LANES]
+    for n in range(18):
+        block = 17 - n
+        flat[:, LANES * n : LANES * (n + 1)] = exact(
+            turned[:, LANES * block : LANES * (block + 1)], flips(), NN
+        )
+    sides[...] = jnp.zeros_like(sides)
+    for b in range(SPAN):
+        base = 24 * b // LANES * LANES
+        part = moved_window(flat, SPAN * b, 24 * b)
+        sides[b % 2, :, base : base + 2 * LANES] += part
+    lane = lax.broadcasted_iota(jnp.int32, (16, LANES), 1)
+    sides[0, :, 1152:1280] = jnp.where(lane < 3, tail, 0.0)
+    for head in range(heads):
+        for par in range(2):
+            strips_out[head, par : par + 1, :] = sides[par, head : head + 1, :]
+
+
+def pack_kernel(place, strip0, strip1, strip2, ffn, fc1_bias, last, result, packed):
+    packed[...] = jnp.zeros_like(packed)
+    for n in range(5):
+        lanes = slice(256 * n, 256 * n + 256)
+        for pair, strip in enumerate((strip0, strip1, strip2)):
+            for head in range(2):
+                for par in range(2):
+                    row = 16 * n + 6 * par + 2 * pair + head
+                    packed[row : row + 1, :] = strip[0, head, par : par + 1, lanes]
+    for n in range(3):
+        lanes = slice(256 * n, 256 * n + 256)
+        row = 80 + 16 * n
+        packed[row : row + 5, :] = ffn[0:5, lanes]
+        packed[row + 5 : row + 6, :] = result[0:1, lanes]
+        packed[row + 6 : row + 9, :] = last[0:3, lanes]
+        for part in range(4):
+            packed[row + 9 + part : row + 10 + part, :] = fc1_bias[
+                :, 768 * part + 256 * n : 768 * part + 256 * n + 256
+            ]
+
+
+def unpack_kernel(
+    place, packed, mate, table_out, norm2_gain, norm2_bias, scale1, proj_bias, fc2_bias, scale2,
+    norm1_gain, norm1_bias, query_bias, value_bias, fc1_bias, flat, sides,
+):
+    heads = table_out.shape[0]
+    half = heads // 2
+    left = place[0] == 0
+    flat[...] = jnp.zeros_like(flat)
+    for n in range(5):
+        lanes = slice(256 * n, 256 * n + 256)
+        for par in range(2):
+            rows = slice(16 * n + half * par, 16 * n + half * par + half)
+            mine = packed[rows, :]
+            theirs = mate[rows, :]
+            sides[par, 0:half, lanes] = jnp.where(left, mine, theirs)
+            sides[par, half:heads, lanes] = jnp.where(left, theirs, mine)
+    for b in range(SPAN):
+        target = SPAN * b
+        base = target // LANES * LANES
+        part = moved_window(sides.at[b % 2], 24 * b, target)
+        flat[:, base : base + 2 * LANES] += part
+    lane = lax.broadcasted_iota(jnp.int32, (16, LANES), 1)
+    blocks = [
+        exact(flat[:, LANES * (17 - n) : LANES * (18 - n)], flips(), NN) for n in range(18)
+    ]
+    blocks[0] = jnp.where(lane < 3, sides[0, :, 1152:1280], blocks[0])
+    turned = pltpu.roll(jnp.concatenate(blocks, axis=1), CELLS, axis=1)
+    table_out[...] = turned[:heads, : CELLS + 3]
+    outs = (norm2_gain, norm2_bias, scale1, proj_bias, fc2_bias, scale2, norm1_gain, norm1_bias)
+    for n in range(3):
+        lanes = slice(256 * n, 256 * n + 256)
+        for at, out in enumerate(outs):
+            row = 80 + 16 * n + at
+            out[0:1, lanes] = packed[row : row + 1, :] + mate[row : row + 1, :]
+        for part in range(4):
+            row = 89 + 16 * n + part
+            fc1_bias[0:1, 768 * part + 256 * n : 768 * part + 256 * n + 256] = (
+                packed[row : row + 1, :] + mate[row : row + 1, :]
+            )
+    for source, side in ((packed, place[0]), (mate, 1 - place[0])):
+        line = jnp.concatenate([source[88 + 16 * n : 89 + 16 * n, :] for n in range(3)], axis=1)
+        lanes = pl.ds(pl.multiple_of(side * 384, LANES), 384)
+        query_bias[0:1, lanes] = line[:, :384]
+        value_bias[0:1, lanes] = line[:, 384:]
 
 
 def even_places():
@@ -954,15 +1087,15 @@
     seq = lax.axis_index("seq")
     img = lax.axis_index("img")
     core = img & 1
-    ring = img >> 2
+    line = img >> 2
     x_bit = (img >> 1) & 1
     place = jnp.stack(
         [
             seq,
             core,
-            rest_label(ORDER_A)(x_bit, ring, seq),
-            rest_label(ORDER_B)(x_bit, ring, seq),
-            rest_label(ORDER_Q)(x_bit, ring, seq),
+            rest_label(ORDER_A)(x_bit, line, seq),
+            rest_label(ORDER_B)(x_bit, line, seq),
+            rest_label(ORDER_Q)(x_bit, line, seq),
         ]
     ).astype(jnp.int32)
     own = tokens.reshape(rows, width)
@@ -971,7 +1104,11 @@
     vecs = jnp.stack(
         [norm1_gain, norm1_bias, proj_bias, scale1, norm2_gain, norm2_bias, fc2_bias, scale2]
     )
-    strips = strips_of(rel_table, seq, heads)
+    strips = run(
+        strips_kernel, place, (1,), [full(rel_table.shape[::-1])], [full((2 * heads, 2, STRIP_WIDTH))],
+        [shape((2 * heads, 2, STRIP_WIDTH), F32)],
+        [pltpu.VMEM((16, 2432), F32), pltpu.VMEM((2, 16, STRIP_WIDTH), F32)], (rel_table.T,), 0,
+    )[0]
     even_mask = jnp.asarray(even_places())
 
     qkv, hidden1 = run(
@@ -991,10 +1128,9 @@
     pair_half = spec((rows, LANES), lambda n, p: (0, n))
     pair_qkv = spec((3, slots, LANES), lambda n, p: (0, 0, n))
     pair_expo = spec((2, slots, slots), lambda n, p: (n, 0, 0))
-    pair_strip = spec((1, 2, 2, STRIP_WIDTH), lambda n, p: (n, 0, 0, 0))
     attn_own, attn_send, expo, inv = run(
         attend_kernel, place, (pairs,),
-        [pair_qkv, pair_strip, full((STRIP, STRIP_WIDTH))],
+        [pair_qkv, full((2 * heads, 2, STRIP_WIDTH)), full((STRIP, STRIP_WIDTH))],
         [pair_half, pair_half, pair_expo, pair_rows],
         [
             shape((rows, share), BF), shape((rows, share), BF),
@@ -1038,72 +1174,126 @@
         2 * rows * width * (3 * hidden + 2 * width),
     )
     grad_other = swapped(grad_send, "y")
-    block = (16, 192, share)
+    block = (16, 240, share)
     keep_a, send_a = run(
-        functools.partial(fc2_grad_kernel, y_shift=0, rest=rest_label(ORDER_A)), place, (parts,),
-        [sliced, whole], [full(block), full(block)], [shape(block, BF), shape(block, BF)],
-        [pltpu.VMEM((part, width), F32)], (act, d_ffn), 2 * rows * width * hidden,
-    )
-    block = (16, 48, 5 * share)
+        functools.partial(fc2_grad_kernel, rest=rest_label(ORDER_A)), place, (parts,),
+        [sliced, whole, whole, whole], [full(block), full(block)],
+        [shape(block, BF), shape(block, BF)],
+        [pltpu.VMEM((part, width), F32)], (act, d_ffn, attn_low, d_mixed),
+        2 * rows * width * hidden,
+        after=(grad_send,),
+    )
+    terms_a = [keep_a, swapped(send_a, "core")]
+    block = (16, 48, 4 * share)
     keep_b, send_b = run(
         functools.partial(fc1_grad_kernel, rest=rest_label(ORDER_B)), place, (parts,),
-        [whole, sliced, whole, whole], [full(block), full(block)],
+        [whole, sliced], [full(block), full(block)],
         [shape(block, BF), shape(block, BF)],
-        [pltpu.VMEM((width, part), F32)], (hidden2, d_pre, attn_low, d_mixed),
-        2 * rows * width * (hidden + width),
-    )
+        [pltpu.VMEM((width, part), F32)], (hidden2, d_pre),
+        2 * rows * width * (hidden + width), after=(send_a, grad_other),
+    )
+    terms_b = [keep_b, swapped(send_b, "core")]
+    out_a1 = half_out(place, terms_a, (send_b,))
+    terms_a = half_in(terms_a, out_a1, ORDER_A[1])
+
+    def attend_back(pair, after):
+        pair_expo = spec((2, slots, slots), lambda n, p: (pair, 0, 0))
+        pair_rows = spec((slots, LANES), lambda n, p: (0, pair))
+        pair_half = spec((rows, LANES), lambda n, p: (0, pair))
+        return run(
+            attend_back_kernel, place, (1,),
+            [
+                spec((3, slots, LANES), lambda n, p: (0, 0, pair)), pair_expo, pair_half, pair_half,
+                pair_half, pair_half, pair_rows, full((STRIP, STRIP_WIDTH)),
+            ],
+            [full((3, slots, LANES)), full((1, 2, 2, STRIP_WIDTH))],
+            [shape((3, slots, LANES), BF), shape((1, 2, 2, STRIP_WIDTH), F32)],
+            [
+                pltpu.VMEM((slots, LANES), F32), pltpu.VMEM((slots, LANES), F32),
+                pltpu.VMEM((2, slots, slots), BF), pltpu.VMEM((2, STRIP, STRIP_WIDTH), F32),
+                pltpu.VMEM((slots, LANES), F32),
+            ],
+            (qkv, expo, attn_own, attn_send, grad_own, grad_other, inv, even_mask),
+            32 * slots * slots * 64 * 2, after=after,
+        )
+
+    dqkv0, strip0 = attend_back(0, (out_a1, send_b))
+    out_b1 = half_out(place, terms_b, (dqkv0,))
+    terms_b = half_in(terms_b, out_b1, ORDER_B[1])
+    dqkv1, strip1 = attend_back(1, (dqkv0, out_b1))
+    dqkv2, strip2 = attend_back(2, (dqkv1,))
+    dqkv = (dqkv0, dqkv1, dqkv2)
+    third = [spec((1, slots, LANES), lambda t, p: (t, 0, 0))] * 3
+    dh_keep, dh_send, small_last = run(
+        hidden1_grad_kernel, place, (3,),
+        [*third, spec((width, share), lambda t, p: (0, 2 * t + p[0])), whole, whole],
+        [whole, whole, full((8, width))],
+        [shape((rows, width), F32), shape((rows, width), BF), shape((8, width), F32)],
+        [pltpu.VMEM((slots, width), F32), pltpu.VMEM((slots, share), BF)], (*dqkv, qkv_weight, own, other),
+        2 * slots * width * 3 * share,
+    )
+    block = (8, 48, 3 * share)
+    keep_q, send_q = run(
+        functools.partial(qkv_grad_kernel, rest=rest_label(ORDER_Q)), place, (3,),
+        [full((slots, width)), *third], [full(block), full(block)],
+        [shape(block, BF), shape(block, BF)],
+        [pltpu.VMEM((width, share), F32), pltpu.VMEM((slots, share), BF)], (hidden1, *dqkv), 2 * slots * width * 3 * share,
+        after=(dh_send,),
+    )
+    terms_q = [keep_q, swapped(send_q, "core")]
     result, small_result = run(
         result_kernel, place, (parts,),
         [sliced, spec((part, width), lambda c, p: (c, 0)), whole, whole, full((8, width))],
         [whole, full((8, width))],
         [shape((rows, width), BF), shape((8, width), F32)],
         [pltpu.VMEM((rows, width), F32)], (act, fc2_weight, resid, cot, vecs),
-        2 * rows * width * hidden,
-    )
-    dqkv, strip_grad = run(
-        attend_back_kernel, place, (pairs,),
-        [
-            pair_qkv, pair_expo, pair_half, pair_half, pair_half, pair_half, pair_rows,
-            full((STRIP, STRIP_WIDTH)),
-        ],
-        [pair_qkv, pair_strip],
-        [shape((3, slots, share), BF), shape((pairs, 2, 2, STRIP_WIDTH), F32)],
-        [
-            pltpu.VMEM((slots, LANES), F32), pltpu.VMEM((slots, LANES), F32),
-            pltpu.VMEM((2, slots, slots), BF), pltpu.VMEM((2, STRIP, STRIP_WIDTH), F32),
-            pltpu.VMEM((slots, LANES), F32),
-        ],
-        (qkv, expo, attn_own, attn_send, grad_own, grad_other, inv, even_mask),
-        32 * slots * slots * 64 * heads,
-    )
-    third = spec((1, slots, share), lambda t, p: (t, 0, 0))
-    dh_keep, dh_send, small_last = run(
-        hidden1_grad_kernel, place, (3,),
-        [third, spec((width, share), lambda t, p: (0, 2 * t + p[0])), whole, whole],
-        [whole, whole, full((8, width))],
-        [shape((rows, width), F32), shape((rows, width), BF), shape((8, width), F32)],
-        [pltpu.VMEM((slots, width), F32)], (dqkv, qkv_weight, own, other),
-        2 * slots * width * 3 * share,
-    )
+        2 * rows * width * hidden, after=(send_q,),
+    )
+    packed = run(
+        pack_kernel, place, (1,),
+        [*[full((1, 2, 2, STRIP_WIDTH))] * 3, full((8, width)), full((1, hidden)), full((8, width)), full((8, width))],
+        [full((128, 256))], [shape((128, 256), F32)], [],
+        (strip0, strip1, strip2, small_ffn, fc1_bias_part, small_last, small_result), 0,
+    )[0]
+    out_a2 = half_out(place, terms_a, (packed,))
+    terms_a = half_in(terms_a, out_a2, "z1")
+    out_b2 = half_out(place, terms_b, (out_a2,))
+    terms_b = half_in(terms_b, out_b2, "x")
+    out_q1 = half_out(place, terms_q, (out_b2,))
+    terms_q = half_in(terms_q, out_q1, "x")
+    mate = swapped(packed, "core")
     dh_recv = swapped(dh_send, "y")
-    block = (8, 48, 3 * share)
-    keep_q, send_q = run(
-        functools.partial(qkv_grad_kernel, rest=rest_label(ORDER_Q)), place, (3,),
-        [full((slots, width)), third], [full(block), full(block)],
-        [shape(block, BF), shape(block, BF)],
-        [pltpu.VMEM((width, share), F32)], (hidden1, dqkv), 2 * slots * width * 3 * share,
-    )
+    out_a3 = half_out(place, terms_a, (out_q1,))
+    terms_a = half_in(terms_a, out_a3, "z2")
+    out_b3 = half_out(place, terms_b, (out_a3,))
+    terms_b = half_in(terms_b, out_b3, "z1")
+    out_q2 = half_out(place, terms_q, (out_b3,))
+    terms_q = half_in(terms_q, out_q2, "z1")
+    packed = summed(place, packed, mate, (out_q2,))
+    mate = swapped(packed, "x")
     tokens_grad = run(
         tokens_grad_kernel, place, (1,),
         [whole, whole, whole, whole, full((8, width))], [whole],
         [shape((rows, width), BF)], [], (dh_keep, dh_recv, own, d_resid, vecs), 0,
+        after=(packed,),
     )[0]
-
-    fc2_grad = reduce_scatter(keep_a, send_a, ORDER_A)
-    fc1_proj = reduce_scatter(keep_b, send_b, ORDER_B)
-    qkv_part = reduce_scatter(keep_q, send_q, ORDER_Q)
-    fc1_grad = fc1_proj[:, : 4 * share]
-    proj_grad = fc1_proj[:, 4 * share :]
+    packed = summed(place, packed, mate, (tokens_grad,))
+    mate = swapped(packed, "z1")
+    out_a4 = half_out(place, terms_a, (packed,))
+    terms_a = half_in(terms_a, out_a4, "y")
+    out_b4 = half_out(place, terms_b, (out_a4,))
+    terms_b = half_in(terms_b, out_b4, "z2")
+    out_q3 = half_out(place, terms_q, (out_b4,))
+    terms_q = half_in(terms_q, out_q3, "z2")
+    packed = summed(place, packed, mate, (out_q3,))
+    mate = swapped(packed, "z2")
+    packed = summed(place, packed, mate)
+    mate = swapped(packed, "y")
+    fc2_proj = added(terms_a)
+    fc1_grad = added(terms_b)
+    qkv_part = added(terms_q)
+    fc2_grad = fc2_proj[:192]
+    proj_grad = fc2_proj[192:]
     on_left = seq == 0
     given = jnp.where(on_left, qkv_part[:, 2 * share :], qkv_part[:, :share]).astype(BF)
     taken = swapped(given, "y").astype(F32)
@@ -1113,43 +1303,33 @@
         jnp.concatenate([qkv_part[:, share : 2 * share], taken, qkv_part[:, 2 * share :]], axis=1),
     )
 
-    both = jnp.concatenate(
-        [small_ffn[:5], small_result[:1], fc1_bias_part.reshape(4, width), small_last[:2]], axis=0
-    )
-    single = jnp.concatenate([strip_grad.reshape(-1, LANES), small_last[2].reshape(-1, LANES)], axis=0)
-    cut = both.size // LANES
-    packed = jnp.concatenate([both.reshape(-1, LANES), single], axis=0)
-    for name in ("core", "x", "za", "zb"):
-        packed = packed + swapped(packed, name)
-    mate = swapped(packed, "y")
-    both = (packed[:cut] + mate[:cut]).reshape(-1, width)
-    ends = [jnp.where(on_left, packed[cut:], mate[cut:]), jnp.where(on_left, mate[cut:], packed[cut:])]
-    count = strip_grad.size // LANES
-    table_grad = jnp.concatenate(
-        [table_of(end[:count].reshape(heads, 2, STRIP_WIDTH)) for end in ends], axis=0
-    ).T
-    tail = [end[count:].reshape(2, share) for end in ends]
-    query_bias_grad = jnp.concatenate([tail[0][0], tail[1][0]])
-    value_bias_grad = jnp.concatenate([tail[0][1], tail[1][1]])
+    vector = shape((1, width), F32)
+    table_grad, *small = run(
+        unpack_kernel, place, (1,), [full((128, 256))] * 2,
+        [full(rel_table.shape[::-1]), *[full((1, width))] * 10, full((1, hidden))],
+        [shape(rel_table.shape[::-1], F32), *[vector] * 10, shape((1, hidden), F32)],
+        [pltpu.VMEM((16, 2432), F32), pltpu.VMEM((2, 16, STRIP_WIDTH), F32)], (packed, mate), 0,
+    )
+    small = [part.reshape(-1) for part in small]
     return (
         result.reshape(tokens.shape),
         tokens_grad.reshape(tokens.shape),
-        both[10],
-        both[11],
+        small[6],
+        small[7],
         qkv_grad,
-        query_bias_grad,
-        value_bias_grad,
-        table_grad,
+        small[8],
+        small[9],
+        table_grad.T,
         proj_grad,
-        both[3],
-        both[2],
-        both[0],
-        both[1],
+        small[3],
+        small[2],
+        small[0],
+        small[1],
         fc1_grad,
-        both[6:10].reshape(hidden),
+        small[10],
         fc2_grad,
-        both[4],
-        both[5],
+        small[4],
+        small[5],
     )
 
 

time: 246 us -> 195 us (0.79)
  the two profiles are of different devices: /device:TPU:8 before, /device:TPU:0 now
where the time goes in v2:
time: 195 us; the launch traced here: 193 us
  Pallas kernels  86.6 us (44%)
  waiting for transfers between devices  36.1 us (19%)
  local copies, waits for them, and re-layouts  29.3 us (15%)
  starting transfers between devices  28 us (14%)
  other arithmetic  11.9 us (6%)
    pallas_call x30, Pallas kernels, run(): pl.pallas_call(kernel, grid_spec=pltpu.PrefetchScalarGridSpec(num_scalar_...  86.6 us
    ppermute x24, waiting for transfers between devices, swapped(): return lax.ppermute(value, ('img', 'seq'), swap_pairs(*names))  36.1 us
    ppermute x24, starting transfers between devices, swapped(): return lax.ppermute(value, ('img', 'seq'), swap_pairs(*names))  28 us
    unnamed x80, local copies, waits for them, and re-layouts  12.3 us
    slice x23, local copies, waits for them, and re-layouts, half_in(): return [term[:size] for term in terms] + [swapped(out, name)]  8.59 us
    pallas_call x10, other arithmetic, run(): pl.pallas_call(kernel, grid_spec=pltpu.PrefetchScalarGridSpec(num_scalar_...  6.05 us
    another operation x9, local copies, waits for them, and re-layouts, split_body(): jnp.stack([norm1_gain, norm1_bias, proj_bias, scale1, norm2_gain, norm2_b...  5.6 us
    add x3, other arithmetic, added(): return sum((term[0].astype(F32) for term in terms))  4.31 us
  transfers between devices with their start and end apart: 24, of which 10 were waited for; matrix products, arithmetic and copies ran while one was open for 12% of the time, Pallas kernels for 27%

profile of v2, /device:TPU:0, one launch (start us, length us, event | category | flops | bytes accessed | tf_op | source)
XLA Modules:
  0.0 193.3 jit_solution(16606633576286241289)
XLA Ops:
  0.7 3.0 %collective-permute-start = (bf16[320,768]{1,0:T(8,128)(2,1)}, bf16[320,768]{1,0:T(8,128)(2,1)S(1)}, u32[]{:S(2)}, u32[]{:S(2)}) collective-permute-start(bf16[320,768]{1,0:T(8,128)(2,1)} %bitcast.22), channel_id=1, source_target_pairs={{0,1},{1,0},{2,3},{3,2},{4,5},{5,4},{6,7},{7,6},{8,9},{9,8},{10,11... | collective-permute-start | bytes 1474568 | tf_op jit(solution)/shard_map/ppermute | solution.py:432
  4.7 1.7 shard_map.332.refs_1_
  15.1 2.0 %copy-done.1 = bf16[768,2304]{1,0:T(8,128)(2,1)S(1)} copy-done((bf16[768,2304]{1,0:T(8,128)(2,1)S(1)}, bf16[768,2304]{1,0:T(8,128)(2,1)}, u32[]{:S(2)}) %copy-start.1) | copy-done | bytes 3538968
  18.2 3.6 %shard_map.331 = (bf16[3,640,384]{2,1,0:T(8,128)(2,1)S(1)}, bf16[640,768]{1,0:T(8,128)(2,1)S(1)}) custom-call(s32[5]{0:T(128)S(1)} %stack.50.place_ref, bf16[320,768]{1,0:T(8,128)(2,1)S(1)} %bitcast.23, bf16[320,768]{1,0:T(8,128)(2,1)S(1)} %collective-permute-done.refs_1_.refs_5_, f32[8,768]{1,0:T(8,128)S(1)} %stack.59.refs_2_.refs_4_, ...), custom_call_target="tpu_custom_call" | custom-call | flops 1 | bytes 1 | tf_op jit(solution)/shard_map/pallas_call | solution.py:476
  21.8 11.3 %shard_map.333 = (bf16[320,384]{1,0:T(8,128)(2,1)S(1)}, bf16[320,384]{1,0:T(8,128)(2,1)S(1)}, bf16[6,640,640]{2,1,0:T(8,128)(2,1)S(1)}, f32[640,384]{1,0:T(8,128)S(1)}) custom-call(s32[5]{0:T(128)S(1)} %stack.50.place_ref, bf16[3,640,384]{2,1,0:T(8,128)(2,1)S(1)} %get-tuple-element.65.refs_0_, f32[12,2,1280]{2,1,0:T(2,128)S(1)} %shard_map.332.refs_1_, ...), custom_call_target="tpu_custom_call" | custom-call | flops 1 | bytes 1 | tf_op jit(solution)/shard_map/pallas_call | solution.py:476
  33.1 1.8 collective-permute-start.1
  35.1 5.2 %collective-permute-done.1.refs_3_ = bf16[320,384]{1,0:T(8,128)(2,1)S(1)} collective-permute-done((bf16[320,384]{1,0:T(8,128)(2,1)S(1)}, bf16[320,384]{1,0:T(8,128)(2,1)S(1)}, u32[]{:S(2)}, u32[]{:S(2)}) %collective-permute-start.1) | collective-permute-done | bytes 245792 | tf_op jit(solution)/shard_map/ppermute | solution.py:432
  40.3 2.3 %copy-done.13 = bf16[768,3072]{1,0:T(8,128)(2,1)S(1)} copy-done((bf16[768,3072]{1,0:T(8,128)(2,1)S(1)}, bf16[768,3072]{1,0:T(8,128)(2,1)}, u32[]{:S(2)}) %copy-start.13) | copy-done | bytes 4718616
  42.6 9.6 %shard_map.334 = (bf16[320,3072]{1,0:T(8,128)(2,1)S(1)}, bf16[320,3072]{1,0:T(8,128)(2,1)S(1)}, f32[1,3072]{1,0:T(1,128)S(1)}, bf16[320,768]{1,0:T(8,128)(2,1)S(...) custom-call(s32[5]{0:T(128)S(1)} %stack.50.place_ref, ...), custom_call_target="tpu_custom_call" | custom-call | flops 1 | bytes 1 | tf_op jit(solution)/shard_map/pallas_call | solution.py:476
  52.2 1.3 copy-done.18
  54.5 7.1 %shard_map.335 = (bf16[16,240,384]{2,1,0:T(8,128)(2,1)S(1)}, bf16[16,240,384]{2,1,0:T(8,128)(2,1)}) custom-call(s32[5]{0:T(128)S(1)} %stack.50.place_ref, bf16[320,3072]{1,0:T(8,128)(2,1)S(1)} %get-tuple-element.68.refs_0_, bf16[320,768]{1,0:T(8,128)(2,1)S(1)} %get-tuple-element.75.refs_1_, bf16[320,768]{1,0:T(8,128)(2,1)S(1)} %get-tuple-element.76.refs_2_, ...), custom_call_target="tpu_custom_call" | custom-call | flops 1 | bytes 1 | tf_op jit(solution)/shard_map/pallas_call | solution.py:476
  61.6 1.4 collective-permute-start.2
  63.0 6.9 %collective-permute-done.2.refs_3_.refs_5_ = bf16[320,384]{1,0:T(8,128)(2,1)S(1)} collective-permute-done((bf16[320,384]{1,0:T(8,128)(2,1)S(1)}, bf16[320,384]{1,0:T(8,128)(2,1)S(1)}, u32[]{:S(2)}, u32[]{:S(2)}) %collective-permute-start.2) | collective-permute-done | bytes 245792 | tf_op jit(solution)/shard_map/ppermute | solution.py:432
  69.9 5.9 %shard_map.336 = (bf16[16,48,1536]{2,1,0:T(8,128)(2,1)S(1)}, bf16[16,48,1536]{2,1,0:T(8,128)(2,1)}) custom-call(s32[5]{0:T(128)S(1)} %stack.50.place_ref, bf16[320,768]{1,0:T(8,128)(2,1)S(1)} %get-tuple-element.80.refs_0_, bf16[320,3072]{1,0:T(8,128)(2,1)S(1)} %copy-done.19, bf16[16,240,384]{2,1,0:T(8,128)(2,1)} %get-tuple-element.79.refs_2_, ...), custom_call_target="tpu_custom_call" | custom-call | flops 1 | bytes 1 | tf_op jit(solution)/shard_map/pallas_call | solution.py:476
  75.9 2.3 %shard_map.337.refs_8_ = bf16[8,240,384]{2,1,0:T(8,128)(2,1)} custom-call(s32[5]{0:T(128)S(1)} %stack.50.place_ref, bf16[16,240,384]{2,1,0:T(8,128)(2,1)S(1)} %get-tuple-element.78.refs_0_, bf16[16,240,384]{2,1,0:T(8,128)(2,1)S(1)} %collective-permute-done.3.refs_1_, bf16[16,48,1536]{2,1,0:T(8,128)(2,1)} %get-tuple-element.82.refs_2_.refs_9_), custom_call_target="tpu_custom_call" | custom-call | flops 1 | bytes 1 | tf_op jit(solution)/shard_map/pallas_call | solution.py:476
  78.2 1.4 collective-permute-start.9
  79.6 4.4 %shard_map.338 = (bf16[3,640,128]{2,1,0:T(8,128)(2,1)S(1)}, f32[1,2,2,1280]{3,2,1,0:T(2,128)S(1)}) custom-call(s32[5]{0:T(128)S(1)} %stack.50.place_ref, bf16[3,640,384]{2,1,0:T(8,128)(2,1)S(1)} %get-tuple-element.65.refs_0_, bf16[6,640,640]{2,1,0:T(8,128)(2,1)S(1)} %get-tuple-element.71.refs_1_, bf16[320,384]{1,0:T(8,128)(2,1)S(1)} %get-tuple-element.66.refs_2_, ...), custom_call_target="tpu_custom_call" | custom-call | flops 1 | bytes 1 | tf_op jit(solution)/shard_map/pallas_call | solution.py:476
  84.0 1.7 copy-done.7
  85.7 2.8 %shard_map.339.refs_9_ = bf16[8,48,1536]{2,1,0:T(8,128)(2,1)} custom-call(s32[5]{0:T(128)S(1)} %stack.50.place_ref, bf16[16,48,1536]{2,1,0:T(8,128)(2,1)S(1)} %copy-done.7, bf16[16,48,1536]{2,1,0:T(8,128)(2,1)} %collective-permute-done.4.refs_1_, bf16[3,640,128]{2,1,0:T(8,128)(2,1)S(1)} %get-tuple-element.83.refs_2_.refs_8_.refs_0_.refs_1_), custom_call_target="tpu_custom_call" | custom-call | flops 1 | bytes 1 | tf_op jit(solution)/shard_map/pallas_call | solution.py:476
  88.5 1.5 collective-permute-start.8
  90.1 4.4 %shard_map.340 = (bf16[3,640,128]{2,1,0:T(8,128)(2,1)S(1)}, f32[1,2,2,1280]{3,2,1,0:T(2,128)S(1)}) custom-call(s32[5]{0:T(128)S(1)} %stack.50.place_ref, bf16[3,640,384]{2,1,0:T(8,128)(2,1)S(1)} %get-tuple-element.65.refs_0_, bf16[6,640,640]{2,1,0:T(8,128)(2,1)S(1)} %get-tuple-element.71.refs_1_, bf16[320,384]{1,0:T(8,128)(2,1)S(1)} %get-tuple-element.66.refs_2_, ...), custom_call_target="tpu_custom_call" | custom-call | flops 1 | bytes 1 | tf_op jit(solution)/shard_map/pallas_call | solution.py:476
  95.4 4.4 %shard_map.341 = (bf16[3,640,128]{2,1,0:T(8,128)(2,1)S(1)}, f32[1,2,2,1280]{3,2,1,0:T(2,128)S(1)}) custom-call(s32[5]{0:T(128)S(1)} %stack.50.place_ref, bf16[3,640,384]{2,1,0:T(8,128)(2,1)S(1)} %get-tuple-element.65.refs_0_, bf16[6,640,640]{2,1,0:T(8,128)(2,1)S(1)} %get-tuple-element.71.refs_1_, bf16[320,384]{1,0:T(8,128)(2,1)S(1)} %get-tuple-element.66.refs_2_, ...), custom_call_target="tpu_custom_call" | custom-call | flops 1 | bytes 1 | tf_op jit(solution)/shard_map/pallas_call | solution.py:476
  99.8 4.2 %shard_map.342 = (f32[320,768]{1,0:T(8,128)S(1)}, bf16[320,768]{1,0:T(8,128)(2,1)S(1)}, f32[8,768]{1,0:T(8,128)S(1)}) custom-call(s32[5]{0:T(128)S(1)} %stack.50.place_ref, bf16[3,640,128]{2,1,0:T(8,128)(2,1)S(1)} %get-tuple-element.83.refs_2_.refs_8_.refs_0_.refs_1_, bf16[3,640,128]{2,1,0:T(8,128)(2,1)S(1)} %get-tuple-element.85.refs_8_.refs_1_.refs_2_, ...), custom_call_target="tpu_custom_call" | custom-call | flops 1 | bytes 1 | tf_op jit(solution)/shard_map/pallas_call | solution.py:476
  104.0 3.1 %shard_map.343 = (bf16[8,48,1152]{2,1,0:T(8,128)(2,1)S(1)}, bf16[8,48,1152]{2,1,0:T(8,128)(2,1)S(1)}) custom-call(s32[5]{0:T(128)S(1)} %stack.50.place_ref, bf16[640,768]{1,0:T(8,128)(2,1)S(1)} %get-tuple-element.70.refs_0_, bf16[3,640,128]{2,1,0:T(8,128)(2,1)S(1)} %get-tuple-element.83.refs_2_.refs_8_.refs_0_.refs_1_, ...), custom_call_target="tpu_custom_call" | custom-call | flops 1 | bytes 1 | tf_op jit(solution)/shard_map/pallas_call | solution.py:476
  107.5 4.0 %shard_map.344 = (bf16[320,768]{1,0:T(8,128)(2,1)}, f32[8,768]{1,0:T(8,128)S(1)}) custom-call(s32[5]{0:T(128)S(1)} %stack.50.place_ref, bf16[320,3072]{1,0:T(8,128)(2,1)S(1)} %copy-done.10, bf16[3072,768]{1,0:T(8,128)(2,1)S(1)} %copy-done, f32[320,768]{1,0:T(8,128)S(1)} %copy-done.28, bf16[320,768]{1,0:T(8,128)(2,1)S(1)} %fusion.refs_1_.refs_3_, ...), custom_call_target="tpu_custom_call" | custom-call | flops 1 | bytes 1 | tf_op jit(solution)/shard_map/pallas_call | solution.py:476
  113.0 1.9 shard_map.346.refs_3_
  114.9 1.5 collective-permute-start.12
  116.5 1.3 slice.197.refs_1_
  117.9 1.8 shard_map.347.refs_2_
  119.7 1.6 collective-permute-start.11
  122.5 1.5 collective-permute-start.5
  125.4 7.9 %collective-permute-done.12.refs_3_ = bf16[4,240,384]{2,1,0:T(8,128)(2,1)S(1)} collective-permute-done((bf16[4,240,384]{2,1,0:T(8,128)(2,1)S(1)}, bf16[4,240,384]{2,1,0:T(8,128)(2,1)S(1)}, u32[]{:S(2)}, u32[]{:S(2)}) %collective-permute-start.12) | collective-permute-done | bytes 737312 | tf_op jit(solution)/shard_map/ppermute | solution.py:432
  134.0 2.6 %collective-permute-start.17 = (bf16[2,240,384]{2,1,0:T(8,128)(2,1)S(1)}, bf16[2,240,384]{2,1,0:T(8,128)(2,1)S(1)}, u32[]{:S(2)}, u32[]{:S(2)}) collective-permute-start(bf16[2,240,384]{2,1,0:T(8,128)(2,1)S(1)} %shard_map.349.refs_4_), channel_id=1, source_target_pairs={{0,16},{1,17},{2,18},{3,19},{4,20},{5,21},{6,22},{7,23},{8,24},{9,... | collective-permute-start | bytes 1105928 | tf_op jit(solution)/shard_map/ppermute | solution.py:432
  139.7 1.6 collective-permute-start.16
  141.4 2.9 %collective-permute-done.10.refs_2_ = bf16[4,48,1152]{2,1,0:T(8,128)(2,1)S(1)} collective-permute-done((bf16[4,48,1152]{2,1,0:T(8,128)(2,1)S(1)}, bf16[4,48,1152]{2,1,0:T(8,128)(2,1)S(1)}, u32[]{:S(2)}, u32[]{:S(2)}) %collective-permute-start.10) | collective-permute-done | bytes 442400 | tf_op jit(solution)/shard_map/ppermute | solution.py:432
  146.9 2.0 %shard_map.353.refs_2_ = bf16[320,768]{1,0:T(8,128)(2,1)} custom-call(s32[5]{0:T(128)S(1)} %stack.50.place_ref, f32[320,768]{1,0:T(8,128)S(1)} %get-tuple-element.90.refs_0_, bf16[320,768]{1,0:T(8,128)(2,1)S(1)} %collective-permute-done.5.refs_1_, bf16[320,768]{1,0:T(8,128)(2,1)S(1)} %bitcast.26, f32[320,768]{1,0:T(8,128)S(1)} %copy-done.26, ...), custom_call_target="tpu_custom_call" | custom-call | flops 1 | bytes 1 | tf_op jit(solution)/shard_map/pallas_call | solution.py:476
  148.9 2.1 %collective-permute-done.13.refs_1_ = f32[128,256]{1,0:T(8,128)S(1)} collective-permute-done((f32[128,256]{1,0:T(8,128)S(1)}, f32[128,256]{1,0:T(8,128)S(1)}, u32[]{:S(2)}, u32[]{:S(2)}) %collective-permute-start.13) | collective-permute-done | bytes 131104 | tf_op jit(solution)/shard_map/ppermute | solution.py:432
  153.2 1.6 collective-permute-start.14
  160.4 1.2 shard_map.357.refs_2_
  161.7 1.8 collective-permute-start.20
  163.4 1.2 collective-permute-start.23
  165.0 1.5 shard_map.358.refs_0_
  166.5 2.4 %collective-permute-start.18 = (f32[128,256]{1,0:T(8,128)S(1)}, f32[128,256]{1,0:T(8,128)S(1)}, u32[]{:S(2)}, u32[]{:S(2)}) collective-permute-start(f32[128,256]{1,0:T(8,128)S(1)} %shard_map.358.refs_0_), channel_id=1, source_target_pairs={{0,16},{1,17},{2,18},{3,19},{4,20},{5,21},{6,22},{7,23},{8,24},{9,... | collective-permute-start | bytes 393224 | tf_op jit(solution)/shard_map/ppermute | solution.py:432
  168.9 6.0 %collective-permute-done.20 = bf16[1,48,1152]{2,1,0:T(8,128)(2,1)} collective-permute-done((bf16[1,48,1152]{2,1,0:T(8,128)(2,1)}, bf16[1,48,1152]{2,1,0:T(8,128)(2,1)}, u32[]{:S(2)}, u32[]{:S(2)}) %collective-permute-start.20) | collective-permute-done | bytes 110624 | tf_op jit(solution)/shard_map/ppermute | solution.py:432
  176.2 2.5 %collective-permute-done.18.refs_1_ = f32[128,256]{1,0:T(8,128)S(1)} collective-permute-done((f32[128,256]{1,0:T(8,128)S(1)}, f32[128,256]{1,0:T(8,128)S(1)}, u32[]{:S(2)}, u32[]{:S(2)}) %collective-permute-start.18) | collective-permute-done | bytes 131104 | tf_op jit(solution)/shard_map/ppermute | solution.py:432
  179.6 1.9 %add_bitcast_fusion = f32[48,1536]{1,0:T(8,128)} fusion(bf16[1,48,1536]{2,1,0:T(8,128)(2,1)S(1)} %collective-permute-done.23, bf16[2,48,1536]{2,1,0:T(8,128)(2,1)} %copy-done.32, bf16[4,48,1536]{2,1,0:T(8,128)(2,1)} %copy-done.24, bf16[8,48,1536]{2,1,0:T(8,128)(2,1)} %collective-permute-done.8.refs_2_, ...), kind=kLoop, calls=%fused_computation.4 | loop fusion | flops 811008 | bytes 1179648 | tf_op jit(solution)/shard_map/add | solution.py:441
  182.3 1.2 add_add_fusion
  184.9 2.4 %shard_map.360 = (f32[12,2212]{1,0:T(8,128)}, f32[1,768]{1,0:T(1,128)S(1)}, f32[1,768]{1,0:T(1,128)S(1)}, f32[1,768]{1,0:T(1,128)S(1)}, f32[1,768]{1,0:T(1,128)S...) custom-call(s32[5]{0:T(128)S(1)} %stack.50.place_ref, ...), custom_call_target="tpu_custom_call" | custom-call | flops 1 | bytes 1 | tf_op jit(solution)/shard_map/pallas_call | solution.py:476
  (166 shorter events, 41.9 us)
Async XLA Ops:
  0.7 14.5 %collective-permute-start = (bf16[320,768]{1,0:T(8,128)(2,1)}, bf16[320,768]{1,0:T(8,128)(2,1)S(1)}, u32[]{:S(2)}, u32[]{:S(2)}) collective-permute-start(bf16[320,768]{1,0:T(8,128)(2,1)} %bitcast.22), channel_id=1, source_target_pairs={{0,1},{1,0},{2,3},{3,2},{4,5},{5,4},{6,7},{7,6},{8,9},{9,8},{10,11... | collective-permute-start | bytes 1474568 | tf_op jit(solution)/shard_map/ppermute | solution.py:432
  6.4 15.3 %copy-start.23 = (f32[24,1280]{1,0:T(8,128)S(1)}, f32[24,1280]{1,0:T(8,128)}, u32[]{:S(2)}) copy-start(f32[24,1280]{1,0:T(8,128)} %constant.16.clone.refs_2_.refs_7_) | copy-start | bytes 368644
  13.4 94.0 %copy-start.33 = (f32[8,768]{1,0:T(8,128)}, f32[8,768]{1,0:T(8,128)S(1)}, u32[]{:S(2)}) copy-start(f32[8,768]{1,0:T(8,128)S(1)} %stack.59.refs_2_.refs_4_) | copy-start | bytes 73732
  18.2 3.6 %copy-start.20 = (bf16[320,768]{1,0:T(8,128)(2,1)}, bf16[320,768]{1,0:T(8,128)(2,1)S(1)}, u32[]{:S(2)}) copy-start(bf16[320,768]{1,0:T(8,128)(2,1)S(1)} %collective-permute-done.refs_1_.refs_5_) | copy-start | bytes 1474564
  18.2 16.7 %copy-start.39 = (bf16[1,320,768]{2,1,0:T(8,128)(2,1)S(1)}, bf16[1,320,768]{2,1,0:T(8,128)(2,1)}, u32[]{:S(2)}) copy-start(bf16[1,320,768]{2,1,0:T(8,128)(2,1)} %param.22) | copy-start | bytes 1474564
  18.2 22.1 %copy-start = (bf16[3072,768]{1,0:T(8,128)(2,1)S(1)}, bf16[3072,768]{1,0:T(8,128)(2,1)}, u32[]{:S(2)}) copy-start(bf16[3072,768]{1,0:T(8,128)(2,1)} %refs_1_.1) | copy-start | bytes 14155780
  21.7 18.6 %copy-start.5 = (bf16[768,768]{1,0:T(8,128)(2,1)S(1)}, bf16[768,768]{1,0:T(8,128)(2,1)}, u32[]{:S(2)}) copy-start(bf16[768,768]{1,0:T(8,128)(2,1)} %refs_10_.1) | copy-start | bytes 3538948
  21.8 18.5 %copy-start.38 = (f32[3072]{0:T(1024)S(1)}, f32[3072]{0:T(1024)}, u32[]{:S(2)}) copy-start(f32[3072]{0:T(1024)} %param.35) | copy-start | bytes 36868
  33.1 57.0 %copy-start.16 = (bf16[320,384]{1,0:T(8,128)(2,1)}, bf16[320,384]{1,0:T(8,128)(2,1)S(1)}, u32[]{:S(2)}) copy-start(bf16[320,384]{1,0:T(8,128)(2,1)S(1)} %get-tuple-element.67.refs_3_) | copy-start | bytes 737284
  33.1 7.2 %collective-permute-start.1 = (bf16[320,384]{1,0:T(8,128)(2,1)S(1)}, bf16[320,384]{1,0:T(8,128)(2,1)S(1)}, u32[]{:S(2)}, u32[]{:S(2)}) collective-permute-start(bf16[320,384]{1,0:T(8,128)(2,1)S(1)} %get-tuple-element.67.refs_3_), channel_id=1, source_target_pairs={{0,1},{1,0},{2,3},{3,2},{4,5},{5,4},{6,7},{7,6},{8,9},{9,8},{10,11... | collective-permute-start | bytes 737288 | tf_op jit(solution)/shard_map/ppermute | solution.py:432
  54.5 15.4 %copy-start.9 = (bf16[320,3072]{1,0:T(8,128)(2,1)}, bf16[320,3072]{1,0:T(8,128)(2,1)S(1)}, u32[]{:S(2)}) copy-start(bf16[320,3072]{1,0:T(8,128)(2,1)S(1)} %get-tuple-element.68.refs_0_) | copy-start | bytes 5898244
  54.5 15.4 %copy-start.27 = (f32[320,768]{1,0:T(8,128)}, f32[320,768]{1,0:T(8,128)S(1)}, u32[]{:S(2)}) copy-start(f32[320,768]{1,0:T(8,128)S(1)} %get-tuple-element.69.refs_2_) | copy-start | bytes 2949124
  54.5 15.4 %copy-start.19 = (bf16[320,3072]{1,0:T(8,128)(2,1)S(1)}, bf16[320,3072]{1,0:T(8,128)(2,1)}, u32[]{:S(2)}) copy-start(bf16[320,3072]{1,0:T(8,128)(2,1)} %copy-done.18) | copy-start | bytes 5898244
  61.6 93.3 %copy-start.3 = (bf16[16,240,384]{2,1,0:T(8,128)(2,1)}, bf16[16,240,384]{2,1,0:T(8,128)(2,1)S(1)}, u32[]{:S(2)}) copy-start(bf16[16,240,384]{2,1,0:T(8,128)(2,1)S(1)} %get-tuple-element.78.refs_0_) | copy-start | bytes 8847364
  61.6 14.3 %collective-permute-start.3 = (bf16[16,240,384]{2,1,0:T(8,128)(2,1)}, bf16[16,240,384]{2,1,0:T(8,128)(2,1)S(1)}, u32[]{:S(2)}, u32[]{:S(2)}) collective-permute-start(bf16[16,240,384]{2,1,0:T(8,128)(2,1)} %get-tuple-element.79.refs_2_), channel_id=1, source_target_pairs={{0,2},{1,3},{2,0},{3,1},{4,6},{5,7},{6,4},{7,5},{8,10},{9,11},{10,... | collective-permute-start | bytes 8847368 | tf_op jit(solution)/shard_map/ppermute | solution.py:432
  61.6 8.4 %collective-permute-start.2 = (bf16[320,384]{1,0:T(8,128)(2,1)S(1)}, bf16[320,384]{1,0:T(8,128)(2,1)S(1)}, u32[]{:S(2)}, u32[]{:S(2)}) collective-permute-start(bf16[320,384]{1,0:T(8,128)(2,1)S(1)} %get-tuple-element.73.refs_4_), channel_id=1, source_target_pairs={{0,1},{1,0},{2,3},{3,2},{4,5},{5,4},{6,7},{7,6},{8,9},{9,8},{10,11... | collective-permute-start | bytes 737288 | tf_op jit(solution)/shard_map/ppermute | solution.py:432
  75.9 8.1 %collective-permute-start.4 = (bf16[16,48,1536]{2,1,0:T(8,128)(2,1)}, bf16[16,48,1536]{2,1,0:T(8,128)(2,1)}, u32[]{:S(2)}, u32[]{:S(2)}) collective-permute-start(bf16[16,48,1536]{2,1,0:T(8,128)(2,1)} %get-tuple-element.82.refs_2_.refs_9_), channel_id=1, source_target_pairs={{0,2},{1,3},{2,0},{3,1},{4,6},{5,7},{6,4},{7,5},{8,10},{9,11},{10,... | collective-permute-start | bytes 7077896 | tf_op jit(solution)/shard_map/ppermute | solution.py:432
  75.9 80.0 %copy-start.4 = (bf16[16,240,384]{2,1,0:T(8,128)(2,1)}, bf16[16,240,384]{2,1,0:T(8,128)(2,1)S(1)}, u32[]{:S(2)}) copy-start(bf16[16,240,384]{2,1,0:T(8,128)(2,1)S(1)} %collective-permute-done.3.refs_1_) | copy-start | bytes 8847364
  78.2 34.8 %collective-permute-start.9 = (bf16[8,240,384]{2,1,0:T(8,128)(2,1)}, bf16[8,240,384]{2,1,0:T(8,128)(2,1)}, u32[]{:S(2)}, u32[]{:S(2)}) collective-permute-start(bf16[8,240,384]{2,1,0:T(8,128)(2,1)} %shard_map.337.refs_8_), channel_id=1, source_target_pairs={{0,4},{1,5},{2,6},{3,7},{4,0},{5,1},{6,2},{7,3},{8,12},{9,13},{10,... | collective-permute-start | bytes 4423688 | tf_op jit(solution)/shard_map/ppermute | solution.py:432
  88.5 29.4 %collective-permute-start.8 = (bf16[8,48,1536]{2,1,0:T(8,128)(2,1)}, bf16[8,48,1536]{2,1,0:T(8,128)(2,1)}, u32[]{:S(2)}, u32[]{:S(2)}) collective-permute-start(bf16[8,48,1536]{2,1,0:T(8,128)(2,1)} %shard_map.339.refs_9_), channel_id=1, source_target_pairs={{0,1},{1,0},{2,3},{3,2},{4,5},{5,4},{6,7},{7,6},{8,9},{9,8},{10,11... | collective-permute-start | bytes 3538952 | tf_op jit(solution)/shard_map/ppermute | solution.py:432
  95.4 4.4 %copy-start.2 = (bf16[768,2304]{1,0:T(8,128)(2,1)S(1)}, bf16[768,2304]{1,0:T(8,128)(2,1)}, u32[]{:S(2)}) copy-start(bf16[768,2304]{1,0:T(8,128)(2,1)} %refs_3_.3) | copy-start | bytes 10616836
  95.4 4.4 %copy-start.12 = (bf16[1,320,768]{2,1,0:T(8,128)(2,1)S(1)}, bf16[1,320,768]{2,1,0:T(8,128)(2,1)}, u32[]{:S(2)}) copy-start(bf16[1,320,768]{2,1,0:T(8,128)(2,1)} %param.20) | copy-start | bytes 1474564
  95.4 4.4 %copy-start.21 = (bf16[320,768]{1,0:T(8,128)(2,1)S(1)}, bf16[320,768]{1,0:T(8,128)(2,1)}, u32[]{:S(2)}) copy-start(bf16[320,768]{1,0:T(8,128)(2,1)} %copy-done.20) | copy-start | bytes 1474564
  107.2 48.7 %copy-start.14 = (bf16[8,48,1152]{2,1,0:T(8,128)(2,1)}, bf16[8,48,1152]{2,1,0:T(8,128)(2,1)S(1)}, u32[]{:S(2)}) copy-start(bf16[8,48,1152]{2,1,0:T(8,128)(2,1)S(1)} %get-tuple-element.99.refs_0_) | copy-start | bytes 2654212
  107.2 14.1 %collective-permute-start.7 = (bf16[8,48,1152]{2,1,0:T(8,128)(2,1)S(1)}, bf16[8,48,1152]{2,1,0:T(8,128)(2,1)S(1)}, u32[]{:S(2)}, u32[]{:S(2)}) collective-permute-start(bf16[8,48,1152]{2,1,0:T(8,128)(2,1)S(1)} %get-tuple-element.88.refs_5_), channel_id=1, source_target_pairs={{0,2},{1,3},{2,0},{3,1},{4,6},{5,7},{6,4},{7,5},{8,10},{9,11},{10,... | collective-permute-start | bytes 2654216 | tf_op jit(solution)/shard_map/ppermute | solution.py:432
  112.2 4.2 %copy-start.8 = (bf16[16,48,1536]{2,1,0:T(8,128)(2,1)S(1)}, bf16[16,48,1536]{2,1,0:T(8,128)(2,1)}, u32[]{:S(2)}) copy-start(bf16[16,48,1536]{2,1,0:T(8,128)(2,1)} %copy-done.6) | copy-start | bytes 7077892
  114.9 18.4 %collective-permute-start.12 = (bf16[4,240,384]{2,1,0:T(8,128)(2,1)S(1)}, bf16[4,240,384]{2,1,0:T(8,128)(2,1)S(1)}, u32[]{:S(2)}, u32[]{:S(2)}) collective-permute-start(bf16[4,240,384]{2,1,0:T(8,128)(2,1)S(1)} %shard_map.346.refs_3_), channel_id=1, source_target_pairs={{0,8},{1,9},{2,10},{3,11},{4,12},{5,13},{6,14},{7,15},{8,0},{9,1},... | collective-permute-start | bytes 2211848 | tf_op jit(solution)/shard_map/ppermute | solution.py:432
  119.7 19.2 %collective-permute-start.11 = (bf16[4,48,1536]{2,1,0:T(8,128)(2,1)S(1)}, bf16[4,48,1536]{2,1,0:T(8,128)(2,1)S(1)}, u32[]{:S(2)}, u32[]{:S(2)}) collective-permute-start(bf16[4,48,1536]{2,1,0:T(8,128)(2,1)S(1)} %shard_map.347.refs_2_), channel_id=1, source_target_pairs={{0,4},{1,5},{2,6},{3,7},{4,0},{5,1},{6,2},{7,3},{8,12},{9,13},{10,... | collective-permute-start | bytes 1769480 | tf_op jit(solution)/shard_map/ppermute | solution.py:432
  121.3 34.7 %copy-start.15 = (bf16[8,48,1152]{2,1,0:T(8,128)(2,1)}, bf16[8,48,1152]{2,1,0:T(8,128)(2,1)S(1)}, u32[]{:S(2)}) copy-start(bf16[8,48,1152]{2,1,0:T(8,128)(2,1)S(1)} %collective-permute-done.7.refs_1_) | copy-start | bytes 2654212
  121.9 22.3 %collective-permute-start.10 = (bf16[4,48,1152]{2,1,0:T(8,128)(2,1)S(1)}, bf16[4,48,1152]{2,1,0:T(8,128)(2,1)S(1)}, u32[]{:S(2)}, u32[]{:S(2)}) collective-permute-start(bf16[4,48,1152]{2,1,0:T(8,128)(2,1)S(1)} %shard_map.348.refs_4_), channel_id=1, source_target_pairs={{0,4},{1,5},{2,6},{3,7},{4,0},{5,1},{6,2},{7,3},{8,12},{9,13},{10,... | collective-permute-start | bytes 1327112 | tf_op jit(solution)/shard_map/ppermute | solution.py:432
  122.5 24.4 %collective-permute-start.5 = (bf16[320,768]{1,0:T(8,128)(2,1)S(1)}, bf16[320,768]{1,0:T(8,128)(2,1)S(1)}, u32[]{:S(2)}, u32[]{:S(2)}) collective-permute-start(bf16[320,768]{1,0:T(8,128)(2,1)S(1)} %get-tuple-element.87.refs_4_), channel_id=1, source_target_pairs={{0,1},{1,0},{2,3},{3,2},{4,5},{5,4},{6,7},{7,6},{8,9},{9,8},{10,11... | collective-permute-start | bytes 1474568 | tf_op jit(solution)/shard_map/ppermute | solution.py:432
  134.0 24.1 %collective-permute-start.17 = (bf16[2,240,384]{2,1,0:T(8,128)(2,1)S(1)}, bf16[2,240,384]{2,1,0:T(8,128)(2,1)S(1)}, u32[]{:S(2)}, u32[]{:S(2)}) collective-permute-start(bf16[2,240,384]{2,1,0:T(8,128)(2,1)S(1)} %shard_map.349.refs_4_), channel_id=1, source_target_pairs={{0,16},{1,17},{2,18},{3,19},{4,20},{5,21},{6,22},{7,23},{8,24},{9,... | collective-permute-start | bytes 1105928 | tf_op jit(solution)/shard_map/ppermute | solution.py:432
  138.9 19.1 %copy-start.24 = (bf16[4,48,1536]{2,1,0:T(8,128)(2,1)}, bf16[4,48,1536]{2,1,0:T(8,128)(2,1)S(1)}, u32[]{:S(2)}) copy-start(bf16[4,48,1536]{2,1,0:T(8,128)(2,1)S(1)} %collective-permute-done.11.refs_3_) | copy-start | bytes 1769476
  139.6 7.3 %copy-start.26 = (f32[320,768]{1,0:T(8,128)S(1)}, f32[320,768]{1,0:T(8,128)}, u32[]{:S(2)}) copy-start(f32[320,768]{1,0:T(8,128)} %copy-done.25) | copy-start | bytes 2949124
  139.7 7.3 %copy-start.34 = (f32[8,768]{1,0:T(8,128)S(1)}, f32[8,768]{1,0:T(8,128)}, u32[]{:S(2)}) copy-start(f32[8,768]{1,0:T(8,128)} %copy-done.33) | copy-start | bytes 73732
  139.7 19.2 %collective-permute-start.16 = (bf16[2,48,1536]{2,1,0:T(8,128)(2,1)S(1)}, bf16[2,48,1536]{2,1,0:T(8,128)(2,1)S(1)}, u32[]{:S(2)}, u32[]{:S(2)}) collective-permute-start(bf16[2,48,1536]{2,1,0:T(8,128)(2,1)S(1)} %shard_map.350.refs_3_), channel_id=1, source_target_pairs={{0,8},{1,9},{2,10},{3,11},{4,12},{5,13},{6,14},{7,15},{8,0},{9,1},... | collective-permute-start | bytes 884744 | tf_op jit(solution)/shard_map/ppermute | solution.py:432
  141.3 4.1 %collective-permute-start.6 = (f32[128,256]{1,0:T(8,128)S(1)}, f32[128,256]{1,0:T(8,128)S(1)}, u32[]{:S(2)}, u32[]{:S(2)}) collective-permute-start(f32[128,256]{1,0:T(8,128)S(1)} %shard_map.345.refs_3_.refs_0_), channel_id=1, source_target_pairs={{0,2},{1,3},{2,0},{3,1},{4,6},{5,7},{6,4},{7,5},{8,10},{9,11},{10,... | collective-permute-start | bytes 393224 | tf_op jit(solution)/shard_map/ppermute | solution.py:432
  144.9 15.5 %collective-permute-start.15 = (bf16[2,48,1152]{2,1,0:T(8,128)(2,1)S(1)}, bf16[2,48,1152]{2,1,0:T(8,128)(2,1)S(1)}, u32[]{:S(2)}, u32[]{:S(2)}) collective-permute-start(bf16[2,48,1152]{2,1,0:T(8,128)(2,1)S(1)} %shard_map.351.refs_2_), channel_id=1, source_target_pairs={{0,8},{1,9},{2,10},{3,11},{4,12},{5,13},{6,14},{7,15},{8,0},{9,1},... | collective-permute-start | bytes 663560 | tf_op jit(solution)/shard_map/ppermute | solution.py:432
  146.0 5.0 %collective-permute-start.13 = (f32[128,256]{1,0:T(8,128)S(1)}, f32[128,256]{1,0:T(8,128)S(1)}, u32[]{:S(2)}, u32[]{:S(2)}) collective-permute-start(f32[128,256]{1,0:T(8,128)S(1)} %shard_map.352.refs_5_.refs_0_), channel_id=1, source_target_pairs={{0,4},{1,5},{2,6},{3,7},{4,0},{5,1},{6,2},{7,3},{8,12},{9,13},{10,... | collective-permute-start | bytes 393224 | tf_op jit(solution)/shard_map/ppermute | solution.py:432
  153.2 11.8 %collective-permute-start.14 = (f32[128,256]{1,0:T(8,128)}, f32[128,256]{1,0:T(8,128)}, u32[]{:S(2)}, u32[]{:S(2)}) collective-permute-start(f32[128,256]{1,0:T(8,128)} %shard_map.354.refs_5_.refs_0_), channel_id=1, source_target_pairs={{0,8},{1,9},{2,10},{3,11},{4,12},{5,13},{6,14},{7,15},{8,0},{9,1},... | collective-permute-start | bytes 393224 | tf_op jit(solution)/shard_map/ppermute | solution.py:432
  158.1 3.5 %copy-start.29 = (bf16[2,240,384]{2,1,0:T(8,128)(2,1)}, bf16[2,240,384]{2,1,0:T(8,128)(2,1)S(1)}, u32[]{:S(2)}) copy-start(bf16[2,240,384]{2,1,0:T(8,128)(2,1)S(1)} %collective-permute-done.17.refs_4_) | copy-start | bytes 1105924
  161.7 13.3 %collective-permute-start.20 = (bf16[1,48,1152]{2,1,0:T(8,128)(2,1)}, bf16[1,48,1152]{2,1,0:T(8,128)(2,1)}, u32[]{:S(2)}, u32[]{:S(2)}) collective-permute-start(bf16[1,48,1152]{2,1,0:T(8,128)(2,1)} %shard_map.357.refs_2_), channel_id=1, source_target_pairs={{0,16},{1,17},{2,18},{3,19},{4,20},{5,21},{6,22},{7,23},{8,24},{9,... | collective-permute-start | bytes 331784 | tf_op jit(solution)/shard_map/ppermute | solution.py:432
  163.4 18.9 %copy-start.30 = (bf16[2,240,384]{2,1,0:T(8,128)(2,1)S(1)}, bf16[2,240,384]{2,1,0:T(8,128)(2,1)}, u32[]{:S(2)}) copy-start(bf16[2,240,384]{2,1,0:T(8,128)(2,1)} %copy-done.29) | copy-start | bytes 1105924
  163.4 16.2 %collective-permute-start.23 = (bf16[1,48,1536]{2,1,0:T(8,128)(2,1)}, bf16[1,48,1536]{2,1,0:T(8,128)(2,1)S(1)}, u32[]{:S(2)}, u32[]{:S(2)}) collective-permute-start(bf16[1,48,1536]{2,1,0:T(8,128)(2,1)} %copy-done.35), channel_id=1, source_target_pairs={{0,16},{1,17},{2,18},{3,19},{4,20},{5,21},{6,22},{7,23},{8,24},{9,... | collective-permute-start | bytes 442376 | tf_op jit(solution)/shard_map/ppermute | solution.py:432
  164.7 17.6 %collective-permute-start.22 = (bf16[1,240,384]{2,1,0:T(8,128)(2,1)}, bf16[1,240,384]{2,1,0:T(8,128)(2,1)S(1)}, u32[]{:S(2)}, u32[]{:S(2)}) collective-permute-start(bf16[1,240,384]{2,1,0:T(8,128)(2,1)} %copy-done.31), channel_id=1, source_target_pairs={{0,1},{1,0},{2,3},{3,2},{4,5},{5,4},{6,7},{7,6},{8,9},{9,8},{10,11... | collective-permute-start | bytes 552968 | tf_op jit(solution)/shard_map/ppermute | solution.py:432
  166.5 12.1 %collective-permute-start.18 = (f32[128,256]{1,0:T(8,128)S(1)}, f32[128,256]{1,0:T(8,128)S(1)}, u32[]{:S(2)}, u32[]{:S(2)}) collective-permute-start(f32[128,256]{1,0:T(8,128)S(1)} %shard_map.358.refs_0_), channel_id=1, source_target_pairs={{0,16},{1,17},{2,18},{3,19},{4,20},{5,21},{6,22},{7,23},{8,24},{9,... | collective-permute-start | bytes 393224 | tf_op jit(solution)/shard_map/ppermute | solution.py:432
  176.1 5.5 %collective-permute-start.21 = (bf16[48,384]{1,0:T(8,128)(2,1)S(1)}, bf16[48,384]{1,0:T(8,128)(2,1)S(1)}, u32[]{:S(2)}, u32[]{:S(2)}) collective-permute-start(bf16[48,384]{1,0:T(8,128)(2,1)S(1)} %select_convert_fusion), channel_id=1, source_target_pairs={{0,1},{1,0},{2,3},{3,2},{4,5},{5,4},{6,7},{7,6},{8,9},{9,8},{10,11... | collective-permute-start | bytes 110600 | tf_op jit(solution)/shard_map/ppermute | solution.py:432
  179.3 5.7 %collective-permute-start.19 = (f32[128,256]{1,0:T(8,128)S(1)}, f32[128,256]{1,0:T(8,128)S(1)}, u32[]{:S(2)}, u32[]{:S(2)}) collective-permute-start(f32[128,256]{1,0:T(8,128)S(1)} %shard_map.359.refs_0_), channel_id=1, source_target_pairs={{0,1},{1,0},{2,3},{3,2},{4,5},{5,4},{6,7},{7,6},{8,9},{9,8},{10,11... | collective-permute-start | bytes 393224 | tf_op jit(solution)/shard_map/ppermute | solution.py:432
  (16 other events, 30.5 us)

commit v3 on v2

--- a/solution.py
+++ b/solution.py
@@ -394,6 +394,7 @@
 
 
 LANES = 128
+RATE = 1.15e9
 STRIP = 24
 STRIP_WIDTH = 1280
 MEGA = 1 << 20
@@ -432,11 +433,6 @@
     return lax.ppermute(value, ("img", "seq"), swap_pairs(*names))
 
 
-def half_in(terms, out, name):
-    size = terms[0].shape[0] // 2
-    return [term[:size] for term in terms] + [swapped(out, name)]
-
-
 def added(terms):
     return sum(term[0].astype(F32) for term in terms)
 
@@ -465,9 +461,26 @@
     return pl.BlockSpec(shape, lambda *_: zeros)
 
 
-def run(kernel, place, grid, in_specs, out_specs, out_shapes, scratch, operands, flops, vmem=32, after=()):
+SIZES = {
+    "strips_kernel": (1.7, 6),
+    "qkv_kernel": (3.5, 12),
+    "attend_kernel": (11.0, 16),
+    "ffn_kernel": (9.5, 26),
+    "fc2_grad_kernel": (5.4, 26),
+    "fc1_grad_kernel": (4.6, 24),
+    "attend_back_kernel": (4.4, 16),
+    "hidden1_grad_kernel": (4.2, 14),
+    "qkv_grad_kernel": (3.2, 16),
+    "result_kernel": (4.0, 12),
+    "tokens_grad_kernel": (2.0, 12),
+}
+
+
+def run(kernel, place, grid, in_specs, out_specs, out_shapes, scratch, operands, flops, after=(), us=None):
     held = len(operands)
     inner = kernel
+    cost, vmem = SIZES.get(getattr(kernel, "func", kernel).__name__, (1.5, 10))
+    us = us or cost
 
     def kernel(place_ref, *refs):
         inner(place_ref, *refs[:held], *refs[held + len(after) :])
@@ -484,7 +497,7 @@
         ),
         out_shape=out_shapes,
         compiler_params=pltpu.CompilerParams(vmem_limit_bytes=vmem * MEGA),
-        cost_estimate=pl.CostEstimate(flops=1, bytes_accessed=1, transcendentals=0),
+        cost_estimate=pl.CostEstimate(flops=int(us * RATE), bytes_accessed=1, transcendentals=0),
     )(place, *operands, *after)
 
 
@@ -493,13 +506,23 @@
 
 
 def half_out(place, terms, after=()):
-    size = terms[0].shape[0] // 2
+    size = terms[-1].shape[0] // 2
     block = (min(size, 4), *terms[0].shape[1:])
     count = size // block[0]
     return run(
         add_kernel, place, (count,), [spec(block, lambda n, p: (n + count, 0, 0))] * len(terms),
         [spec(block, lambda n, p: (n, 0, 0))], [shape((size, *block[1:]), BF)], [], tuple(terms), 0,
         after=after,
+    )[0]
+
+
+def rest_of(place, terms, after=()):
+    size = terms[-1].shape[0] // 2
+    block = (min(size, 4), *terms[0].shape[1:])
+    same = spec(block, lambda n, p: (n, 0, 0))
+    return run(
+        add_kernel, place, (size // block[0],), [same] * len(terms), [same],
+        [shape((size, *block[1:]), BF)], [], tuple(terms), 0, after=after,
     )[0]
 
 
@@ -1037,17 +1060,17 @@
         lanes = slice(256 * n, 256 * n + 256)
         for at, out in enumerate(outs):
             row = 80 + 16 * n + at
-            out[0:1, lanes] = packed[row : row + 1, :] + mate[row : row + 1, :]
+            out[lanes] = (packed[row : row + 1, :] + mate[row : row + 1, :]).reshape(256)
         for part in range(4):
             row = 89 + 16 * n + part
-            fc1_bias[0:1, 768 * part + 256 * n : 768 * part + 256 * n + 256] = (
+            fc1_bias[768 * part + 256 * n : 768 * part + 256 * n + 256] = (
                 packed[row : row + 1, :] + mate[row : row + 1, :]
-            )
+            ).reshape(256)
     for source, side in ((packed, place[0]), (mate, 1 - place[0])):
         line = jnp.concatenate([source[88 + 16 * n : 89 + 16 * n, :] for n in range(3)], axis=1)
         lanes = pl.ds(pl.multiple_of(side * 384, LANES), 384)
-        query_bias[0:1, lanes] = line[:, :384]
-        value_bias[0:1, lanes] = line[:, 384:]
+        query_bias[lanes] = line[:, :384].reshape(384)
+        value_bias[lanes] = line[:, 384:].reshape(384)
 
 
 def even_places():
@@ -1190,11 +1213,12 @@
         [whole, sliced], [full(block), full(block)],
         [shape(block, BF), shape(block, BF)],
         [pltpu.VMEM((width, part), F32)], (hidden2, d_pre),
-        2 * rows * width * (hidden + width), after=(send_a, grad_other),
+        2 * rows * width * (hidden + width), after=(send_a,),
     )
     terms_b = [keep_b, swapped(send_b, "core")]
+
     out_a1 = half_out(place, terms_a, (send_b,))
-    terms_a = half_in(terms_a, out_a1, ORDER_A[1])
+    terms_a = [rest_of(place, terms_a, (out_a1,)), swapped(out_a1, ORDER_A[1])]
 
     def attend_back(pair, after):
         pair_expo = spec((2, slots, slots), lambda n, p: (pair, 0, 0))
@@ -1214,13 +1238,13 @@
                 pltpu.VMEM((slots, LANES), F32),
             ],
             (qkv, expo, attn_own, attn_send, grad_own, grad_other, inv, even_mask),
-            32 * slots * slots * 64 * 2, after=after,
+            32 * slots * slots * 64 * 2, after=after, us=40.0 if pair == 0 else None,
         )
 
-    dqkv0, strip0 = attend_back(0, (out_a1, send_b))
+    dqkv0, strip0 = attend_back(0, (out_a1, terms_a[0]))
     out_b1 = half_out(place, terms_b, (dqkv0,))
-    terms_b = half_in(terms_b, out_b1, ORDER_B[1])
-    dqkv1, strip1 = attend_back(1, (dqkv0, out_b1))
+    terms_b = [rest_of(place, terms_b, (out_b1,)), swapped(out_b1, ORDER_B[1])]
+    dqkv1, strip1 = attend_back(1, (dqkv0, out_b1, terms_b[0]))
     dqkv2, strip2 = attend_back(2, (dqkv1,))
     dqkv = (dqkv0, dqkv1, dqkv2)
     third = [spec((1, slots, LANES), lambda t, p: (t, 0, 0))] * 3
@@ -1256,19 +1280,19 @@
         (strip0, strip1, strip2, small_ffn, fc1_bias_part, small_last, small_result), 0,
     )[0]
     out_a2 = half_out(place, terms_a, (packed,))
-    terms_a = half_in(terms_a, out_a2, "z1")
+    terms_a = [*terms_a, swapped(out_a2, "z1")]
     out_b2 = half_out(place, terms_b, (out_a2,))
-    terms_b = half_in(terms_b, out_b2, "x")
+    terms_b = [*terms_b, swapped(out_b2, "x")]
     out_q1 = half_out(place, terms_q, (out_b2,))
-    terms_q = half_in(terms_q, out_q1, "x")
+    terms_q = [*terms_q, swapped(out_q1, "x")]
     mate = swapped(packed, "core")
     dh_recv = swapped(dh_send, "y")
     out_a3 = half_out(place, terms_a, (out_q1,))
-    terms_a = half_in(terms_a, out_a3, "z2")
+    terms_a = [*terms_a, swapped(out_a3, "z2")]
     out_b3 = half_out(place, terms_b, (out_a3,))
-    terms_b = half_in(terms_b, out_b3, "z1")
+    terms_b = [*terms_b, swapped(out_b3, "z1")]
     out_q2 = half_out(place, terms_q, (out_b3,))
-    terms_q = half_in(terms_q, out_q2, "z1")
+    terms_q = [*terms_q, swapped(out_q2, "z1")]
     packed = summed(place, packed, mate, (out_q2,))
     mate = swapped(packed, "x")
     tokens_grad = run(
@@ -1280,11 +1304,11 @@
     packed = summed(place, packed, mate, (tokens_grad,))
     mate = swapped(packed, "z1")
     out_a4 = half_out(place, terms_a, (packed,))
-    terms_a = half_in(terms_a, out_a4, "y")
+    terms_a = [*terms_a, swapped(out_a4, "y")]
     out_b4 = half_out(place, terms_b, (out_a4,))
-    terms_b = half_in(terms_b, out_b4, "z2")
+    terms_b = [*terms_b, swapped(out_b4, "z2")]
     out_q3 = half_out(place, terms_q, (out_b4,))
-    terms_q = half_in(terms_q, out_q3, "z2")
+    terms_q = [*terms_q, swapped(out_q3, "z2")]
     packed = summed(place, packed, mate, (out_q3,))
     mate = swapped(packed, "z2")
     packed = summed(place, packed, mate)
@@ -1303,14 +1327,13 @@
         jnp.concatenate([qkv_part[:, share : 2 * share], taken, qkv_part[:, 2 * share :]], axis=1),
     )
 
-    vector = shape((1, width), F32)
+    vector = shape((width,), F32)
     table_grad, *small = run(
         unpack_kernel, place, (1,), [full((128, 256))] * 2,
-        [full(rel_table.shape[::-1]), *[full((1, width))] * 10, full((1, hidden))],
-        [shape(rel_table.shape[::-1], F32), *[vector] * 10, shape((1, hidden), F32)],
+        [full(rel_table.shape[::-1]), *[full((width,))] * 10, full((hidden,))],
+        [shape(rel_table.shape[::-1], F32), *[vector] * 10, shape((hidden,), F32)],
         [pltpu.VMEM((16, 2432), F32), pltpu.VMEM((2, 16, STRIP_WIDTH), F32)], (packed, mate), 0,
     )
-    small = [part.reshape(-1) for part in small]
     return (
         result.reshape(tokens.shape),
         tokens_grad.reshape(tokens.shape),

time: 195 us -> 167 us (0.86)
  local copies, waits for them, and re-layouts: 29.3 us -> 13.8 us
  other arithmetic: 11.9 us -> 4.37 us
  Pallas kernels: 86.6 us -> 84.1 us
    slice x23 -> x0, local copies, waits for them, and re-layouts: 8.59 us -> none  [half_in(): return [term[:size] for term in terms] + [swapped(out, name)]]
    unnamed x80 -> x62, local copies, waits for them, and re-layouts: 12.3 us -> 5.37 us
    pallas_call x10 -> x0, other arithmetic: 6.05 us -> none  [run(): pl.pallas_call(kernel, grid_spec=pltpu.PrefetchScalarGridSpec(num_scalar_...]
    pallas_call x30 -> x32, Pallas kernels: 86.6 us -> 84.1 us  [run(): pl.pallas_call(kernel, grid_spec=pltpu.PrefetchScalarGridSpec(num_scalar_...]
  transfers between devices with their start and end apart: 24 -> 24, of which waited for: 10 -> 10; matrix products, arithmetic and copies ran while one was open for 12% -> 8% of each run, Pallas kernels for 27% -> 31%
where the time goes in v3:
time: 167 us
  Pallas kernels  84.1 us (50%)
  waiting for transfers between devices  34.9 us (21%)
  starting transfers between devices  28.2 us (17%)
  local copies, waits for them, and re-layouts  13.8 us (8%)
  other arithmetic  4.37 us (3%)
    pallas_call x32, Pallas kernels, run(): pl.pallas_call(kernel, grid_spec=pltpu.PrefetchScalarGridSpec(num_scalar_...  84.1 us
    ppermute x24, waiting for transfers between devices, swapped(): return lax.ppermute(value, ('img', 'seq'), swap_pairs(*names))  34.9 us
    ppermute x24, starting transfers between devices, swapped(): return lax.ppermute(value, ('img', 'seq'), swap_pairs(*names))  28.2 us
    another operation x9, local copies, waits for them, and re-layouts, split_body(): jnp.stack([norm1_gain, norm1_bias, proj_bias, scale1, norm2_gain, norm2_b...  5.56 us
    unnamed x62, local copies, waits for them, and re-layouts  5.37 us
  transfers between devices with their start and end apart: 24, of which 10 were waited for; matrix products, arithmetic and copies ran while one was open for 8% of the time, Pallas kernels for 31%

profile of v3, /device:TPU:0, one launch (start us, length us, event | category | flops | bytes accessed | tf_op | source)
XLA Modules:
  0.0 166.7 jit_solution(14683183121832022601)
XLA Ops:
  0.7 3.0 %collective-permute-start = (bf16[320,768]{1,0:T(8,128)(2,1)}, bf16[320,768]{1,0:T(8,128)(2,1)S(1)}, u32[]{:S(2)}, u32[]{:S(2)}) collective-permute-start(bf16[320,768]{1,0:T(8,128)(2,1)} %bitcast.25), channel_id=1, source_target_pairs={{0,1},{1,0},{2,3},{3,2},{4,5},{5,4},{6,7},{7,6},{8,9},{9,8},{10,11... | collective-permute-start | bytes 1474568 | tf_op jit(solution)/shard_map/ppermute | solution.py:433
  12.3 1.7 %shard_map.332.refs_1_ = f32[12,2,1280]{2,1,0:T(2,128)S(1)} custom-call(s32[5]{0:T(128)S(1)} %stack.50.place_ref, f32[12,2212]{1,0:T(8,128)S(1)} %bitcast.30), custom_call_target="tpu_custom_call" | custom-call | flops 1955000064 | bytes 1 | tf_op jit(solution)/shard_map/pallas_call | solution.py:489
  14.1 1.0 collective-permute-done.refs_1_.refs_5_
  15.2 3.6 %shard_map.331 = (bf16[3,640,384]{2,1,0:T(8,128)(2,1)S(1)}, bf16[640,768]{1,0:T(8,128)(2,1)S(1)}) custom-call(s32[5]{0:T(128)S(1)} %stack.50.place_ref, bf16[320,768]{1,0:T(8,128)(2,1)S(1)} %bitcast.26, bf16[320,768]{1,0:T(8,128)(2,1)S(1)} %collective-permute-done.refs_1_.refs_5_, f32[8,768]{1,0:T(8,128)S(1)} %stack.59.refs_2_.refs_4_, ...), custom_call_target="tpu_custom_call" | custom-call | flops 4024999936 | bytes 1 | tf_op jit(solution)/shard_map/pallas_call | solution.py:489
  18.8 1.0 copy-done.24
  19.8 11.3 %shard_map.333 = (bf16[320,384]{1,0:T(8,128)(2,1)S(1)}, bf16[320,384]{1,0:T(8,128)(2,1)S(1)}, bf16[6,640,640]{2,1,0:T(8,128)(2,1)S(1)}, f32[640,384]{1,0:T(8,128)S(1)}) custom-call(s32[5]{0:T(128)S(1)} %stack.50.place_ref, bf16[3,640,384]{2,1,0:T(8,128)(2,1)S(1)} %get-tuple-element.65.refs_0_, f32[12,2,1280]{2,1,0:T(2,128)S(1)} %shard_map.332.refs_1_, ...), custom_call_target="tpu_custom_call" | custom-call | flops 12650000384 | bytes 1 | tf_op jit(solution)/shard_map/pallas_call | solution.py:489
  31.1 1.8 %collective-permute-start.1 = (bf16[320,384]{1,0:T(8,128)(2,1)S(1)}, bf16[320,384]{1,0:T(8,128)(2,1)S(1)}, u32[]{:S(2)}, u32[]{:S(2)}) collective-permute-start(bf16[320,384]{1,0:T(8,128)(2,1)S(1)} %get-tuple-element.67.refs_3_), channel_id=1, source_target_pairs={{0,1},{1,0},{2,3},{3,2},{4,5},{5,4},{6,7},{7,6},{8,9},{9,8},{10,11... | collective-permute-start | bytes 737288 | tf_op jit(solution)/shard_map/ppermute | solution.py:433
  33.0 5.3 %collective-permute-done.1.refs_3_ = bf16[320,384]{1,0:T(8,128)(2,1)S(1)} collective-permute-done((bf16[320,384]{1,0:T(8,128)(2,1)S(1)}, bf16[320,384]{1,0:T(8,128)(2,1)S(1)}, u32[]{:S(2)}, u32[]{:S(2)}) %collective-permute-start.1) | collective-permute-done | bytes 245792 | tf_op jit(solution)/shard_map/ppermute | solution.py:433
  38.4 9.7 %shard_map.334 = (bf16[320,3072]{1,0:T(8,128)(2,1)S(1)}, bf16[320,3072]{1,0:T(8,128)(2,1)S(1)}, f32[1,3072]{1,0:T(1,128)S(1)}, bf16[320,768]{1,0:T(8,128)(2,1)S(...) custom-call(s32[5]{0:T(128)S(1)} %stack.50.place_ref, ...), custom_call_target="tpu_custom_call" | custom-call | flops 10924999680 | bytes 1 | tf_op jit(solution)/shard_map/pallas_call | solution.py:489
  48.1 5.5 %shard_map.335 = (bf16[16,240,384]{2,1,0:T(8,128)(2,1)S(1)}, bf16[16,240,384]{2,1,0:T(8,128)(2,1)S(1)}) custom-call(s32[5]{0:T(128)S(1)} %stack.50.place_ref, bf16[320,3072]{1,0:T(8,128)(2,1)S(1)} %get-tuple-element.68.refs_0_, bf16[320,768]{1,0:T(8,128)(2,1)S(1)} %get-tuple-element.75.refs_1_, bf16[320,768]{1,0:T(8,128)(2,1)S(1)} %get-tuple-element.76.refs_2_, ...), custom_call_target="tpu_custom_call" | custom-call | flops 6209999872 | bytes 1 | tf_op jit(solution)/shard_map/pallas_call | solution.py:489
  53.7 1.5 collective-permute-start.2
  55.1 4.5 %shard_map.336 = (bf16[16,48,1536]{2,1,0:T(8,128)(2,1)S(1)}, bf16[16,48,1536]{2,1,0:T(8,128)(2,1)S(1)}) custom-call(s32[5]{0:T(128)S(1)} %stack.50.place_ref, bf16[320,768]{1,0:T(8,128)(2,1)S(1)} %get-tuple-element.80.refs_0_, bf16[320,3072]{1,0:T(8,128)(2,1)S(1)} %get-tuple-element.81.refs_1_, bf16[16,240,384]{2,1,0:T(8,128)(2,1)S(1)} %get-tuple-element.79.refs_2_), custom_call_target="tpu_custom_call" | custom-call | flops 5289999872 | bytes 1 | tf_op jit(solution)/shard_map/pallas_call | solution.py:489
  60.8 1.6 collective-permute-start.9
  62.4 1.1 shard_map.338.refs_9_.refs_0_
  63.5 4.4 %shard_map.339 = (bf16[3,640,128]{2,1,0:T(8,128)(2,1)S(1)}, f32[1,2,2,1280]{3,2,1,0:T(2,128)S(1)}) custom-call(s32[5]{0:T(128)S(1)} %stack.50.place_ref, bf16[3,640,384]{2,1,0:T(8,128)(2,1)S(1)} %get-tuple-element.65.refs_0_, bf16[6,640,640]{2,1,0:T(8,128)(2,1)S(1)} %get-tuple-element.71.refs_1_, bf16[320,384]{1,0:T(8,128)(2,1)S(1)} %get-tuple-element.66.refs_2_, ...), custom_call_target="tpu_custom_call" | custom-call | flops 46000001024 | bytes 1 | tf_op jit(solution)/shard_map/pallas_call | solution.py:489
  70.3 4.4 %shard_map.342 = (bf16[3,640,128]{2,1,0:T(8,128)(2,1)S(1)}, f32[1,2,2,1280]{3,2,1,0:T(2,128)S(1)}) custom-call(s32[5]{0:T(128)S(1)} %stack.50.place_ref, bf16[3,640,384]{2,1,0:T(8,128)(2,1)S(1)} %get-tuple-element.65.refs_0_, bf16[6,640,640]{2,1,0:T(8,128)(2,1)S(1)} %get-tuple-element.71.refs_1_, bf16[320,384]{1,0:T(8,128)(2,1)S(1)} %get-tuple-element.66.refs_2_, ...), custom_call_target="tpu_custom_call" | custom-call | flops 5059999744 | bytes 1 | tf_op jit(solution)/shard_map/pallas_call | solution.py:489
  74.8 4.4 %shard_map.343 = (bf16[3,640,128]{2,1,0:T(8,128)(2,1)S(1)}, f32[1,2,2,1280]{3,2,1,0:T(2,128)S(1)}) custom-call(s32[5]{0:T(128)S(1)} %stack.50.place_ref, bf16[3,640,384]{2,1,0:T(8,128)(2,1)S(1)} %get-tuple-element.65.refs_0_, bf16[6,640,640]{2,1,0:T(8,128)(2,1)S(1)} %get-tuple-element.71.refs_1_, bf16[320,384]{1,0:T(8,128)(2,1)S(1)} %get-tuple-element.66.refs_2_, ...), custom_call_target="tpu_custom_call" | custom-call | flops 5059999744 | bytes 1 | tf_op jit(solution)/shard_map/pallas_call | solution.py:489
  79.3 4.2 %shard_map.344 = (f32[320,768]{1,0:T(8,128)S(1)}, bf16[320,768]{1,0:T(8,128)(2,1)S(1)}, f32[8,768]{1,0:T(8,128)S(1)}) custom-call(s32[5]{0:T(128)S(1)} %stack.50.place_ref, bf16[3,640,128]{2,1,0:T(8,128)(2,1)S(1)} %get-tuple-element.83.refs_2_.refs_8_.refs_0_.refs_1_, bf16[3,640,128]{2,1,0:T(8,128)(2,1)S(1)} %get-tuple-element.85.refs_8_.refs_1_.refs_2_, ...), custom_call_target="tpu_custom_call" | custom-call | flops 4830000128 | bytes 1 | tf_op jit(solution)/shard_map/pallas_call | solution.py:489
  84.4 3.1 %shard_map.345 = (bf16[8,48,1152]{2,1,0:T(8,128)(2,1)S(1)}, bf16[8,48,1152]{2,1,0:T(8,128)(2,1)S(1)}) custom-call(s32[5]{0:T(128)S(1)} %stack.50.place_ref, bf16[640,768]{1,0:T(8,128)(2,1)S(1)} %copy-done.25, bf16[3,640,128]{2,1,0:T(8,128)(2,1)S(1)} %get-tuple-element.83.refs_2_.refs_8_.refs_0_.refs_1_, ...), custom_call_target="tpu_custom_call" | custom-call | flops 3680000000 | bytes 1 | tf_op jit(solution)/shard_map/pallas_call | solution.py:489
  87.7 4.0 %shard_map.346 = (bf16[320,768]{1,0:T(8,128)(2,1)}, f32[8,768]{1,0:T(8,128)S(1)}) custom-call(s32[5]{0:T(128)S(1)} %stack.50.place_ref, bf16[320,3072]{1,0:T(8,128)(2,1)S(1)} %get-tuple-element.68.refs_0_, bf16[3072,768]{1,0:T(8,128)(2,1)S(1)} %bitcast.24, f32[320,768]{1,0:T(8,128)S(1)} %get-tuple-element.69.refs_2_, ...), custom_call_target="tpu_custom_call" | custom-call | flops 4600000000 | bytes 1 | tf_op jit(solution)/shard_map/pallas_call | solution.py:489
  92.3 3.1 %collective-permute-done.9.refs_1_ = bf16[8,240,384]{2,1,0:T(8,128)(2,1)S(1)} collective-permute-done((bf16[8,240,384]{2,1,0:T(8,128)(2,1)S(1)}, bf16[8,240,384]{2,1,0:T(8,128)(2,1)S(1)}, u32[]{:S(2)}, u32[]{:S(2)}) %collective-permute-start.9) | collective-permute-done | bytes 1474592 | tf_op jit(solution)/shard_map/ppermute | solution.py:433
  95.4 1.6 shard_map.348.refs_2_
  97.0 1.6 collective-permute-start.12
  98.6 1.6 shard_map.349.refs_2_
  100.2 1.5 collective-permute-start.11
  101.7 1.4 shard_map.350.refs_3_
  104.2 11.0 %collective-permute-done.12.refs_2_ = bf16[4,240,384]{2,1,0:T(8,128)(2,1)S(1)} collective-permute-done((bf16[4,240,384]{2,1,0:T(8,128)(2,1)}, bf16[4,240,384]{2,1,0:T(8,128)(2,1)S(1)}, u32[]{:S(2)}, u32[]{:S(2)}) %collective-permute-start.12) | collective-permute-done | bytes 737312 | tf_op jit(solution)/shard_map/ppermute | solution.py:433
  115.2 1.4 copy-done.1
  117.2 2.6 %collective-permute-start.17 = (bf16[2,240,384]{2,1,0:T(8,128)(2,1)S(1)}, bf16[2,240,384]{2,1,0:T(8,128)(2,1)S(1)}, u32[]{:S(2)}, u32[]{:S(2)}) collective-permute-start(bf16[2,240,384]{2,1,0:T(8,128)(2,1)S(1)} %shard_map.351.refs_3_), channel_id=1, source_target_pairs={{0,16},{1,17},{2,18},{3,19},{4,20},{5,21},{6,22},{7,23},{8,24},{9,... | collective-permute-start | bytes 1105928 | tf_op jit(solution)/shard_map/ppermute | solution.py:433
  119.9 1.6 shard_map.352.refs_3_
  121.5 1.6 collective-permute-start.16
  123.2 1.3 collective-permute-done.10.refs_2_
  124.5 1.6 shard_map.353.refs_2_
  127.2 1.6 collective-permute-start.13
  128.7 2.0 %shard_map.355.refs_2_ = bf16[320,768]{1,0:T(8,128)(2,1)} custom-call(s32[5]{0:T(128)S(1)} %stack.50.place_ref, f32[320,768]{1,0:T(8,128)S(1)} %copy-done.23, bf16[320,768]{1,0:T(8,128)(2,1)S(1)} %collective-permute-done.5.refs_1_, bf16[320,768]{1,0:T(8,128)(2,1)S(1)} %bitcast.29, f32[320,768]{1,0:T(8,128)S(1)} %copy-done.21, ...), custom_call_target="tpu_custom_call" | custom-call | flops 2300000000 | bytes 1 | tf_op jit(solution)/shard_map/pallas_call | solution.py:489
  130.8 1.4 collective-permute-done.13.refs_1_
  132.2 1.0 copy-done.18
  133.8 1.6 collective-permute-start.14
  136.8 1.1 collective-permute-done.16.refs_3_
  137.9 1.5 shard_map.358.refs_4_
  139.4 1.3 collective-permute-start.23
  140.8 2.7 %collective-permute-done.15.refs_3_ = bf16[2,48,1152]{2,1,0:T(8,128)(2,1)S(1)} collective-permute-done((bf16[2,48,1152]{2,1,0:T(8,128)(2,1)S(1)}, bf16[2,48,1152]{2,1,0:T(8,128)(2,1)S(1)}, u32[]{:S(2)}, u32[]{:S(2)}) %collective-permute-start.15) | collective-permute-done | bytes 221216 | tf_op jit(solution)/shard_map/ppermute | solution.py:433
  143.5 1.5 shard_map.359.refs_2_
  145.6 3.0 %collective-permute-start.18 = (f32[128,256]{1,0:T(8,128)S(1)}, f32[128,256]{1,0:T(8,128)S(1)}, u32[]{:S(2)}, u32[]{:S(2)}) collective-permute-start(f32[128,256]{1,0:T(8,128)S(1)} %shard_map.360.refs_0_), channel_id=1, source_target_pairs={{0,16},{1,17},{2,18},{3,19},{4,20},{5,21},{6,22},{7,23},{8,24},{9,... | collective-permute-start | bytes 393224 | tf_op jit(solution)/shard_map/ppermute | solution.py:433
  148.6 7.5 %collective-permute-done.20 = bf16[1,48,1152]{2,1,0:T(8,128)(2,1)S(1)} collective-permute-done((bf16[1,48,1152]{2,1,0:T(8,128)(2,1)S(1)}, bf16[1,48,1152]{2,1,0:T(8,128)(2,1)S(1)}, u32[]{:S(2)}, u32[]{:S(2)}) %collective-permute-start.20) | collective-permute-done | bytes 110624 | tf_op jit(solution)/shard_map/ppermute | solution.py:433
  157.0 1.5 collective-permute-start.21
  159.8 1.7 %add_bitcast_fusion = f32[48,1536]{1,0:T(8,128)} fusion(bf16[1,48,1536]{2,1,0:T(8,128)(2,1)S(1)} %collective-permute-done.23, bf16[2,48,1536]{2,1,0:T(8,128)(2,1)S(1)} %collective-permute-done.16.refs_3_, bf16[4,48,1536]{2,1,0:T(8,128)(2,1)} %collective-permute-done.11.refs_2_, bf16[8,48,1536]{2,1,0:T(8,128)(2,1)S(1)} %copy-done.4, ...), kind=kLoop, calls=%fused_computation.4 | loop fusion | flops 663552 | bytes 1032192 | tf_op jit(solution)/shard_map/add | solution.py:437
  164.1 2.4 %shard_map.362 = (f32[12,2212]{1,0:T(8,128)}, f32[768]{0:T(1024)}, f32[768]{0:T(1024)}, f32[768]{0:T(1024)}, f32[768]{0:T(1024)}, /*index=5*/f32[768]{0:T(1024)}...) custom-call(s32[5]{0:T(128)S(1)} %stack.50.place_ref, ...), custom_call_target="tpu_custom_call" | custom-call | flops 1724999936 | bytes 1 | tf_op jit(solution)/shard_map/pallas_call | solution.py:489
  (119 shorter events, 24.3 us)
Async XLA Ops:
  0.7 14.5 %collective-permute-start = (bf16[320,768]{1,0:T(8,128)(2,1)}, bf16[320,768]{1,0:T(8,128)(2,1)S(1)}, u32[]{:S(2)}, u32[]{:S(2)}) collective-permute-start(bf16[320,768]{1,0:T(8,128)(2,1)} %bitcast.25), channel_id=1, source_target_pairs={{0,1},{1,0},{2,3},{3,2},{4,5},{5,4},{6,7},{7,6},{8,9},{9,8},{10,11... | collective-permute-start | bytes 1474568 | tf_op jit(solution)/shard_map/ppermute | solution.py:433
  12.3 2.8 %copy-start.9 = (bf16[768,2304]{1,0:T(8,128)(2,1)S(1)}, bf16[768,2304]{1,0:T(8,128)(2,1)}, u32[]{:S(2)}) copy-start(bf16[768,2304]{1,0:T(8,128)(2,1)} %refs_3_.3) | copy-start | bytes 10616836
  12.3 2.8 %copy-start.11 = (bf16[1,320,768]{2,1,0:T(8,128)(2,1)S(1)}, bf16[1,320,768]{2,1,0:T(8,128)(2,1)}, u32[]{:S(2)}) copy-start(bf16[1,320,768]{2,1,0:T(8,128)(2,1)} %param.20) | copy-start | bytes 1474564
  14.1 5.7 %copy-start.19 = (f32[24,1280]{1,0:T(8,128)S(1)}, f32[24,1280]{1,0:T(8,128)}, u32[]{:S(2)}) copy-start(f32[24,1280]{1,0:T(8,128)} %constant.16.clone.refs_2_.refs_7_) | copy-start | bytes 368644
  15.1 3.6 %copy-start.13 = (bf16[320,768]{1,0:T(8,128)(2,1)}, bf16[320,768]{1,0:T(8,128)(2,1)S(1)}, u32[]{:S(2)}) copy-start(bf16[320,768]{1,0:T(8,128)(2,1)S(1)} %collective-permute-done.refs_1_.refs_5_) | copy-start | bytes 1474564
  15.1 23.2 %slice-start = ((s8[4718592]{0:T(1024)(128)(4,1)}), s8[4194304]{0:T(1024)(128)(4,1)S(1)}, s32[]{:S(2)}) async-start(s8[4718592]{0:T(1024)(128)(4,1)} %bitcast.21), calls=%async_computation | async-start | bytes 8388608
  15.1 23.2 %slice-start.2 = ((s8[4718592]{0:T(1024)(128)(4,1)}), s8[4194304]{0:T(1024)(128)(4,1)S(1)}, s32[]{:S(2)}) async-start(s8[4718592]{0:T(1024)(128)(4,1)} %bitcast.23), calls=%async_computation.2 | async-start | bytes 8388608
  19.8 13.1 %copy-start.26 = (bf16[1,320,768]{2,1,0:T(8,128)(2,1)S(1)}, bf16[1,320,768]{2,1,0:T(8,128)(2,1)}, u32[]{:S(2)}) copy-start(bf16[1,320,768]{2,1,0:T(8,128)(2,1)} %param.22) | copy-start | bytes 1474564
  19.8 18.6 %slice-start.1 = ((s8[4718592]{0:T(1024)(128)(4,1)}), s8[524288]{0:T(1024)(128)(4,1)S(1)}, s32[]{:S(2)}) async-start(s8[4718592]{0:T(1024)(128)(4,1)} %bitcast.21), calls=%async_computation.1 | async-start | bytes 1048576
  19.8 18.6 %slice-start.3 = ((s8[4718592]{0:T(1024)(128)(4,1)}), s8[524288]{0:T(1024)(128)(4,1)S(1)}, s32[]{:S(2)}) async-start(s8[4718592]{0:T(1024)(128)(4,1)} %bitcast.23), calls=%async_computation.3 | async-start | bytes 1048576
  19.8 18.6 %copy-start.10 = (bf16[768,768]{1,0:T(8,128)(2,1)S(1)}, bf16[768,768]{1,0:T(8,128)(2,1)}, u32[]{:S(2)}) copy-start(bf16[768,768]{1,0:T(8,128)(2,1)} %refs_10_.1) | copy-start | bytes 3538948
  19.8 18.6 %copy-start.17 = (f32[3072]{0:T(1024)S(1)}, f32[3072]{0:T(1024)}, u32[]{:S(2)}) copy-start(f32[3072]{0:T(1024)} %param.35) | copy-start | bytes 36868
  31.1 7.2 %collective-permute-start.1 = (bf16[320,384]{1,0:T(8,128)(2,1)S(1)}, bf16[320,384]{1,0:T(8,128)(2,1)S(1)}, u32[]{:S(2)}, u32[]{:S(2)}) collective-permute-start(bf16[320,384]{1,0:T(8,128)(2,1)S(1)} %get-tuple-element.67.refs_3_), channel_id=1, source_target_pairs={{0,1},{1,0},{2,3},{3,2},{4,5},{5,4},{6,7},{7,6},{8,9},{9,8},{10,11... | collective-permute-start | bytes 737288 | tf_op jit(solution)/shard_map/ppermute | solution.py:433
  48.1 5.5 %copy-start.20 = (f32[320,768]{1,0:T(8,128)}, f32[320,768]{1,0:T(8,128)S(1)}, u32[]{:S(2)}) copy-start(f32[320,768]{1,0:T(8,128)S(1)} %get-tuple-element.91.refs_3_) | copy-start | bytes 2949124
  53.6 6.3 %collective-permute-start.3 = (bf16[16,240,384]{2,1,0:T(8,128)(2,1)S(1)}, bf16[16,240,384]{2,1,0:T(8,128)(2,1)S(1)}, u32[]{:S(2)}, u32[]{:S(2)}) collective-permute-start(bf16[16,240,384]{2,1,0:T(8,128)(2,1)S(1)} %get-tuple-element.79.refs_2_), channel_id=1, source_target_pairs={{0,2},{1,3},{2,0},{3,1},{4,6},{5,7},{6,4},{7,5},{8,10},{9,11},{10,... | collective-permute-start | bytes 8847368 | tf_op jit(solution)/shard_map/ppermute | solution.py:433
  53.7 9.8 %collective-permute-start.2 = (bf16[320,384]{1,0:T(8,128)(2,1)S(1)}, bf16[320,384]{1,0:T(8,128)(2,1)S(1)}, u32[]{:S(2)}, u32[]{:S(2)}) collective-permute-start(bf16[320,384]{1,0:T(8,128)(2,1)S(1)} %get-tuple-element.73.refs_4_), channel_id=1, source_target_pairs={{0,1},{1,0},{2,3},{3,2},{4,5},{5,4},{6,7},{7,6},{8,9},{9,8},{10,11... | collective-permute-start | bytes 737288 | tf_op jit(solution)/shard_map/ppermute | solution.py:433
  59.6 8.3 %collective-permute-start.4 = (bf16[16,48,1536]{2,1,0:T(8,128)(2,1)S(1)}, bf16[16,48,1536]{2,1,0:T(8,128)(2,1)S(1)}, u32[]{:S(2)}, u32[]{:S(2)}) collective-permute-start(bf16[16,48,1536]{2,1,0:T(8,128)(2,1)S(1)} %get-tuple-element.82.refs_2_), channel_id=1, source_target_pairs={{0,2},{1,3},{2,0},{3,1},{4,6},{5,7},{6,4},{7,5},{8,10},{9,11},{10,... | collective-permute-start | bytes 7077896 | tf_op jit(solution)/shard_map/ppermute | solution.py:433
  60.8 34.6 %collective-permute-start.9 = (bf16[8,240,384]{2,1,0:T(8,128)(2,1)S(1)}, bf16[8,240,384]{2,1,0:T(8,128)(2,1)S(1)}, u32[]{:S(2)}, u32[]{:S(2)}) collective-permute-start(bf16[8,240,384]{2,1,0:T(8,128)(2,1)S(1)} %shard_map.337.refs_2_.refs_8_), channel_id=1, source_target_pairs={{0,4},{1,5},{2,6},{3,7},{4,0},{5,1},{6,2},{7,3},{8,12},{9,13},{10,... | collective-permute-start | bytes 4423688 | tf_op jit(solution)/shard_map/ppermute | solution.py:433
  68.8 29.8 %collective-permute-start.8 = (bf16[8,48,1536]{2,1,0:T(8,128)(2,1)S(1)}, bf16[8,48,1536]{2,1,0:T(8,128)(2,1)S(1)}, u32[]{:S(2)}, u32[]{:S(2)}) collective-permute-start(bf16[8,48,1536]{2,1,0:T(8,128)(2,1)S(1)} %shard_map.340.refs_2_.refs_9_), channel_id=1, source_target_pairs={{0,1},{1,0},{2,3},{3,2},{4,5},{5,4},{6,7},{7,6},{8,9},{9,8},{10,11... | collective-permute-start | bytes 3538952 | tf_op jit(solution)/shard_map/ppermute | solution.py:433
  74.8 4.5 %copy-start.14 = (bf16[320,768]{1,0:T(8,128)(2,1)S(1)}, bf16[320,768]{1,0:T(8,128)(2,1)}, u32[]{:S(2)}) copy-start(bf16[320,768]{1,0:T(8,128)(2,1)} %copy-done.13) | copy-start | bytes 1474564
  79.3 5.1 %copy-start.25 = (bf16[640,768]{1,0:T(8,128)(2,1)S(1)}, bf16[640,768]{1,0:T(8,128)(2,1)}, u32[]{:S(2)}) copy-start(bf16[640,768]{1,0:T(8,128)(2,1)} %copy-done.24) | copy-start | bytes 2949124
  84.4 3.2 %copy-start.15 = (bf16[320,768]{1,0:T(8,128)(2,1)}, bf16[320,768]{1,0:T(8,128)(2,1)S(1)}, u32[]{:S(2)}) copy-start(bf16[320,768]{1,0:T(8,128)(2,1)S(1)} %get-tuple-element.87.refs_4_) | copy-start | bytes 1474564
  87.6 14.1 %copy-start.5 = (bf16[8,48,1152]{2,1,0:T(8,128)(2,1)}, bf16[8,48,1152]{2,1,0:T(8,128)(2,1)S(1)}, u32[]{:S(2)}) copy-start(bf16[8,48,1152]{2,1,0:T(8,128)(2,1)S(1)} %get-tuple-element.99.refs_0_) | copy-start | bytes 2654212
  87.6 14.1 %collective-permute-start.7 = (bf16[8,48,1152]{2,1,0:T(8,128)(2,1)S(1)}, bf16[8,48,1152]{2,1,0:T(8,128)(2,1)S(1)}, u32[]{:S(2)}, u32[]{:S(2)}) collective-permute-start(bf16[8,48,1152]{2,1,0:T(8,128)(2,1)S(1)} %get-tuple-element.88.refs_5_), channel_id=1, source_target_pairs={{0,2},{1,3},{2,0},{3,1},{4,6},{5,7},{6,4},{7,5},{8,10},{9,11},{10,... | collective-permute-start | bytes 2654216 | tf_op jit(solution)/shard_map/ppermute | solution.py:433
  97.0 18.1 %collective-permute-start.12 = (bf16[4,240,384]{2,1,0:T(8,128)(2,1)}, bf16[4,240,384]{2,1,0:T(8,128)(2,1)S(1)}, u32[]{:S(2)}, u32[]{:S(2)}) collective-permute-start(bf16[4,240,384]{2,1,0:T(8,128)(2,1)} %shard_map.348.refs_2_), channel_id=1, source_target_pairs={{0,8},{1,9},{2,10},{3,11},{4,12},{5,13},{6,14},{7,15},{8,0},{9,1},... | collective-permute-start | bytes 2211848 | tf_op jit(solution)/shard_map/ppermute | solution.py:433
  98.6 1.6 copy-start.3
  100.2 19.7 %collective-permute-start.11 = (bf16[4,48,1536]{2,1,0:T(8,128)(2,1)}, bf16[4,48,1536]{2,1,0:T(8,128)(2,1)}, u32[]{:S(2)}, u32[]{:S(2)}) collective-permute-start(bf16[4,48,1536]{2,1,0:T(8,128)(2,1)} %shard_map.349.refs_2_), channel_id=1, source_target_pairs={{0,4},{1,5},{2,6},{3,7},{4,0},{5,1},{6,2},{7,3},{8,12},{9,13},{10,... | collective-permute-start | bytes 1769480 | tf_op jit(solution)/shard_map/ppermute | solution.py:433
  103.1 21.4 %collective-permute-start.10 = (bf16[4,48,1152]{2,1,0:T(8,128)(2,1)}, bf16[4,48,1152]{2,1,0:T(8,128)(2,1)}, u32[]{:S(2)}, u32[]{:S(2)}) collective-permute-start(bf16[4,48,1152]{2,1,0:T(8,128)(2,1)} %shard_map.350.refs_3_), channel_id=1, source_target_pairs={{0,4},{1,5},{2,6},{3,7},{4,0},{5,1},{6,2},{7,3},{8,12},{9,13},{10,... | collective-permute-start | bytes 1327112 | tf_op jit(solution)/shard_map/ppermute | solution.py:433
  103.6 23.0 %collective-permute-start.6 = (f32[128,256]{1,0:T(8,128)S(1)}, f32[128,256]{1,0:T(8,128)S(1)}, u32[]{:S(2)}, u32[]{:S(2)}) collective-permute-start(f32[128,256]{1,0:T(8,128)S(1)} %shard_map.347.refs_2_.refs_0_), channel_id=1, source_target_pairs={{0,2},{1,3},{2,0},{3,1},{4,6},{5,7},{6,4},{7,5},{8,10},{9,11},{10,... | collective-permute-start | bytes 393224 | tf_op jit(solution)/shard_map/ppermute | solution.py:433
  103.6 25.1 %collective-permute-start.5 = (bf16[320,768]{1,0:T(8,128)(2,1)}, bf16[320,768]{1,0:T(8,128)(2,1)S(1)}, u32[]{:S(2)}, u32[]{:S(2)}) collective-permute-start(bf16[320,768]{1,0:T(8,128)(2,1)} %copy-done.15), channel_id=1, source_target_pairs={{0,1},{1,0},{2,3},{3,2},{4,5},{5,4},{6,7},{7,6},{8,9},{9,8},{10,11... | collective-permute-start | bytes 1474568 | tf_op jit(solution)/shard_map/ppermute | solution.py:433
  116.5 3.4 %copy-start.4 = (bf16[8,48,1536]{2,1,0:T(8,128)(2,1)S(1)}, bf16[8,48,1536]{2,1,0:T(8,128)(2,1)}, u32[]{:S(2)}) copy-start(bf16[8,48,1536]{2,1,0:T(8,128)(2,1)} %copy-done.3) | copy-start | bytes 3538948
  117.2 7.3 %copy-start.6 = (bf16[8,48,1152]{2,1,0:T(8,128)(2,1)S(1)}, bf16[8,48,1152]{2,1,0:T(8,128)(2,1)}, u32[]{:S(2)}) copy-start(bf16[8,48,1152]{2,1,0:T(8,128)(2,1)} %copy-done.5) | copy-start | bytes 2654212
  117.2 7.3 %copy-start.8 = (bf16[8,48,1152]{2,1,0:T(8,128)(2,1)S(1)}, bf16[8,48,1152]{2,1,0:T(8,128)(2,1)}, u32[]{:S(2)}) copy-start(bf16[8,48,1152]{2,1,0:T(8,128)(2,1)} %copy-done.7) | copy-start | bytes 2654212
  117.2 18.2 %collective-permute-start.17 = (bf16[2,240,384]{2,1,0:T(8,128)(2,1)S(1)}, bf16[2,240,384]{2,1,0:T(8,128)(2,1)S(1)}, u32[]{:S(2)}, u32[]{:S(2)}) collective-permute-start(bf16[2,240,384]{2,1,0:T(8,128)(2,1)S(1)} %shard_map.351.refs_3_), channel_id=1, source_target_pairs={{0,16},{1,17},{2,18},{3,19},{4,20},{5,21},{6,22},{7,23},{8,24},{9,... | collective-permute-start | bytes 1105928 | tf_op jit(solution)/shard_map/ppermute | solution.py:433
  121.5 16.4 %collective-permute-start.16 = (bf16[2,48,1536]{2,1,0:T(8,128)(2,1)S(1)}, bf16[2,48,1536]{2,1,0:T(8,128)(2,1)S(1)}, u32[]{:S(2)}, u32[]{:S(2)}) collective-permute-start(bf16[2,48,1536]{2,1,0:T(8,128)(2,1)S(1)} %shard_map.352.refs_3_), channel_id=1, source_target_pairs={{0,8},{1,9},{2,10},{3,11},{4,12},{5,13},{6,14},{7,15},{8,0},{9,1},... | collective-permute-start | bytes 884744 | tf_op jit(solution)/shard_map/ppermute | solution.py:433
  126.0 2.7 %copy-start.12 = (bf16[1,320,768]{2,1,0:T(8,128)(2,1)S(1)}, bf16[1,320,768]{2,1,0:T(8,128)(2,1)}, u32[]{:S(2)}) copy-start(bf16[1,320,768]{2,1,0:T(8,128)(2,1)} %param.20) | copy-start | bytes 1474564
  126.1 2.7 %copy-start.21 = (f32[320,768]{1,0:T(8,128)S(1)}, f32[320,768]{1,0:T(8,128)}, u32[]{:S(2)}) copy-start(f32[320,768]{1,0:T(8,128)} %copy-done.20) | copy-start | bytes 2949124
  126.1 2.7 %copy-start.23 = (f32[320,768]{1,0:T(8,128)S(1)}, f32[320,768]{1,0:T(8,128)}, u32[]{:S(2)}) copy-start(f32[320,768]{1,0:T(8,128)} %copy-done.22) | copy-start | bytes 2949124
  126.1 17.4 %collective-permute-start.15 = (bf16[2,48,1152]{2,1,0:T(8,128)(2,1)S(1)}, bf16[2,48,1152]{2,1,0:T(8,128)(2,1)S(1)}, u32[]{:S(2)}, u32[]{:S(2)}) collective-permute-start(bf16[2,48,1152]{2,1,0:T(8,128)(2,1)S(1)} %shard_map.353.refs_2_), channel_id=1, source_target_pairs={{0,8},{1,9},{2,10},{3,11},{4,12},{5,13},{6,14},{7,15},{8,0},{9,1},... | collective-permute-start | bytes 663560 | tf_op jit(solution)/shard_map/ppermute | solution.py:433
  127.2 5.0 %collective-permute-start.13 = (f32[128,256]{1,0:T(8,128)S(1)}, f32[128,256]{1,0:T(8,128)S(1)}, u32[]{:S(2)}, u32[]{:S(2)}) collective-permute-start(f32[128,256]{1,0:T(8,128)S(1)} %shard_map.354.refs_5_.refs_0_), channel_id=1, source_target_pairs={{0,4},{1,5},{2,6},{3,7},{4,0},{5,1},{6,2},{7,3},{8,12},{9,13},{10,... | collective-permute-start | bytes 393224 | tf_op jit(solution)/shard_map/ppermute | solution.py:433
  130.8 4.7 %copy-start.2 = (bf16[8,240,384]{2,1,0:T(8,128)(2,1)S(1)}, bf16[8,240,384]{2,1,0:T(8,128)(2,1)}, u32[]{:S(2)}) copy-start(bf16[8,240,384]{2,1,0:T(8,128)(2,1)} %copy-done) | copy-start | bytes 4423684
  133.8 11.2 %collective-permute-start.14 = (f32[128,256]{1,0:T(8,128)S(1)}, f32[128,256]{1,0:T(8,128)S(1)}, u32[]{:S(2)}, u32[]{:S(2)}) collective-permute-start(f32[128,256]{1,0:T(8,128)S(1)} %shard_map.356.refs_4_.refs_0_), channel_id=1, source_target_pairs={{0,8},{1,9},{2,10},{3,11},{4,12},{5,13},{6,14},{7,15},{8,0},{9,1},... | collective-permute-start | bytes 393224 | tf_op jit(solution)/shard_map/ppermute | solution.py:433
  136.1 26.2 %collective-permute-start.22 = (bf16[1,240,384]{2,1,0:T(8,128)(2,1)S(1)}, bf16[1,240,384]{2,1,0:T(8,128)(2,1)S(1)}, u32[]{:S(2)}, u32[]{:S(2)}) collective-permute-start(bf16[1,240,384]{2,1,0:T(8,128)(2,1)S(1)} %shard_map.357.refs_4_), channel_id=1, source_target_pairs={{0,1},{1,0},{2,3},{3,2},{4,5},{5,4},{6,7},{7,6},{8,9},{9,8},{10,11... | collective-permute-start | bytes 552968 | tf_op jit(solution)/shard_map/ppermute | solution.py:433
  139.4 20.4 %collective-permute-start.23 = (bf16[1,48,1536]{2,1,0:T(8,128)(2,1)S(1)}, bf16[1,48,1536]{2,1,0:T(8,128)(2,1)S(1)}, u32[]{:S(2)}, u32[]{:S(2)}) collective-permute-start(bf16[1,48,1536]{2,1,0:T(8,128)(2,1)S(1)} %shard_map.358.refs_4_), channel_id=1, source_target_pairs={{0,16},{1,17},{2,18},{3,19},{4,20},{5,21},{6,22},{7,23},{8,24},{9,... | collective-permute-start | bytes 442376 | tf_op jit(solution)/shard_map/ppermute | solution.py:433
  145.0 11.1 %collective-permute-start.20 = (bf16[1,48,1152]{2,1,0:T(8,128)(2,1)S(1)}, bf16[1,48,1152]{2,1,0:T(8,128)(2,1)S(1)}, u32[]{:S(2)}, u32[]{:S(2)}) collective-permute-start(bf16[1,48,1152]{2,1,0:T(8,128)(2,1)S(1)} %shard_map.359.refs_2_), channel_id=1, source_target_pairs={{0,16},{1,17},{2,18},{3,19},{4,20},{5,21},{6,22},{7,23},{8,24},{9,... | collective-permute-start | bytes 331784 | tf_op jit(solution)/shard_map/ppermute | solution.py:433
  145.6 12.9 %collective-permute-start.18 = (f32[128,256]{1,0:T(8,128)S(1)}, f32[128,256]{1,0:T(8,128)S(1)}, u32[]{:S(2)}, u32[]{:S(2)}) collective-permute-start(f32[128,256]{1,0:T(8,128)S(1)} %shard_map.360.refs_0_), channel_id=1, source_target_pairs={{0,16},{1,17},{2,18},{3,19},{4,20},{5,21},{6,22},{7,23},{8,24},{9,... | collective-permute-start | bytes 393224 | tf_op jit(solution)/shard_map/ppermute | solution.py:433
  157.0 4.5 %collective-permute-start.21 = (bf16[48,384]{1,0:T(8,128)(2,1)S(1)}, bf16[48,384]{1,0:T(8,128)(2,1)S(1)}, u32[]{:S(2)}, u32[]{:S(2)}) collective-permute-start(bf16[48,384]{1,0:T(8,128)(2,1)S(1)} %select_convert_fusion), channel_id=1, source_target_pairs={{0,1},{1,0},{2,3},{3,2},{4,5},{5,4},{6,7},{7,6},{8,9},{9,8},{10,11... | collective-permute-start | bytes 110600 | tf_op jit(solution)/shard_map/ppermute | solution.py:433
  159.1 5.0 %collective-permute-start.19 = (f32[128,256]{1,0:T(8,128)S(1)}, f32[128,256]{1,0:T(8,128)S(1)}, u32[]{:S(2)}, u32[]{:S(2)}) collective-permute-start(f32[128,256]{1,0:T(8,128)S(1)} %shard_map.361.refs_0_), channel_id=1, source_target_pairs={{0,1},{1,0},{2,3},{3,2},{4,5},{5,4},{6,7},{7,6},{8,9},{9,8},{10,11... | collective-permute-start | bytes 393224 | tf_op jit(solution)/shard_map/ppermute | solution.py:433
  (7 other events, 8.3 us)

commit v4 on v3

--- a/solution.py
+++ b/solution.py
@@ -458,28 +458,30 @@
 
 def full(shape):
     zeros = (0,) * len(shape)
-    return pl.BlockSpec(shape, lambda *_: zeros)
+    return pl.BlockSpec(shape, lambda *_: zeros, pipeline_mode=pl.Buffered(1))
 
 
 SIZES = {
-    "strips_kernel": (1.7, 6),
-    "qkv_kernel": (3.5, 12),
-    "attend_kernel": (11.0, 16),
-    "ffn_kernel": (9.5, 26),
-    "fc2_grad_kernel": (5.4, 26),
-    "fc1_grad_kernel": (4.6, 24),
-    "attend_back_kernel": (4.4, 16),
-    "hidden1_grad_kernel": (4.2, 14),
-    "qkv_grad_kernel": (3.2, 16),
-    "result_kernel": (4.0, 12),
-    "tokens_grad_kernel": (2.0, 12),
+    "strips_kernel": (1.7, 5),
+    "qkv_kernel": (1.9, 10),
+    "attend_kernel": (9.0, 15),
+    "ffn_kernel": (5.5, 16),
+    "ffn_back_kernel": (4.5, 14),
+    "d_act_kernel": (2.5, 12),
+    "fc2_grad_kernel": (4.6, 14),
+    "fc1_grad_kernel": (5.5, 14),
+    "attend_back_kernel": (4.4, 14),
+    "hidden1_grad_kernel": (4.2, 12),
+    "qkv_grad_kernel": (3.2, 12),
+    "result_kernel": (40.0, 10),
+    "tokens_grad_kernel": (2.0, 10),
 }
 
 
-def run(kernel, place, grid, in_specs, out_specs, out_shapes, scratch, operands, flops, after=(), us=None):
+def run(kernel, place, grid, in_specs, out_specs, out_shapes, scratch, operands, flops, after=(), us=None, reuse=()):
     held = len(operands)
     inner = kernel
-    cost, vmem = SIZES.get(getattr(kernel, "func", kernel).__name__, (1.5, 10))
+    cost, vmem = SIZES.get(getattr(kernel, "func", kernel).__name__, (0.01, 10))
     us = us or cost
 
     def kernel(place_ref, *refs):
@@ -496,6 +498,7 @@
             scratch_shapes=scratch,
         ),
         out_shape=out_shapes,
+        input_output_aliases={1 + held + i: o for i, o in reuse},
         compiler_params=pltpu.CompilerParams(vmem_limit_bytes=vmem * MEGA),
         cost_estimate=pl.CostEstimate(flops=int(us * RATE), bytes_accessed=1, transcendentals=0),
     )(place, *operands, *after)
@@ -505,52 +508,122 @@
     refs[-1][...] = sum(ref[...].astype(F32) for ref in refs[:-1]).astype(BF)
 
 
-def half_out(place, terms, after=()):
+def half_sum(place, terms, side, after=(), column=0, columns=None):
     size = terms[-1].shape[0] // 2
-    block = (min(size, 4), *terms[0].shape[1:])
+    _, height, columns = (*terms[0].shape[:2], columns or terms[0].shape[2])
+    block = (min(size, 4), height, columns)
     count = size // block[0]
     return run(
-        add_kernel, place, (count,), [spec(block, lambda n, p: (n + count, 0, 0))] * len(terms),
+        add_kernel, place, (count,),
+        [spec(block, lambda n, p: (n + side * count, 0, column))] * len(terms),
         [spec(block, lambda n, p: (n, 0, 0))], [shape((size, *block[1:]), BF)], [], tuple(terms), 0,
         after=after,
     )[0]
 
 
-def rest_of(place, terms, after=()):
-    size = terms[-1].shape[0] // 2
-    block = (min(size, 4), *terms[0].shape[1:])
-    same = spec(block, lambda n, p: (n, 0, 0))
+def half_out(place, terms, after=(), **how):
+    return half_sum(place, terms, 1, after, **how)
+
+
+def rest_of(place, terms, after=(), **how):
+    return half_sum(place, terms, 0, after, **how)
+
+
+def join_kernel(place, *refs):
+    cut = refs[0].shape[1]
+    for n, out in enumerate(refs[-2:]):
+        first, second, third, fourth = refs[4 * n : 4 * n + 4]
+        out[:, :cut, :] = (first[...].astype(F32) + second[...].astype(F32)).astype(BF)
+        out[:, cut:, :] = (third[...].astype(F32) + fourth[...].astype(F32)).astype(BF)
+
+
+def joined_halves(place, terms, others, after=()):
+    size = terms[0].shape[0] // 2
+    tall, low = terms[0].shape[1:], others[0].shape[1:]
+    total = (size, tall[0] + low[0], tall[1])
+    specs = [
+        spec((size, *part), lambda n, p, side=side: (side, 0, 0))
+        for side in (1, 0)
+        for part in (tall, tall, low, low)
+    ]
     return run(
-        add_kernel, place, (size // block[0],), [same] * len(terms), [same],
-        [shape((size, *block[1:]), BF)], [], tuple(terms), 0, after=after,
-    )[0]
-
-
-def sum_kernel(place, left, right, out):
-    out[...] = left[...] + right[...]
-
-
-def summed(place, left, right, after=()):
+        join_kernel, place, (1,), specs, [full(total)] * 2, [shape(total, BF)] * 2, [],
+        (*terms, *others) * 2, 0, after=after,
+    )
+
+
+def x_part(place, terms, side, after=()):
+    line, _, seqs, *block = terms[0].shape
     return run(
-        sum_kernel, place, (1,), [full(left.shape)] * 2, [full(left.shape)],
-        [shape(left.shape, F32)], [], (left, right), 0, after=after,
-    )[0]
+        add_kernel, place, (line,),
+        [spec((None, None, seqs, *block), lambda n, p: (n, side, 0, 0, 0))] * len(terms),
+        [spec((seqs, None, *block), lambda n, p: (0, n, 0, 0))], [shape((seqs, line, *block), BF)], [],
+        tuple(terms), 0, after=after,
+    )[0].reshape(line * seqs, *block)
+
+
+NOTE = (32, 1024)
+
+
+def note_sum(left, right):
+    return (left.astype(F32) + right.astype(F32)).astype(BF)
+
+
+def qs_first_kernel(place, keep, recv, note, mate, send_out, rest_out):
+    count, height, _ = keep.shape
+    half = count // 2
+    total = note_sum(note[...], mate[...])
+    for out, base in ((send_out, half), (rest_out, 0)):
+        for n in range(half):
+            out[height * n : height * (n + 1), :] = note_sum(keep[base + n], recv[base + n])
+        out[height * half :, :] = jnp.zeros((NOTE[0], out.shape[1]), BF)
+        out[height * half :, : NOTE[1]] = total
+
+
+def qs_next_kernel(place, keep, recv, send_out, rest_out):
+    part = send_out.shape[0] - NOTE[0]
+    total = note_sum(keep[...], recv[...])
+    for out, base in ((send_out, part), (rest_out, 0)):
+        out[:part, :] = total[base : base + part, :]
+        out[part:, :] = total[2 * part :, :]
+
+
+def qs_last_kernel(place, keep, recv, keep_out, line_out, side_out, cross_out, note_out, total):
+    share = side_out.shape[1]
+    height = side_out.shape[0]
+    stay = pl.ds(pl.multiple_of(place[0] * share, LANES), 2 * share)
+    leave = pl.ds(pl.multiple_of((1 - place[0]) * 2 * share, LANES), share)
+    total[...] = keep[...].astype(F32) + recv[...].astype(F32)
+    keep_out[...] = total[:height, stay]
+    side_out[...] = total[:height, leave].astype(BF)
+    cross_out[...] = total[height : 2 * height, leave].astype(BF)
+    note = total[2 * height :, : NOTE[1]].astype(BF)
+    note_out[...] = note
+    line_out[...] = jnp.zeros_like(line_out)
+    line_out[:height, : 2 * share] = total[height : 2 * height, stay].astype(BF)
+    line_out[height:, :] = note
+
+
+def qs_join_kernel(place, keep, line, side, cross, note, out, note_out):
+    height, share = side.shape
+    both = keep[...] + line[:height, : 2 * share].astype(F32)
+    out[:, :share] = both[:, :share]
+    out[:, share : 2 * share] = side[...].astype(F32) + cross[...].astype(F32)
+    out[:, 2 * share :] = both[:, share:]
+    note_out[...] = note_sum(note[...], line[height:, :])
 
 
 def shape(dims, dtype):
     return jax.ShapeDtypeStruct(dims, dtype)
 
 
-def qkv_kernel(place, own, other, vecs, weight, qb, vb, qkv_out, hidden_out):
+def qkv_kernel(place, source, vecs, weight, qb, vb, qkv_out, hidden_out):
     step = pl.program_id(0)
-    rows = own.shape[0]
 
     @pl.when(step == 0)
     def _():
-        for source, side in ((own, place[0]), (other, 1 - place[0])):
-            normed, _ = layer_norm(source[...].astype(F32))
-            low = (normed * vecs[0:1, :] + vecs[1:2, :]).astype(BF)
-            hidden_out[pl.ds(pl.multiple_of(side * rows, 64), rows), :] = low
+        normed, _ = layer_norm(source[...].astype(F32))
+        hidden_out[...] = (normed * vecs[0:1, :] + vecs[1:2, :]).astype(BF)
 
     wide = mul(hidden_out[...], weight[...])
     shift = jnp.where(step == 0, qb[...], jnp.where(step == 2, vb[...], 0.0))
@@ -567,6 +640,7 @@
     return held[:, : 5 * LANES]
 
 
+FORWARD_CHUNKS = ((0, 288), (288, 288), (576, 64))
 CHUNKS = tuple((start * 144, 144) for start in range(4)) + ((576, 64),)
 
 
@@ -595,7 +669,7 @@
         strip[head] = jnp.where(picks, rolled[0], rolled[1])
     block_lane = lax.broadcasted_iota(jnp.int32, (STRIP, LANES), 1)
     block_row = lax.broadcasted_iota(jnp.int32, (STRIP, LANES), 0)
-    for start, count in CHUNKS:
+    for start, count in FORWARD_CHUNKS:
         query = qkv[0, start : start + count, :]
         total = None
         scale = None
@@ -605,45 +679,35 @@
             near = lone[:, 1:2]
             corner = lone[:, 2:3]
             biases = []
-            for block in range(start // STRIP, -(-(start + count) // STRIP)):
-                if start == 576:
-                    row = window(strip.at[head, 0:8, :], STRIP)[0:1, :]
-                    piece = jnp.broadcast_to(row, (count, 5 * LANES))
-                    ids = lax.broadcasted_iota(jnp.int32, (count, LANES), 1)
-                else:
-                    piece = window(strip.at[head], block)
-                    ids = block_lane
-                left = jnp.where(ids == 0, near, piece[:, :LANES])
+            for block in range(start // STRIP, min(start + count, 576) // STRIP):
+                piece = window(strip.at[head], block)
+                left = jnp.where(block_lane == 0, near, piece[:, :LANES])
+                middle = piece[:, LANES : 4 * LANES]
+                right = piece[:, 4 * LANES :]
                 if block == 0:
-                    piece = jnp.concatenate(
+                    top_row = block_row == 0
+                    left = jnp.where(top_row, jnp.where(block_lane == 0, corner, far), left)
+                    middle = jnp.concatenate(
                         [
-                            jnp.where(
-                                block_row == 0, jnp.where(ids == 0, corner, far), left
-                            )
-                        ]
-                        + [
-                            jnp.where(block_row == 0, far, piece[:, n * LANES : (n + 1) * LANES])
-                            for n in range(1, 4)
-                        ]
-                        + [
-                            jnp.where(
-                                ids > 64, NEGATIVE, jnp.where(block_row == 0, far, piece[:, 4 * LANES :])
-                            )
+                            jnp.where(top_row, far, middle[:, n * LANES : (n + 1) * LANES])
+                            for n in range(3)
                         ],
                         axis=1,
                     )
-                else:
-                    piece = jnp.concatenate(
-                        [
-                            left,
-                            piece[:, LANES : 4 * LANES],
-                            jnp.where(ids > 64, NEGATIVE, piece[:, 4 * LANES :]),
-                        ],
-                        axis=1,
-                    )
-                biases.append(piece)
-                if start == 576:
-                    break
+                    right = jnp.where(top_row, far, right)
+                right = jnp.where(block_lane > 64, NEGATIVE, right)
+                biases.append(jnp.concatenate([left, middle, right], axis=1))
+            if start + count > 576:
+                row = window(strip.at[head, 0:8, :], STRIP)[0:1, :]
+                row = jnp.concatenate(
+                    [
+                        jnp.where(lane == 0, near, row[:, :LANES]),
+                        row[:, LANES : 4 * LANES],
+                        jnp.where(lane > 64, NEGATIVE, row[:, 4 * LANES :]),
+                    ],
+                    axis=1,
+                )
+                biases.append(jnp.broadcast_to(row, (start + count - 576, 5 * LANES)))
             scores = mul(query, keys[head], NT) + jnp.concatenate(biases, axis=0)
             top = jnp.max(scores, axis=1, keepdims=True)
             expo = jnp.exp(scores - top)
@@ -733,16 +797,15 @@
                     )
         dq_all[start : start + count, :] = total
     dqkv_out[0] = dq_all[...].astype(BF) * BF(0.125)
-    d_key = None
-    d_value = None
-    low_grads = grad_all[...].astype(BF)
-    for head in range(2):
-        part = mul(d_scores[head], qkv[0] * masks[head], TN)
-        d_key = part if head == 0 else d_key + part
-        part = mul(expo[head], low_grads * masks[head], TN)
-        d_value = part if head == 0 else d_value + part
-    dqkv_out[1] = d_key.astype(BF)
-    dqkv_out[2] = d_value.astype(BF)
+    turned_query = qkv[0].astype(F32).T.astype(BF)
+    turned_grads = grad_all[...].T.astype(BF)
+    half_lanes = LANES // 2
+    for at, left, right in ((1, turned_query, d_scores), (2, turned_grads, expo)):
+        sides = [
+            mul(left[half_lanes * head : half_lanes * (head + 1), :], right[head])
+            for head in range(2)
+        ]
+        dqkv_out[at] = jnp.concatenate(sides, axis=0).T.astype(BF)
     picks = even_mask[...] > 0.5
     row_id = lax.broadcasted_iota(jnp.int32, (STRIP, STRIP_WIDTH), 0)
     wide_lane = lax.broadcasted_iota(jnp.int32, (1, STRIP_WIDTH), 1)
@@ -769,83 +832,88 @@
         strip_out[0, head, 1:2, :] = lines[1]
 
 
+def d_act_kernel(place, cot, vecs, fc2, d_ffn_out, d_act_out):
+    @pl.when(pl.program_id(0) == 0)
+    def _():
+        d_ffn_out[...] = (vecs[7:8, :] * cot[...].astype(F32)).astype(BF)
+
+    d_act_out[...] = mul(d_ffn_out[...], fc2[...], NT).astype(BF)
+
+
 def ffn_kernel(
-    place, tokens, cot, attn_own, attn_other, vecs, proj, fc1, fc1_bias, fc2, proj_own, proj_other,
-    act_out, d_pre_out, fc1_bias_out, hidden_out, resid_out, d_ffn_out, attn_out, d_mixed_out, d_resid_out,
-    grad_own_out, grad_send_out, small_out, mixed_held, d_hidden,
+    place, tokens, attn_own, attn_other, vecs, proj, fc1, fc1_bias, d_act,
+    act_out, d_pre_out, fc1_bias_out, hidden_out, resid_out, attn_out, mixed_out,
 ):
-    step = pl.program_id(0)
     width = attn_own.shape[1]
 
-    @pl.when(step == 0)
+    @pl.when(pl.program_id(0) == 0)
     def _():
         attn_out[:, pl.ds(pl.multiple_of(place[0] * width, LANES), width)] = attn_own[...]
         attn_out[:, pl.ds(pl.multiple_of((1 - place[0]) * width, LANES), width)] = attn_other[...]
         mixed = mul(attn_out[...], proj[...]) + vecs[2:3, :]
-        mixed_held[...] = mixed
+        mixed_out[...] = mixed
         resid = tokens[...].astype(F32) + vecs[3:4, :] * mixed
         resid_out[...] = resid
         normed, _ = layer_norm(resid)
         hidden_out[...] = (normed * vecs[4:5, :] + vecs[5:6, :]).astype(BF)
-        d_ffn = (vecs[7:8, :] * cot[...].astype(F32)).astype(BF)
-        d_ffn_out[...] = d_ffn
-        d_hidden[...] = jnp.zeros_like(d_hidden)
 
     pre = mul(hidden_out[...], fc1[...]) + fc1_bias[...]
     gate = 0.5 * (1.0 + lax.erf(pre * ROOT_HALF))
     act_out[...] = (pre * gate).astype(BF)
     slope = gate + pre * jnp.exp(-0.5 * pre * pre) * GAUSS_NORM
-    d_pre = (mul(d_ffn_out[...], fc2[...], NT) * slope).astype(BF)
+    d_pre = (d_act[...].astype(F32) * slope).astype(BF)
     d_pre_out[...] = d_pre
     fc1_bias_out[...] = jnp.sum(d_pre.astype(F32), axis=0, keepdims=True)
-    d_hidden[...] += mul(d_pre, fc1[...], NT)
+
+
+def ffn_back_kernel(
+    place, d_pre, fc1, cot, d_ffn, resid, mixed_in, vecs, proj_own, proj_other,
+    d_mixed_out, d_resid_out, grad_own_out, grad_send_out, small_out, d_hidden,
+):
+    step = pl.program_id(0)
+    part = mul(d_pre[...], fc1[...], NT)
+
+    @pl.when(step == 0)
+    def _():
+        d_hidden[...] = part
+
+    @pl.when(step > 0)
+    def _():
+        d_hidden[...] += part
 
     @pl.when(step == pl.num_programs(0) - 1)
     def _():
         grad = d_hidden[...]
-        mixed = mixed_held[...]
-        normed, inverse = layer_norm(resid_out[...])
+        mixed = mixed_in[...]
+        normed, inverse = layer_norm(resid[...])
         d_resid = cot[...].astype(F32) + layer_norm_back(grad, normed, inverse, vecs[4:5, :])
         d_resid_out[...] = d_resid
         d_mixed = (vecs[3:4, :] * d_resid).astype(BF)
         d_mixed_out[...] = d_mixed
+        grad_send_out[...] = mul(d_mixed, proj_other[...], NT).astype(BF)
+        grad_own_out[...] = mul(d_mixed, proj_own[...], NT).astype(BF)
         small_out[0:1, :] = jnp.sum(grad * normed, axis=0, keepdims=True)
         small_out[1:2, :] = jnp.sum(grad, axis=0, keepdims=True)
         small_out[2:3, :] = jnp.sum(d_resid * mixed, axis=0, keepdims=True)
         small_out[3:4, :] = jnp.sum(d_mixed.astype(F32), axis=0, keepdims=True)
-        small_out[4:5, :] = jnp.sum(d_ffn_out[...].astype(F32), axis=0, keepdims=True)
+        small_out[4:5, :] = jnp.sum(d_ffn[...].astype(F32), axis=0, keepdims=True)
         small_out[5:8, :] = jnp.zeros((3, small_out.shape[1]), F32)
-        grad_own_out[...] = mul(d_mixed, proj_own[...], NT).astype(BF)
-        grad_send_out[...] = mul(d_mixed, proj_other[...], NT).astype(BF)
-
-
-def fc2_grad_kernel(place, act, d_ffn, attn, d_mixed, keep_out, send_out, held, *, rest):
-    step = pl.program_id(0)
+
+
+def fc2_grad_kernel(place, act, d_ffn, keep_out, send_out, held):
+    core = place[1]
     held[...] = mul(act[...], d_ffn[...], TN)
-    core = place[1]
     for pair in range(2):
         for seq in range(2):
-            at = rest(pair, step, seq) ^ place[2]
+            at = (0, pair ^ place[6], seq ^ place[0])
             columns = slice(384 * seq, 384 * seq + 384)
             low = pl.multiple_of(384 * pair + 192 * core, 64)
             high = pl.multiple_of(384 * pair + 192 * (1 - core), 64)
-            keep_out[at, :192] = held[pl.ds(low, 192), columns].astype(BF)
-            send_out[at, :192] = held[pl.ds(high, 192), columns].astype(BF)
-
-    @pl.when(step == pl.num_programs(0) - 1)
-    def _():
-        held[...] = mul(attn[...], d_mixed[...], TN)
-        for pair in range(8):
-            low = pl.multiple_of(96 * pair + 48 * core, 16)
-            high = pl.multiple_of(96 * pair + 48 * (1 - core), 16)
-            for side in range(2):
-                at = rest(pair % 2, pair // 2, side) ^ place[2]
-                columns = slice(384 * side, 384 * side + 384)
-                keep_out[at, 192:] = held[pl.ds(low, 48), columns].astype(BF)
-                send_out[at, 192:] = held[pl.ds(high, 48), columns].astype(BF)
-
-
-def fc1_grad_kernel(place, hidden, d_pre, keep_out, send_out, held, *, rest):
+            keep_out[at] = held[pl.ds(low, 192), columns].astype(BF)
+            send_out[at] = held[pl.ds(high, 192), columns].astype(BF)
+
+
+def fc1_grad_kernel(place, hidden, d_pre, attn, d_mixed, keep_out, send_out, held, *, rest):
     step = pl.program_id(0)
     core = place[1]
     held[...] = mul(hidden[...], d_pre[...], TN)
@@ -857,6 +925,18 @@
         high = pl.multiple_of(96 * pair + 48 * (1 - core), 16)
         keep_out[at, :, lanes] = held[pl.ds(low, 48), :].astype(BF)
         send_out[at, :, lanes] = held[pl.ds(high, 48), :].astype(BF)
+
+    @pl.when(step == pl.num_programs(0) - 1)
+    def _():
+        held[...] = mul(attn[...], d_mixed[...], TN)
+        for pair in range(8):
+            low = pl.multiple_of(96 * pair + 48 * core, 16)
+            high = pl.multiple_of(96 * pair + 48 * (1 - core), 16)
+            for side in range(2):
+                at = rest_label(ORDER_A)(pair % 2, pair // 2, side) ^ place[2]
+                columns = slice(384 * side, 384 * side + 384)
+                keep_out[at, :, 1536:1920] = held[pl.ds(low, 48), columns].astype(BF)
+                send_out[at, :, 1536:1920] = held[pl.ds(high, 48), columns].astype(BF)
 
 
 def result_kernel(place, act, fc2, resid, cot, vecs, result_out, small_out, total):
@@ -919,18 +999,16 @@
 def qkv_grad_kernel(
     place, hidden, dqkv0, dqkv1, dqkv2, keep_out, send_out, held, joined, *, rest
 ):
-    step = pl.program_id(0)
     core = place[1]
     for n, part in enumerate((dqkv0, dqkv1, dqkv2)):
         joined[:, LANES * n : LANES * (n + 1)] = part[0]
     held[...] = mul(hidden[...], joined[...], TN)
-    lanes = pl.ds(pl.multiple_of(step * 384, LANES), 384)
     for pair in range(8):
         at = rest(pair % 2, pair // 2, 0) ^ place[4]
         low = pl.multiple_of(96 * pair + 48 * core, 16)
         high = pl.multiple_of(96 * pair + 48 * (1 - core), 16)
-        keep_out[at, :, lanes] = held[pl.ds(low, 48), :].astype(BF)
-        send_out[at, :, lanes] = held[pl.ds(high, 48), :].astype(BF)
+        keep_out[at] = held[pl.ds(low, 48), :].astype(BF)
+        send_out[at] = held[pl.ds(high, 48), :].astype(BF)
 
 
 def tokens_grad_kernel(place, keep, recv, own, d_resid, vecs, grad_out):
@@ -951,8 +1029,8 @@
     return rest
 
 
-ORDER_A = ("core", "x", "z1", "z2", "y")
-ORDER_B = ("core", "y", "x", "z1", "z2")
+ORDER_A = ("core", "x", "y", "z1", "z2")
+ORDER_B = ("core", "z1", "x", "y", "z2")
 ORDER_Q = ("core", "x", "z1", "z2")
 
 
@@ -1006,7 +1084,7 @@
             strips_out[head, par : par + 1, :] = sides[par, head : head + 1, :]
 
 
-def pack_kernel(place, strip0, strip1, strip2, ffn, fc1_bias, last, result, packed):
+def pack_kernel(place, strip0, strip1, strip2, ffn, fc1_bias, last, result, packed_out, packed):
     packed[...] = jnp.zeros_like(packed)
     for n in range(5):
         lanes = slice(256 * n, 256 * n + 256)
@@ -1025,12 +1103,21 @@
             packed[row + 9 + part : row + 10 + part, :] = fc1_bias[
                 :, 768 * part + 256 * n : 768 * part + 256 * n + 256
             ]
+    for n in range(8):
+        packed_out[16 * (n // 4) : 16 * (n // 4) + 16, 256 * (n % 4) : 256 * (n % 4) + 256] = packed[
+            16 * n : 16 * n + 16, :
+        ].astype(BF)
 
 
 def unpack_kernel(
-    place, packed, mate, table_out, norm2_gain, norm2_bias, scale1, proj_bias, fc2_bias, scale2,
-    norm1_gain, norm1_bias, query_bias, value_bias, fc1_bias, flat, sides,
+    place, packed_in, mate_in, table_out, norm2_gain, norm2_bias, scale1, proj_bias, fc2_bias, scale2,
+    norm1_gain, norm1_bias, query_bias, value_bias, fc1_bias, flat, sides, packed, mate,
 ):
+    for held, source in ((packed, packed_in), (mate, mate_in)):
+        for n in range(8):
+            held[16 * n : 16 * n + 16, :] = source[
+                16 * (n // 4) : 16 * (n // 4) + 16, 256 * (n % 4) : 256 * (n % 4) + 256
+            ].astype(F32)
     heads = table_out.shape[0]
     half = heads // 2
     left = place[0] == 0
@@ -1119,6 +1206,8 @@
             rest_label(ORDER_A)(x_bit, line, seq),
             rest_label(ORDER_B)(x_bit, line, seq),
             rest_label(ORDER_Q)(x_bit, line, seq),
+            line,
+            x_bit,
         ]
     ).astype(jnp.int32)
     own = tokens.reshape(rows, width)
@@ -1134,19 +1223,28 @@
     )[0]
     even_mask = jnp.asarray(even_places())
 
-    qkv, hidden1 = run(
-        qkv_kernel, place, (3,),
-        [
-            full((rows, width)), full((rows, width)), full((8, width)),
-            spec((width, share), lambda t, p: (0, 2 * t + p[0])),
-            spec((1, share), lambda t, p: (0, p[0])), spec((1, share), lambda t, p: (0, p[0])),
-        ],
-        [spec((1, slots, share), lambda t, p: (t, 0, 0)), full((slots, width))],
-        [shape((3, slots, share), BF), shape((slots, width), BF)],
-        [],
-        (own, other, vecs, qkv_weight, query_bias.reshape(1, width), value_bias.reshape(1, width)),
-        2 * slots * width * 3 * share,
-    )
+    def qkv_rows(source, mine, held):
+        def side(p):
+            return p[0] if mine else 1 - p[0]
+
+        return run(
+            qkv_kernel, place, (3,),
+            [
+                full((rows, width)), full((8, width)),
+                spec((width, share), lambda t, p: (0, 2 * t + p[0])),
+                spec((1, share), lambda t, p: (0, p[0])), spec((1, share), lambda t, p: (0, p[0])),
+            ],
+            [
+                spec((1, rows, share), lambda t, p: (t, side(p), 0)),
+                spec((rows, width), lambda t, p: (side(p), 0)),
+            ],
+            [shape((3, slots, share), BF), shape((slots, width), BF)],
+            [],
+            (source, vecs, qkv_weight, query_bias.reshape(1, width), value_bias.reshape(1, width)),
+            0, after=held, reuse=() if mine else ((0, 0), (1, 1)),
+        )
+
+    qkv, hidden1 = qkv_rows(other, False, qkv_rows(own, True, ()))
     pair_rows = spec((slots, LANES), lambda n, p: (0, n))
     pair_half = spec((rows, LANES), lambda n, p: (0, n))
     pair_qkv = spec((3, slots, LANES), lambda n, p: (0, 0, n))
@@ -1168,57 +1266,66 @@
     part = hidden // parts
     whole = full((rows, width))
     sliced = spec((rows, part), lambda c, p: (0, c))
-    (
-        act, d_pre, fc1_bias_part, hidden2, resid, d_ffn, attn_low, d_mixed, d_resid,
-        grad_own, grad_send, small_ffn,
-    ) = run(
+    d_ffn, d_act = run(
+        d_act_kernel, place, (parts,),
+        [whole, full((8, width)), spec((part, width), lambda c, p: (c, 0))],
+        [whole, sliced], [shape((rows, width), BF), shape((rows, hidden), BF)], [],
+        (cot, vecs, fc2_weight), 0, after=(attn_send,),
+    )
+    act, d_pre, fc1_bias_part, hidden2, resid, attn_low, mixed = run(
         ffn_kernel, place, (parts,),
         [
-            whole, whole, full((rows, share)), full((rows, share)), full((8, width)),
+            whole, full((rows, share)), full((rows, share)), full((8, width)),
             full((width, width)), spec((width, part), lambda c, p: (0, c)),
-            spec((1, part), lambda c, p: (0, c)), spec((part, width), lambda c, p: (c, 0)),
-            spec((share, width), lambda c, p: (p[0], 0)), spec((share, width), lambda c, p: (1 - p[0], 0)),
+            spec((1, part), lambda c, p: (0, c)), sliced,
         ],
-        [
-            sliced, sliced, spec((1, part), lambda c, p: (0, c)), whole, whole, whole, whole, whole, whole,
-            full((rows, share)), full((rows, share)), full((8, width)),
-        ],
+        [sliced, sliced, spec((1, part), lambda c, p: (0, c)), whole, whole, whole, whole],
         [
             shape((rows, hidden), BF), shape((rows, hidden), BF), shape((1, hidden), F32),
             shape((rows, width), BF), shape((rows, width), F32), shape((rows, width), BF),
-            shape((rows, width), BF), shape((rows, width), BF), shape((rows, width), F32),
-            shape((rows, share), BF), shape((rows, share), BF), shape((8, width), F32),
+            shape((rows, width), F32),
         ],
-        [pltpu.VMEM((rows, width), F32), pltpu.VMEM((rows, width), F32)],
-        (
-            own, cot, attn_own, attn_other, vecs, proj_weight, fc1_weight, fc1_bias.reshape(1, hidden),
-            fc2_weight, proj_weight, proj_weight,
-        ),
-        2 * rows * width * (3 * hidden + 2 * width),
+        [],
+        (own, attn_own, attn_other, vecs, proj_weight, fc1_weight, fc1_bias.reshape(1, hidden), d_act),
+        0,
+    )
+    cube = (4, 2, 2, 192, share)
+
+    def line_place(c, p):
+        far = c ^ p[5]
+        return (far & 1) * 2 + (far >> 1), 0, 0, 0, 0
+
+    block = spec((1, *cube[1:]), line_place)
+    keep_a, send_a = run(
+        fc2_grad_kernel, place, (parts,), [sliced, whole], [block, block],
+        [shape(cube, BF), shape(cube, BF)], [pltpu.VMEM((part, width), F32)], (act, d_ffn), 0,
+    )
+    terms_a = [keep_a, swapped(send_a, "core")]
+    d_mixed, d_resid, grad_own, grad_send, small_ffn = run(
+        ffn_back_kernel, place, (parts,),
+        [
+            sliced, spec((width, part), lambda c, p: (0, c)), whole, whole, whole, whole, full((8, width)),
+            spec((share, width), lambda c, p: (p[0], 0)), spec((share, width), lambda c, p: (1 - p[0], 0)),
+        ],
+        [whole, whole, full((rows, share)), full((rows, share)), full((8, width))],
+        [
+            shape((rows, width), BF), shape((rows, width), F32), shape((rows, share), BF),
+            shape((rows, share), BF), shape((8, width), F32),
+        ],
+        [pltpu.VMEM((rows, width), F32)],
+        (d_pre, fc1_weight, cot, d_ffn, resid, mixed, vecs, proj_weight, proj_weight), 0, after=(send_a,),
     )
     grad_other = swapped(grad_send, "y")
-    block = (16, 240, share)
-    keep_a, send_a = run(
-        functools.partial(fc2_grad_kernel, rest=rest_label(ORDER_A)), place, (parts,),
-        [sliced, whole, whole, whole], [full(block), full(block)],
-        [shape(block, BF), shape(block, BF)],
-        [pltpu.VMEM((part, width), F32)], (act, d_ffn, attn_low, d_mixed),
-        2 * rows * width * hidden,
-        after=(grad_send,),
-    )
-    terms_a = [keep_a, swapped(send_a, "core")]
-    block = (16, 48, 4 * share)
+    out_a1 = x_part(place, terms_a, 1, (grad_send,))
+    terms_a = [x_part(place, terms_a, 0, (out_a1,)), swapped(out_a1, ORDER_A[1])]
+    block = (16, 48, 5 * share)
     keep_b, send_b = run(
         functools.partial(fc1_grad_kernel, rest=rest_label(ORDER_B)), place, (parts,),
-        [whole, sliced], [full(block), full(block)],
+        [whole, sliced, whole, whole], [full(block), full(block)],
         [shape(block, BF), shape(block, BF)],
-        [pltpu.VMEM((width, part), F32)], (hidden2, d_pre),
-        2 * rows * width * (hidden + width), after=(send_a,),
+        [pltpu.VMEM((width, part), F32)], (hidden2, d_pre, attn_low, d_mixed), 0, after=(out_a1, terms_a[0]),
     )
     terms_b = [keep_b, swapped(send_b, "core")]
-
-    out_a1 = half_out(place, terms_a, (send_b,))
-    terms_a = [rest_of(place, terms_a, (out_a1,)), swapped(out_a1, ORDER_A[1])]
 
     def attend_back(pair, after):
         pair_expo = spec((2, slots, slots), lambda n, p: (pair, 0, 0))
@@ -1241,10 +1348,15 @@
             32 * slots * slots * 64 * 2, after=after, us=40.0 if pair == 0 else None,
         )
 
-    dqkv0, strip0 = attend_back(0, (out_a1, terms_a[0]))
-    out_b1 = half_out(place, terms_b, (dqkv0,))
-    terms_b = [rest_of(place, terms_b, (out_b1,)), swapped(out_b1, ORDER_B[1])]
-    dqkv1, strip1 = attend_back(1, (dqkv0, out_b1, terms_b[0]))
+    dqkv0, strip0 = attend_back(0, (send_b,))
+    out_p1 = half_out(place, terms_b, (dqkv0,), column=4, columns=share)
+    terms_p = [
+        rest_of(place, terms_b, (out_p1,), column=4, columns=share),
+        swapped(out_p1, ORDER_A[1]),
+    ]
+    out_b1 = half_out(place, terms_b, (out_p1,), columns=4 * share)
+    terms_b = [rest_of(place, terms_b, (out_b1,), columns=4 * share), swapped(out_b1, ORDER_B[1])]
+    dqkv1, strip1 = attend_back(1, (dqkv0, out_b1, terms_b[0], terms_p[0]))
     dqkv2, strip2 = attend_back(2, (dqkv1,))
     dqkv = (dqkv0, dqkv1, dqkv2)
     third = [spec((1, slots, LANES), lambda t, p: (t, 0, 0))] * 3
@@ -1259,80 +1371,97 @@
     block = (8, 48, 3 * share)
     keep_q, send_q = run(
         functools.partial(qkv_grad_kernel, rest=rest_label(ORDER_Q)), place, (3,),
-        [full((slots, width)), *third], [full(block), full(block)],
+        [full((slots, width)), *third], [spec((8, 48, share), lambda t, p: (0, 0, t))] * 2,
         [shape(block, BF), shape(block, BF)],
         [pltpu.VMEM((width, share), F32), pltpu.VMEM((slots, share), BF)], (hidden1, *dqkv), 2 * slots * width * 3 * share,
         after=(dh_send,),
     )
-    terms_q = [keep_q, swapped(send_q, "core")]
+    recv_q = swapped(send_q, "core")
+    out_a2, rest_a = joined_halves(place, terms_a, terms_p, (send_q,))
+    terms_a = [rest_a, swapped(out_a2, "y")]
     result, small_result = run(
         result_kernel, place, (parts,),
         [sliced, spec((part, width), lambda c, p: (c, 0)), whole, whole, full((8, width))],
         [whole, full((8, width))],
         [shape((rows, width), BF), shape((8, width), F32)],
         [pltpu.VMEM((rows, width), F32)], (act, fc2_weight, resid, cot, vecs),
-        2 * rows * width * hidden, after=(send_q,),
+        2 * rows * width * hidden, after=(out_a2, rest_a),
     )
     packed = run(
         pack_kernel, place, (1,),
         [*[full((1, 2, 2, STRIP_WIDTH))] * 3, full((8, width)), full((1, hidden)), full((8, width)), full((8, width))],
-        [full((128, 256))], [shape((128, 256), F32)], [],
+        [full(NOTE)], [shape(NOTE, BF)], [pltpu.VMEM((128, 256), F32)],
         (strip0, strip1, strip2, small_ffn, fc1_bias_part, small_last, small_result), 0,
     )[0]
-    out_a2 = half_out(place, terms_a, (packed,))
-    terms_a = [*terms_a, swapped(out_a2, "z1")]
-    out_b2 = half_out(place, terms_b, (out_a2,))
+    mate = swapped(packed, "core")
+    out_b2 = half_out(place, terms_b, (packed,))
     terms_b = [*terms_b, swapped(out_b2, "x")]
-    out_q1 = half_out(place, terms_q, (out_b2,))
-    terms_q = [*terms_q, swapped(out_q1, "x")]
-    mate = swapped(packed, "core")
-    dh_recv = swapped(dh_send, "y")
-    out_a3 = half_out(place, terms_a, (out_q1,))
-    terms_a = [*terms_a, swapped(out_a3, "z2")]
+
+    def wide(blocks, columns):
+        return (48 * blocks + NOTE[0], columns)
+
+    send, rest = run(
+        qs_first_kernel, place, (1,),
+        [full((8, 48, 3 * share))] * 2 + [full(NOTE)] * 2, [full(wide(4, 3 * share))] * 2,
+        [shape(wide(4, 3 * share), BF)] * 2, [], (keep_q, recv_q, packed, mate), 0, after=(out_b2,),
+    )
+    recv = swapped(send, "x")
+    out_a3 = half_out(place, terms_a, (send,))
+    terms_a = [*terms_a, swapped(out_a3, "z1")]
     out_b3 = half_out(place, terms_b, (out_a3,))
-    terms_b = [*terms_b, swapped(out_b3, "z1")]
-    out_q2 = half_out(place, terms_q, (out_b3,))
-    terms_q = [*terms_q, swapped(out_q2, "z1")]
-    packed = summed(place, packed, mate, (out_q2,))
-    mate = swapped(packed, "x")
+    terms_b = [*terms_b, swapped(out_b3, "y")]
+    dh_late = run(
+        add_kernel, place, (1,), [whole], [whole], [shape((rows, width), BF)], [], (dh_send,), 0,
+        after=(out_b3,),
+    )[0]
+    dh_recv = swapped(dh_late, "y")
+    out_a4 = half_out(place, terms_a, (dh_late,))
+    terms_a = [*terms_a, swapped(out_a4, "z2")]
+    send, rest = run(
+        qs_next_kernel, place, (1,), [full(wide(4, 3 * share))] * 2, [full(wide(2, 3 * share))] * 2,
+        [shape(wide(2, 3 * share), BF)] * 2, [], (rest, recv), 0, after=(out_a4,),
+    )
+    recv = swapped(send, "z1")
+    out_b4 = half_out(place, terms_b, (send,))
+    terms_b = [*terms_b, swapped(out_b4, "z2")]
+    q_keep, q_line, q_side, q_cross, note = run(
+        qs_last_kernel, place, (1,), [full(wide(2, 3 * share))] * 2,
+        [
+            full((48, 2 * share)), full(wide(1, NOTE[1])), full((48, share)), full((48, share)), full(NOTE),
+        ],
+        [
+            shape((48, 2 * share), F32), shape(wide(1, NOTE[1]), BF), shape((48, share), BF),
+            shape((48, share), BF), shape(NOTE, BF),
+        ],
+        [pltpu.VMEM(wide(2, 3 * share), F32)], (rest, recv), 0, after=(out_b4,),
+    )
+    q_sends = (swapped(q_line, "z2"), swapped(q_side, "y"), swapped(q_cross, "z2", "y"))
+    qkv_grad, packed = run(
+        qs_join_kernel, place, (1,),
+        [full((48, 2 * share)), full(wide(1, NOTE[1])), full((48, share)), full((48, share)), full(NOTE)],
+        [full((48, 3 * share)), full(NOTE)], [shape((48, 3 * share), F32), shape(NOTE, BF)], [],
+        (q_keep, *q_sends, note), 0,
+    )
+    mate = swapped(packed, "y")
     tokens_grad = run(
         tokens_grad_kernel, place, (1,),
         [whole, whole, whole, whole, full((8, width))], [whole],
         [shape((rows, width), BF)], [], (dh_keep, dh_recv, own, d_resid, vecs), 0,
         after=(packed,),
     )[0]
-    packed = summed(place, packed, mate, (tokens_grad,))
-    mate = swapped(packed, "z1")
-    out_a4 = half_out(place, terms_a, (packed,))
-    terms_a = [*terms_a, swapped(out_a4, "y")]
-    out_b4 = half_out(place, terms_b, (out_a4,))
-    terms_b = [*terms_b, swapped(out_b4, "z2")]
-    out_q3 = half_out(place, terms_q, (out_b4,))
-    terms_q = [*terms_q, swapped(out_q3, "z2")]
-    packed = summed(place, packed, mate, (out_q3,))
-    mate = swapped(packed, "z2")
-    packed = summed(place, packed, mate)
-    mate = swapped(packed, "y")
     fc2_proj = added(terms_a)
     fc1_grad = added(terms_b)
-    qkv_part = added(terms_q)
     fc2_grad = fc2_proj[:192]
     proj_grad = fc2_proj[192:]
-    on_left = seq == 0
-    given = jnp.where(on_left, qkv_part[:, 2 * share :], qkv_part[:, :share]).astype(BF)
-    taken = swapped(given, "y").astype(F32)
-    qkv_grad = jnp.where(
-        on_left,
-        jnp.concatenate([qkv_part[:, :share], taken, qkv_part[:, share : 2 * share]], axis=1),
-        jnp.concatenate([qkv_part[:, share : 2 * share], taken, qkv_part[:, 2 * share :]], axis=1),
-    )
-
     vector = shape((width,), F32)
     table_grad, *small = run(
-        unpack_kernel, place, (1,), [full((128, 256))] * 2,
+        unpack_kernel, place, (1,), [full(NOTE)] * 2,
         [full(rel_table.shape[::-1]), *[full((width,))] * 10, full((hidden,))],
         [shape(rel_table.shape[::-1], F32), *[vector] * 10, shape((hidden,), F32)],
-        [pltpu.VMEM((16, 2432), F32), pltpu.VMEM((2, 16, STRIP_WIDTH), F32)], (packed, mate), 0,
+        [
+            pltpu.VMEM((16, 2432), F32), pltpu.VMEM((2, 16, STRIP_WIDTH), F32),
+            pltpu.VMEM((128, 256), F32), pltpu.VMEM((128, 256), F32),
+        ], (packed, mate), 0,
     )
     return (
         result.reshape(tokens.shape),

time: 167 us -> 156 us (0.934)
  local copies, waits for them, and re-layouts: 13.8 us -> 4.58 us
  waiting for transfers between devices: 34.9 us -> 41.3 us
  other arithmetic: 4.37 us -> 1.06 us
  starting transfers between devices: 28.2 us -> 25.6 us
  Pallas kernels: 84.1 us -> 82.2 us
    ppermute x24 -> x23, waiting for transfers between devices: 34.9 us -> 41.3 us  [swapped(): return lax.ppermute(value, ('img', 'seq'), swap_pairs(*names))]
    another operation x9, local copies, waits for them, and re-layouts: 5.56 us -> 0.09 us  [split_body(): jnp.stack([norm1_gain, norm1_bias, proj_bias, scale1, norm2_gain, norm2_b...]
    ppermute x24 -> x23, starting transfers between devices: 28.2 us -> 25.6 us  [swapped(): return lax.ppermute(value, ('img', 'seq'), swap_pairs(*names))]
    unnamed x62 -> x50, local copies, waits for them, and re-layouts: 5.37 us -> 3.03 us
    add x3 -> x2, other arithmetic: 2.79 us -> 0.9 us  [added(): return sum((term[0].astype(F32) for term in terms))]
    pallas_call x32 -> x35, Pallas kernels: 84.1 us -> 82.2 us  [run(): pl.pallas_call(kernel, grid_spec=pltpu.PrefetchScalarGridSpec(num_scalar_...]
  transfers between devices with their start and end apart: 24 -> 23, of which waited for: 10 -> 13; matrix products, arithmetic and copies ran while one was open for 8% -> 2% of each run, Pallas kernels for 31% -> 37%
where the time goes in v4:
time: 156 us
  Pallas kernels  82.2 us (53%)
  waiting for transfers between devices  41.3 us (26%)
  starting transfers between devices  25.6 us (16%)
  local copies, waits for them, and re-layouts  4.58 us (3%)
    pallas_call x35, Pallas kernels, run(): pl.pallas_call(kernel, grid_spec=pltpu.PrefetchScalarGridSpec(num_scalar_...  82.2 us
    ppermute x23, waiting for transfers between devices, swapped(): return lax.ppermute(value, ('img', 'seq'), swap_pairs(*names))  41.3 us
    ppermute x23, starting transfers between devices, swapped(): return lax.ppermute(value, ('img', 'seq'), swap_pairs(*names))  25.6 us
  transfers between devices with their start and end apart: 23, of which 13 were waited for; matrix products, arithmetic and copies ran while one was open for 2% of the time, Pallas kernels for 37%

profile of v4, /device:TPU:0, one launch (start us, length us, event | category | flops | bytes accessed | tf_op | source)
XLA Modules:
  0.0 156.2 jit_solution(14484072668402590732)
XLA Ops:
  0.7 3.0 %collective-permute-start = (bf16[320,768]{1,0:T(8,128)(2,1)}, bf16[320,768]{1,0:T(8,128)(2,1)S(1)}, u32[]{:S(2)}, u32[]{:S(2)}) collective-permute-start(bf16[320,768]{1,0:T(8,128)(2,1)} %bitcast.33), channel_id=1, source_target_pairs={{0,1},{1,0},{2,3},{3,2},{4,5},{5,4},{6,7},{7,6},{8,9},{9,8},{10,11... | collective-permute-start | bytes 1474568 | tf_op jit(solution)/shard_map/ppermute | solution.py:433
  3.8 0.9 copy-done.4
  4.8 1.7 %shard_map.333.refs_1_ = f32[12,2,1280]{2,1,0:T(2,128)S(1)} custom-call(s32[7]{0:T(128)S(1)} %stack.58.place_ref, f32[12,2212]{1,0:T(8,128)S(1)} %bitcast.38), custom_call_target="tpu_custom_call" | custom-call | flops 1955000064 | bytes 1 | tf_op jit(solution)/shard_map/pallas_call | solution.py:491
  6.9 2.0 %copy-done = bf16[768,2304]{1,0:T(8,128)(2,1)S(1)} copy-done((bf16[768,2304]{1,0:T(8,128)(2,1)S(1)}, bf16[768,2304]{1,0:T(8,128)(2,1)}, u32[]{:S(2)}) %copy-start) | copy-done | bytes 3538968
  8.9 2.5 %shard_map.331 = (bf16[3,640,384]{2,1,0:T(8,128)(2,1)S(1)}, bf16[640,768]{1,0:T(8,128)(2,1)S(1)}) custom-call(s32[7]{0:T(128)S(1)} %stack.58.place_ref, bf16[320,768]{1,0:T(8,128)(2,1)S(1)} %bitcast.34, f32[8,768]{1,0:T(8,128)S(1)} %stack.67.refs_1_.refs_3_.refs_6_.refs_4_, bf16[768,2304]{1,0:T(8,128)(2,1)S(1)} %copy-done, f32[1,768]{1,0:T(1,128)S(1)} %reshape.87.refs_3_, ...), custom_call_target="tpu_custom_call" | custom-call | flops 2184999936 | bytes 1 | tf_op jit(solution)/shard_map/pallas_call | solution.py:491
  11.5 3.6 %collective-permute-done.refs_0_.refs_5_ = bf16[320,768]{1,0:T(8,128)(2,1)S(1)} collective-permute-done((bf16[320,768]{1,0:T(8,128)(2,1)}, bf16[320,768]{1,0:T(8,128)(2,1)S(1)}, u32[]{:S(2)}, u32[]{:S(2)}) %collective-permute-start) | collective-permute-done | bytes 491552 | tf_op jit(solution)/shard_map/ppermute | solution.py:433
  15.1 2.5 %shard_map.332 = (bf16[3,640,384]{2,1,0:T(8,128)(2,1)S(1)}, bf16[640,768]{1,0:T(8,128)(2,1)S(1)}) custom-call(s32[7]{0:T(128)S(1)} %stack.58.place_ref, bf16[320,768]{1,0:T(8,128)(2,1)S(1)} %collective-permute-done.refs_0_.refs_5_, f32[8,768]{1,0:T(8,128)S(1)} %stack.67.refs_1_.refs_3_.refs_6_.refs_4_, ...), custom_call_target="tpu_custom_call", output_to_operand_aliasing={{0}: (6, {}), {1}: (7, {})} | custom-call | flops 2184999936 | bytes 1 | tf_op jit(solution)/shard_map/pallas_call | solution.py:491
  17.6 9.0 %shard_map.334 = (bf16[320,384]{1,0:T(8,128)(2,1)S(1)}, bf16[320,384]{1,0:T(8,128)(2,1)S(1)}, bf16[6,640,640]{2,1,0:T(8,128)(2,1)S(1)}, f32[640,384]{1,0:T(8,128)S(1)}) custom-call(s32[7]{0:T(128)S(1)} %stack.58.place_ref, bf16[3,640,384]{2,1,0:T(8,128)(2,1)S(1)} %get-tuple-element.84.refs_0_, f32[12,2,1280]{2,1,0:T(2,128)S(1)} %shard_map.333.refs_1_, ...), custom_call_target="tpu_custom_call" | custom-call | flops 10350000128 | bytes 1 | tf_op jit(solution)/shard_map/pallas_call | solution.py:491
  26.6 1.8 %collective-permute-start.1 = (bf16[320,384]{1,0:T(8,128)(2,1)S(1)}, bf16[320,384]{1,0:T(8,128)(2,1)S(1)}, u32[]{:S(2)}, u32[]{:S(2)}) collective-permute-start(bf16[320,384]{1,0:T(8,128)(2,1)S(1)} %get-tuple-element.86.refs_3_), channel_id=1, source_target_pairs={{0,1},{1,0},{2,3},{3,2},{4,5},{5,4},{6,7},{7,6},{8,9},{9,8},{10,11... | collective-permute-start | bytes 737288 | tf_op jit(solution)/shard_map/ppermute | solution.py:433
  28.5 3.1 %shard_map.335 = (bf16[320,768]{1,0:T(8,128)(2,1)S(1)}, bf16[320,3072]{1,0:T(8,128)(2,1)S(1)}) custom-call(s32[7]{0:T(128)S(1)} %stack.58.place_ref, bf16[320,768]{1,0:T(8,128)(2,1)S(1)} %fusion.refs_0_.refs_2_.refs_3_, f32[8,768]{1,0:T(8,128)S(1)} %stack.67.refs_1_.refs_3_.refs_6_.refs_4_, bf16[3072,768]{1,0:T(8,128)(2,1)S(1)} %bitcast.32, ...), custom_call_target="tpu_custom_call" | custom-call | flops 2875000064 | bytes 1 | tf_op jit(solution)/shard_map/pallas_call | solution.py:491
  31.6 2.3 %collective-permute-done.1.refs_2_ = bf16[320,384]{1,0:T(8,128)(2,1)S(1)} collective-permute-done((bf16[320,384]{1,0:T(8,128)(2,1)S(1)}, bf16[320,384]{1,0:T(8,128)(2,1)S(1)}, u32[]{:S(2)}, u32[]{:S(2)}) %collective-permute-start.1) | collective-permute-done | bytes 245792 | tf_op jit(solution)/shard_map/ppermute | solution.py:433
  33.9 6.0 %shard_map.336 = (bf16[320,3072]{1,0:T(8,128)(2,1)S(1)}, bf16[320,3072]{1,0:T(8,128)(2,1)S(1)}, f32[1,3072]{1,0:T(1,128)S(1)}, bf16[320,768]{1,0:T(8,128)(2,1)S(...) custom-call(s32[7]{0:T(128)S(1)} %stack.58.place_ref, ...), custom_call_target="tpu_custom_call" | custom-call | flops 6325000192 | bytes 1 | tf_op jit(solution)/shard_map/pallas_call | solution.py:491
  39.9 4.5 %shard_map.337 = (bf16[4,2,2,192,384]{4,3,2,1,0:T(8,128)(2,1)S(1)}, bf16[4,2,2,192,384]{4,3,2,1,0:T(8,128)(2,1)S(1)}) custom-call(s32[7]{0:T(128)S(1)} %stack.58.place_ref, bf16[320,3072]{1,0:T(8,128)(2,1)S(1)} %get-tuple-element.88.refs_0_, bf16[320,768]{1,0:T(8,128)(2,1)S(1)} %get-tuple-element.90.refs_1_.refs_3_), custom_call_target="tpu_custom_call" | custom-call | flops 5289999872 | bytes 1 | tf_op jit(solution)/shard_map/pallas_call | solution.py:491
  44.5 5.2 %shard_map.338 = (bf16[320,768]{1,0:T(8,128)(2,1)S(1)}, f32[320,768]{1,0:T(8,128)S(1)}, bf16[320,384]{1,0:T(8,128)(2,1)S(1)}, bf16[320,384]{1,0:T(8,128)(2,1)S(1)}, f32[8,768]{1,0:T(8,128)S(1)}) custom-call(s32[7]{0:T(128)S(1)} %stack.58.place_ref, bf16[320,3072]{1,0:T(8,128)(2,1)S(1)} %get-tuple-element.93.refs_0_.refs_1_, bf16[768,3072]{1,0:T(8,128)(2,1)S(1)} %bitcast.30, ...), custom_call_target="tpu_custom_call" | custom-call | flops 5175000064 | bytes 1 | tf_op jit(solution)/shard_map/pallas_call | solution.py:491
  49.7 1.5 collective-permute-start.5
  51.1 1.0 shard_map.339
  52.2 1.6 %collective-permute-start.3 = (bf16[8,192,384]{2,1,0:T(8,128)(2,1)S(1)}, bf16[8,192,384]{2,1,0:T(8,128)(2,1)S(1)}, u32[]{:S(2)}, u32[]{:S(2)}) collective-permute-start(bf16[8,192,384]{2,1,0:T(8,128)(2,1)S(1)} %bitcast.26), channel_id=1, source_target_pairs={{0,4},{1,5},{2,6},{3,7},{4,0},{5,1},{6,2},{7,3},{8,12},{9,13},{10,... | collective-permute-start | bytes 3538952 | tf_op jit(solution)/shard_map/ppermute | solution.py:433
  53.7 1.0 shard_map.340
  54.7 5.6 %shard_map.341 = (bf16[16,48,1920]{2,1,0:T(8,128)(2,1)S(1)}, bf16[16,48,1920]{2,1,0:T(8,128)(2,1)S(1)}) custom-call(s32[7]{0:T(128)S(1)} %stack.58.place_ref, bf16[320,768]{1,0:T(8,128)(2,1)S(1)} %get-tuple-element.96.refs_0_, bf16[320,3072]{1,0:T(8,128)(2,1)S(1)} %get-tuple-element.93.refs_0_.refs_1_, bf16[320,768]{1,0:T(8,128)(2,1)S(1)} %get-tuple-element.97.refs_2_, ...), custom_call_target="tpu_custom_call" | custom-call | flops 6325000192 | bytes 1 | tf_op jit(solution)/shard_map/pallas_call | solution.py:491
  60.5 4.0 %shard_map.342 = (bf16[3,640,128]{2,1,0:T(8,128)(2,1)S(1)}, f32[1,2,2,1280]{3,2,1,0:T(2,128)S(1)}) custom-call(s32[7]{0:T(128)S(1)} %stack.58.place_ref, bf16[3,640,384]{2,1,0:T(8,128)(2,1)S(1)} %get-tuple-element.84.refs_0_, bf16[6,640,640]{2,1,0:T(8,128)(2,1)S(1)} %get-tuple-element.101.refs_1_, bf16[320,384]{1,0:T(8,128)(2,1)S(1)} %get-tuple-element.85.refs_1_.refs_2_, ...), custom_call_target="tpu_custom_call" | custom-call | flops 46000001024 | bytes 1 | tf_op jit(solution)/shard_map/pallas_call | solution.py:491
  64.4 1.4 collective-permute-done.4.refs_1_
  67.2 1.0 shard_map.345.refs_2_.refs_9_
  68.2 1.6 %collective-permute-start.7 = (bf16[8,48,1536]{2,1,0:T(8,128)(2,1)S(1)}, bf16[8,48,1536]{2,1,0:T(8,128)(2,1)S(1)}, u32[]{:S(2)}, u32[]{:S(2)}) collective-permute-start(bf16[8,48,1536]{2,1,0:T(8,128)(2,1)S(1)} %shard_map.345.refs_2_.refs_9_), channel_id=1, source_target_pairs={{0,8},{1,9},{2,10},{3,11},{4,12},{5,13},{6,14},{7,15},{8,0},{9,1},... | collective-permute-start | bytes 3538952 | tf_op jit(solution)/shard_map/ppermute | solution.py:433
  69.9 1.0 shard_map.346.refs_10_.refs_0_
  71.7 4.0 %shard_map.347 = (bf16[3,640,128]{2,1,0:T(8,128)(2,1)S(1)}, f32[1,2,2,1280]{3,2,1,0:T(2,128)S(1)}) custom-call(s32[7]{0:T(128)S(1)} %stack.58.place_ref, bf16[3,640,384]{2,1,0:T(8,128)(2,1)S(1)} %get-tuple-element.84.refs_0_, bf16[6,640,640]{2,1,0:T(8,128)(2,1)S(1)} %get-tuple-element.101.refs_1_, bf16[320,384]{1,0:T(8,128)(2,1)S(1)} %get-tuple-element.85.refs_1_.refs_2_, ...), custom_call_target="tpu_custom_call" | custom-call | flops 5059999744 | bytes 1 | tf_op jit(solution)/shard_map/pallas_call | solution.py:491
  75.6 4.0 %shard_map.348 = (bf16[3,640,128]{2,1,0:T(8,128)(2,1)S(1)}, f32[1,2,2,1280]{3,2,1,0:T(2,128)S(1)}) custom-call(s32[7]{0:T(128)S(1)} %stack.58.place_ref, bf16[3,640,384]{2,1,0:T(8,128)(2,1)S(1)} %get-tuple-element.84.refs_0_, bf16[6,640,640]{2,1,0:T(8,128)(2,1)S(1)} %get-tuple-element.101.refs_1_, bf16[320,384]{1,0:T(8,128)(2,1)S(1)} %get-tuple-element.85.refs_1_.refs_2_, ...), custom_call_target="tpu_custom_call" | custom-call | flops 5059999744 | bytes 1 | tf_op jit(solution)/shard_map/pallas_call | solution.py:491
  79.6 4.0 %shard_map.349 = (f32[320,768]{1,0:T(8,128)S(1)}, bf16[320,768]{1,0:T(8,128)(2,1)S(1)}, f32[8,768]{1,0:T(8,128)S(1)}) custom-call(s32[7]{0:T(128)S(1)} %stack.58.place_ref, bf16[3,640,128]{2,1,0:T(8,128)(2,1)S(1)} %get-tuple-element.104.refs_2_.refs_8_.refs_0_.refs_1_, bf16[3,640,128]{2,1,0:T(8,128)(2,1)S(1)} %get-tuple-element.106.refs_8_.refs_1_.refs_2_, ...), custom_call_target="tpu_custom_call" | custom-call | flops 4830000128 | bytes 1 | tf_op jit(solution)/shard_map/pallas_call | solution.py:491
  83.6 3.6 %shard_map.350 = (bf16[8,48,1152]{2,1,0:T(8,128)(2,1)S(1)}, bf16[8,48,1152]{2,1,0:T(8,128)(2,1)S(1)}) custom-call(s32[7]{0:T(128)S(1)} %stack.58.place_ref, bf16[640,768]{1,0:T(8,128)(2,1)S(1)} %get-tuple-element.105.refs_0_, bf16[3,640,128]{2,1,0:T(8,128)(2,1)S(1)} %get-tuple-element.104.refs_2_.refs_8_.refs_0_.refs_1_, ...), custom_call_target="tpu_custom_call" | custom-call | flops 3680000000 | bytes 1 | tf_op jit(solution)/shard_map/pallas_call | solution.py:491
  88.7 4.1 %shard_map.352 = (bf16[320,768]{1,0:T(8,128)(2,1)}, f32[8,768]{1,0:T(8,128)S(1)}) custom-call(s32[7]{0:T(128)S(1)} %stack.58.place_ref, bf16[320,3072]{1,0:T(8,128)(2,1)S(1)} %copy-done.8, bf16[3072,768]{1,0:T(8,128)(2,1)S(1)} %bitcast.32, f32[320,768]{1,0:T(8,128)S(1)} %get-tuple-element.89.refs_4_.refs_2_, ...), custom_call_target="tpu_custom_call" | custom-call | flops 46000001024 | bytes 1 | tf_op jit(solution)/shard_map/pallas_call | solution.py:491
  93.5 2.6 %collective-permute-done.7.refs_1_ = bf16[8,48,1536]{2,1,0:T(8,128)(2,1)S(1)} collective-permute-done((bf16[8,48,1536]{2,1,0:T(8,128)(2,1)S(1)}, bf16[8,48,1536]{2,1,0:T(8,128)(2,1)S(1)}, u32[]{:S(2)}, u32[]{:S(2)}) %collective-permute-start.7) | collective-permute-done | bytes 1179680 | tf_op jit(solution)/shard_map/ppermute | solution.py:433
  96.7 1.6 collective-permute-start.8
  98.3 1.3 collective-permute-done.11.refs_3_
  100.3 6.8 %collective-permute-done.9.refs_1_ = bf16[4,240,384]{2,1,0:T(8,128)(2,1)S(1)} collective-permute-done((bf16[4,240,384]{2,1,0:T(8,128)(2,1)S(1)}, bf16[4,240,384]{2,1,0:T(8,128)(2,1)S(1)}, u32[]{:S(2)}, u32[]{:S(2)}) %collective-permute-start.9) | collective-permute-done | bytes 737312 | tf_op jit(solution)/shard_map/ppermute | solution.py:433
  108.2 1.5 collective-permute-start.13
  109.7 2.0 %collective-permute-done.8.refs_2_ = bf16[4,48,1536]{2,1,0:T(8,128)(2,1)S(1)} collective-permute-done((bf16[4,48,1536]{2,1,0:T(8,128)(2,1)S(1)}, bf16[4,48,1536]{2,1,0:T(8,128)(2,1)S(1)}, u32[]{:S(2)}, u32[]{:S(2)}) %collective-permute-start.8) | collective-permute-done | bytes 589856 | tf_op jit(solution)/shard_map/ppermute | solution.py:433
  113.0 5.0 %collective-permute-done.14.refs_2_ = bf16[2,240,384]{2,1,0:T(8,128)(2,1)S(1)} collective-permute-done((bf16[2,240,384]{2,1,0:T(8,128)(2,1)S(1)}, bf16[2,240,384]{2,1,0:T(8,128)(2,1)S(1)}, u32[]{:S(2)}, u32[]{:S(2)}) %collective-permute-start.14) | collective-permute-done | bytes 368672 | tf_op jit(solution)/shard_map/ppermute | solution.py:433
  118.6 2.7 %collective-permute-start.21 = (bf16[1,240,384]{2,1,0:T(8,128)(2,1)S(1)}, bf16[1,240,384]{2,1,0:T(8,128)(2,1)S(1)}, u32[]{:S(2)}, u32[]{:S(2)}) collective-permute-start(bf16[1,240,384]{2,1,0:T(8,128)(2,1)S(1)} %shard_map.359.refs_2_), channel_id=1, source_target_pairs={{0,16},{1,17},{2,18},{3,19},{4,20},{5,21},{6,22},{7,23},{8,24},{9,... | collective-permute-start | bytes 552968 | tf_op jit(solution)/shard_map/ppermute | solution.py:433
  121.8 1.5 collective-permute-start.12
  124.4 4.1 %collective-permute-done.21 = bf16[1,240,384]{2,1,0:T(8,128)(2,1)S(1)} collective-permute-done((bf16[1,240,384]{2,1,0:T(8,128)(2,1)S(1)}, bf16[1,240,384]{2,1,0:T(8,128)(2,1)S(1)}, u32[]{:S(2)}, u32[]{:S(2)}) %collective-permute-start.21) | collective-permute-done | bytes 184352 | tf_op jit(solution)/shard_map/ppermute | solution.py:433
  129.3 1.9 %collective-permute-done.16.refs_3_ = bf16[2,48,1536]{2,1,0:T(8,128)(2,1)S(1)} collective-permute-done((bf16[2,48,1536]{2,1,0:T(8,128)(2,1)S(1)}, bf16[2,48,1536]{2,1,0:T(8,128)(2,1)S(1)}, u32[]{:S(2)}, u32[]{:S(2)}) %collective-permute-start.16) | collective-permute-done | bytes 294944 | tf_op jit(solution)/shard_map/ppermute | solution.py:433
  132.9 3.2 %collective-permute-done.15.refs_1_ = bf16[128,1152]{1,0:T(8,128)(2,1)S(1)} collective-permute-done((bf16[128,1152]{1,0:T(8,128)(2,1)S(1)}, bf16[128,1152]{1,0:T(8,128)(2,1)S(1)}, u32[]{:S(2)}, u32[]{:S(2)}) %collective-permute-start.15) | collective-permute-done | bytes 294944 | tf_op jit(solution)/shard_map/ppermute | solution.py:433
  137.8 3.4 %collective-permute-start.19 = (bf16[48,384]{1,0:T(8,128)(2,1)S(1)}, bf16[48,384]{1,0:T(8,128)(2,1)S(1)}, u32[]{:S(2)}, u32[]{:S(2)}) collective-permute-start(bf16[48,384]{1,0:T(8,128)(2,1)S(1)} %get-tuple-element.130), channel_id=1, source_target_pairs={{0,17},{1,16},{2,19},{3,18},{4,21},{5,20},{6,23},{7,22},{8,25},{9,... | collective-permute-start | bytes 110600 | tf_op jit(solution)/shard_map/ppermute | solution.py:433
  142.0 6.1 %collective-permute-done.19.refs_3_ = bf16[48,384]{1,0:T(8,128)(2,1)S(1)} collective-permute-done((bf16[48,384]{1,0:T(8,128)(2,1)S(1)}, bf16[48,384]{1,0:T(8,128)(2,1)S(1)}, u32[]{:S(2)}, u32[]{:S(2)}) %collective-permute-start.19) | collective-permute-done | bytes 36896 | tf_op jit(solution)/shard_map/ppermute | solution.py:433
  148.1 1.3 shard_map.363
  149.4 1.2 collective-permute-start.20
  150.6 2.0 %shard_map.364 = bf16[320,768]{1,0:T(8,128)(2,1)} custom-call(s32[7]{0:T(128)S(1)} %stack.58.place_ref, f32[320,768]{1,0:T(8,128)S(1)} %get-tuple-element.113.refs_0_, bf16[320,768]{1,0:T(8,128)(2,1)S(1)} %collective-permute-done.12.refs_1_, bf16[320,768]{1,0:T(8,128)(2,1)S(1)} %bitcast.37, f32[320,768]{1,0:T(8,128)S(1)} %get-tuple-element.123.refs_3_, ...), custom_call_target="tpu_custom_call" | custom-call | flops 2300000000 | bytes 1 | tf_op jit(solution)/shard_map/pallas_call | solution.py:491
  152.6 1.0 collective-permute-done.20.refs_1_
  153.6 2.4 %shard_map.365 = (f32[12,2212]{1,0:T(8,128)}, f32[768]{0:T(1024)}, f32[768]{0:T(1024)}, f32[768]{0:T(1024)}, f32[768]{0:T(1024)}, /*index=5*/f32[768]{0:T(1024)}...) custom-call(s32[7]{0:T(128)S(1)} %stack.58.place_ref, ...), custom_call_target="tpu_custom_call" | custom-call | flops 11500000 | bytes 1 | tf_op jit(solution)/shard_map/pallas_call | solution.py:491
  (103 shorter events, 15.8 us)
Async XLA Ops:
  0.7 14.5 %collective-permute-start = (bf16[320,768]{1,0:T(8,128)(2,1)}, bf16[320,768]{1,0:T(8,128)(2,1)S(1)}, u32[]{:S(2)}, u32[]{:S(2)}) collective-permute-start(bf16[320,768]{1,0:T(8,128)(2,1)} %bitcast.33), channel_id=1, source_target_pairs={{0,1},{1,0},{2,3},{3,2},{4,5},{5,4},{6,7},{7,6},{8,9},{9,8},{10,11... | collective-permute-start | bytes 1474568 | tf_op jit(solution)/shard_map/ppermute | solution.py:433
  3.8 0.9 copy-start.4
  4.7 1.9 %copy-start.20 = (s32[1,320]{1,0:T(1,128)S(1)}, s32[1,320]{1,0:T(1,128)}, u32[]{:S(2)}) copy-start(s32[1,320]{1,0:T(1,128)} %param.21) | copy-start | bytes 3844
  4.7 1.9 %copy-start.10 = (f32[768]{0:T(1024)S(1)}, f32[768]{0:T(1024)}, u32[]{:S(2)}) copy-start(f32[768]{0:T(1024)} %param.23) | copy-start | bytes 9220
  4.7 1.9 %copy-start.11 = (f32[768]{0:T(1024)S(1)}, f32[768]{0:T(1024)}, u32[]{:S(2)}) copy-start(f32[768]{0:T(1024)} %param.24) | copy-start | bytes 9220
  4.7 1.9 %copy-start.12 = (f32[768]{0:T(1024)S(1)}, f32[768]{0:T(1024)}, u32[]{:S(2)}) copy-start(f32[768]{0:T(1024)} %param.30) | copy-start | bytes 9220
  4.7 1.9 %copy-start.13 = (f32[768]{0:T(1024)S(1)}, f32[768]{0:T(1024)}, u32[]{:S(2)}) copy-start(f32[768]{0:T(1024)} %param.31) | copy-start | bytes 9220
  4.7 1.9 %copy-start.14 = (f32[768]{0:T(1024)S(1)}, f32[768]{0:T(1024)}, u32[]{:S(2)}) copy-start(f32[768]{0:T(1024)} %param.32) | copy-start | bytes 9220
  4.7 2.0 %copy-start.15 = (f32[768]{0:T(1024)S(1)}, f32[768]{0:T(1024)}, u32[]{:S(2)}) copy-start(f32[768]{0:T(1024)} %param.33) | copy-start | bytes 9220
  4.7 2.0 %copy-start.16 = (f32[768]{0:T(1024)S(1)}, f32[768]{0:T(1024)}, u32[]{:S(2)}) copy-start(f32[768]{0:T(1024)} %param.37) | copy-start | bytes 9220
  4.7 2.0 %copy-start.17 = (f32[768]{0:T(1024)S(1)}, f32[768]{0:T(1024)}, u32[]{:S(2)}) copy-start(f32[768]{0:T(1024)} %param.38) | copy-start | bytes 9220
  4.8 2.0 %copy-start.18 = (f32[768]{0:T(1024)S(1)}, f32[768]{0:T(1024)}, u32[]{:S(2)}) copy-start(f32[768]{0:T(1024)} %param.26) | copy-start | bytes 9220
  4.8 2.0 %copy-start.19 = (f32[768]{0:T(1024)S(1)}, f32[768]{0:T(1024)}, u32[]{:S(2)}) copy-start(f32[768]{0:T(1024)} %param.27) | copy-start | bytes 9220
  4.8 2.1 %copy-start.3 = (bf16[1,320,768]{2,1,0:T(8,128)(2,1)S(1)}, bf16[1,320,768]{2,1,0:T(8,128)(2,1)}, u32[]{:S(2)}) copy-start(bf16[1,320,768]{2,1,0:T(8,128)(2,1)} %param.20) | copy-start | bytes 1474564
  6.8 2.0 %copy-start = (bf16[768,2304]{1,0:T(8,128)(2,1)S(1)}, bf16[768,2304]{1,0:T(8,128)(2,1)}, u32[]{:S(2)}) copy-start(bf16[768,2304]{1,0:T(8,128)(2,1)} %refs_3_.1) | copy-start | bytes 10616836
  8.9 2.5 %copy-start.9 = (bf16[1,320,768]{2,1,0:T(8,128)(2,1)S(1)}, bf16[1,320,768]{2,1,0:T(8,128)(2,1)}, u32[]{:S(2)}) copy-start(bf16[1,320,768]{2,1,0:T(8,128)(2,1)} %param.22) | copy-start | bytes 1474564
  8.9 6.3 %copy-start.1 = (bf16[768,2304]{1,0:T(8,128)(2,1)S(1)}, bf16[768,2304]{1,0:T(8,128)(2,1)}, u32[]{:S(2)}) copy-start(bf16[768,2304]{1,0:T(8,128)(2,1)} %refs_3_.1) | copy-start | bytes 10616836
  15.1 2.5 %copy-start.6 = (f32[24,1280]{1,0:T(8,128)S(1)}, f32[24,1280]{1,0:T(8,128)}, u32[]{:S(2)}) copy-start(f32[24,1280]{1,0:T(8,128)} %constant.14.clone.refs_2_.refs_7_) | copy-start | bytes 368644
  15.1 13.3 %slice-start.2 = ((s8[4718592]{0:T(1024)(128)(4,1)}), s8[4194304]{0:T(1024)(128)(4,1)S(1)}, s32[]{:S(2)}) async-start(s8[4718592]{0:T(1024)(128)(4,1)} %bitcast.31), calls=%async_computation.2 | async-start | bytes 8388608
  17.6 10.8 %slice-start.3 = ((s8[4718592]{0:T(1024)(128)(4,1)}), s8[524288]{0:T(1024)(128)(4,1)S(1)}, s32[]{:S(2)}) async-start(s8[4718592]{0:T(1024)(128)(4,1)} %bitcast.31), calls=%async_computation.3 | async-start | bytes 1048576
  26.6 7.3 %slice-start = ((s8[4718592]{0:T(1024)(128)(4,1)}), s8[4194304]{0:T(1024)(128)(4,1)S(1)}, s32[]{:S(2)}) async-start(s8[4718592]{0:T(1024)(128)(4,1)} %bitcast.29), calls=%async_computation | async-start | bytes 8388608
  26.6 7.2 %slice-start.1 = ((s8[4718592]{0:T(1024)(128)(4,1)}), s8[524288]{0:T(1024)(128)(4,1)S(1)}, s32[]{:S(2)}) async-start(s8[4718592]{0:T(1024)(128)(4,1)} %bitcast.29), calls=%async_computation.1 | async-start | bytes 1048576
  26.6 7.2 %copy-start.2 = (bf16[768,768]{1,0:T(8,128)(2,1)S(1)}, bf16[768,768]{1,0:T(8,128)(2,1)}, u32[]{:S(2)}) copy-start(bf16[768,768]{1,0:T(8,128)(2,1)} %refs_8_.1) | copy-start | bytes 3538948
  26.6 7.2 %copy-start.5 = (f32[3072]{0:T(1024)S(1)}, f32[3072]{0:T(1024)}, u32[]{:S(2)}) copy-start(f32[3072]{0:T(1024)} %param.35) | copy-start | bytes 36868
  26.6 7.2 %collective-permute-start.1 = (bf16[320,384]{1,0:T(8,128)(2,1)S(1)}, bf16[320,384]{1,0:T(8,128)(2,1)S(1)}, u32[]{:S(2)}, u32[]{:S(2)}) collective-permute-start(bf16[320,384]{1,0:T(8,128)(2,1)S(1)} %get-tuple-element.86.refs_3_), channel_id=1, source_target_pairs={{0,1},{1,0},{2,3},{3,2},{4,5},{5,4},{6,7},{7,6},{8,9},{9,8},{10,11... | collective-permute-start | bytes 737288 | tf_op jit(solution)/shard_map/ppermute | solution.py:433
  39.9 4.5 %copy-start.7 = (bf16[320,3072]{1,0:T(8,128)(2,1)}, bf16[320,3072]{1,0:T(8,128)(2,1)S(1)}, u32[]{:S(2)}) copy-start(bf16[320,3072]{1,0:T(8,128)(2,1)S(1)} %get-tuple-element.88.refs_0_) | copy-start | bytes 5898244
  44.4 6.7 %collective-permute-start.2 = (bf16[4,2,2,192,384]{4,3,2,1,0:T(8,128)(2,1)S(1)}, bf16[4,2,2,192,384]{4,3,2,1,0:T(8,128)(2,1)S(1)}, u32[]{:S(2)}, u32[]{:S(2)}) collective-permute-start(bf16[4,2,2,192,384]{4,3,2,1,0:T(8,128)(2,1)S(1)} %get-tuple-element.92.refs_9_), channel_id=1, source_target_pairs={{0,2},{1,3},{2,0},{3,1},{4,6},{5,7},{6,4},{7,5},{8,10},{9,11},{10,... | collective-permute-start | bytes 7077896 | tf_op jit(solution)/shard_map/ppermute | solution.py:433
  49.7 10.8 %collective-permute-start.5 = (bf16[320,384]{1,0:T(8,128)(2,1)S(1)}, bf16[320,384]{1,0:T(8,128)(2,1)S(1)}, u32[]{:S(2)}, u32[]{:S(2)}) collective-permute-start(bf16[320,384]{1,0:T(8,128)(2,1)S(1)} %get-tuple-element.95.refs_2_), channel_id=1, source_target_pairs={{0,1},{1,0},{2,3},{3,2},{4,5},{5,4},{6,7},{7,6},{8,9},{9,8},{10,11... | collective-permute-start | bytes 737288 | tf_op jit(solution)/shard_map/ppermute | solution.py:433
  52.2 35.1 %collective-permute-start.3 = (bf16[8,192,384]{2,1,0:T(8,128)(2,1)S(1)}, bf16[8,192,384]{2,1,0:T(8,128)(2,1)S(1)}, u32[]{:S(2)}, u32[]{:S(2)}) collective-permute-start(bf16[8,192,384]{2,1,0:T(8,128)(2,1)S(1)} %bitcast.26), channel_id=1, source_target_pairs={{0,4},{1,5},{2,6},{3,7},{4,0},{5,1},{6,2},{7,3},{8,12},{9,13},{10,... | collective-permute-start | bytes 3538952 | tf_op jit(solution)/shard_map/ppermute | solution.py:433
  60.4 5.4 %collective-permute-start.4 = (bf16[16,48,1920]{2,1,0:T(8,128)(2,1)S(1)}, bf16[16,48,1920]{2,1,0:T(8,128)(2,1)S(1)}, u32[]{:S(2)}, u32[]{:S(2)}) collective-permute-start(bf16[16,48,1920]{2,1,0:T(8,128)(2,1)S(1)} %get-tuple-element.100.refs_8_), channel_id=1, source_target_pairs={{0,2},{1,3},{2,0},{3,1},{4,6},{5,7},{6,4},{7,5},{8,10},{9,11},{10,... | collective-permute-start | bytes 8847368 | tf_op jit(solution)/shard_map/ppermute | solution.py:433
  66.6 20.7 %collective-permute-start.6 = (bf16[8,48,384]{2,1,0:T(8,128)(2,1)S(1)}, bf16[8,48,384]{2,1,0:T(8,128)(2,1)S(1)}, u32[]{:S(2)}, u32[]{:S(2)}) collective-permute-start(bf16[8,48,384]{2,1,0:T(8,128)(2,1)S(1)} %shard_map.343.refs_2_), channel_id=1, source_target_pairs={{0,4},{1,5},{2,6},{3,7},{4,0},{5,1},{6,2},{7,3},{8,12},{9,13},{10,... | collective-permute-start | bytes 884744 | tf_op jit(solution)/shard_map/ppermute | solution.py:433
  68.2 27.8 %collective-permute-start.7 = (bf16[8,48,1536]{2,1,0:T(8,128)(2,1)S(1)}, bf16[8,48,1536]{2,1,0:T(8,128)(2,1)S(1)}, u32[]{:S(2)}, u32[]{:S(2)}) collective-permute-start(bf16[8,48,1536]{2,1,0:T(8,128)(2,1)S(1)} %shard_map.345.refs_2_.refs_9_), channel_id=1, source_target_pairs={{0,8},{1,9},{2,10},{3,11},{4,12},{5,13},{6,14},{7,15},{8,0},{9,1},... | collective-permute-start | bytes 3538952 | tf_op jit(solution)/shard_map/ppermute | solution.py:433
  87.2 1.6 %copy-start.8 = (bf16[320,3072]{1,0:T(8,128)(2,1)S(1)}, bf16[320,3072]{1,0:T(8,128)(2,1)}, u32[]{:S(2)}) copy-start(bf16[320,3072]{1,0:T(8,128)(2,1)} %copy-done.7) | copy-start | bytes 5898244
  87.2 12.4 %collective-permute-start.10 = (bf16[8,48,1152]{2,1,0:T(8,128)(2,1)S(1)}, bf16[8,48,1152]{2,1,0:T(8,128)(2,1)S(1)}, u32[]{:S(2)}, u32[]{:S(2)}) collective-permute-start(bf16[8,48,1152]{2,1,0:T(8,128)(2,1)S(1)} %get-tuple-element.109.refs_8_), channel_id=1, source_target_pairs={{0,2},{1,3},{2,0},{3,1},{4,6},{5,7},{6,4},{7,5},{8,10},{9,11},{10,... | collective-permute-start | bytes 2654216 | tf_op jit(solution)/shard_map/ppermute | solution.py:433
  88.2 18.9 %collective-permute-start.9 = (bf16[4,240,384]{2,1,0:T(8,128)(2,1)S(1)}, bf16[4,240,384]{2,1,0:T(8,128)(2,1)S(1)}, u32[]{:S(2)}, u32[]{:S(2)}) collective-permute-start(bf16[4,240,384]{2,1,0:T(8,128)(2,1)S(1)} %get-tuple-element.110.refs_5_), channel_id=1, source_target_pairs={{0,1},{1,0},{2,3},{3,2},{4,5},{5,4},{6,7},{7,6},{8,9},{9,8},{10,11... | collective-permute-start | bytes 2211848 | tf_op jit(solution)/shard_map/ppermute | solution.py:433
  96.7 15.0 %collective-permute-start.8 = (bf16[4,48,1536]{2,1,0:T(8,128)(2,1)S(1)}, bf16[4,48,1536]{2,1,0:T(8,128)(2,1)S(1)}, u32[]{:S(2)}, u32[]{:S(2)}) collective-permute-start(bf16[4,48,1536]{2,1,0:T(8,128)(2,1)S(1)} %shard_map.354.refs_4_), channel_id=1, source_target_pairs={{0,4},{1,5},{2,6},{3,7},{4,0},{5,1},{6,2},{7,3},{8,12},{9,13},{10,... | collective-permute-start | bytes 1769480 | tf_op jit(solution)/shard_map/ppermute | solution.py:433
  98.3 1.3 collective-permute-start.11
  107.7 10.3 %collective-permute-start.14 = (bf16[2,240,384]{2,1,0:T(8,128)(2,1)S(1)}, bf16[2,240,384]{2,1,0:T(8,128)(2,1)S(1)}, u32[]{:S(2)}, u32[]{:S(2)}) collective-permute-start(bf16[2,240,384]{2,1,0:T(8,128)(2,1)S(1)} %shard_map.356.refs_3_), channel_id=1, source_target_pairs={{0,8},{1,9},{2,10},{3,11},{4,12},{5,13},{6,14},{7,15},{8,0},{9,1},... | collective-permute-start | bytes 1105928 | tf_op jit(solution)/shard_map/ppermute | solution.py:433
  108.2 15.1 %collective-permute-start.13 = (bf16[224,1152]{1,0:T(8,128)(2,1)S(1)}, bf16[224,1152]{1,0:T(8,128)(2,1)S(1)}, u32[]{:S(2)}, u32[]{:S(2)}) collective-permute-start(bf16[224,1152]{1,0:T(8,128)(2,1)S(1)} %get-tuple-element.122.refs_2_), channel_id=1, source_target_pairs={{0,4},{1,5},{2,6},{3,7},{4,0},{5,1},{6,2},{7,3},{8,12},{9,13},{10,... | collective-permute-start | bytes 1548296 | tf_op jit(solution)/shard_map/ppermute | solution.py:433
  118.6 9.9 %collective-permute-start.21 = (bf16[1,240,384]{2,1,0:T(8,128)(2,1)S(1)}, bf16[1,240,384]{2,1,0:T(8,128)(2,1)S(1)}, u32[]{:S(2)}, u32[]{:S(2)}) collective-permute-start(bf16[1,240,384]{2,1,0:T(8,128)(2,1)S(1)} %shard_map.359.refs_2_), channel_id=1, source_target_pairs={{0,16},{1,17},{2,18},{3,19},{4,20},{5,21},{6,22},{7,23},{8,24},{9,... | collective-permute-start | bytes 552968 | tf_op jit(solution)/shard_map/ppermute | solution.py:433
  121.3 9.9 %collective-permute-start.16 = (bf16[2,48,1536]{2,1,0:T(8,128)(2,1)S(1)}, bf16[2,48,1536]{2,1,0:T(8,128)(2,1)S(1)}, u32[]{:S(2)}, u32[]{:S(2)}) collective-permute-start(bf16[2,48,1536]{2,1,0:T(8,128)(2,1)S(1)} %shard_map.357.refs_1_), channel_id=1, source_target_pairs={{0,1},{1,0},{2,3},{3,2},{4,5},{5,4},{6,7},{7,6},{8,9},{9,8},{10,11... | collective-permute-start | bytes 884744 | tf_op jit(solution)/shard_map/ppermute | solution.py:433
  121.8 28.8 %collective-permute-start.12 = (bf16[320,768]{1,0:T(8,128)(2,1)S(1)}, bf16[320,768]{1,0:T(8,128)(2,1)S(1)}, u32[]{:S(2)}, u32[]{:S(2)}) collective-permute-start(bf16[320,768]{1,0:T(8,128)(2,1)S(1)} %shard_map.358.refs_3_), channel_id=1, source_target_pairs={{0,1},{1,0},{2,3},{3,2},{4,5},{5,4},{6,7},{7,6},{8,9},{9,8},{10,11... | collective-permute-start | bytes 1474568 | tf_op jit(solution)/shard_map/ppermute | solution.py:433
  124.0 12.1 %collective-permute-start.15 = (bf16[128,1152]{1,0:T(8,128)(2,1)S(1)}, bf16[128,1152]{1,0:T(8,128)(2,1)S(1)}, u32[]{:S(2)}, u32[]{:S(2)}) collective-permute-start(bf16[128,1152]{1,0:T(8,128)(2,1)S(1)} %get-tuple-element.126.refs_4_), channel_id=1, source_target_pairs={{0,8},{1,9},{2,10},{3,11},{4,12},{5,13},{6,14},{7,15},{8,0},{9,1},... | collective-permute-start | bytes 884744 | tf_op jit(solution)/shard_map/ppermute | solution.py:433
  131.9 9.4 %collective-permute-start.22 = (bf16[1,48,1536]{2,1,0:T(8,128)(2,1)S(1)}, bf16[1,48,1536]{2,1,0:T(8,128)(2,1)S(1)}, u32[]{:S(2)}, u32[]{:S(2)}) collective-permute-start(bf16[1,48,1536]{2,1,0:T(8,128)(2,1)S(1)} %shard_map.361.refs_2_), channel_id=1, source_target_pairs={{0,16},{1,17},{2,18},{3,19},{4,20},{5,21},{6,22},{7,23},{8,24},{9,... | collective-permute-start | bytes 442376 | tf_op jit(solution)/shard_map/ppermute | solution.py:433
  136.8 11.3 %collective-permute-start.17 = (bf16[80,1024]{1,0:T(8,128)(2,1)S(1)}, bf16[80,1024]{1,0:T(8,128)(2,1)S(1)}, u32[]{:S(2)}, u32[]{:S(2)}) collective-permute-start(bf16[80,1024]{1,0:T(8,128)(2,1)S(1)} %get-tuple-element.128), channel_id=1, source_target_pairs={{0,16},{1,17},{2,18},{3,19},{4,20},{5,21},{6,22},{7,23},{8,24},{9,... | collective-permute-start | bytes 491528 | tf_op jit(solution)/shard_map/ppermute | solution.py:433
  137.3 4.8 %collective-permute-start.18 = (bf16[48,384]{1,0:T(8,128)(2,1)S(1)}, bf16[48,384]{1,0:T(8,128)(2,1)S(1)}, u32[]{:S(2)}, u32[]{:S(2)}) collective-permute-start(bf16[48,384]{1,0:T(8,128)(2,1)S(1)} %get-tuple-element.129), channel_id=1, source_target_pairs={{0,1},{1,0},{2,3},{3,2},{4,5},{5,4},{6,7},{7,6},{8,9},{9,8},{10,11... | collective-permute-start | bytes 110600 | tf_op jit(solution)/shard_map/ppermute | solution.py:433
  137.8 10.3 %collective-permute-start.19 = (bf16[48,384]{1,0:T(8,128)(2,1)S(1)}, bf16[48,384]{1,0:T(8,128)(2,1)S(1)}, u32[]{:S(2)}, u32[]{:S(2)}) collective-permute-start(bf16[48,384]{1,0:T(8,128)(2,1)S(1)} %get-tuple-element.130), channel_id=1, source_target_pairs={{0,17},{1,16},{2,19},{3,18},{4,21},{5,20},{6,23},{7,22},{8,25},{9,... | collective-permute-start | bytes 110600 | tf_op jit(solution)/shard_map/ppermute | solution.py:433
  149.4 4.3 %collective-permute-start.20 = (bf16[32,1024]{1,0:T(8,128)(2,1)S(1)}, bf16[32,1024]{1,0:T(8,128)(2,1)S(1)}, u32[]{:S(2)}, u32[]{:S(2)}) collective-permute-start(bf16[32,1024]{1,0:T(8,128)(2,1)S(1)} %get-tuple-element.132.refs_5_.refs_0_), channel_id=1, source_target_pairs={{0,1},{1,0},{2,3},{3,2},{4,5},{5,4},{6,7},{7,6},{8,9},{9,8},{10,11... | collective-permute-start | bytes 196616 | tf_op jit(solution)/shard_map/ppermute | solution.py:433

commit v5 on v4

--- a/solution.py
+++ b/solution.py
@@ -464,7 +464,7 @@
 SIZES = {
     "strips_kernel": (1.7, 5),
     "qkv_kernel": (1.9, 10),
-    "attend_kernel": (9.0, 15),
+    "attend_kernel": (9.0, 42),
     "ffn_kernel": (5.5, 16),
     "ffn_back_kernel": (4.5, 14),
     "d_act_kernel": (2.5, 12),
@@ -472,6 +472,7 @@
     "fc1_grad_kernel": (5.5, 14),
     "attend_back_kernel": (4.4, 14),
     "hidden1_grad_kernel": (4.2, 12),
+    "join_kernel": (1.0, 12),
     "qkv_grad_kernel": (3.2, 12),
     "result_kernel": (40.0, 10),
     "tokens_grad_kernel": (2.0, 10),
@@ -525,27 +526,24 @@
     return half_sum(place, terms, 1, after, **how)
 
 
-def rest_of(place, terms, after=(), **how):
-    return half_sum(place, terms, 0, after, **how)
-
-
 def join_kernel(place, *refs):
     cut = refs[0].shape[1]
     for n, out in enumerate(refs[-2:]):
-        first, second, third, fourth = refs[4 * n : 4 * n + 4]
-        out[:, :cut, :] = (first[...].astype(F32) + second[...].astype(F32)).astype(BF)
-        out[:, cut:, :] = (third[...].astype(F32) + fourth[...].astype(F32)).astype(BF)
+        six = [ref[...].astype(F32) for ref in refs[6 * n : 6 * n + 6]]
+        out[:, :cut, :] = (six[0] + six[1] + six[2]).astype(BF)
+        out[:, cut:, :] = (six[3] + six[4] + six[5]).astype(BF)
 
 
 def joined_halves(place, terms, others, after=()):
-    size = terms[0].shape[0] // 2
-    tall, low = terms[0].shape[1:], others[0].shape[1:]
-    total = (size, tall[0] + low[0], tall[1])
-    specs = [
-        spec((size, *part), lambda n, p, side=side: (side, 0, 0))
-        for side in (1, 0)
-        for part in (tall, tall, low, low)
-    ]
+    line, _, _, high, wide = terms[0].shape
+    low = others[-1].shape[1]
+    total = (line, high + low, wide)
+    specs = []
+    for side in (1, 0):
+        cube = spec((line, None, None, high, wide), lambda n, p, side=side: (0, 0, side, 0, 0))
+        specs += [cube, cube, spec((line, high, wide), lambda n, p, side=side: (side, 0, 0))]
+        under = spec((line, low, wide), lambda n, p, side=side: (side, 0, 4))
+        specs += [under, under, spec((line, low, wide), lambda n, p, side=side: (side, 0, 0))]
     return run(
         join_kernel, place, (1,), specs, [full(total)] * 2, [shape(total, BF)] * 2, [],
         (*terms, *others) * 2, 0, after=after,
@@ -1317,13 +1315,13 @@
     )
     grad_other = swapped(grad_send, "y")
     out_a1 = x_part(place, terms_a, 1, (grad_send,))
-    terms_a = [x_part(place, terms_a, 0, (out_a1,)), swapped(out_a1, ORDER_A[1])]
+    terms_a = [*terms_a, swapped(out_a1, ORDER_A[1])]
     block = (16, 48, 5 * share)
     keep_b, send_b = run(
         functools.partial(fc1_grad_kernel, rest=rest_label(ORDER_B)), place, (parts,),
         [whole, sliced, whole, whole], [full(block), full(block)],
         [shape(block, BF), shape(block, BF)],
-        [pltpu.VMEM((width, part), F32)], (hidden2, d_pre, attn_low, d_mixed), 0, after=(out_a1, terms_a[0]),
+        [pltpu.VMEM((width, part), F32)], (hidden2, d_pre, attn_low, d_mixed), 0, after=(out_a1,),
     )
     terms_b = [keep_b, swapped(send_b, "core")]
 
@@ -1350,13 +1348,10 @@
 
     dqkv0, strip0 = attend_back(0, (send_b,))
     out_p1 = half_out(place, terms_b, (dqkv0,), column=4, columns=share)
-    terms_p = [
-        rest_of(place, terms_b, (out_p1,), column=4, columns=share),
-        swapped(out_p1, ORDER_A[1]),
-    ]
+    terms_p = [*terms_b, swapped(out_p1, ORDER_A[1])]
     out_b1 = half_out(place, terms_b, (out_p1,), columns=4 * share)
-    terms_b = [rest_of(place, terms_b, (out_b1,), columns=4 * share), swapped(out_b1, ORDER_B[1])]
-    dqkv1, strip1 = attend_back(1, (dqkv0, out_b1, terms_b[0], terms_p[0]))
+    terms_b = [*terms_b, swapped(out_b1, ORDER_B[1])]
+    dqkv1, strip1 = attend_back(1, (dqkv0, out_b1))
     dqkv2, strip2 = attend_back(2, (dqkv1,))
     dqkv = (dqkv0, dqkv1, dqkv2)
     third = [spec((1, slots, LANES), lambda t, p: (t, 0, 0))] * 3
@@ -1394,36 +1389,33 @@
         (strip0, strip1, strip2, small_ffn, fc1_bias_part, small_last, small_result), 0,
     )[0]
     mate = swapped(packed, "core")
-    out_b2 = half_out(place, terms_b, (packed,))
-    terms_b = [*terms_b, swapped(out_b2, "x")]
-
     def wide(blocks, columns):
         return (48 * blocks + NOTE[0], columns)
 
     send, rest = run(
         qs_first_kernel, place, (1,),
         [full((8, 48, 3 * share))] * 2 + [full(NOTE)] * 2, [full(wide(4, 3 * share))] * 2,
-        [shape(wide(4, 3 * share), BF)] * 2, [], (keep_q, recv_q, packed, mate), 0, after=(out_b2,),
+        [shape(wide(4, 3 * share), BF)] * 2, [], (keep_q, recv_q, packed, mate), 0, after=(),
     )
     recv = swapped(send, "x")
-    out_a3 = half_out(place, terms_a, (send,))
+    out_b2 = half_out(place, terms_b, (send,), columns=4 * share)
+    terms_b = [*terms_b, swapped(out_b2, "x")]
+    out_a3 = half_out(place, terms_a, (out_b2,))
     terms_a = [*terms_a, swapped(out_a3, "z1")]
-    out_b3 = half_out(place, terms_b, (out_a3,))
-    terms_b = [*terms_b, swapped(out_b3, "y")]
     dh_late = run(
         add_kernel, place, (1,), [whole], [whole], [shape((rows, width), BF)], [], (dh_send,), 0,
-        after=(out_b3,),
+        after=(out_a3,),
     )[0]
     dh_recv = swapped(dh_late, "y")
-    out_a4 = half_out(place, terms_a, (dh_late,))
-    terms_a = [*terms_a, swapped(out_a4, "z2")]
     send, rest = run(
         qs_next_kernel, place, (1,), [full(wide(4, 3 * share))] * 2, [full(wide(2, 3 * share))] * 2,
-        [shape(wide(2, 3 * share), BF)] * 2, [], (rest, recv), 0, after=(out_a4,),
+        [shape(wide(2, 3 * share), BF)] * 2, [], (rest, recv), 0, after=(dh_late,),
     )
     recv = swapped(send, "z1")
-    out_b4 = half_out(place, terms_b, (send,))
-    terms_b = [*terms_b, swapped(out_b4, "z2")]
+    out_a4 = half_out(place, terms_a, (send,))
+    terms_a = [*terms_a, swapped(out_a4, "z2")]
+    out_b3 = half_out(place, terms_b, (out_a4,), columns=4 * share)
+    terms_b = [*terms_b, swapped(out_b3, "y")]
     q_keep, q_line, q_side, q_cross, note = run(
         qs_last_kernel, place, (1,), [full(wide(2, 3 * share))] * 2,
         [
@@ -1433,24 +1425,26 @@
             shape((48, 2 * share), F32), shape(wide(1, NOTE[1]), BF), shape((48, share), BF),
             shape((48, share), BF), shape(NOTE, BF),
         ],
-        [pltpu.VMEM(wide(2, 3 * share), F32)], (rest, recv), 0, after=(out_b4,),
+        [pltpu.VMEM(wide(2, 3 * share), F32)], (rest, recv), 0, after=(out_b3,),
     )
     q_sends = (swapped(q_line, "z2"), swapped(q_side, "y"), swapped(q_cross, "z2", "y"))
+    tokens_grad = run(
+        tokens_grad_kernel, place, (1,),
+        [whole, whole, whole, whole, full((8, width))], [whole],
+        [shape((rows, width), BF)], [], (dh_keep, dh_recv, own, d_resid, vecs), 0,
+        after=(q_line,),
+    )[0]
+    out_b4 = half_out(place, terms_b, (tokens_grad,), columns=4 * share)
+    terms_b = [*terms_b, swapped(out_b4, "z2")]
     qkv_grad, packed = run(
         qs_join_kernel, place, (1,),
         [full((48, 2 * share)), full(wide(1, NOTE[1])), full((48, share)), full((48, share)), full(NOTE)],
         [full((48, 3 * share)), full(NOTE)], [shape((48, 3 * share), F32), shape(NOTE, BF)], [],
-        (q_keep, *q_sends, note), 0,
+        (q_keep, *q_sends, note), 0, after=(out_b4,),
     )
     mate = swapped(packed, "y")
-    tokens_grad = run(
-        tokens_grad_kernel, place, (1,),
-        [whole, whole, whole, whole, full((8, width))], [whole],
-        [shape((rows, width), BF)], [], (dh_keep, dh_recv, own, d_resid, vecs), 0,
-        after=(packed,),
-    )[0]
     fc2_proj = added(terms_a)
-    fc1_grad = added(terms_b)
+    fc1_grad = added([term[:, :, : 4 * share] for term in terms_b])
     fc2_grad = fc2_proj[:192]
     proj_grad = fc2_proj[192:]
     vector = shape((width,), F32)

time: 156 us -> 151 us (0.968)
  waiting for transfers between devices: 41.3 us -> 35.3 us
  local copies, waits for them, and re-layouts: 4.58 us -> 6.28 us
  Pallas kernels: 82.2 us -> 80.6 us
    ppermute x23, waiting for transfers between devices: 41.3 us -> 35.3 us  [swapped(): return lax.ppermute(value, ('img', 'seq'), swap_pairs(*names))]
    unnamed x50 -> x68, local copies, waits for them, and re-layouts: 3.03 us -> 4.73 us
    pallas_call x35 -> x32, Pallas kernels: 82.2 us -> 80.6 us  [run(): pl.pallas_call(kernel, grid_spec=pltpu.PrefetchScalarGridSpec(num_scalar_...]
  transfers between devices with their start and end apart: 23 -> 23, of which waited for: 13 -> 12; matrix products, arithmetic and copies ran while one was open for 2% -> 1% of each run, Pallas kernels for 37% -> 39%
where the time goes in v5:
time: 151 us
  Pallas kernels  80.6 us (53%)
  waiting for transfers between devices  35.3 us (23%)
  starting transfers between devices  26.5 us (18%)
  local copies, waits for them, and re-layouts  6.28 us (4%)
    pallas_call x32, Pallas kernels, run(): pl.pallas_call(kernel, grid_spec=pltpu.PrefetchScalarGridSpec(num_scalar_...  80.6 us
    ppermute x23, waiting for transfers between devices, swapped(): return lax.ppermute(value, ('img', 'seq'), swap_pairs(*names))  35.3 us
    ppermute x23, starting transfers between devices, swapped(): return lax.ppermute(value, ('img', 'seq'), swap_pairs(*names))  26.5 us
    unnamed x68, local copies, waits for them, and re-layouts  4.73 us
  transfers between devices with their start and end apart: 23, of which 12 were waited for; matrix products, arithmetic and copies ran while one was open for 1% of the time, Pallas kernels for 39%

profile of v5, /device:TPU:0, one launch (start us, length us, event | category | flops | bytes accessed | tf_op | source)
XLA Modules:
  0.0 151.1 jit_solution(5562820723381150546)
XLA Ops:
  0.7 3.0 %collective-permute-start = (bf16[320,768]{1,0:T(8,128)(2,1)}, bf16[320,768]{1,0:T(8,128)(2,1)S(1)}, u32[]{:S(2)}, u32[]{:S(2)}) collective-permute-start(bf16[320,768]{1,0:T(8,128)(2,1)} %bitcast.29), channel_id=1, source_target_pairs={{0,1},{1,0},{2,3},{3,2},{4,5},{5,4},{6,7},{7,6},{8,9},{9,8},{10,11... | collective-permute-start | bytes 1474568 | tf_op jit(solution)/shard_map/ppermute | solution.py:433
  3.8 0.9 copy-done.5
  4.8 1.7 %shard_map.333.refs_1_ = f32[12,2,1280]{2,1,0:T(2,128)S(1)} custom-call(s32[7]{0:T(128)S(1)} %stack.58.place_ref, f32[12,2212]{1,0:T(8,128)S(1)} %bitcast.34), custom_call_target="tpu_custom_call" | custom-call | flops 1955000064 | bytes 1 | tf_op jit(solution)/shard_map/pallas_call | solution.py:492
  7.5 2.0 %copy-done.1 = bf16[768,2304]{1,0:T(8,128)(2,1)S(1)} copy-done((bf16[768,2304]{1,0:T(8,128)(2,1)S(1)}, bf16[768,2304]{1,0:T(8,128)(2,1)}, u32[]{:S(2)}) %copy-start.1) | copy-done | bytes 3538968
  9.5 2.5 %shard_map.331 = (bf16[3,640,384]{2,1,0:T(8,128)(2,1)S(1)}, bf16[640,768]{1,0:T(8,128)(2,1)S(1)}) custom-call(s32[7]{0:T(128)S(1)} %stack.58.place_ref, bf16[320,768]{1,0:T(8,128)(2,1)S(1)} %bitcast.30, f32[8,768]{1,0:T(8,128)S(1)} %stack.67.refs_1_.refs_3_.refs_6_.refs_4_, bf16[768,2304]{1,0:T(8,128)(2,1)S(1)} %copy-done.1, f32[1,768]{1,0:T(1,128)S(1)} %reshape.86.refs_3_, ...), custom_call_target="tpu_custom_call" | custom-call | flops 2184999936 | bytes 1 | tf_op jit(solution)/shard_map/pallas_call | solution.py:492
  12.1 3.0 %collective-permute-done.refs_0_.refs_5_ = bf16[320,768]{1,0:T(8,128)(2,1)S(1)} collective-permute-done((bf16[320,768]{1,0:T(8,128)(2,1)}, bf16[320,768]{1,0:T(8,128)(2,1)S(1)}, u32[]{:S(2)}, u32[]{:S(2)}) %collective-permute-start) | collective-permute-done | bytes 491552 | tf_op jit(solution)/shard_map/ppermute | solution.py:433
  15.1 2.5 %shard_map.332 = (bf16[3,640,384]{2,1,0:T(8,128)(2,1)S(1)}, bf16[640,768]{1,0:T(8,128)(2,1)S(1)}) custom-call(s32[7]{0:T(128)S(1)} %stack.58.place_ref, bf16[320,768]{1,0:T(8,128)(2,1)S(1)} %collective-permute-done.refs_0_.refs_5_, f32[8,768]{1,0:T(8,128)S(1)} %stack.67.refs_1_.refs_3_.refs_6_.refs_4_, ...), custom_call_target="tpu_custom_call", output_to_operand_aliasing={{0}: (6, {}), {1}: (7, {})} | custom-call | flops 2184999936 | bytes 1 | tf_op jit(solution)/shard_map/pallas_call | solution.py:492
  17.6 9.0 %shard_map.334 = (bf16[320,384]{1,0:T(8,128)(2,1)S(1)}, bf16[320,384]{1,0:T(8,128)(2,1)S(1)}, bf16[6,640,640]{2,1,0:T(8,128)(2,1)S(1)}, f32[640,384]{1,0:T(8,128)S(1)}) custom-call(s32[7]{0:T(128)S(1)} %stack.58.place_ref, bf16[3,640,384]{2,1,0:T(8,128)(2,1)S(1)} %get-tuple-element.84.refs_0_, f32[12,2,1280]{2,1,0:T(2,128)S(1)} %copy-done.17, ...), custom_call_target="tpu_custom_call" | custom-call | flops 10350000128 | bytes 1 | tf_op jit(solution)/shard_map/pallas_call | solution.py:492
  26.7 1.8 %collective-permute-start.1 = (bf16[320,384]{1,0:T(8,128)(2,1)S(1)}, bf16[320,384]{1,0:T(8,128)(2,1)S(1)}, u32[]{:S(2)}, u32[]{:S(2)}) collective-permute-start(bf16[320,384]{1,0:T(8,128)(2,1)S(1)} %get-tuple-element.86.refs_3_), channel_id=1, source_target_pairs={{0,1},{1,0},{2,3},{3,2},{4,5},{5,4},{6,7},{7,6},{8,9},{9,8},{10,11... | collective-permute-start | bytes 737288 | tf_op jit(solution)/shard_map/ppermute | solution.py:433
  28.5 3.1 %shard_map.335 = (bf16[320,768]{1,0:T(8,128)(2,1)S(1)}, bf16[320,3072]{1,0:T(8,128)(2,1)S(1)}) custom-call(s32[7]{0:T(128)S(1)} %stack.58.place_ref, bf16[320,768]{1,0:T(8,128)(2,1)S(1)} %fusion.refs_0_.refs_2_.refs_3_, f32[8,768]{1,0:T(8,128)S(1)} %stack.67.refs_1_.refs_3_.refs_6_.refs_4_, bf16[3072,768]{1,0:T(8,128)(2,1)S(1)} %bitcast.28, ...), custom_call_target="tpu_custom_call" | custom-call | flops 2875000064 | bytes 1 | tf_op jit(solution)/shard_map/pallas_call | solution.py:492
  31.6 2.3 %collective-permute-done.1.refs_2_ = bf16[320,384]{1,0:T(8,128)(2,1)S(1)} collective-permute-done((bf16[320,384]{1,0:T(8,128)(2,1)S(1)}, bf16[320,384]{1,0:T(8,128)(2,1)S(1)}, u32[]{:S(2)}, u32[]{:S(2)}) %collective-permute-start.1) | collective-permute-done | bytes 245792 | tf_op jit(solution)/shard_map/ppermute | solution.py:433
  33.9 6.0 %shard_map.336 = (bf16[320,3072]{1,0:T(8,128)(2,1)S(1)}, bf16[320,3072]{1,0:T(8,128)(2,1)S(1)}, f32[1,3072]{1,0:T(1,128)S(1)}, bf16[320,768]{1,0:T(8,128)(2,1)S(...) custom-call(s32[7]{0:T(128)S(1)} %stack.58.place_ref, ...), custom_call_target="tpu_custom_call" | custom-call | flops 6325000192 | bytes 1 | tf_op jit(solution)/shard_map/pallas_call | solution.py:492
  39.9 4.5 %shard_map.337 = (bf16[4,2,2,192,384]{4,3,2,1,0:T(8,128)(2,1)S(1)}, bf16[4,2,2,192,384]{4,3,2,1,0:T(8,128)(2,1)S(1)}) custom-call(s32[7]{0:T(128)S(1)} %stack.58.place_ref, bf16[320,3072]{1,0:T(8,128)(2,1)S(1)} %get-tuple-element.88.refs_0_, bf16[320,768]{1,0:T(8,128)(2,1)S(1)} %get-tuple-element.90.refs_1_.refs_3_), custom_call_target="tpu_custom_call" | custom-call | flops 5289999872 | bytes 1 | tf_op jit(solution)/shard_map/pallas_call | solution.py:492
  44.6 5.2 %shard_map.338 = (bf16[320,768]{1,0:T(8,128)(2,1)S(1)}, f32[320,768]{1,0:T(8,128)S(1)}, bf16[320,384]{1,0:T(8,128)(2,1)S(1)}, bf16[320,384]{1,0:T(8,128)(2,1)S(1)}, f32[8,768]{1,0:T(8,128)S(1)}) custom-call(s32[7]{0:T(128)S(1)} %stack.58.place_ref, bf16[320,3072]{1,0:T(8,128)(2,1)S(1)} %get-tuple-element.93.refs_0_.refs_1_, bf16[768,3072]{1,0:T(8,128)(2,1)S(1)} %bitcast.26, ...), custom_call_target="tpu_custom_call" | custom-call | flops 5175000064 | bytes 1 | tf_op jit(solution)/shard_map/pallas_call | solution.py:492
  49.8 1.5 collective-permute-start.5
  51.3 1.0 shard_map.339
  52.3 1.6 %collective-permute-start.3 = (bf16[8,192,384]{2,1,0:T(8,128)(2,1)S(1)}, bf16[8,192,384]{2,1,0:T(8,128)(2,1)S(1)}, u32[]{:S(2)}, u32[]{:S(2)}) collective-permute-start(bf16[8,192,384]{2,1,0:T(8,128)(2,1)S(1)} %bitcast.22), channel_id=1, source_target_pairs={{0,4},{1,5},{2,6},{3,7},{4,0},{5,1},{6,2},{7,3},{8,12},{9,13},{10,... | collective-permute-start | bytes 3538952 | tf_op jit(solution)/shard_map/ppermute | solution.py:433
  53.9 5.6 %shard_map.340 = (bf16[16,48,1920]{2,1,0:T(8,128)(2,1)S(1)}, bf16[16,48,1920]{2,1,0:T(8,128)(2,1)S(1)}) custom-call(s32[7]{0:T(128)S(1)} %stack.58.place_ref, bf16[320,768]{1,0:T(8,128)(2,1)S(1)} %get-tuple-element.96.refs_0_, bf16[320,3072]{1,0:T(8,128)(2,1)S(1)} %get-tuple-element.93.refs_0_.refs_1_, bf16[320,768]{1,0:T(8,128)(2,1)S(1)} %get-tuple-element.97.refs_2_, ...), custom_call_target="tpu_custom_call" | custom-call | flops 6325000192 | bytes 1 | tf_op jit(solution)/shard_map/pallas_call | solution.py:492
  59.6 4.0 %shard_map.341 = (bf16[3,640,128]{2,1,0:T(8,128)(2,1)S(1)}, f32[1,2,2,1280]{3,2,1,0:T(2,128)S(1)}) custom-call(s32[7]{0:T(128)S(1)} %stack.58.place_ref, bf16[3,640,384]{2,1,0:T(8,128)(2,1)S(1)} %get-tuple-element.84.refs_0_, bf16[6,640,640]{2,1,0:T(8,128)(2,1)S(1)} %get-tuple-element.101.refs_1_, bf16[320,384]{1,0:T(8,128)(2,1)S(1)} %copy-done.15, ...), custom_call_target="tpu_custom_call" | custom-call | flops 46000001024 | bytes 1 | tf_op jit(solution)/shard_map/pallas_call | solution.py:492
  63.6 1.4 collective-permute-done.4.refs_1_.refs_4_.refs_10_
  66.3 1.0 shard_map.343.refs_9_
  67.4 1.6 %collective-permute-start.8 = (bf16[8,48,1536]{2,1,0:T(8,128)(2,1)S(1)}, bf16[8,48,1536]{2,1,0:T(8,128)(2,1)S(1)}, u32[]{:S(2)}, u32[]{:S(2)}) collective-permute-start(bf16[8,48,1536]{2,1,0:T(8,128)(2,1)S(1)} %shard_map.343.refs_9_), channel_id=1, source_target_pairs={{0,8},{1,9},{2,10},{3,11},{4,12},{5,13},{6,14},{7,15},{8,0},{9,1},... | collective-permute-start | bytes 3538952 | tf_op jit(solution)/shard_map/ppermute | solution.py:433
  69.0 3.9 %shard_map.344 = (bf16[3,640,128]{2,1,0:T(8,128)(2,1)S(1)}, f32[1,2,2,1280]{3,2,1,0:T(2,128)S(1)}) custom-call(s32[7]{0:T(128)S(1)} %stack.58.place_ref, bf16[3,640,384]{2,1,0:T(8,128)(2,1)S(1)} %get-tuple-element.84.refs_0_, bf16[6,640,640]{2,1,0:T(8,128)(2,1)S(1)} %get-tuple-element.101.refs_1_, bf16[320,384]{1,0:T(8,128)(2,1)S(1)} %copy-done.15, ...), custom_call_target="tpu_custom_call" | custom-call | flops 5059999744 | bytes 1 | tf_op jit(solution)/shard_map/pallas_call | solution.py:492
  73.0 4.0 %shard_map.345 = (bf16[3,640,128]{2,1,0:T(8,128)(2,1)S(1)}, f32[1,2,2,1280]{3,2,1,0:T(2,128)S(1)}) custom-call(s32[7]{0:T(128)S(1)} %stack.58.place_ref, bf16[3,640,384]{2,1,0:T(8,128)(2,1)S(1)} %get-tuple-element.84.refs_0_, bf16[6,640,640]{2,1,0:T(8,128)(2,1)S(1)} %get-tuple-element.101.refs_1_, bf16[320,384]{1,0:T(8,128)(2,1)S(1)} %copy-done.15, ...), custom_call_target="tpu_custom_call" | custom-call | flops 5059999744 | bytes 1 | tf_op jit(solution)/shard_map/pallas_call | solution.py:492
  76.9 4.0 %shard_map.346 = (f32[320,768]{1,0:T(8,128)S(1)}, bf16[320,768]{1,0:T(8,128)(2,1)S(1)}, f32[8,768]{1,0:T(8,128)S(1)}) custom-call(s32[7]{0:T(128)S(1)} %stack.58.place_ref, bf16[3,640,128]{2,1,0:T(8,128)(2,1)S(1)} %get-tuple-element.104.refs_2_.refs_8_.refs_0_.refs_1_, bf16[3,640,128]{2,1,0:T(8,128)(2,1)S(1)} %get-tuple-element.106.refs_8_.refs_1_.refs_2_, ...), custom_call_target="tpu_custom_call" | custom-call | flops 4830000128 | bytes 1 | tf_op jit(solution)/shard_map/pallas_call | solution.py:492
  80.9 3.6 %shard_map.347 = (bf16[8,48,1152]{2,1,0:T(8,128)(2,1)S(1)}, bf16[8,48,1152]{2,1,0:T(8,128)(2,1)S(1)}) custom-call(s32[7]{0:T(128)S(1)} %stack.58.place_ref, bf16[640,768]{1,0:T(8,128)(2,1)S(1)} %get-tuple-element.105.refs_0_, bf16[3,640,128]{2,1,0:T(8,128)(2,1)S(1)} %get-tuple-element.104.refs_2_.refs_8_.refs_0_.refs_1_, ...), custom_call_target="tpu_custom_call" | custom-call | flops 3680000000 | bytes 1 | tf_op jit(solution)/shard_map/pallas_call | solution.py:492
  84.6 2.1 %collective-permute-done.6.refs_5_.refs_11_ = bf16[8,48,384]{2,1,0:T(8,128)(2,1)S(1)} collective-permute-done((bf16[8,48,384]{2,1,0:T(8,128)(2,1)S(1)}, bf16[8,48,384]{2,1,0:T(8,128)(2,1)S(1)}, u32[]{:S(2)}, u32[]{:S(2)}) %collective-permute-start.6) | collective-permute-done | bytes 294944 | tf_op jit(solution)/shard_map/ppermute | solution.py:433
  86.8 1.8 %shard_map.348 = (bf16[4,240,384]{2,1,0:T(8,128)(2,1)S(1)}, bf16[4,240,384]{2,1,0:T(8,128)(2,1)S(1)}) custom-call(s32[7]{0:T(128)S(1)} %stack.58.place_ref, bf16[4,2,2,192,384]{4,3,2,1,0:T(8,128)(2,1)S(1)} %get-tuple-element.91.refs_0_.refs_6_, bf16[4,2,2,192,384]{4,3,2,1,0:T(8,128)(2,1)S(1)} %collective-permute-done.2.refs_1_.refs_7_, ...), custom_call_target="tpu_custom_call" | custom-call | flops 1150000000 | bytes 1 | tf_op jit(solution)/shard_map/pallas_call | solution.py:492
  89.2 4.1 %shard_map.349 = (bf16[320,768]{1,0:T(8,128)(2,1)}, f32[8,768]{1,0:T(8,128)S(1)}) custom-call(s32[7]{0:T(128)S(1)} %stack.58.place_ref, bf16[320,3072]{1,0:T(8,128)(2,1)S(1)} %copy-done.13, bf16[3072,768]{1,0:T(8,128)(2,1)S(1)} %bitcast.28, f32[320,768]{1,0:T(8,128)S(1)} %copy-done.9, bf16[320,768]{1,0:T(8,128)(2,1)S(1)} %fusion.refs_0_.refs_2_.refs_3_, ...), custom_call_target="tpu_custom_call" | custom-call | flops 46000001024 | bytes 1 | tf_op jit(solution)/shard_map/pallas_call | solution.py:492
  94.1 1.2 collective-permute-done.10.refs_3_
  96.1 1.5 collective-permute-start.12
  98.3 8.1 %collective-permute-done.7.refs_1_ = bf16[4,240,384]{2,1,0:T(8,128)(2,1)S(1)} collective-permute-done((bf16[4,240,384]{2,1,0:T(8,128)(2,1)S(1)}, bf16[4,240,384]{2,1,0:T(8,128)(2,1)S(1)}, u32[]{:S(2)}, u32[]{:S(2)}) %collective-permute-start.7) | collective-permute-done | bytes 737312 | tf_op jit(solution)/shard_map/ppermute | solution.py:433
  107.0 1.6 %collective-permute-start.15 = (bf16[2,240,384]{2,1,0:T(8,128)(2,1)S(1)}, bf16[2,240,384]{2,1,0:T(8,128)(2,1)S(1)}, u32[]{:S(2)}, u32[]{:S(2)}) collective-permute-start(bf16[2,240,384]{2,1,0:T(8,128)(2,1)S(1)} %shard_map.353.refs_1_), channel_id=1, source_target_pairs={{0,8},{1,9},{2,10},{3,11},{4,12},{5,13},{6,14},{7,15},{8,0},{9,1},... | collective-permute-start | bytes 1105928 | tf_op jit(solution)/shard_map/ppermute | solution.py:433
  108.7 1.5 collective-permute-start.14
  111.4 4.6 %collective-permute-done.15.refs_2_ = bf16[2,240,384]{2,1,0:T(8,128)(2,1)S(1)} collective-permute-done((bf16[2,240,384]{2,1,0:T(8,128)(2,1)S(1)}, bf16[2,240,384]{2,1,0:T(8,128)(2,1)S(1)}, u32[]{:S(2)}, u32[]{:S(2)}) %collective-permute-start.15) | collective-permute-done | bytes 368672 | tf_op jit(solution)/shard_map/ppermute | solution.py:433
  116.7 2.7 %collective-permute-start.21 = (bf16[1,240,384]{2,1,0:T(8,128)(2,1)S(1)}, bf16[1,240,384]{2,1,0:T(8,128)(2,1)S(1)}, u32[]{:S(2)}, u32[]{:S(2)}) collective-permute-start(bf16[1,240,384]{2,1,0:T(8,128)(2,1)S(1)} %shard_map.356.refs_4_), channel_id=1, source_target_pairs={{0,16},{1,17},{2,18},{3,19},{4,20},{5,21},{6,22},{7,23},{8,24},{9,... | collective-permute-start | bytes 552968 | tf_op jit(solution)/shard_map/ppermute | solution.py:433
  119.8 1.6 %collective-permute-start.13 = (bf16[128,1152]{1,0:T(8,128)(2,1)S(1)}, bf16[128,1152]{1,0:T(8,128)(2,1)S(1)}, u32[]{:S(2)}, u32[]{:S(2)}) collective-permute-start(bf16[128,1152]{1,0:T(8,128)(2,1)S(1)} %get-tuple-element.126.refs_3_), channel_id=1, source_target_pairs={{0,8},{1,9},{2,10},{3,11},{4,12},{5,13},{6,14},{7,15},{8,0},{9,1},... | collective-permute-start | bytes 884744 | tf_op jit(solution)/shard_map/ppermute | solution.py:433
  121.4 3.7 %collective-permute-done.21 = bf16[1,240,384]{2,1,0:T(8,128)(2,1)S(1)} collective-permute-done((bf16[1,240,384]{2,1,0:T(8,128)(2,1)S(1)}, bf16[1,240,384]{2,1,0:T(8,128)(2,1)S(1)}, u32[]{:S(2)}, u32[]{:S(2)}) %collective-permute-start.21) | collective-permute-done | bytes 184352 | tf_op jit(solution)/shard_map/ppermute | solution.py:433
  127.5 1.1 collective-permute-done.13.refs_1_
  129.2 1.3 collective-permute-start.16
  130.6 1.4 collective-permute-start.17
  132.0 1.7 %collective-permute-start.18 = (bf16[48,384]{1,0:T(8,128)(2,1)S(1)}, bf16[48,384]{1,0:T(8,128)(2,1)S(1)}, u32[]{:S(2)}, u32[]{:S(2)}) collective-permute-start(bf16[48,384]{1,0:T(8,128)(2,1)S(1)} %get-tuple-element.130), channel_id=1, source_target_pairs={{0,17},{1,16},{2,19},{3,18},{4,21},{5,20},{6,23},{7,22},{8,25},{9,... | collective-permute-start | bytes 110600 | tf_op jit(solution)/shard_map/ppermute | solution.py:433
  133.7 2.0 %shard_map.359.refs_5_ = bf16[320,768]{1,0:T(8,128)(2,1)} custom-call(s32[7]{0:T(128)S(1)} %stack.58.place_ref, f32[320,768]{1,0:T(8,128)S(1)} %get-tuple-element.113.refs_0_, bf16[320,768]{1,0:T(8,128)(2,1)S(1)} %collective-permute-done.11.refs_1_, bf16[320,768]{1,0:T(8,128)(2,1)S(1)} %bitcast.33, f32[320,768]{1,0:T(8,128)S(1)} %get-tuple-element.123.refs_3_, ...), custom_call_target="tpu_custom_call" | custom-call | flops 2300000000 | bytes 1 | tf_op jit(solution)/shard_map/pallas_call | solution.py:492
  136.4 1.0 copy-done
  138.9 3.4 %collective-permute-done.18.refs_3_ = bf16[48,384]{1,0:T(8,128)(2,1)S(1)} collective-permute-done((bf16[48,384]{1,0:T(8,128)(2,1)S(1)}, bf16[48,384]{1,0:T(8,128)(2,1)S(1)}, u32[]{:S(2)}, u32[]{:S(2)}) %collective-permute-start.18) | collective-permute-done | bytes 36896 | tf_op jit(solution)/shard_map/ppermute | solution.py:433
  142.3 1.2 shard_map.361
  144.2 3.6 %collective-permute-done.20.refs_1_ = bf16[32,1024]{1,0:T(8,128)(2,1)S(1)} collective-permute-done((bf16[32,1024]{1,0:T(8,128)(2,1)S(1)}, bf16[32,1024]{1,0:T(8,128)(2,1)S(1)}, u32[]{:S(2)}, u32[]{:S(2)}) %collective-permute-start.20) | collective-permute-done | bytes 65568 | tf_op jit(solution)/shard_map/ppermute | solution.py:433
  147.8 2.4 %shard_map.362 = (f32[12,2212]{1,0:T(8,128)}, f32[768]{0:T(1024)}, f32[768]{0:T(1024)}, f32[768]{0:T(1024)}, f32[768]{0:T(1024)}, /*index=5*/f32[768]{0:T(1024)}...) custom-call(s32[7]{0:T(128)S(1)} %stack.58.place_ref, ...), custom_call_target="tpu_custom_call" | custom-call | flops 11500000 | bytes 1 | tf_op jit(solution)/shard_map/pallas_call | solution.py:492
  (118 shorter events, 15.2 us)
Async XLA Ops:
  0.7 14.5 %collective-permute-start = (bf16[320,768]{1,0:T(8,128)(2,1)}, bf16[320,768]{1,0:T(8,128)(2,1)S(1)}, u32[]{:S(2)}, u32[]{:S(2)}) collective-permute-start(bf16[320,768]{1,0:T(8,128)(2,1)} %bitcast.29), channel_id=1, source_target_pairs={{0,1},{1,0},{2,3},{3,2},{4,5},{5,4},{6,7},{7,6},{8,9},{9,8},{10,11... | collective-permute-start | bytes 1474568 | tf_op jit(solution)/shard_map/ppermute | solution.py:433
  4.7 2.5 %copy-start.20 = (f32[768]{0:T(1024)S(1)}, f32[768]{0:T(1024)}, u32[]{:S(2)}) copy-start(f32[768]{0:T(1024)} %param.24) | copy-start | bytes 9220
  4.7 2.6 %copy-start.21 = (f32[768]{0:T(1024)S(1)}, f32[768]{0:T(1024)}, u32[]{:S(2)}) copy-start(f32[768]{0:T(1024)} %param.30) | copy-start | bytes 9220
  4.7 2.6 %copy-start.22 = (f32[768]{0:T(1024)S(1)}, f32[768]{0:T(1024)}, u32[]{:S(2)}) copy-start(f32[768]{0:T(1024)} %param.31) | copy-start | bytes 9220
  4.7 2.6 %copy-start.23 = (f32[768]{0:T(1024)S(1)}, f32[768]{0:T(1024)}, u32[]{:S(2)}) copy-start(f32[768]{0:T(1024)} %param.32) | copy-start | bytes 9220
  4.7 2.6 %copy-start.24 = (f32[768]{0:T(1024)S(1)}, f32[768]{0:T(1024)}, u32[]{:S(2)}) copy-start(f32[768]{0:T(1024)} %param.33) | copy-start | bytes 9220
  4.7 2.6 %copy-start.25 = (f32[768]{0:T(1024)S(1)}, f32[768]{0:T(1024)}, u32[]{:S(2)}) copy-start(f32[768]{0:T(1024)} %param.37) | copy-start | bytes 9220
  4.7 2.6 %copy-start.26 = (f32[768]{0:T(1024)S(1)}, f32[768]{0:T(1024)}, u32[]{:S(2)}) copy-start(f32[768]{0:T(1024)} %param.38) | copy-start | bytes 9220
  4.8 2.6 %copy-start.27 = (f32[768]{0:T(1024)S(1)}, f32[768]{0:T(1024)}, u32[]{:S(2)}) copy-start(f32[768]{0:T(1024)} %param.26) | copy-start | bytes 9220
  4.8 2.6 %copy-start.28 = (f32[768]{0:T(1024)S(1)}, f32[768]{0:T(1024)}, u32[]{:S(2)}) copy-start(f32[768]{0:T(1024)} %param.27) | copy-start | bytes 9220
  4.8 2.7 %copy-start.4 = (bf16[1,320,768]{2,1,0:T(8,128)(2,1)S(1)}, bf16[1,320,768]{2,1,0:T(8,128)(2,1)}, u32[]{:S(2)}) copy-start(bf16[1,320,768]{2,1,0:T(8,128)(2,1)} %param.20) | copy-start | bytes 1474564
  9.5 5.6 %copy-start.2 = (bf16[768,2304]{1,0:T(8,128)(2,1)S(1)}, bf16[768,2304]{1,0:T(8,128)(2,1)}, u32[]{:S(2)}) copy-start(bf16[768,2304]{1,0:T(8,128)(2,1)} %refs_3_.1) | copy-start | bytes 10616836
  15.1 13.4 %slice-start.2 = ((s8[4718592]{0:T(1024)(128)(4,1)}), s8[4194304]{0:T(1024)(128)(4,1)S(1)}, s32[]{:S(2)}) async-start(s8[4718592]{0:T(1024)(128)(4,1)} %bitcast.27), calls=%async_computation.2 | async-start | bytes 8388608
  17.6 10.9 %slice-start.3 = ((s8[4718592]{0:T(1024)(128)(4,1)}), s8[524288]{0:T(1024)(128)(4,1)S(1)}, s32[]{:S(2)}) async-start(s8[4718592]{0:T(1024)(128)(4,1)} %bitcast.27), calls=%async_computation.3 | async-start | bytes 1048576
  26.6 5.0 %copy-start.10 = (f32[640,384]{1,0:T(8,128)}, f32[640,384]{1,0:T(8,128)S(1)}, u32[]{:S(2)}) copy-start(f32[640,384]{1,0:T(8,128)S(1)} %get-tuple-element.103.refs_6_) | copy-start | bytes 2949124
  26.6 7.3 %copy-start.14 = (bf16[320,384]{1,0:T(8,128)(2,1)}, bf16[320,384]{1,0:T(8,128)(2,1)S(1)}, u32[]{:S(2)}) copy-start(bf16[320,384]{1,0:T(8,128)(2,1)S(1)} %get-tuple-element.85.refs_1_.refs_2_) | copy-start | bytes 737284
  26.6 7.3 %slice-start = ((s8[4718592]{0:T(1024)(128)(4,1)}), s8[4194304]{0:T(1024)(128)(4,1)S(1)}, s32[]{:S(2)}) async-start(s8[4718592]{0:T(1024)(128)(4,1)} %bitcast.25), calls=%async_computation | async-start | bytes 8388608
  26.7 7.2 %slice-start.1 = ((s8[4718592]{0:T(1024)(128)(4,1)}), s8[524288]{0:T(1024)(128)(4,1)S(1)}, s32[]{:S(2)}) async-start(s8[4718592]{0:T(1024)(128)(4,1)} %bitcast.25), calls=%async_computation.1 | async-start | bytes 1048576
  26.7 7.2 %copy-start.3 = (bf16[768,768]{1,0:T(8,128)(2,1)S(1)}, bf16[768,768]{1,0:T(8,128)(2,1)}, u32[]{:S(2)}) copy-start(bf16[768,768]{1,0:T(8,128)(2,1)} %refs_8_.1) | copy-start | bytes 3538948
  26.7 7.2 %copy-start.6 = (f32[3072]{0:T(1024)S(1)}, f32[3072]{0:T(1024)}, u32[]{:S(2)}) copy-start(f32[3072]{0:T(1024)} %param.35) | copy-start | bytes 36868
  26.7 7.2 %collective-permute-start.1 = (bf16[320,384]{1,0:T(8,128)(2,1)S(1)}, bf16[320,384]{1,0:T(8,128)(2,1)S(1)}, u32[]{:S(2)}, u32[]{:S(2)}) collective-permute-start(bf16[320,384]{1,0:T(8,128)(2,1)S(1)} %get-tuple-element.86.refs_3_), channel_id=1, source_target_pairs={{0,1},{1,0},{2,3},{3,2},{4,5},{5,4},{6,7},{7,6},{8,9},{9,8},{10,11... | collective-permute-start | bytes 737288 | tf_op jit(solution)/shard_map/ppermute | solution.py:433
  39.9 4.6 %copy-start.12 = (bf16[320,3072]{1,0:T(8,128)(2,1)}, bf16[320,3072]{1,0:T(8,128)(2,1)S(1)}, u32[]{:S(2)}) copy-start(bf16[320,3072]{1,0:T(8,128)(2,1)S(1)} %get-tuple-element.88.refs_0_) | copy-start | bytes 5898244
  39.9 4.6 %copy-start.8 = (f32[320,768]{1,0:T(8,128)}, f32[320,768]{1,0:T(8,128)S(1)}, u32[]{:S(2)}) copy-start(f32[320,768]{1,0:T(8,128)S(1)} %get-tuple-element.89.refs_4_.refs_2_) | copy-start | bytes 2949124
  44.5 6.8 %collective-permute-start.2 = (bf16[4,2,2,192,384]{4,3,2,1,0:T(8,128)(2,1)S(1)}, bf16[4,2,2,192,384]{4,3,2,1,0:T(8,128)(2,1)S(1)}, u32[]{:S(2)}, u32[]{:S(2)}) collective-permute-start(bf16[4,2,2,192,384]{4,3,2,1,0:T(8,128)(2,1)S(1)} %get-tuple-element.92.refs_9_), channel_id=1, source_target_pairs={{0,2},{1,3},{2,0},{3,1},{4,6},{5,7},{6,4},{7,5},{8,10},{9,11},{10,... | collective-permute-start | bytes 7077896 | tf_op jit(solution)/shard_map/ppermute | solution.py:433
  49.8 9.8 %collective-permute-start.5 = (bf16[320,384]{1,0:T(8,128)(2,1)S(1)}, bf16[320,384]{1,0:T(8,128)(2,1)S(1)}, u32[]{:S(2)}, u32[]{:S(2)}) collective-permute-start(bf16[320,384]{1,0:T(8,128)(2,1)S(1)} %get-tuple-element.95.refs_2_), channel_id=1, source_target_pairs={{0,1},{1,0},{2,3},{3,2},{4,5},{5,4},{6,7},{7,6},{8,9},{9,8},{10,11... | collective-permute-start | bytes 737288 | tf_op jit(solution)/shard_map/ppermute | solution.py:433
  52.3 32.3 %collective-permute-start.3 = (bf16[8,192,384]{2,1,0:T(8,128)(2,1)S(1)}, bf16[8,192,384]{2,1,0:T(8,128)(2,1)S(1)}, u32[]{:S(2)}, u32[]{:S(2)}) collective-permute-start(bf16[8,192,384]{2,1,0:T(8,128)(2,1)S(1)} %bitcast.22), channel_id=1, source_target_pairs={{0,4},{1,5},{2,6},{3,7},{4,0},{5,1},{6,2},{7,3},{8,12},{9,13},{10,... | collective-permute-start | bytes 3538952 | tf_op jit(solution)/shard_map/ppermute | solution.py:433
  53.9 5.8 %copy-start.11 = (f32[640,384]{1,0:T(8,128)S(1)}, f32[640,384]{1,0:T(8,128)}, u32[]{:S(2)}) copy-start(f32[640,384]{1,0:T(8,128)} %copy-done.10) | copy-start | bytes 2949124
  53.9 5.8 %copy-start.15 = (bf16[320,384]{1,0:T(8,128)(2,1)S(1)}, bf16[320,384]{1,0:T(8,128)(2,1)}, u32[]{:S(2)}) copy-start(bf16[320,384]{1,0:T(8,128)(2,1)} %copy-done.14) | copy-start | bytes 737284
  59.5 5.4 %collective-permute-start.4 = (bf16[16,48,1920]{2,1,0:T(8,128)(2,1)S(1)}, bf16[16,48,1920]{2,1,0:T(8,128)(2,1)S(1)}, u32[]{:S(2)}, u32[]{:S(2)}) collective-permute-start(bf16[16,48,1920]{2,1,0:T(8,128)(2,1)S(1)} %get-tuple-element.100.refs_8_), channel_id=1, source_target_pairs={{0,2},{1,3},{2,0},{3,1},{4,6},{5,7},{6,4},{7,5},{8,10},{9,11},{10,... | collective-permute-start | bytes 8847368 | tf_op jit(solution)/shard_map/ppermute | solution.py:433
  65.7 21.0 %collective-permute-start.6 = (bf16[8,48,384]{2,1,0:T(8,128)(2,1)S(1)}, bf16[8,48,384]{2,1,0:T(8,128)(2,1)S(1)}, u32[]{:S(2)}, u32[]{:S(2)}) collective-permute-start(bf16[8,48,384]{2,1,0:T(8,128)(2,1)S(1)} %shard_map.342.refs_2_), channel_id=1, source_target_pairs={{0,4},{1,5},{2,6},{3,7},{4,0},{5,1},{6,2},{7,3},{8,12},{9,13},{10,... | collective-permute-start | bytes 884744 | tf_op jit(solution)/shard_map/ppermute | solution.py:433
  67.4 30.2 %collective-permute-start.8 = (bf16[8,48,1536]{2,1,0:T(8,128)(2,1)S(1)}, bf16[8,48,1536]{2,1,0:T(8,128)(2,1)S(1)}, u32[]{:S(2)}, u32[]{:S(2)}) collective-permute-start(bf16[8,48,1536]{2,1,0:T(8,128)(2,1)S(1)} %shard_map.343.refs_9_), channel_id=1, source_target_pairs={{0,8},{1,9},{2,10},{3,11},{4,12},{5,13},{6,14},{7,15},{8,0},{9,1},... | collective-permute-start | bytes 3538952 | tf_op jit(solution)/shard_map/ppermute | solution.py:433
  84.5 4.7 %copy-start.9 = (f32[320,768]{1,0:T(8,128)S(1)}, f32[320,768]{1,0:T(8,128)}, u32[]{:S(2)}) copy-start(f32[320,768]{1,0:T(8,128)} %copy-done.8) | copy-start | bytes 2949124
  84.5 4.7 %copy-start.13 = (bf16[320,3072]{1,0:T(8,128)(2,1)S(1)}, bf16[320,3072]{1,0:T(8,128)(2,1)}, u32[]{:S(2)}) copy-start(bf16[320,3072]{1,0:T(8,128)(2,1)} %copy-done.12) | copy-start | bytes 5898244
  84.5 10.8 %collective-permute-start.9 = (bf16[8,48,1152]{2,1,0:T(8,128)(2,1)S(1)}, bf16[8,48,1152]{2,1,0:T(8,128)(2,1)S(1)}, u32[]{:S(2)}, u32[]{:S(2)}) collective-permute-start(bf16[8,48,1152]{2,1,0:T(8,128)(2,1)S(1)} %get-tuple-element.109.refs_12_), channel_id=1, source_target_pairs={{0,2},{1,3},{2,0},{3,1},{4,6},{5,7},{6,4},{7,5},{8,10},{9,11},{10,... | collective-permute-start | bytes 2654216 | tf_op jit(solution)/shard_map/ppermute | solution.py:433
  88.6 17.8 %collective-permute-start.7 = (bf16[4,240,384]{2,1,0:T(8,128)(2,1)S(1)}, bf16[4,240,384]{2,1,0:T(8,128)(2,1)S(1)}, u32[]{:S(2)}, u32[]{:S(2)}) collective-permute-start(bf16[4,240,384]{2,1,0:T(8,128)(2,1)S(1)} %get-tuple-element.110.refs_5_), channel_id=1, source_target_pairs={{0,1},{1,0},{2,3},{3,2},{4,5},{5,4},{6,7},{7,6},{8,9},{9,8},{10,11... | collective-permute-start | bytes 2211848 | tf_op jit(solution)/shard_map/ppermute | solution.py:433
  94.0 1.3 collective-permute-start.10
  96.1 14.7 %collective-permute-start.12 = (bf16[224,1152]{1,0:T(8,128)(2,1)S(1)}, bf16[224,1152]{1,0:T(8,128)(2,1)S(1)}, u32[]{:S(2)}, u32[]{:S(2)}) collective-permute-start(bf16[224,1152]{1,0:T(8,128)(2,1)S(1)} %get-tuple-element.122.refs_3_), channel_id=1, source_target_pairs={{0,4},{1,5},{2,6},{3,7},{4,0},{5,1},{6,2},{7,3},{8,12},{9,13},{10,... | collective-permute-start | bytes 1548296 | tf_op jit(solution)/shard_map/ppermute | solution.py:433
  107.0 9.0 %collective-permute-start.15 = (bf16[2,240,384]{2,1,0:T(8,128)(2,1)S(1)}, bf16[2,240,384]{2,1,0:T(8,128)(2,1)S(1)}, u32[]{:S(2)}, u32[]{:S(2)}) collective-permute-start(bf16[2,240,384]{2,1,0:T(8,128)(2,1)S(1)} %shard_map.353.refs_1_), channel_id=1, source_target_pairs={{0,8},{1,9},{2,10},{3,11},{4,12},{5,13},{6,14},{7,15},{8,0},{9,1},... | collective-permute-start | bytes 1105928 | tf_op jit(solution)/shard_map/ppermute | solution.py:433
  108.7 16.6 %collective-permute-start.14 = (bf16[4,48,1536]{2,1,0:T(8,128)(2,1)S(1)}, bf16[4,48,1536]{2,1,0:T(8,128)(2,1)S(1)}, u32[]{:S(2)}, u32[]{:S(2)}) collective-permute-start(bf16[4,48,1536]{2,1,0:T(8,128)(2,1)S(1)} %shard_map.352.refs_2_), channel_id=1, source_target_pairs={{0,4},{1,5},{2,6},{3,7},{4,0},{5,1},{6,2},{7,3},{8,12},{9,13},{10,... | collective-permute-start | bytes 1769480 | tf_op jit(solution)/shard_map/ppermute | solution.py:433
  116.7 8.5 %collective-permute-start.21 = (bf16[1,240,384]{2,1,0:T(8,128)(2,1)S(1)}, bf16[1,240,384]{2,1,0:T(8,128)(2,1)S(1)}, u32[]{:S(2)}, u32[]{:S(2)}) collective-permute-start(bf16[1,240,384]{2,1,0:T(8,128)(2,1)S(1)} %shard_map.356.refs_4_), channel_id=1, source_target_pairs={{0,16},{1,17},{2,18},{3,19},{4,20},{5,21},{6,22},{7,23},{8,24},{9,... | collective-permute-start | bytes 552968 | tf_op jit(solution)/shard_map/ppermute | solution.py:433
  119.3 14.4 %collective-permute-start.11 = (bf16[320,768]{1,0:T(8,128)(2,1)S(1)}, bf16[320,768]{1,0:T(8,128)(2,1)S(1)}, u32[]{:S(2)}, u32[]{:S(2)}) collective-permute-start(bf16[320,768]{1,0:T(8,128)(2,1)S(1)} %shard_map.354.refs_2_), channel_id=1, source_target_pairs={{0,1},{1,0},{2,3},{3,2},{4,5},{5,4},{6,7},{7,6},{8,9},{9,8},{10,11... | collective-permute-start | bytes 1474568 | tf_op jit(solution)/shard_map/ppermute | solution.py:433
  119.8 8.7 %collective-permute-start.13 = (bf16[128,1152]{1,0:T(8,128)(2,1)S(1)}, bf16[128,1152]{1,0:T(8,128)(2,1)S(1)}, u32[]{:S(2)}, u32[]{:S(2)}) collective-permute-start(bf16[128,1152]{1,0:T(8,128)(2,1)S(1)} %get-tuple-element.126.refs_3_), channel_id=1, source_target_pairs={{0,8},{1,9},{2,10},{3,11},{4,12},{5,13},{6,14},{7,15},{8,0},{9,1},... | collective-permute-start | bytes 884744 | tf_op jit(solution)/shard_map/ppermute | solution.py:433
  126.0 10.5 %collective-permute-start.19 = (bf16[2,48,1536]{2,1,0:T(8,128)(2,1)S(1)}, bf16[2,48,1536]{2,1,0:T(8,128)(2,1)S(1)}, u32[]{:S(2)}, u32[]{:S(2)}) collective-permute-start(bf16[2,48,1536]{2,1,0:T(8,128)(2,1)S(1)} %shard_map.357.refs_2_), channel_id=1, source_target_pairs={{0,1},{1,0},{2,3},{3,2},{4,5},{5,4},{6,7},{7,6},{8,9},{9,8},{10,11... | collective-permute-start | bytes 884744 | tf_op jit(solution)/shard_map/ppermute | solution.py:433
  129.2 13.1 %collective-permute-start.16 = (bf16[80,1024]{1,0:T(8,128)(2,1)S(1)}, bf16[80,1024]{1,0:T(8,128)(2,1)S(1)}, u32[]{:S(2)}, u32[]{:S(2)}) collective-permute-start(bf16[80,1024]{1,0:T(8,128)(2,1)S(1)} %get-tuple-element.127.refs_5_), channel_id=1, source_target_pairs={{0,16},{1,17},{2,18},{3,19},{4,20},{5,21},{6,22},{7,23},{8,24},{9,... | collective-permute-start | bytes 491528 | tf_op jit(solution)/shard_map/ppermute | solution.py:433
  130.6 8.3 %collective-permute-start.17 = (bf16[48,384]{1,0:T(8,128)(2,1)S(1)}, bf16[48,384]{1,0:T(8,128)(2,1)S(1)}, u32[]{:S(2)}, u32[]{:S(2)}) collective-permute-start(bf16[48,384]{1,0:T(8,128)(2,1)S(1)} %get-tuple-element.129), channel_id=1, source_target_pairs={{0,1},{1,0},{2,3},{3,2},{4,5},{5,4},{6,7},{7,6},{8,9},{9,8},{10,11... | collective-permute-start | bytes 110600 | tf_op jit(solution)/shard_map/ppermute | solution.py:433
  132.0 10.4 %collective-permute-start.18 = (bf16[48,384]{1,0:T(8,128)(2,1)S(1)}, bf16[48,384]{1,0:T(8,128)(2,1)S(1)}, u32[]{:S(2)}, u32[]{:S(2)}) collective-permute-start(bf16[48,384]{1,0:T(8,128)(2,1)S(1)} %get-tuple-element.130), channel_id=1, source_target_pairs={{0,17},{1,16},{2,19},{3,18},{4,21},{5,20},{6,23},{7,22},{8,25},{9,... | collective-permute-start | bytes 110600 | tf_op jit(solution)/shard_map/ppermute | solution.py:433
  138.1 12.2 %collective-permute-start.22 = (bf16[1,48,1536]{2,1,0:T(8,128)(2,1)S(1)}, bf16[1,48,1536]{2,1,0:T(8,128)(2,1)S(1)}, u32[]{:S(2)}, u32[]{:S(2)}) collective-permute-start(bf16[1,48,1536]{2,1,0:T(8,128)(2,1)S(1)} %shard_map.360.refs_5_), channel_id=1, source_target_pairs={{0,16},{1,17},{2,18},{3,19},{4,20},{5,21},{6,22},{7,23},{8,24},{9,... | collective-permute-start | bytes 442376 | tf_op jit(solution)/shard_map/ppermute | solution.py:433
  143.6 4.3 %collective-permute-start.20 = (bf16[32,1024]{1,0:T(8,128)(2,1)S(1)}, bf16[32,1024]{1,0:T(8,128)(2,1)S(1)}, u32[]{:S(2)}, u32[]{:S(2)}) collective-permute-start(bf16[32,1024]{1,0:T(8,128)(2,1)S(1)} %get-tuple-element.132.refs_0_), channel_id=1, source_target_pairs={{0,1},{1,0},{2,3},{3,2},{4,5},{5,4},{6,7},{7,6},{8,9},{9,8},{10,11... | collective-permute-start | bytes 196616 | tf_op jit(solution)/shard_map/ppermute | solution.py:433
  (9 other events, 17.1 us)

commit v6 on v5

--- a/solution.py
+++ b/solution.py
@@ -602,13 +602,16 @@
     line_out[height:, :] = note
 
 
-def qs_join_kernel(place, keep, line, side, cross, note, out, note_out):
+def note_kernel(place, note, line, note_out):
+    note_out[...] = note_sum(note[...], line[line.shape[0] - NOTE[0] :, :])
+
+
+def qs_join_kernel(place, keep, line, side, cross, out):
     height, share = side.shape
     both = keep[...] + line[:height, : 2 * share].astype(F32)
     out[:, :share] = both[:, :share]
     out[:, share : 2 * share] = side[...].astype(F32) + cross[...].astype(F32)
     out[:, 2 * share :] = both[:, share:]
-    note_out[...] = note_sum(note[...], line[height:, :])
 
 
 def shape(dims, dtype):
@@ -955,51 +958,46 @@
 
 
 def hidden1_grad_kernel(
-    place, dqkv0, dqkv1, dqkv2, weight, own, other, keep_out, send_out, small_out, total, joined
+    place, first, others, weight, hidden, vecs, keep_out, send_out, small_out, total, joined
 ):
     step = pl.program_id(0)
-    rows = own.shape[0]
+    rows = keep_out.shape[0]
     here = pl.ds(pl.multiple_of(place[0] * rows, 64), rows)
     there = pl.ds(pl.multiple_of((1 - place[0]) * rows, 64), rows)
+    joined[:, :LANES] = first[0]
+    joined[:, LANES:] = others[0]
+    grads = joined[...]
+    part = mul(grads, weight[...], NT)
+    line = jnp.sum(grads.astype(F32), axis=0, keepdims=True)
 
     @pl.when(step == 0)
     def _():
-        total[...] = jnp.zeros_like(total)
+        total[...] = part
         small_out[...] = jnp.zeros_like(small_out)
-
-    for n, part in enumerate((dqkv0, dqkv1, dqkv2)):
-        joined[:, LANES * n : LANES * (n + 1)] = part[0]
-    grads = joined[...]
-    total[...] += mul(grads, weight[...], NT)
-    line = jnp.sum(grads.astype(F32), axis=0, keepdims=True)
-
-    @pl.when(step == 0)
+        small_out[2:3, :384] = line
+
+    @pl.when(step > 0)
     def _():
-        small_out[2:3, :384] = line
+        total[...] += part
 
     @pl.when(step == 2)
     def _():
         small_out[2:3, 384:] = line
-        mine = total[here, :]
-        theirs = total[there, :]
-        keep_out[...] = mine
-        send_out[...] = theirs.astype(BF)
-        normed_mine, _ = layer_norm(own[...].astype(F32))
-        normed_theirs, _ = layer_norm(other[...].astype(F32))
-        small_out[0:1, :] = jnp.sum(mine * normed_mine, axis=0, keepdims=True) + jnp.sum(
-            theirs * normed_theirs, axis=0, keepdims=True
-        )
-        small_out[1:2, :] = jnp.sum(mine, axis=0, keepdims=True) + jnp.sum(
-            theirs, axis=0, keepdims=True
-        )
+        keep_out[...] = total[here, :]
+        send_out[...] = total[there, :].astype(BF)
+        both = total[...]
+        plain = jnp.sum(both, axis=0, keepdims=True)
+        scaled = jnp.sum(both * hidden[...].astype(F32), axis=0, keepdims=True)
+        small_out[0:1, :] = (scaled - vecs[1:2, :] * plain) / vecs[0:1, :]
+        small_out[1:2, :] = plain
 
 
 def qkv_grad_kernel(
-    place, hidden, dqkv0, dqkv1, dqkv2, keep_out, send_out, held, joined, *, rest
+    place, hidden, first, others, keep_out, send_out, held, joined, *, rest
 ):
     core = place[1]
-    for n, part in enumerate((dqkv0, dqkv1, dqkv2)):
-        joined[:, LANES * n : LANES * (n + 1)] = part[0]
+    joined[:, :LANES] = first[0]
+    joined[:, LANES:] = others[0]
     held[...] = mul(hidden[...], joined[...], TN)
     for pair in range(8):
         at = rest(pair % 2, pair // 2, 0) ^ place[4]
@@ -1082,15 +1080,16 @@
             strips_out[head, par : par + 1, :] = sides[par, head : head + 1, :]
 
 
-def pack_kernel(place, strip0, strip1, strip2, ffn, fc1_bias, last, result, packed_out, packed):
+def pack_kernel(place, first, others, ffn, fc1_bias, last, result, packed_out, packed):
     packed[...] = jnp.zeros_like(packed)
     for n in range(5):
         lanes = slice(256 * n, 256 * n + 256)
-        for pair, strip in enumerate((strip0, strip1, strip2)):
+        for pair in range(3):
+            strip, at = (first, 0) if pair == 0 else (others, pair - 1)
             for head in range(2):
                 for par in range(2):
                     row = 16 * n + 6 * par + 2 * pair + head
-                    packed[row : row + 1, :] = strip[0, head, par : par + 1, lanes]
+                    packed[row : row + 1, :] = strip[at, head, par : par + 1, lanes]
     for n in range(3):
         lanes = slice(256 * n, 256 * n + 256)
         row = 80 + 16 * n
@@ -1134,8 +1133,9 @@
         part = moved_window(sides.at[b % 2], 24 * b, target)
         flat[:, base : base + 2 * LANES] += part
     lane = lax.broadcasted_iota(jnp.int32, (16, LANES), 1)
+    turn = flips().astype(BF)
     blocks = [
-        exact(flat[:, LANES * (17 - n) : LANES * (18 - n)], flips(), NN) for n in range(18)
+        mul(flat[:, LANES * (17 - n) : LANES * (18 - n)].astype(BF), turn) for n in range(18)
     ]
     blocks[0] = jnp.where(lane < 3, sides[0, :, 1152:1280], blocks[0])
     turned = pltpu.roll(jnp.concatenate(blocks, axis=1), CELLS, axis=1)
@@ -1325,42 +1325,47 @@
     )
     terms_b = [keep_b, swapped(send_b, "core")]
 
-    def attend_back(pair, after):
-        pair_expo = spec((2, slots, slots), lambda n, p: (pair, 0, 0))
-        pair_rows = spec((slots, LANES), lambda n, p: (0, pair))
-        pair_half = spec((rows, LANES), lambda n, p: (0, pair))
+    def attend_back(pair, count, after):
+        half_rows = spec((rows, LANES), lambda n, p: (0, pair + n))
         return run(
-            attend_back_kernel, place, (1,),
+            attend_back_kernel, place, (count,),
             [
-                spec((3, slots, LANES), lambda n, p: (0, 0, pair)), pair_expo, pair_half, pair_half,
-                pair_half, pair_half, pair_rows, full((STRIP, STRIP_WIDTH)),
+                spec((3, slots, LANES), lambda n, p: (0, 0, pair + n)),
+                spec((2, slots, slots), lambda n, p: (pair + n, 0, 0)),
+                half_rows, half_rows, half_rows, half_rows,
+                spec((slots, LANES), lambda n, p: (0, pair + n)), full((STRIP, STRIP_WIDTH)),
             ],
-            [full((3, slots, LANES)), full((1, 2, 2, STRIP_WIDTH))],
-            [shape((3, slots, LANES), BF), shape((1, 2, 2, STRIP_WIDTH), F32)],
+            [
+                spec((3, slots, LANES), lambda n, p: (0, 0, n)),
+                spec((1, 2, 2, STRIP_WIDTH), lambda n, p: (n, 0, 0, 0)),
+            ],
+            [shape((3, slots, count * LANES), BF), shape((count, 2, 2, STRIP_WIDTH), F32)],
             [
                 pltpu.VMEM((slots, LANES), F32), pltpu.VMEM((slots, LANES), F32),
                 pltpu.VMEM((2, slots, slots), BF), pltpu.VMEM((2, STRIP, STRIP_WIDTH), F32),
                 pltpu.VMEM((slots, LANES), F32),
             ],
-            (qkv, expo, attn_own, attn_send, grad_own, grad_other, inv, even_mask),
-            32 * slots * slots * 64 * 2, after=after, us=40.0 if pair == 0 else None,
+            (qkv, expo, attn_own, attn_send, grad_own, grad_other, inv, even_mask), 0, after=after,
+            us=40.0 if pair == 0 else 8.0,
         )
 
-    dqkv0, strip0 = attend_back(0, (send_b,))
+    dqkv0, strip0 = attend_back(0, 1, (send_b,))
     out_p1 = half_out(place, terms_b, (dqkv0,), column=4, columns=share)
     terms_p = [*terms_b, swapped(out_p1, ORDER_A[1])]
     out_b1 = half_out(place, terms_b, (out_p1,), columns=4 * share)
     terms_b = [*terms_b, swapped(out_b1, ORDER_B[1])]
-    dqkv1, strip1 = attend_back(1, (dqkv0, out_b1))
-    dqkv2, strip2 = attend_back(2, (dqkv1,))
-    dqkv = (dqkv0, dqkv1, dqkv2)
-    third = [spec((1, slots, LANES), lambda t, p: (t, 0, 0))] * 3
+    dqkv1, strip1 = attend_back(1, pairs - 1, (dqkv0, out_b1))
+    dqkv = (dqkv0, dqkv1)
+    third = [
+        spec((1, slots, LANES), lambda t, p: (t, 0, 0)),
+        spec((1, slots, share - LANES), lambda t, p: (t, 0, 0)),
+    ]
     dh_keep, dh_send, small_last = run(
         hidden1_grad_kernel, place, (3,),
-        [*third, spec((width, share), lambda t, p: (0, 2 * t + p[0])), whole, whole],
+        [*third, spec((width, share), lambda t, p: (0, 2 * t + p[0])), full((slots, width)), full((8, width))],
         [whole, whole, full((8, width))],
         [shape((rows, width), F32), shape((rows, width), BF), shape((8, width), F32)],
-        [pltpu.VMEM((slots, width), F32), pltpu.VMEM((slots, share), BF)], (*dqkv, qkv_weight, own, other),
+        [pltpu.VMEM((slots, width), F32), pltpu.VMEM((slots, share), BF)], (*dqkv, qkv_weight, hidden1, vecs),
         2 * slots * width * 3 * share,
     )
     block = (8, 48, 3 * share)
@@ -1384,9 +1389,9 @@
     )
     packed = run(
         pack_kernel, place, (1,),
-        [*[full((1, 2, 2, STRIP_WIDTH))] * 3, full((8, width)), full((1, hidden)), full((8, width)), full((8, width))],
+        [full((1, 2, 2, STRIP_WIDTH)), full((2, 2, 2, STRIP_WIDTH)), full((8, width)), full((1, hidden)), full((8, width)), full((8, width))],
         [full(NOTE)], [shape(NOTE, BF)], [pltpu.VMEM((128, 256), F32)],
-        (strip0, strip1, strip2, small_ffn, fc1_bias_part, small_last, small_result), 0,
+        (strip0, strip1, small_ffn, fc1_bias_part, small_last, small_result), 0,
     )[0]
     mate = swapped(packed, "core")
     def wide(blocks, columns):
@@ -1436,13 +1441,17 @@
     )[0]
     out_b4 = half_out(place, terms_b, (tokens_grad,), columns=4 * share)
     terms_b = [*terms_b, swapped(out_b4, "z2")]
-    qkv_grad, packed = run(
+    packed = run(
+        note_kernel, place, (1,), [full(NOTE), full(wide(1, NOTE[1]))], [full(NOTE)],
+        [shape(NOTE, BF)], [], (note, q_sends[0]), 0, after=(out_b4,),
+    )[0]
+    mate = swapped(packed, "y")
+    qkv_grad = run(
         qs_join_kernel, place, (1,),
-        [full((48, 2 * share)), full(wide(1, NOTE[1])), full((48, share)), full((48, share)), full(NOTE)],
-        [full((48, 3 * share)), full(NOTE)], [shape((48, 3 * share), F32), shape(NOTE, BF)], [],
-        (q_keep, *q_sends, note), 0, after=(out_b4,),
-    )
-    mate = swapped(packed, "y")
+        [full((48, 2 * share)), full(wide(1, NOTE[1])), full((48, share)), full((48, share))],
+        [full((48, 3 * share))], [shape((48, 3 * share), F32)], [], (q_keep, *q_sends), 0,
+        after=(packed,),
+    )[0]
     fc2_proj = added(terms_a)
     fc1_grad = added([term[:, :, : 4 * share] for term in terms_b])
     fc2_grad = fc2_proj[:192]

time: 151 us -> 148 us (0.980)
  waiting for transfers between devices: 35.3 us -> 26.9 us
  starting transfers between devices: 26.5 us -> 29.7 us
  local copies, waits for them, and re-layouts: 6.28 us -> 8.65 us
    ppermute x23, waiting for transfers between devices: 35.3 us -> 26.9 us  [swapped(): return lax.ppermute(value, ('img', 'seq'), swap_pairs(*names))]
    ppermute x23, starting transfers between devices: 26.5 us -> 29.7 us  [swapped(): return lax.ppermute(value, ('img', 'seq'), swap_pairs(*names))]
    unnamed x68 -> x60, local copies, waits for them, and re-layouts: 4.73 us -> 7.1 us
  transfers between devices with their start and end apart: 23 -> 23, of which waited for: 12 -> 10; matrix products, arithmetic and copies ran while one was open for 1% -> 1% of each run, Pallas kernels for 39% -> 39%
where the time goes in v6:
time: 148 us
  Pallas kernels  79.8 us (54%)
  starting transfers between devices  29.7 us (20%)
  waiting for transfers between devices  26.9 us (18%)
  local copies, waits for them, and re-layouts  8.65 us (6%)
    pallas_call x32, Pallas kernels, run(): pl.pallas_call(kernel, grid_spec=pltpu.PrefetchScalarGridSpec(num_scalar_...  79.8 us
    ppermute x23, starting transfers between devices, swapped(): return lax.ppermute(value, ('img', 'seq'), swap_pairs(*names))  29.7 us
    ppermute x23, waiting for transfers between devices, swapped(): return lax.ppermute(value, ('img', 'seq'), swap_pairs(*names))  26.9 us
    unnamed x60, local copies, waits for them, and re-layouts  7.1 us
  transfers between devices with their start and end apart: 23, of which 10 were waited for; matrix products, arithmetic and copies ran while one was open for 1% of the time, Pallas kernels for 39%

profile of v6, /device:TPU:0, one launch (start us, length us, event | category | flops | bytes accessed | tf_op | source)
XLA Modules:
  0.0 147.5 jit_solution(5803843851386004910)
XLA Ops:
  0.7 3.0 %collective-permute-start = (bf16[320,768]{1,0:T(8,128)(2,1)}, bf16[320,768]{1,0:T(8,128)(2,1)S(1)}, u32[]{:S(2)}, u32[]{:S(2)}) collective-permute-start(bf16[320,768]{1,0:T(8,128)(2,1)} %bitcast.29), channel_id=1, source_target_pairs={{0,1},{1,0},{2,3},{3,2},{4,5},{5,4},{6,7},{7,6},{8,9},{9,8},{10,11... | collective-permute-start | bytes 1474568 | tf_op jit(solution)/shard_map/ppermute | solution.py:433
  3.8 0.9 copy-done.5
  4.8 1.7 %shard_map.333.refs_1_ = f32[12,2,1280]{2,1,0:T(2,128)S(1)} custom-call(s32[7]{0:T(128)S(1)} %stack.58.place_ref, f32[12,2212]{1,0:T(8,128)S(1)} %bitcast.33), custom_call_target="tpu_custom_call" | custom-call | flops 1955000064 | bytes 1 | tf_op jit(solution)/shard_map/pallas_call | solution.py:492
  7.5 2.0 %copy-done.1 = bf16[768,2304]{1,0:T(8,128)(2,1)S(1)} copy-done((bf16[768,2304]{1,0:T(8,128)(2,1)S(1)}, bf16[768,2304]{1,0:T(8,128)(2,1)}, u32[]{:S(2)}) %copy-start.1) | copy-done | bytes 3538968
  9.5 2.5 %shard_map.331 = (bf16[3,640,384]{2,1,0:T(8,128)(2,1)S(1)}, bf16[640,768]{1,0:T(8,128)(2,1)S(1)}) custom-call(s32[7]{0:T(128)S(1)} %stack.58.place_ref, bf16[320,768]{1,0:T(8,128)(2,1)S(1)} %bitcast.30, f32[8,768]{1,0:T(8,128)S(1)} %stack.67.refs_1_.refs_3_.refs_6_.refs_4_, bf16[768,2304]{1,0:T(8,128)(2,1)S(1)} %copy-done.1, f32[1,768]{1,0:T(1,128)S(1)} %reshape.86.refs_3_, ...), custom_call_target="tpu_custom_call" | custom-call | flops 2184999936 | bytes 1 | tf_op jit(solution)/shard_map/pallas_call | solution.py:492
  12.1 3.0 %collective-permute-done.refs_0_ = bf16[320,768]{1,0:T(8,128)(2,1)S(1)} collective-permute-done((bf16[320,768]{1,0:T(8,128)(2,1)}, bf16[320,768]{1,0:T(8,128)(2,1)S(1)}, u32[]{:S(2)}, u32[]{:S(2)}) %collective-permute-start) | collective-permute-done | bytes 491552 | tf_op jit(solution)/shard_map/ppermute | solution.py:433
  15.1 2.5 %shard_map.332 = (bf16[3,640,384]{2,1,0:T(8,128)(2,1)S(1)}, bf16[640,768]{1,0:T(8,128)(2,1)S(1)}) custom-call(s32[7]{0:T(128)S(1)} %stack.58.place_ref, bf16[320,768]{1,0:T(8,128)(2,1)S(1)} %collective-permute-done.refs_0_, f32[8,768]{1,0:T(8,128)S(1)} %stack.67.refs_1_.refs_3_.refs_6_.refs_4_, ...), custom_call_target="tpu_custom_call", output_to_operand_aliasing={{0}: (6, {}), {1}: (7, {})} | custom-call | flops 2184999936 | bytes 1 | tf_op jit(solution)/shard_map/pallas_call | solution.py:492
  17.6 9.0 %shard_map.334 = (bf16[320,384]{1,0:T(8,128)(2,1)S(1)}, bf16[320,384]{1,0:T(8,128)(2,1)S(1)}, bf16[6,640,640]{2,1,0:T(8,128)(2,1)S(1)}, f32[640,384]{1,0:T(8,128)S(1)}) custom-call(s32[7]{0:T(128)S(1)} %stack.58.place_ref, bf16[3,640,384]{2,1,0:T(8,128)(2,1)S(1)} %get-tuple-element.80.refs_0_, f32[12,2,1280]{2,1,0:T(2,128)S(1)} %copy-done.11, ...), custom_call_target="tpu_custom_call" | custom-call | flops 10350000128 | bytes 1 | tf_op jit(solution)/shard_map/pallas_call | solution.py:492
  26.7 1.8 %collective-permute-start.1 = (bf16[320,384]{1,0:T(8,128)(2,1)S(1)}, bf16[320,384]{1,0:T(8,128)(2,1)S(1)}, u32[]{:S(2)}, u32[]{:S(2)}) collective-permute-start(bf16[320,384]{1,0:T(8,128)(2,1)S(1)} %get-tuple-element.82.refs_3_), channel_id=1, source_target_pairs={{0,1},{1,0},{2,3},{3,2},{4,5},{5,4},{6,7},{7,6},{8,9},{9,8},{10,11... | collective-permute-start | bytes 737288 | tf_op jit(solution)/shard_map/ppermute | solution.py:433
  28.5 3.1 %shard_map.335 = (bf16[320,768]{1,0:T(8,128)(2,1)S(1)}, bf16[320,3072]{1,0:T(8,128)(2,1)S(1)}) custom-call(s32[7]{0:T(128)S(1)} %stack.58.place_ref, bf16[320,768]{1,0:T(8,128)(2,1)S(1)} %fusion.refs_0_.refs_2_.refs_3_, f32[8,768]{1,0:T(8,128)S(1)} %stack.67.refs_1_.refs_3_.refs_6_.refs_4_, bf16[3072,768]{1,0:T(8,128)(2,1)S(1)} %bitcast.28, ...), custom_call_target="tpu_custom_call" | custom-call | flops 2875000064 | bytes 1 | tf_op jit(solution)/shard_map/pallas_call | solution.py:492
  31.6 2.3 %collective-permute-done.1.refs_2_ = bf16[320,384]{1,0:T(8,128)(2,1)S(1)} collective-permute-done((bf16[320,384]{1,0:T(8,128)(2,1)S(1)}, bf16[320,384]{1,0:T(8,128)(2,1)S(1)}, u32[]{:S(2)}, u32[]{:S(2)}) %collective-permute-start.1) | collective-permute-done | bytes 245792 | tf_op jit(solution)/shard_map/ppermute | solution.py:433
  33.9 5.9 %shard_map.336 = (bf16[320,3072]{1,0:T(8,128)(2,1)S(1)}, bf16[320,3072]{1,0:T(8,128)(2,1)S(1)}, f32[1,3072]{1,0:T(1,128)S(1)}, bf16[320,768]{1,0:T(8,128)(2,1)S(...) custom-call(s32[7]{0:T(128)S(1)} %stack.58.place_ref, ...), custom_call_target="tpu_custom_call" | custom-call | flops 6325000192 | bytes 1 | tf_op jit(solution)/shard_map/pallas_call | solution.py:492
  39.9 4.5 %shard_map.337 = (bf16[4,2,2,192,384]{4,3,2,1,0:T(8,128)(2,1)S(1)}, bf16[4,2,2,192,384]{4,3,2,1,0:T(8,128)(2,1)S(1)}) custom-call(s32[7]{0:T(128)S(1)} %stack.58.place_ref, bf16[320,3072]{1,0:T(8,128)(2,1)S(1)} %get-tuple-element.84.refs_0_, bf16[320,768]{1,0:T(8,128)(2,1)S(1)} %get-tuple-element.86.refs_1_.refs_3_), custom_call_target="tpu_custom_call" | custom-call | flops 5289999872 | bytes 1 | tf_op jit(solution)/shard_map/pallas_call | solution.py:492
  44.5 5.2 %shard_map.338 = (bf16[320,768]{1,0:T(8,128)(2,1)S(1)}, f32[320,768]{1,0:T(8,128)S(1)}, bf16[320,384]{1,0:T(8,128)(2,1)S(1)}, bf16[320,384]{1,0:T(8,128)(2,1)S(1)}, f32[8,768]{1,0:T(8,128)S(1)}) custom-call(s32[7]{0:T(128)S(1)} %stack.58.place_ref, bf16[320,3072]{1,0:T(8,128)(2,1)S(1)} %get-tuple-element.89.refs_0_.refs_1_, bf16[768,3072]{1,0:T(8,128)(2,1)S(1)} %bitcast.26, ...), custom_call_target="tpu_custom_call" | custom-call | flops 5175000064 | bytes 1 | tf_op jit(solution)/shard_map/pallas_call | solution.py:492
  49.7 1.5 %collective-permute-start.5 = (bf16[320,384]{1,0:T(8,128)(2,1)S(1)}, bf16[320,384]{1,0:T(8,128)(2,1)S(1)}, u32[]{:S(2)}, u32[]{:S(2)}) collective-permute-start(bf16[320,384]{1,0:T(8,128)(2,1)S(1)} %get-tuple-element.91.refs_2_), channel_id=1, source_target_pairs={{0,1},{1,0},{2,3},{3,2},{4,5},{5,4},{6,7},{7,6},{8,9},{9,8},{10,11... | collective-permute-start | bytes 737288 | tf_op jit(solution)/shard_map/ppermute | solution.py:433
  51.2 1.0 shard_map.339
  52.2 1.6 %collective-permute-start.3 = (bf16[8,192,384]{2,1,0:T(8,128)(2,1)S(1)}, bf16[8,192,384]{2,1,0:T(8,128)(2,1)S(1)}, u32[]{:S(2)}, u32[]{:S(2)}) collective-permute-start(bf16[8,192,384]{2,1,0:T(8,128)(2,1)S(1)} %bitcast.22), channel_id=1, source_target_pairs={{0,4},{1,5},{2,6},{3,7},{4,0},{5,1},{6,2},{7,3},{8,12},{9,13},{10,... | collective-permute-start | bytes 3538952 | tf_op jit(solution)/shard_map/ppermute | solution.py:433
  53.8 5.7 %shard_map.340 = (bf16[16,48,1920]{2,1,0:T(8,128)(2,1)S(1)}, bf16[16,48,1920]{2,1,0:T(8,128)(2,1)S(1)}) custom-call(s32[7]{0:T(128)S(1)} %stack.58.place_ref, bf16[320,768]{1,0:T(8,128)(2,1)S(1)} %get-tuple-element.92.refs_0_, bf16[320,3072]{1,0:T(8,128)(2,1)S(1)} %get-tuple-element.89.refs_0_.refs_1_, bf16[320,768]{1,0:T(8,128)(2,1)S(1)} %get-tuple-element.93.refs_2_, ...), custom_call_target="tpu_custom_call" | custom-call | flops 6325000192 | bytes 1 | tf_op jit(solution)/shard_map/pallas_call | solution.py:492
  59.6 2.4 %copy-done.9 = bf16[6,640,640]{2,1,0:T(8,128)(2,1)S(1)} copy-done((bf16[6,640,640]{2,1,0:T(8,128)(2,1)S(1)}, bf16[6,640,640]{2,1,0:T(8,128)(2,1)}, u32[]{:S(2)}) %copy-start.9) | copy-done | bytes 4915224
  61.9 3.9 %shard_map.341 = (bf16[3,640,128]{2,1,0:T(8,128)(2,1)S(1)}, f32[1,2,2,1280]{3,2,1,0:T(2,128)S(1)}) custom-call(s32[7]{0:T(128)S(1)} %stack.58.place_ref, bf16[3,640,384]{2,1,0:T(8,128)(2,1)S(1)} %get-tuple-element.80.refs_0_, bf16[6,640,640]{2,1,0:T(8,128)(2,1)S(1)} %copy-done.9, bf16[320,384]{1,0:T(8,128)(2,1)S(1)} %copy-done.13, ...), custom_call_target="tpu_custom_call" | custom-call | flops 46000001024 | bytes 1 | tf_op jit(solution)/shard_map/pallas_call | solution.py:492
  67.3 1.0 shard_map.343.refs_9_
  68.3 1.6 %collective-permute-start.8 = (bf16[8,48,1536]{2,1,0:T(8,128)(2,1)S(1)}, bf16[8,48,1536]{2,1,0:T(8,128)(2,1)S(1)}, u32[]{:S(2)}, u32[]{:S(2)}) collective-permute-start(bf16[8,48,1536]{2,1,0:T(8,128)(2,1)S(1)} %shard_map.343.refs_9_), channel_id=1, source_target_pairs={{0,8},{1,9},{2,10},{3,11},{4,12},{5,13},{6,14},{7,15},{8,0},{9,1},... | collective-permute-start | bytes 3538952 | tf_op jit(solution)/shard_map/ppermute | solution.py:433
  70.0 7.7 %shard_map.344 = (bf16[3,640,256]{2,1,0:T(8,128)(2,1)S(1)}, f32[2,2,2,1280]{3,2,1,0:T(2,128)S(1)}) custom-call(s32[7]{0:T(128)S(1)} %stack.58.place_ref, bf16[3,640,384]{2,1,0:T(8,128)(2,1)S(1)} %get-tuple-element.80.refs_0_, bf16[6,640,640]{2,1,0:T(8,128)(2,1)S(1)} %copy-done.9, bf16[320,384]{1,0:T(8,128)(2,1)S(1)} %copy-done.13, ...), custom_call_target="tpu_custom_call" | custom-call | flops 9200000000 | bytes 1 | tf_op jit(solution)/shard_map/pallas_call | solution.py:492
  77.6 4.0 %shard_map.345 = (f32[320,768]{1,0:T(8,128)S(1)}, bf16[320,768]{1,0:T(8,128)(2,1)S(1)}, f32[8,768]{1,0:T(8,128)S(1)}) custom-call(s32[7]{0:T(128)S(1)} %stack.58.place_ref, bf16[3,640,128]{2,1,0:T(8,128)(2,1)S(1)} %get-tuple-element.100.refs_2_.refs_8_.refs_0_.refs_1_, bf16[3,640,256]{2,1,0:T(8,128)(2,1)S(1)} %get-tuple-element.102.refs_1_.refs_2_, ...), custom_call_target="tpu_custom_call" | custom-call | flops 4830000128 | bytes 1 | tf_op jit(solution)/shard_map/pallas_call | solution.py:492
  81.7 3.3 %shard_map.346 = (bf16[8,48,1152]{2,1,0:T(8,128)(2,1)S(1)}, bf16[8,48,1152]{2,1,0:T(8,128)(2,1)S(1)}) custom-call(s32[7]{0:T(128)S(1)} %stack.58.place_ref, bf16[640,768]{1,0:T(8,128)(2,1)S(1)} %get-tuple-element.101.refs_3_.refs_0_, bf16[3,640,128]{2,1,0:T(8,128)(2,1)S(1)} %get-tuple-element.100.refs_2_.refs_8_.refs_0_.refs_1_, ...), custom_call_target="tpu_custom_call" | custom-call | flops 3680000000 | bytes 1 | tf_op jit(solution)/shard_map/pallas_call | solution.py:492
  85.1 1.6 %collective-permute-done.6.refs_5_.refs_11_ = bf16[8,48,384]{2,1,0:T(8,128)(2,1)S(1)} collective-permute-done((bf16[8,48,384]{2,1,0:T(8,128)(2,1)S(1)}, bf16[8,48,384]{2,1,0:T(8,128)(2,1)S(1)}, u32[]{:S(2)}, u32[]{:S(2)}) %collective-permute-start.6) | collective-permute-done | bytes 294944 | tf_op jit(solution)/shard_map/ppermute | solution.py:433
  86.7 1.8 %shard_map.347 = (bf16[4,240,384]{2,1,0:T(8,128)(2,1)S(1)}, bf16[4,240,384]{2,1,0:T(8,128)(2,1)S(1)}) custom-call(s32[7]{0:T(128)S(1)} %stack.58.place_ref, bf16[4,2,2,192,384]{4,3,2,1,0:T(8,128)(2,1)S(1)} %get-tuple-element.87.refs_0_.refs_6_, bf16[4,2,2,192,384]{4,3,2,1,0:T(8,128)(2,1)S(1)} %collective-permute-done.2.refs_1_.refs_7_, ...), custom_call_target="tpu_custom_call" | custom-call | flops 1150000000 | bytes 1 | tf_op jit(solution)/shard_map/pallas_call | solution.py:492
  89.2 4.1 %shard_map.348 = (bf16[320,768]{1,0:T(8,128)(2,1)}, f32[8,768]{1,0:T(8,128)S(1)}) custom-call(s32[7]{0:T(128)S(1)} %stack.58.place_ref, bf16[320,3072]{1,0:T(8,128)(2,1)S(1)} %get-tuple-element.84.refs_0_, bf16[3072,768]{1,0:T(8,128)(2,1)S(1)} %bitcast.28, f32[320,768]{1,0:T(8,128)S(1)} %get-tuple-element.85.refs_4_.refs_2_, ...), custom_call_target="tpu_custom_call" | custom-call | flops 46000001024 | bytes 1 | tf_op jit(solution)/shard_map/pallas_call | solution.py:492
  94.0 1.2 collective-permute-done.10.refs_3_
  96.0 1.5 collective-permute-start.12
  98.2 8.1 %collective-permute-done.7.refs_1_ = bf16[4,240,384]{2,1,0:T(8,128)(2,1)S(1)} collective-permute-done((bf16[4,240,384]{2,1,0:T(8,128)(2,1)S(1)}, bf16[4,240,384]{2,1,0:T(8,128)(2,1)S(1)}, u32[]{:S(2)}, u32[]{:S(2)}) %collective-permute-start.7) | collective-permute-done | bytes 737312 | tf_op jit(solution)/shard_map/ppermute | solution.py:433
  107.0 1.6 %collective-permute-start.15 = (bf16[2,240,384]{2,1,0:T(8,128)(2,1)S(1)}, bf16[2,240,384]{2,1,0:T(8,128)(2,1)S(1)}, u32[]{:S(2)}, u32[]{:S(2)}) collective-permute-start(bf16[2,240,384]{2,1,0:T(8,128)(2,1)S(1)} %shard_map.352.refs_1_), channel_id=1, source_target_pairs={{0,8},{1,9},{2,10},{3,11},{4,12},{5,13},{6,14},{7,15},{8,0},{9,1},... | collective-permute-start | bytes 1105928 | tf_op jit(solution)/shard_map/ppermute | solution.py:433
  108.6 1.5 %collective-permute-start.14 = (bf16[4,48,1536]{2,1,0:T(8,128)(2,1)S(1)}, bf16[4,48,1536]{2,1,0:T(8,128)(2,1)S(1)}, u32[]{:S(2)}, u32[]{:S(2)}) collective-permute-start(bf16[4,48,1536]{2,1,0:T(8,128)(2,1)S(1)} %shard_map.351.refs_2_), channel_id=1, source_target_pairs={{0,4},{1,5},{2,6},{3,7},{4,0},{5,1},{6,2},{7,3},{8,12},{9,13},{10,... | collective-permute-start | bytes 1769480 | tf_op jit(solution)/shard_map/ppermute | solution.py:433
  111.4 4.6 %collective-permute-done.15.refs_2_ = bf16[2,240,384]{2,1,0:T(8,128)(2,1)S(1)} collective-permute-done((bf16[2,240,384]{2,1,0:T(8,128)(2,1)S(1)}, bf16[2,240,384]{2,1,0:T(8,128)(2,1)S(1)}, u32[]{:S(2)}, u32[]{:S(2)}) %collective-permute-start.15) | collective-permute-done | bytes 368672 | tf_op jit(solution)/shard_map/ppermute | solution.py:433
  116.7 2.7 %collective-permute-start.21 = (bf16[1,240,384]{2,1,0:T(8,128)(2,1)S(1)}, bf16[1,240,384]{2,1,0:T(8,128)(2,1)S(1)}, u32[]{:S(2)}, u32[]{:S(2)}) collective-permute-start(bf16[1,240,384]{2,1,0:T(8,128)(2,1)S(1)} %shard_map.355.refs_4_), channel_id=1, source_target_pairs={{0,16},{1,17},{2,18},{3,19},{4,20},{5,21},{6,22},{7,23},{8,24},{9,... | collective-permute-start | bytes 552968 | tf_op jit(solution)/shard_map/ppermute | solution.py:433
  119.8 1.6 %collective-permute-start.13 = (bf16[128,1152]{1,0:T(8,128)(2,1)S(1)}, bf16[128,1152]{1,0:T(8,128)(2,1)S(1)}, u32[]{:S(2)}, u32[]{:S(2)}) collective-permute-start(bf16[128,1152]{1,0:T(8,128)(2,1)S(1)} %get-tuple-element.120.refs_3_), channel_id=1, source_target_pairs={{0,8},{1,9},{2,10},{3,11},{4,12},{5,13},{6,14},{7,15},{8,0},{9,1},... | collective-permute-start | bytes 884744 | tf_op jit(solution)/shard_map/ppermute | solution.py:433
  121.4 3.8 %collective-permute-done.21 = bf16[1,240,384]{2,1,0:T(8,128)(2,1)S(1)} collective-permute-done((bf16[1,240,384]{2,1,0:T(8,128)(2,1)S(1)}, bf16[1,240,384]{2,1,0:T(8,128)(2,1)S(1)}, u32[]{:S(2)}, u32[]{:S(2)}) %collective-permute-start.21) | collective-permute-done | bytes 184352 | tf_op jit(solution)/shard_map/ppermute | solution.py:433
  127.5 1.1 collective-permute-done.13.refs_1_
  129.2 1.3 collective-permute-start.16
  130.5 1.4 collective-permute-start.19
  132.0 1.7 %collective-permute-start.20 = (bf16[48,384]{1,0:T(8,128)(2,1)S(1)}, bf16[48,384]{1,0:T(8,128)(2,1)S(1)}, u32[]{:S(2)}, u32[]{:S(2)}) collective-permute-start(bf16[48,384]{1,0:T(8,128)(2,1)S(1)} %get-tuple-element.127), channel_id=1, source_target_pairs={{0,17},{1,16},{2,19},{3,18},{4,21},{5,20},{6,23},{7,22},{8,25},{9,... | collective-permute-start | bytes 110600 | tf_op jit(solution)/shard_map/ppermute | solution.py:433
  133.7 2.0 %shard_map.358.refs_5_ = bf16[320,768]{1,0:T(8,128)(2,1)} custom-call(s32[7]{0:T(128)S(1)} %stack.58.place_ref, f32[320,768]{1,0:T(8,128)S(1)} %get-tuple-element.108.refs_0_, bf16[320,768]{1,0:T(8,128)(2,1)S(1)} %collective-permute-done.11.refs_1_, bf16[320,768]{1,0:T(8,128)(2,1)S(1)} %bitcast.32, f32[320,768]{1,0:T(8,128)S(1)} %get-tuple-element.117.refs_3_, ...), custom_call_target="tpu_custom_call" | custom-call | flops 2300000000 | bytes 1 | tf_op jit(solution)/shard_map/pallas_call | solution.py:492
  136.4 1.0 copy-done
  138.1 0.8 collective-permute-start.22
  139.5 3.3 %collective-permute-start.18 = (bf16[32,1024]{1,0:T(8,128)(2,1)S(1)}, bf16[32,1024]{1,0:T(8,128)(2,1)S(1)}, u32[]{:S(2)}, u32[]{:S(2)}) collective-permute-start(bf16[32,1024]{1,0:T(8,128)(2,1)S(1)} %shard_map.360.refs_0_.refs_4_), channel_id=1, source_target_pairs={{0,1},{1,0},{2,3},{3,2},{4,5},{5,4},{6,7},{7,6},{8,9},{9,8},{10,11... | collective-permute-start | bytes 196616 | tf_op jit(solution)/shard_map/ppermute | solution.py:433
  143.4 1.2 shard_map.362
  145.0 1.6 %shard_map.361 = (f32[12,2212]{1,0:T(8,128)}, f32[768]{0:T(1024)}, f32[768]{0:T(1024)}, f32[768]{0:T(1024)}, f32[768]{0:T(1024)}, /*index=5*/f32[768]{0:T(1024)}...) custom-call(s32[7]{0:T(128)S(1)} %stack.58.place_ref, ...), custom_call_target="tpu_custom_call" | custom-call | flops 11500000 | bytes 1 | tf_op jit(solution)/shard_map/pallas_call | solution.py:492
  146.7 0.8 add_bitcast_fusion
  (110 shorter events, 14.4 us)
Async XLA Ops:
  0.7 14.5 %collective-permute-start = (bf16[320,768]{1,0:T(8,128)(2,1)}, bf16[320,768]{1,0:T(8,128)(2,1)S(1)}, u32[]{:S(2)}, u32[]{:S(2)}) collective-permute-start(bf16[320,768]{1,0:T(8,128)(2,1)} %bitcast.29), channel_id=1, source_target_pairs={{0,1},{1,0},{2,3},{3,2},{4,5},{5,4},{6,7},{7,6},{8,9},{9,8},{10,11... | collective-permute-start | bytes 1474568 | tf_op jit(solution)/shard_map/ppermute | solution.py:433
  4.7 2.5 %copy-start.25 = (s32[1,320]{1,0:T(1,128)S(1)}, s32[1,320]{1,0:T(1,128)}, u32[]{:S(2)}) copy-start(s32[1,320]{1,0:T(1,128)} %param.21) | copy-start | bytes 3844
  4.7 2.5 %copy-start.15 = (f32[768]{0:T(1024)S(1)}, f32[768]{0:T(1024)}, u32[]{:S(2)}) copy-start(f32[768]{0:T(1024)} %param.23) | copy-start | bytes 9220
  4.7 2.5 %copy-start.16 = (f32[768]{0:T(1024)S(1)}, f32[768]{0:T(1024)}, u32[]{:S(2)}) copy-start(f32[768]{0:T(1024)} %param.24) | copy-start | bytes 9220
  4.7 2.6 %copy-start.17 = (f32[768]{0:T(1024)S(1)}, f32[768]{0:T(1024)}, u32[]{:S(2)}) copy-start(f32[768]{0:T(1024)} %param.30) | copy-start | bytes 9220
  4.7 2.6 %copy-start.18 = (f32[768]{0:T(1024)S(1)}, f32[768]{0:T(1024)}, u32[]{:S(2)}) copy-start(f32[768]{0:T(1024)} %param.31) | copy-start | bytes 9220
  4.7 2.6 %copy-start.19 = (f32[768]{0:T(1024)S(1)}, f32[768]{0:T(1024)}, u32[]{:S(2)}) copy-start(f32[768]{0:T(1024)} %param.32) | copy-start | bytes 9220
  4.7 2.6 %copy-start.20 = (f32[768]{0:T(1024)S(1)}, f32[768]{0:T(1024)}, u32[]{:S(2)}) copy-start(f32[768]{0:T(1024)} %param.33) | copy-start | bytes 9220
  4.7 2.6 %copy-start.21 = (f32[768]{0:T(1024)S(1)}, f32[768]{0:T(1024)}, u32[]{:S(2)}) copy-start(f32[768]{0:T(1024)} %param.37) | copy-start | bytes 9220
  4.7 2.6 %copy-start.22 = (f32[768]{0:T(1024)S(1)}, f32[768]{0:T(1024)}, u32[]{:S(2)}) copy-start(f32[768]{0:T(1024)} %param.38) | copy-start | bytes 9220
  4.8 2.6 %copy-start.23 = (f32[768]{0:T(1024)S(1)}, f32[768]{0:T(1024)}, u32[]{:S(2)}) copy-start(f32[768]{0:T(1024)} %param.26) | copy-start | bytes 9220
  4.8 2.6 %copy-start.24 = (f32[768]{0:T(1024)S(1)}, f32[768]{0:T(1024)}, u32[]{:S(2)}) copy-start(f32[768]{0:T(1024)} %param.27) | copy-start | bytes 9220
  4.8 2.7 %copy-start.4 = (bf16[1,320,768]{2,1,0:T(8,128)(2,1)S(1)}, bf16[1,320,768]{2,1,0:T(8,128)(2,1)}, u32[]{:S(2)}) copy-start(bf16[1,320,768]{2,1,0:T(8,128)(2,1)} %param.20) | copy-start | bytes 1474564
  9.5 2.5 %copy-start.14 = (bf16[1,320,768]{2,1,0:T(8,128)(2,1)S(1)}, bf16[1,320,768]{2,1,0:T(8,128)(2,1)}, u32[]{:S(2)}) copy-start(bf16[1,320,768]{2,1,0:T(8,128)(2,1)} %param.22) | copy-start | bytes 1474564
  9.5 5.6 %copy-start.2 = (bf16[768,2304]{1,0:T(8,128)(2,1)S(1)}, bf16[768,2304]{1,0:T(8,128)(2,1)}, u32[]{:S(2)}) copy-start(bf16[768,2304]{1,0:T(8,128)(2,1)} %refs_2_.8) | copy-start | bytes 10616836
  15.1 2.5 %copy-start.7 = (f32[24,1280]{1,0:T(8,128)S(1)}, f32[24,1280]{1,0:T(8,128)}, u32[]{:S(2)}) copy-start(f32[24,1280]{1,0:T(8,128)} %constant.14.clone.refs_2_.refs_7_) | copy-start | bytes 368644
  15.1 2.5 %copy-start.11 = (f32[12,2,1280]{2,1,0:T(2,128)S(1)}, f32[12,2,1280]{2,1,0:T(2,128)}, u32[]{:S(2)}) copy-start(f32[12,2,1280]{2,1,0:T(2,128)} %copy-done.10) | copy-start | bytes 368644
  15.1 13.4 %slice-start.2 = ((s8[4718592]{0:T(1024)(128)(4,1)}), s8[4194304]{0:T(1024)(128)(4,1)S(1)}, s32[]{:S(2)}) async-start(s8[4718592]{0:T(1024)(128)(4,1)} %bitcast.27), calls=%async_computation.2 | async-start | bytes 8388608
  17.6 10.9 %slice-start.3 = ((s8[4718592]{0:T(1024)(128)(4,1)}), s8[524288]{0:T(1024)(128)(4,1)S(1)}, s32[]{:S(2)}) async-start(s8[4718592]{0:T(1024)(128)(4,1)} %bitcast.27), calls=%async_computation.3 | async-start | bytes 1048576
  26.6 5.0 %copy-start.8 = (bf16[6,640,640]{2,1,0:T(8,128)(2,1)}, bf16[6,640,640]{2,1,0:T(8,128)(2,1)S(1)}, u32[]{:S(2)}) copy-start(bf16[6,640,640]{2,1,0:T(8,128)(2,1)S(1)} %get-tuple-element.97.refs_1_) | copy-start | bytes 14745604
  26.6 7.3 %copy-start.12 = (bf16[320,384]{1,0:T(8,128)(2,1)}, bf16[320,384]{1,0:T(8,128)(2,1)S(1)}, u32[]{:S(2)}) copy-start(bf16[320,384]{1,0:T(8,128)(2,1)S(1)} %get-tuple-element.81.refs_1_.refs_2_) | copy-start | bytes 737284
  26.6 7.3 %slice-start = ((s8[4718592]{0:T(1024)(128)(4,1)}), s8[4194304]{0:T(1024)(128)(4,1)S(1)}, s32[]{:S(2)}) async-start(s8[4718592]{0:T(1024)(128)(4,1)} %bitcast.25), calls=%async_computation | async-start | bytes 8388608
  26.7 7.2 %slice-start.1 = ((s8[4718592]{0:T(1024)(128)(4,1)}), s8[524288]{0:T(1024)(128)(4,1)S(1)}, s32[]{:S(2)}) async-start(s8[4718592]{0:T(1024)(128)(4,1)} %bitcast.25), calls=%async_computation.1 | async-start | bytes 1048576
  26.7 7.2 %copy-start.3 = (bf16[768,768]{1,0:T(8,128)(2,1)S(1)}, bf16[768,768]{1,0:T(8,128)(2,1)}, u32[]{:S(2)}) copy-start(bf16[768,768]{1,0:T(8,128)(2,1)} %refs_8_.1) | copy-start | bytes 3538948
  26.7 7.2 %copy-start.6 = (f32[3072]{0:T(1024)S(1)}, f32[3072]{0:T(1024)}, u32[]{:S(2)}) copy-start(f32[3072]{0:T(1024)} %param.35) | copy-start | bytes 36868
  26.7 7.2 %collective-permute-start.1 = (bf16[320,384]{1,0:T(8,128)(2,1)S(1)}, bf16[320,384]{1,0:T(8,128)(2,1)S(1)}, u32[]{:S(2)}, u32[]{:S(2)}) collective-permute-start(bf16[320,384]{1,0:T(8,128)(2,1)S(1)} %get-tuple-element.82.refs_3_), channel_id=1, source_target_pairs={{0,1},{1,0},{2,3},{3,2},{4,5},{5,4},{6,7},{7,6},{8,9},{9,8},{10,11... | collective-permute-start | bytes 737288 | tf_op jit(solution)/shard_map/ppermute | solution.py:433
  44.4 6.8 %collective-permute-start.2 = (bf16[4,2,2,192,384]{4,3,2,1,0:T(8,128)(2,1)S(1)}, bf16[4,2,2,192,384]{4,3,2,1,0:T(8,128)(2,1)S(1)}, u32[]{:S(2)}, u32[]{:S(2)}) collective-permute-start(bf16[4,2,2,192,384]{4,3,2,1,0:T(8,128)(2,1)S(1)} %get-tuple-element.88.refs_9_), channel_id=1, source_target_pairs={{0,2},{1,3},{2,0},{3,1},{4,6},{5,7},{6,4},{7,5},{8,10},{9,11},{10,... | collective-permute-start | bytes 7077896 | tf_op jit(solution)/shard_map/ppermute | solution.py:433
  49.7 9.8 %collective-permute-start.5 = (bf16[320,384]{1,0:T(8,128)(2,1)S(1)}, bf16[320,384]{1,0:T(8,128)(2,1)S(1)}, u32[]{:S(2)}, u32[]{:S(2)}) collective-permute-start(bf16[320,384]{1,0:T(8,128)(2,1)S(1)} %get-tuple-element.91.refs_2_), channel_id=1, source_target_pairs={{0,1},{1,0},{2,3},{3,2},{4,5},{5,4},{6,7},{7,6},{8,9},{9,8},{10,11... | collective-permute-start | bytes 737288 | tf_op jit(solution)/shard_map/ppermute | solution.py:433
  52.2 32.8 %collective-permute-start.3 = (bf16[8,192,384]{2,1,0:T(8,128)(2,1)S(1)}, bf16[8,192,384]{2,1,0:T(8,128)(2,1)S(1)}, u32[]{:S(2)}, u32[]{:S(2)}) collective-permute-start(bf16[8,192,384]{2,1,0:T(8,128)(2,1)S(1)} %bitcast.22), channel_id=1, source_target_pairs={{0,4},{1,5},{2,6},{3,7},{4,0},{5,1},{6,2},{7,3},{8,12},{9,13},{10,... | collective-permute-start | bytes 3538952 | tf_op jit(solution)/shard_map/ppermute | solution.py:433
  53.8 5.8 %copy-start.13 = (bf16[320,384]{1,0:T(8,128)(2,1)S(1)}, bf16[320,384]{1,0:T(8,128)(2,1)}, u32[]{:S(2)}) copy-start(bf16[320,384]{1,0:T(8,128)(2,1)} %copy-done.12) | copy-start | bytes 737284
  59.5 6.4 %collective-permute-start.4 = (bf16[16,48,1920]{2,1,0:T(8,128)(2,1)S(1)}, bf16[16,48,1920]{2,1,0:T(8,128)(2,1)S(1)}, u32[]{:S(2)}, u32[]{:S(2)}) collective-permute-start(bf16[16,48,1920]{2,1,0:T(8,128)(2,1)S(1)} %get-tuple-element.96.refs_8_), channel_id=1, source_target_pairs={{0,2},{1,3},{2,0},{3,1},{4,6},{5,7},{6,4},{7,5},{8,10},{9,11},{10,... | collective-permute-start | bytes 8847368 | tf_op jit(solution)/shard_map/ppermute | solution.py:433
  66.7 20.0 %collective-permute-start.6 = (bf16[8,48,384]{2,1,0:T(8,128)(2,1)S(1)}, bf16[8,48,384]{2,1,0:T(8,128)(2,1)S(1)}, u32[]{:S(2)}, u32[]{:S(2)}) collective-permute-start(bf16[8,48,384]{2,1,0:T(8,128)(2,1)S(1)} %shard_map.342.refs_2_), channel_id=1, source_target_pairs={{0,4},{1,5},{2,6},{3,7},{4,0},{5,1},{6,2},{7,3},{8,12},{9,13},{10,... | collective-permute-start | bytes 884744 | tf_op jit(solution)/shard_map/ppermute | solution.py:433
  68.3 29.2 %collective-permute-start.8 = (bf16[8,48,1536]{2,1,0:T(8,128)(2,1)S(1)}, bf16[8,48,1536]{2,1,0:T(8,128)(2,1)S(1)}, u32[]{:S(2)}, u32[]{:S(2)}) collective-permute-start(bf16[8,48,1536]{2,1,0:T(8,128)(2,1)S(1)} %shard_map.343.refs_9_), channel_id=1, source_target_pairs={{0,8},{1,9},{2,10},{3,11},{4,12},{5,13},{6,14},{7,15},{8,0},{9,1},... | collective-permute-start | bytes 3538952 | tf_op jit(solution)/shard_map/ppermute | solution.py:433
  85.0 10.2 %collective-permute-start.9 = (bf16[8,48,1152]{2,1,0:T(8,128)(2,1)S(1)}, bf16[8,48,1152]{2,1,0:T(8,128)(2,1)S(1)}, u32[]{:S(2)}, u32[]{:S(2)}) collective-permute-start(bf16[8,48,1152]{2,1,0:T(8,128)(2,1)S(1)} %get-tuple-element.104.refs_12_), channel_id=1, source_target_pairs={{0,2},{1,3},{2,0},{3,1},{4,6},{5,7},{6,4},{7,5},{8,10},{9,11},{10,... | collective-permute-start | bytes 2654216 | tf_op jit(solution)/shard_map/ppermute | solution.py:433
  88.5 17.9 %collective-permute-start.7 = (bf16[4,240,384]{2,1,0:T(8,128)(2,1)S(1)}, bf16[4,240,384]{2,1,0:T(8,128)(2,1)S(1)}, u32[]{:S(2)}, u32[]{:S(2)}) collective-permute-start(bf16[4,240,384]{2,1,0:T(8,128)(2,1)S(1)} %get-tuple-element.105.refs_5_), channel_id=1, source_target_pairs={{0,1},{1,0},{2,3},{3,2},{4,5},{5,4},{6,7},{7,6},{8,9},{9,8},{10,11... | collective-permute-start | bytes 2211848 | tf_op jit(solution)/shard_map/ppermute | solution.py:433
  93.9 1.3 collective-permute-start.10
  96.0 14.7 %collective-permute-start.12 = (bf16[224,1152]{1,0:T(8,128)(2,1)S(1)}, bf16[224,1152]{1,0:T(8,128)(2,1)S(1)}, u32[]{:S(2)}, u32[]{:S(2)}) collective-permute-start(bf16[224,1152]{1,0:T(8,128)(2,1)S(1)} %get-tuple-element.116.refs_3_), channel_id=1, source_target_pairs={{0,4},{1,5},{2,6},{3,7},{4,0},{5,1},{6,2},{7,3},{8,12},{9,13},{10,... | collective-permute-start | bytes 1548296 | tf_op jit(solution)/shard_map/ppermute | solution.py:433
  107.0 9.0 %collective-permute-start.15 = (bf16[2,240,384]{2,1,0:T(8,128)(2,1)S(1)}, bf16[2,240,384]{2,1,0:T(8,128)(2,1)S(1)}, u32[]{:S(2)}, u32[]{:S(2)}) collective-permute-start(bf16[2,240,384]{2,1,0:T(8,128)(2,1)S(1)} %shard_map.352.refs_1_), channel_id=1, source_target_pairs={{0,8},{1,9},{2,10},{3,11},{4,12},{5,13},{6,14},{7,15},{8,0},{9,1},... | collective-permute-start | bytes 1105928 | tf_op jit(solution)/shard_map/ppermute | solution.py:433
  108.6 16.7 %collective-permute-start.14 = (bf16[4,48,1536]{2,1,0:T(8,128)(2,1)S(1)}, bf16[4,48,1536]{2,1,0:T(8,128)(2,1)S(1)}, u32[]{:S(2)}, u32[]{:S(2)}) collective-permute-start(bf16[4,48,1536]{2,1,0:T(8,128)(2,1)S(1)} %shard_map.351.refs_2_), channel_id=1, source_target_pairs={{0,4},{1,5},{2,6},{3,7},{4,0},{5,1},{6,2},{7,3},{8,12},{9,13},{10,... | collective-permute-start | bytes 1769480 | tf_op jit(solution)/shard_map/ppermute | solution.py:433
  116.7 8.6 %collective-permute-start.21 = (bf16[1,240,384]{2,1,0:T(8,128)(2,1)S(1)}, bf16[1,240,384]{2,1,0:T(8,128)(2,1)S(1)}, u32[]{:S(2)}, u32[]{:S(2)}) collective-permute-start(bf16[1,240,384]{2,1,0:T(8,128)(2,1)S(1)} %shard_map.355.refs_4_), channel_id=1, source_target_pairs={{0,16},{1,17},{2,18},{3,19},{4,20},{5,21},{6,22},{7,23},{8,24},{9,... | collective-permute-start | bytes 552968 | tf_op jit(solution)/shard_map/ppermute | solution.py:433
  119.3 14.4 %collective-permute-start.11 = (bf16[320,768]{1,0:T(8,128)(2,1)S(1)}, bf16[320,768]{1,0:T(8,128)(2,1)S(1)}, u32[]{:S(2)}, u32[]{:S(2)}) collective-permute-start(bf16[320,768]{1,0:T(8,128)(2,1)S(1)} %shard_map.353.refs_2_), channel_id=1, source_target_pairs={{0,1},{1,0},{2,3},{3,2},{4,5},{5,4},{6,7},{7,6},{8,9},{9,8},{10,11... | collective-permute-start | bytes 1474568 | tf_op jit(solution)/shard_map/ppermute | solution.py:433
  119.8 8.7 %collective-permute-start.13 = (bf16[128,1152]{1,0:T(8,128)(2,1)S(1)}, bf16[128,1152]{1,0:T(8,128)(2,1)S(1)}, u32[]{:S(2)}, u32[]{:S(2)}) collective-permute-start(bf16[128,1152]{1,0:T(8,128)(2,1)S(1)} %get-tuple-element.120.refs_3_), channel_id=1, source_target_pairs={{0,8},{1,9},{2,10},{3,11},{4,12},{5,13},{6,14},{7,15},{8,0},{9,1},... | collective-permute-start | bytes 884744 | tf_op jit(solution)/shard_map/ppermute | solution.py:433
  126.0 10.4 %collective-permute-start.17 = (bf16[2,48,1536]{2,1,0:T(8,128)(2,1)S(1)}, bf16[2,48,1536]{2,1,0:T(8,128)(2,1)S(1)}, u32[]{:S(2)}, u32[]{:S(2)}) collective-permute-start(bf16[2,48,1536]{2,1,0:T(8,128)(2,1)S(1)} %shard_map.356.refs_2_), channel_id=1, source_target_pairs={{0,1},{1,0},{2,3},{3,2},{4,5},{5,4},{6,7},{7,6},{8,9},{9,8},{10,11... | collective-permute-start | bytes 884744 | tf_op jit(solution)/shard_map/ppermute | solution.py:433
  129.2 9.7 %collective-permute-start.16 = (bf16[80,1024]{1,0:T(8,128)(2,1)S(1)}, bf16[80,1024]{1,0:T(8,128)(2,1)S(1)}, u32[]{:S(2)}, u32[]{:S(2)}) collective-permute-start(bf16[80,1024]{1,0:T(8,128)(2,1)S(1)} %get-tuple-element.121.refs_5_), channel_id=1, source_target_pairs={{0,16},{1,17},{2,18},{3,19},{4,20},{5,21},{6,22},{7,23},{8,24},{9,... | collective-permute-start | bytes 491528 | tf_op jit(solution)/shard_map/ppermute | solution.py:433
  130.5 12.9 %collective-permute-start.19 = (bf16[48,384]{1,0:T(8,128)(2,1)S(1)}, bf16[48,384]{1,0:T(8,128)(2,1)S(1)}, u32[]{:S(2)}, u32[]{:S(2)}) collective-permute-start(bf16[48,384]{1,0:T(8,128)(2,1)S(1)} %get-tuple-element.126), channel_id=1, source_target_pairs={{0,1},{1,0},{2,3},{3,2},{4,5},{5,4},{6,7},{7,6},{8,9},{9,8},{10,11... | collective-permute-start | bytes 110600 | tf_op jit(solution)/shard_map/ppermute | solution.py:433
  132.0 11.4 %collective-permute-start.20 = (bf16[48,384]{1,0:T(8,128)(2,1)S(1)}, bf16[48,384]{1,0:T(8,128)(2,1)S(1)}, u32[]{:S(2)}, u32[]{:S(2)}) collective-permute-start(bf16[48,384]{1,0:T(8,128)(2,1)S(1)} %get-tuple-element.127), channel_id=1, source_target_pairs={{0,17},{1,16},{2,19},{3,18},{4,21},{5,20},{6,23},{7,22},{8,25},{9,... | collective-permute-start | bytes 110600 | tf_op jit(solution)/shard_map/ppermute | solution.py:433
  138.1 8.6 %collective-permute-start.22 = (bf16[1,48,1536]{2,1,0:T(8,128)(2,1)S(1)}, bf16[1,48,1536]{2,1,0:T(8,128)(2,1)S(1)}, u32[]{:S(2)}, u32[]{:S(2)}) collective-permute-start(bf16[1,48,1536]{2,1,0:T(8,128)(2,1)S(1)} %shard_map.359.refs_2_), channel_id=1, source_target_pairs={{0,16},{1,17},{2,18},{3,19},{4,20},{5,21},{6,22},{7,23},{8,24},{9,... | collective-permute-start | bytes 442376 | tf_op jit(solution)/shard_map/ppermute | solution.py:433
  139.5 5.5 %collective-permute-start.18 = (bf16[32,1024]{1,0:T(8,128)(2,1)S(1)}, bf16[32,1024]{1,0:T(8,128)(2,1)S(1)}, u32[]{:S(2)}, u32[]{:S(2)}) collective-permute-start(bf16[32,1024]{1,0:T(8,128)(2,1)S(1)} %shard_map.360.refs_0_.refs_4_), channel_id=1, source_target_pairs={{0,1},{1,0},{2,3},{3,2},{4,5},{5,4},{6,7},{7,6},{8,9},{9,8},{10,11... | collective-permute-start | bytes 196616 | tf_op jit(solution)/shard_map/ppermute | solution.py:433
  (5 other events, 7.0 us)
